TPU v7x, 32 devices: a whole 2x2x4 slice. The times are simulated.
32 devices in a mesh: dp: 2 (over x), seq: 4 (over z), expert: 4 (over y, core).
Axes of the slice: x: 2, y: 2, z: 4, core: 2. Of those that a mesh axis runs over, the one named last changes fastest.
Arguments:
- tokens: bfloat16 [32, 1024, 1152], P(('dp', 'expert'), 'seq'), may hold values from -6 to 6
- segment_ids: int32 [32, 1024], P(('dp', 'expert'), 'seq'), may hold values from 0 to 7, never falling along the last dimension, each value on 1 to 512 neighbouring positions
- routes: int32 [32, 1024, 1], P(('dp', 'expert'), 'seq'), may hold values from 0 to 7; in each aligned block of 256 rows (0 to 255, 256 to 511, ..., all dimensions but the last counted through in order) at most 48 rows name the same one
- keep_mask: int32 [32, 1024], P(('dp', 'expert'), 'seq'), may hold values 0 or 1
- out_grad: bfloat16 [32, 1024, 1152], P(('dp', 'expert'), 'seq'), may hold values from -6 to 6
- norm_one: bfloat16 [1152], replicated, may hold values from 0.5 to 1.5
- in_proj: bfloat16 [1152, 4608], P(None, ('dp', 'seq', 'expert')), may hold values from -0.1875 to 0.1875
- conv_weight: bfloat16 [4, 2304], P(None, ('dp', 'seq', 'expert')), may hold values from -3 to 3
- conv_bias: bfloat16 [2304], P(('dp', 'seq', 'expert')), may hold values from -3 to 3
- x_proj: bfloat16 [2304, 104], P(('dp', 'seq', 'expert')), may hold values from -0.125 to 0.125
- dt_proj: bfloat16 [72, 2304], P(None, ('dp', 'seq', 'expert')), may hold values from -0.75 to 0.75
- dt_bias: bfloat16 [2304], P(('dp', 'seq', 'expert')), may hold values from -7 to -2
- a_log: bfloat16 [16, 2304], P(None, ('dp', 'seq', 'expert')), may hold values from -4 to 2
- d_skip: bfloat16 [2304], P(('dp', 'seq', 'expert')), may hold values from 0.5 to 1.5
- out_proj: bfloat16 [2304, 1152], P(('dp', 'seq', 'expert')), may hold values from -0.5 to 0.5
- norm_two: bfloat16 [1152], replicated, may hold values from 0.5 to 1.5
- router: bfloat16 [1152, 8], replicated, may hold values from -0.125 to 0.125
- expert_up: bfloat16 [8, 1152, 3072], P('expert', None, ('dp', 'seq')), may hold values from -0.1875 to 0.1875
- expert_down: bfloat16 [8, 3072, 1152], P('expert', ('dp', 'seq')), may hold values from -0.4375 to 0.4375
Outputs:
- out_tokens: bfloat16 [32, 1024, 1152], P(('dp', 'expert'), 'seq')
- grad_tokens: float32 [32, 1024, 1152], P(('dp', 'expert'), 'seq')
- grad_norm_one: float32 [1152], replicated
- grad_in_proj: float32 [1152, 4608], P(None, ('dp', 'seq', 'expert'))
- grad_conv_weight: float32 [4, 2304], P(None, ('dp', 'seq', 'expert'))
- grad_conv_bias: float32 [2304], P(('dp', 'seq', 'expert'))
- grad_x_proj: float32 [2304, 104], P(('dp', 'seq', 'expert'))
- grad_dt_proj: float32 [72, 2304], P(None, ('dp', 'seq', 'expert'))
- grad_dt_bias: float32 [2304], P(('dp', 'seq', 'expert'))
- grad_a_log: float32 [16, 2304], P(None, ('dp', 'seq', 'expert'))
- grad_d_skip: float32 [2304], P(('dp', 'seq', 'expert'))
- grad_out_proj: float32 [2304, 1152], P(('dp', 'seq', 'expert'))
- grad_norm_two: float32 [1152], replicated
- grad_router: float32 [1152, 8], replicated
- grad_expert_up: float32 [8, 1152, 3072], P('expert', None, ('dp', 'seq'))
- grad_expert_down: float32 [8, 3072, 1152], P('expert', ('dp', 'seq'))
Inputs may be any that keep to these rules, and one draw needn't show every extreme that they name: `segment_ids`: along each sequence the ids never fall. `routes`: in each aligned block of 256 positions of a sequence no expert is named more than 48 times.
All inputs are finite; a program needn't handle non-finite values. No bound on the sum of `keep_mask` on one device may be relied on, other than what follows from the above.
Results may differ from a plain program's by a relative error of at most 0.011.
Values may be sent and summed in bfloat16 or wider, within the bound.
A program may use at most 384 MiB of HBM per device.

v0:
```python
import jax
import jax.numpy as jnp
from jax import lax
from jax.sharding import PartitionSpec as P

D = 1152
DI = 2304
NSTATE = 16
DTR = 72
CONVK = 4
EXPERTS = 8
SEQ_MB = 2
MB = 2


norm_eps = 1e-05
block_len = 16


def shifted(value, axis, steps):
    count = lax.axis_size(axis)
    first, last = (max(0, -steps), min(count, count - steps))
    return lax.ppermute(value, axis, [(source, source + steps) for source in range(first, last)])


def carried_in(value, axis, combine, identity, reverse):
    peers, index = (lax.axis_size(axis), lax.axis_index(axis))
    everything = jax.tree.map(lambda part: lax.all_gather(part, axis), value)
    start = jax.tree.map(
        lambda part, zero: jnp.broadcast_to(jnp.asarray(zero, part.dtype), part.shape),
        value,
        identity,
    )

    def step(k, before):
        at = peers - 1 - k if reverse else k
        reached = at > index if reverse else at < index
        new = combine(before, jax.tree.map(lambda part: part[at], everything))
        return jax.tree.map(lambda a, b: jnp.where(reached, a, b), new, before)

    return lax.fori_loop(0, peers, step, start)


def rms_norm(values, gain_vec):
    inv_rms = lax.rsqrt(jnp.mean(values * values, axis=-1, keepdims=True) + norm_eps)
    return values * inv_rms * gain_vec


def gelu_tanh(values):
    return jax.nn.gelu(values, approximate=True)


def low_dot(formula, left_op, right_op):
    return jnp.einsum(formula, left_op, right_op, preferred_element_type=jnp.float32)


def exact_dot(formula, left_op, right_op):
    return jnp.einsum(
        formula,
        left_op,
        right_op,
        precision=lax.Precision.HIGHEST,
        preferred_element_type=jnp.float32,
    )


def conv_apply(extended, seg_ext, weight, bias_vec):
    length = extended.shape[1] - (CONVK - 1)
    current = seg_ext[:, CONVK - 1 :]
    summed = jnp.zeros((extended.shape[0], length, extended.shape[2]), jnp.float32) + bias_vec
    for offset in range(CONVK):
        same_seg = (seg_ext[:, offset : offset + length] == current).astype(jnp.float32)
        summed = (
            summed + weight[offset] * extended[:, offset : offset + length] * same_seg[..., None]
        )
    return summed


def chain_link(earlier, later):
    return (earlier[0] * later[0], later[0] * earlier[1] + later[1])


def chain_terms(xs_vals, delta_val, b_mat, keep_flag, a_mat):
    alive_pre = jnp.cumprod(keep_flag, axis=1)
    suffix = jnp.flip(jnp.cumprod(jnp.flip(keep_flag, 1), axis=1), 1)
    alive_post = jnp.concatenate([suffix[:, 1:], jnp.ones_like(suffix[:, :1])], axis=1)
    running = jnp.cumsum(delta_val, axis=1)
    decay_all = jnp.exp(a_mat * running[:, -1, :, None]) * alive_pre[:, -1, None, None]
    remaining = running[:, -1:, :] - running
    weighted = delta_val * xs_vals * alive_post[..., None]
    end_state = jnp.sum(
        jnp.exp(remaining[..., None] * a_mat) * weighted[..., None] * b_mat[:, :, None, :], axis=1
    )
    return (decay_all, end_state)


def start_grad(delta_val, c_mat, keep_flag, a_mat, grad_ssm):
    alive_pre = jnp.cumprod(keep_flag, axis=1)
    running = jnp.cumsum(delta_val, axis=1)
    weighted = grad_ssm * alive_pre[..., None]
    return jnp.sum(
        jnp.exp(running[..., None] * a_mat) * weighted[..., None] * c_mat[:, :, None, :], axis=1
    )


def ssm_local(xs_vals, delta_val, b_mat, c_mat, keep_flag, a_mat, start_state):
    seq_rows, length = (xs_vals.shape[0], xs_vals.shape[1])
    block_count = length // block_len

    def arrange(values):
        shaped = values.reshape((seq_rows, block_count, block_len) + values.shape[2:])
        return jnp.moveaxis(shaped, 1, 0)

    def token_step(state_now, token_in):
        xs_t, delta_t, b_t, c_t, keep_t = token_in
        decay_now = jnp.exp(delta_t[:, :, None] * a_mat) * keep_t[:, None, None]
        state_now = decay_now * state_now + (delta_t * xs_t)[:, :, None] * b_t[:, None, :]
        return (state_now, jnp.sum(state_now * c_t[:, None, :], axis=-1))

    def block_step(state_now, block_in):
        ordered = tuple((jnp.moveaxis(piece, 1, 0) for piece in block_in))
        state_end, outs = lax.scan(token_step, state_now, ordered)
        return (state_end, jnp.moveaxis(outs, 0, 1))

    end_state, outputs = lax.scan(
        jax.checkpoint(block_step),
        start_state,
        (arrange(xs_vals), arrange(delta_val), arrange(b_mat), arrange(c_mat), arrange(keep_flag)),
    )
    return (jnp.moveaxis(outputs, 0, 1).reshape(seq_rows, length, -1), end_state)


def slot_table(onehot, capacity):
    length = onehot.shape[1]
    below_mask = (jnp.arange(length)[None, :] < jnp.arange(length)[:, None]).astype(jnp.float32)
    counts = exact_dot("tu,sue->ste", below_mask, onehot)
    rank_vals = jnp.sum(counts * onehot, axis=-1)
    slot_hot = (rank_vals[..., None] == jnp.arange(capacity).astype(jnp.float32)).astype(
        jnp.float32
    )
    return onehot[..., None] * slot_hot[:, :, None, :]


def forward_micro(
    token_rows,
    seg_rows,
    route_rows,
    drop_rows,
    norm_one,
    norm_two,
    router,
    mixer,
    experts,
    capacity,
):
    (
        in_full,
        conv_full,
        cbias_full,
        xproj_full,
        dtproj_full,
        dtbias_full,
        alog_full,
        dskip_full,
        outproj_full,
    ) = mixer
    up_full, down_full = experts
    inputs = token_rows.astype(jnp.float32)
    normed_one = rms_norm(inputs, norm_one.astype(jnp.float32)).astype(jnp.bfloat16)
    mixed_all = low_dot("std,de->ste", normed_one, in_full)
    conv_in = mixed_all[..., :DI]
    gate_z = mixed_all[..., DI:]
    seg_float = seg_rows.astype(jnp.float32)
    rim_vals, rim_segs = shifted(
        (conv_in[:, -(CONVK - 1) :], seg_float[:, -(CONVK - 1) :]), "seq", 1
    )
    extended = jnp.concatenate([rim_vals, conv_in], axis=1)
    seg_ext = jnp.concatenate([rim_segs, seg_float], axis=1)
    conv_out = conv_apply(
        extended, seg_ext, conv_full.astype(jnp.float32), cbias_full.astype(jnp.float32)
    )
    xs_low = jax.nn.silu(conv_out).astype(jnp.bfloat16)
    xs_vals = xs_low.astype(jnp.float32)
    proj_out = low_dot("ste,ef->stf", xs_low, xproj_full)
    delta_in = proj_out[..., :DTR].astype(jnp.bfloat16)
    b_mat = proj_out[..., DTR : DTR + NSTATE]
    c_mat = proj_out[..., DTR + NSTATE :]
    delta_pre = low_dot("str,re->ste", delta_in, dtproj_full) + dtbias_full.astype(jnp.float32)
    delta_val = jax.nn.softplus(delta_pre)
    keep_flag = (seg_ext[:, CONVK - 1 :] == seg_ext[:, CONVK - 2 : -1]).astype(jnp.float32)
    a_mat = -jnp.exp(alog_full.astype(jnp.float32)).T
    decay_all, end_state = chain_terms(xs_vals, delta_val, b_mat, keep_flag, a_mat)
    _, start_state = carried_in(
        (decay_all, end_state),
        "seq",
        chain_link,
        (jnp.ones_like(decay_all), jnp.zeros_like(end_state)),
        False,
    )
    ssm_part, _ = ssm_local(xs_vals, delta_val, b_mat, c_mat, keep_flag, a_mat, start_state)
    ssm_out = ssm_part + dskip_full.astype(jnp.float32) * xs_vals
    branch = (ssm_out * jax.nn.silu(gate_z)).astype(jnp.bfloat16)
    first_sum = inputs + low_dot("ste,ed->std", branch, outproj_full)
    normed_two = rms_norm(first_sum, norm_two.astype(jnp.float32)).astype(jnp.bfloat16)
    probs_all = jax.nn.softmax(low_dot("std,de->ste", normed_two, router), axis=-1)
    onehot = (route_rows[..., None] == jnp.arange(EXPERTS, dtype=jnp.int32)).astype(jnp.float32)
    gate_raw = jnp.sum(probs_all * onehot, axis=-1)
    gate_val = gate_raw * drop_rows.astype(jnp.float32)
    placing = slot_table(onehot, capacity).astype(jnp.bfloat16)
    expert_devs = lax.axis_size("expert")
    seq_rows = token_rows.shape[0]
    sent_rows = (
        low_dot("stec,std->escd", placing, normed_two)
        .astype(jnp.bfloat16)
        .reshape(expert_devs, EXPERTS // expert_devs, seq_rows * capacity, D)
    )
    arrived = lax.all_to_all(sent_rows, "expert", split_axis=0, concat_axis=0, tiled=True)
    hidden_pre = low_dot("rlkd,ldf->rlkf", arrived, up_full)
    hidden = gelu_tanh(hidden_pre).astype(jnp.bfloat16)
    produced = low_dot("rlkf,lfd->rlkd", hidden, down_full).astype(jnp.bfloat16)
    returned = lax.all_to_all(produced, "expert", split_axis=0, concat_axis=0, tiled=True).reshape(
        EXPERTS, seq_rows, capacity, D
    )
    expert_rows = low_dot("stec,escd->std", placing, returned)
    output = first_sum + gate_val[..., None] * expert_rows
    kept_vals = (
        inputs,
        normed_one,
        gate_z,
        extended,
        seg_ext,
        conv_out,
        xs_low,
        delta_in,
        b_mat,
        c_mat,
        delta_pre,
        delta_val,
        keep_flag,
        a_mat,
        decay_all,
        start_state,
        ssm_out,
        branch,
        first_sum,
        normed_two,
        probs_all,
        onehot,
        gate_raw,
        placing,
        arrived,
        hidden_pre,
        hidden,
        expert_rows,
    )
    return (output, kept_vals)


def backward_micro(
    grad_rows, drop_rows, kept_vals, norm_one, norm_two, router, mixer, experts, capacity
):
    (
        in_full,
        conv_full,
        cbias_full,
        xproj_full,
        dtproj_full,
        dtbias_full,
        alog_full,
        dskip_full,
        outproj_full,
    ) = mixer
    up_full, down_full = experts
    (
        inputs,
        normed_one,
        gate_z,
        extended,
        seg_ext,
        conv_out,
        xs_low,
        delta_in,
        b_mat,
        c_mat,
        delta_pre,
        delta_val,
        keep_flag,
        a_mat,
        decay_all,
        start_state,
        ssm_out,
        branch,
        first_sum,
        normed_two,
        probs_all,
        onehot,
        gate_raw,
        placing,
        arrived,
        hidden_pre,
        hidden,
        expert_rows,
    ) = kept_vals
    seq_rows = grad_rows.shape[0]
    grad_final = grad_rows.astype(jnp.float32)
    drop_float = drop_rows.astype(jnp.float32)
    gate_val = gate_raw * drop_float
    grad_gate = jnp.sum(grad_final * expert_rows, axis=-1) * drop_float
    token_grad = (gate_val[..., None] * grad_final).astype(jnp.bfloat16)
    grad_sent = (
        low_dot("stec,std->escd", placing, token_grad).astype(jnp.bfloat16).reshape(arrived.shape)
    )
    grad_arrived = lax.all_to_all(grad_sent, "expert", split_axis=0, concat_axis=0, tiled=True)
    down_grad = low_dot("rlkf,rlkd->lfd", hidden, grad_arrived)
    grad_hidden = low_dot("rlkd,lfd->rlkf", grad_arrived, down_full)
    _, gelu_back = jax.vjp(gelu_tanh, hidden_pre)
    grad_pre = gelu_back(grad_hidden)[0].astype(jnp.bfloat16)
    up_grad = low_dot("rlkd,rlkf->ldf", arrived, grad_pre)
    grad_input = low_dot("rlkf,ldf->rlkd", grad_pre, up_full)
    grad_back = (
        lax.all_to_all(
            grad_input.astype(jnp.bfloat16), "expert", split_axis=0, concat_axis=0, tiled=True
        )
        .astype(grad_input.dtype)
        .reshape(EXPERTS, seq_rows, capacity, D)
    )
    grad_normed = exact_dot("stec,escd->std", placing.astype(jnp.float32), grad_back)
    grad_logits = (grad_gate * gate_raw)[..., None] * (onehot - probs_all)
    router_grad = exact_dot("std,ste->de", normed_two.astype(jnp.float32), grad_logits)
    grad_normed = grad_normed + exact_dot("ste,de->std", grad_logits, router.astype(jnp.float32))
    _, norm_two_back = jax.vjp(rms_norm, first_sum, norm_two.astype(jnp.float32))
    grad_first_part, gain_two_grad = norm_two_back(grad_normed)
    grad_first = grad_final + grad_first_part
    grad_first_low = grad_first.astype(jnp.bfloat16)
    outproj_grad = low_dot("ste,std->ed", branch, grad_first_low)
    grad_branch = low_dot("std,ed->ste", grad_first_low, outproj_full)
    grad_ssm = grad_branch * jax.nn.silu(gate_z)
    _, silu_back = jax.vjp(jax.nn.silu, gate_z)
    grad_z = silu_back(grad_branch * ssm_out)[0]
    xs_vals = xs_low.astype(jnp.float32)
    dskip_grad = jnp.sum(grad_ssm * xs_vals, axis=(0, 1))
    direct = start_grad(delta_val, c_mat, keep_flag, a_mat, grad_ssm)
    _, end_grad = carried_in(
        (decay_all, direct),
        "seq",
        chain_link,
        (jnp.ones_like(decay_all), jnp.zeros_like(direct)),
        True,
    )

    def local_scan(xs_in, delta_arg, b_in, c_in, a_in):
        return ssm_local(xs_in, delta_arg, b_in, c_in, keep_flag, a_in, start_state)

    _, ssm_back = jax.vjp(local_scan, xs_vals, delta_val, b_mat, c_mat, a_mat)
    grad_xs_part, grad_delta, grad_b, grad_c, grad_a = ssm_back((grad_ssm, end_grad))
    alog_grad = (grad_a * a_mat).T
    grad_xs = grad_xs_part + grad_ssm * dskip_full.astype(jnp.float32)
    grad_dpre = grad_delta * jax.nn.sigmoid(delta_pre)
    dtbias_grad = jnp.sum(grad_dpre, axis=(0, 1))
    grad_dpre_low = grad_dpre.astype(jnp.bfloat16)
    dtproj_grad = low_dot("str,ste->re", delta_in, grad_dpre_low)
    grad_delta_in = low_dot("ste,re->str", grad_dpre_low, dtproj_full)
    grad_proj = jnp.concatenate([grad_delta_in, grad_b, grad_c], axis=-1).astype(jnp.bfloat16)
    xproj_grad = low_dot("ste,stf->ef", xs_low, grad_proj)
    grad_xs = grad_xs + low_dot("stf,ef->ste", grad_proj, xproj_full)
    _, act_back = jax.vjp(jax.nn.silu, conv_out)
    grad_conv_out = act_back(grad_xs)[0]

    def conv_local(ext_in, weight_in, bias_in):
        return conv_apply(ext_in, seg_ext, weight_in, bias_in)

    _, conv_back = jax.vjp(
        conv_local, extended, conv_full.astype(jnp.float32), cbias_full.astype(jnp.float32)
    )
    grad_ext, conv_grad, cbias_grad = conv_back(grad_conv_out)
    rim_grad = shifted(grad_ext[:, : CONVK - 1].astype(jnp.bfloat16), "seq", -1).astype(jnp.float32)
    length = grad_ext.shape[1] - (CONVK - 1)
    grad_conv_in = grad_ext[:, CONVK - 1 :] + jnp.pad(
        rim_grad, ((0, 0), (length - (CONVK - 1), 0), (0, 0))
    )
    grad_mixed = jnp.concatenate([grad_conv_in, grad_z], axis=-1).astype(jnp.bfloat16)
    inproj_grad = low_dot("std,ste->de", normed_one, grad_mixed)
    grad_normed_one = low_dot("ste,de->std", grad_mixed, in_full)
    _, norm_one_back = jax.vjp(rms_norm, inputs, norm_one.astype(jnp.float32))
    grad_in_part, gain_one_grad = norm_one_back(grad_normed_one)
    grad_tokens = grad_first + grad_in_part
    mixer_grads = (
        inproj_grad,
        conv_grad,
        cbias_grad,
        xproj_grad,
        dtproj_grad,
        dtbias_grad,
        alog_grad,
        dskip_grad,
        outproj_grad,
    )
    return (
        grad_tokens,
        mixer_grads,
        (up_grad, down_grad),
        (gain_one_grad, gain_two_grad, router_grad),
    )


def local(
    tokens,
    segment_ids,
    routes,
    keep_mask,
    out_grad,
    norm_one,
    in_proj,
    conv_weight,
    conv_bias,
    x_proj,
    dt_proj,
    dt_bias,
    a_log,
    d_skip,
    out_proj,
    norm_two,
    router,
    expert_up,
    expert_down,
):
    capacity = max(2, tokens.shape[1] * 3 // 16)

    def fetch_weights():
        mixer = (
            lax.all_gather(in_proj, ("dp", "seq", "expert"), axis=1, tiled=True),
            lax.all_gather(conv_weight, ("dp", "seq", "expert"), axis=1, tiled=True),
            lax.all_gather(conv_bias, ("dp", "seq", "expert"), axis=0, tiled=True),
            lax.all_gather(x_proj, ("dp", "seq", "expert"), axis=0, tiled=True),
            lax.all_gather(dt_proj, ("dp", "seq", "expert"), axis=1, tiled=True),
            lax.all_gather(dt_bias, ("dp", "seq", "expert"), axis=0, tiled=True),
            lax.all_gather(a_log, ("dp", "seq", "expert"), axis=1, tiled=True),
            lax.all_gather(d_skip, ("dp", "seq", "expert"), axis=0, tiled=True),
            lax.all_gather(out_proj, ("dp", "seq", "expert"), axis=0, tiled=True),
        )
        experts = (
            lax.all_gather(expert_up, ("dp", "seq"), axis=2, tiled=True),
            lax.all_gather(expert_down, ("dp", "seq"), axis=1, tiled=True),
        )
        return (mixer, experts)

    outputs = []
    kept_list = []
    for micro_idx in range(MB):
        fetched = fetch_weights()
        rows_pick = slice(micro_idx * SEQ_MB, (micro_idx + 1) * SEQ_MB)
        result, kept_vals = forward_micro(
            tokens[rows_pick],
            segment_ids[rows_pick],
            routes[rows_pick, :, 0],
            keep_mask[rows_pick],
            norm_one,
            norm_two,
            router,
            fetched[0],
            fetched[1],
            capacity,
        )
        outputs.append(result)
        kept_list.append(kept_vals)
    grad_parts = []
    totals = None
    for micro_idx in range(MB):
        fetched = fetch_weights()
        rows_pick = slice(micro_idx * SEQ_MB, (micro_idx + 1) * SEQ_MB)
        grad_tokens, mixer_grads, expert_grads, small_grads = backward_micro(
            out_grad[rows_pick],
            keep_mask[rows_pick],
            kept_list[micro_idx],
            norm_one,
            norm_two,
            router,
            fetched[0],
            fetched[1],
            capacity,
        )
        grad_parts.append(grad_tokens)
        current = (mixer_grads, expert_grads, small_grads)
        totals = current if totals is None else jax.tree.map(jnp.add, totals, current)
    mixer_tot, expert_tot, small_tot = totals
    mixer_sum = (
        lax.psum_scatter(mixer_tot[0], ("dp", "seq", "expert"), scatter_dimension=1, tiled=True),
        lax.psum_scatter(mixer_tot[1], ("dp", "seq", "expert"), scatter_dimension=1, tiled=True),
        lax.psum_scatter(mixer_tot[2], ("dp", "seq", "expert"), scatter_dimension=0, tiled=True),
        lax.psum_scatter(mixer_tot[3], ("dp", "seq", "expert"), scatter_dimension=0, tiled=True),
        lax.psum_scatter(mixer_tot[4], ("dp", "seq", "expert"), scatter_dimension=1, tiled=True),
        lax.psum_scatter(mixer_tot[5], ("dp", "seq", "expert"), scatter_dimension=0, tiled=True),
        lax.psum_scatter(mixer_tot[6], ("dp", "seq", "expert"), scatter_dimension=1, tiled=True),
        lax.psum_scatter(mixer_tot[7], ("dp", "seq", "expert"), scatter_dimension=0, tiled=True),
        lax.psum_scatter(mixer_tot[8], ("dp", "seq", "expert"), scatter_dimension=0, tiled=True),
    )
    up_sum, down_sum = (
        lax.psum_scatter(expert_tot[0], ("dp", "seq"), scatter_dimension=2, tiled=True),
        lax.psum_scatter(expert_tot[1], ("dp", "seq"), scatter_dimension=1, tiled=True),
    )
    gain_one_sum, gain_two_sum, router_sum = lax.psum(
        (small_tot[0], small_tot[1], small_tot[2]), ("dp", "seq", "expert")
    )
    return (
        jnp.concatenate(outputs, axis=0).astype(jnp.bfloat16),
        jnp.concatenate(grad_parts, axis=0),
        gain_one_sum,
        mixer_sum[0],
        mixer_sum[1],
        mixer_sum[2],
        mixer_sum[3],
        mixer_sum[4],
        mixer_sum[5],
        mixer_sum[6],
        mixer_sum[7],
        mixer_sum[8],
        gain_two_sum,
        router_sum,
        up_sum,
        down_sum,
    )


def solution(mesh):
    return jax.shard_map(
        local,
        mesh=mesh,
        in_specs=(
            P(("dp", "expert"), "seq", None),
            P(("dp", "expert"), "seq"),
            P(("dp", "expert"), "seq", None),
            P(("dp", "expert"), "seq"),
            P(("dp", "expert"), "seq", None),
            P(),
            P(None, ("dp", "seq", "expert")),
            P(None, ("dp", "seq", "expert")),
            P(("dp", "seq", "expert")),
            P(("dp", "seq", "expert"), None),
            P(None, ("dp", "seq", "expert")),
            P(("dp", "seq", "expert")),
            P(None, ("dp", "seq", "expert")),
            P(("dp", "seq", "expert")),
            P(("dp", "seq", "expert"), None),
            P(),
            P(),
            P("expert", None, ("dp", "seq")),
            P("expert", ("dp", "seq"), None),
        ),
        out_specs=(
            P(("dp", "expert"), "seq", None),
            P(("dp", "expert"), "seq", None),
            P(),
            P(None, ("dp", "seq", "expert")),
            P(None, ("dp", "seq", "expert")),
            P(("dp", "seq", "expert")),
            P(("dp", "seq", "expert"), None),
            P(None, ("dp", "seq", "expert")),
            P(("dp", "seq", "expert")),
            P(None, ("dp", "seq", "expert")),
            P(("dp", "seq", "expert")),
            P(("dp", "seq", "expert"), None),
            P(),
            P(),
            P("expert", None, ("dp", "seq")),
            P("expert", ("dp", "seq"), None),
        ),
        check_vma=False,
    )
```

profile of v0, /device:TPU:0, one launch (start us, length us, event | category | flops | bytes accessed | tf_op | source)
XLA Modules:
  0.0 6371.7 jit_solution(14151093631875069327)
XLA Ops:
  18.0 38.2 all-gather.5
  58.9 39.0 all-reduce.33
  98.8 41.0 all-gather.4
  140.3 40.9 all_gather.47
  184.0 39.6 all_gather.46
  411.9 690.8 %while.445 = (s32[]{:T(128)}, f32[2,2304,16]{1,2,0:T(8,128)S(1)}, f32[16,2,16,2304]{3,1,2,0:T(2,128)}, f32[16,2,16,2304]{3,1,2,0:T(2,128)}, f32[16,2,16,2304]{3,...) while((s32[]{:T(128)}, f32[2,2304,16]{1,2,0:T(8,128)S(1)}, ...), condition=%wide.region_14.15_spmd, body=%wide.region_10.14_spmd.sunk | while | flops 516100 | bytes 2700926 | solution.py:125
  415.4 38.0 while.462
  458.5 38.0 while.462
  501.7 38.1 while.462
  545.0 38.0 while.462
  588.1 38.1 while.462
  631.4 38.0 while.462
  674.5 38.0 while.462
  717.7 38.0 while.462
  760.9 38.1 while.462
  804.1 38.0 while.462
  847.3 38.0 while.462
  890.5 38.0 while.462
  933.6 38.0 while.462
  976.8 38.0 while.462
  1019.9 38.0 while.462
  1112.2 502.0 %while.447 = (s32[]{:T(128)}, f32[2,2304,16]{1,2,0:T(8,128)S(1)}, f32[16,2,16,2304]{3,1,2,0:T(2,128)}, f32[16,2,16,2304]{3,1,2,0:T(2,128)}, f32[16,2,16,2304]{3,...) while((s32[]{:T(128)}, f32[2,2304,16]{1,2,0:T(8,128)S(1)}, ...), condition=%wide.region_34.35_spmd, body=%wide.region_30.34_spmd.sunk | while | flops 516100 | bytes 2700926 | solution.py:125
  1880.5 123.7 %while.449 = (s32[]{:T(128)}, f32[2,2304,16]{1,2,0:T(8,128)S(1)}, f32[16,2,2304,16]{2,3,1,0:T(8,128)}, f32[16,2,16,2304]{3,1,2,0:T(2,128)}, f32[16,2,16,2304]{3,...) while((s32[]{:T(128)}, f32[2,2304,16]{1,2,0:T(8,128)S(1)}, ...), condition=%wide.region_48.49_spmd, body=%wide.region_45.48_spmd.sunk | while | flops 373252 | bytes 2641106 | solution.py:125
  2086.9 317.2 %while.451 = (s32[]{:T(128)}, f32[2,2304,16]{1,2,0:T(8,128)S(1)}, f32[16,2,2304,16]{2,3,1,0:T(8,128)}, f32[16,2,16,2304]{3,1,2,0:T(2,128)}, f32[16,2,16,2304]{3,...) while((s32[]{:T(128)}, f32[2,2304,16]{1,2,0:T(8,128)S(1)}, ...), condition=%wide.region_69.70_spmd, body=%wide.region_66.69_spmd.sunk | while | flops 373252 | bytes 2641106 | solution.py:125
  2435.2 917.6 %while.457 = (s32[]{:T(128)}, f32[2304,16]{0,1:T(8,128)S(1)}, f32[2,2304,16]{1,2,0:T(8,128)S(1)}, f32[16,2,16,2304]{3,1,2,0:T(2,128)}, f32[16,2,16,2304]{3,1,2,0...) while((s32[]{:T(128)}, f32[2304,16]{0,1:T(8,128)S(1)}, ...), condition=%wide.region_59.60_spmd.clone, body=%wide.region_49.59_spmd.clone.sunk | while | flops 1820106 | bytes 10321663 | solution.py:125
  3372.4 1226.0 %while.461 = (s32[]{:T(128)}, f32[2304,16]{0,1:T(8,128)S(1)}, f32[2,2304,16]{1,2,0:T(8,128)S(1)}, f32[16,2,16,2304]{3,1,2,0:T(2,128)}, f32[16,2,16,2304]{3,1,2,0...) while((s32[]{:T(128)}, f32[2304,16]{0,1:T(8,128)S(1)}, ...), condition=%wide.region_80.81_spmd.clone, body=%wide.region_70.80_spmd.clone.sunk | while | flops 1820106 | bytes 10319863 | solution.py:125
  3407.1 40.3 while.469
  3483.7 40.3 while.469
  3560.3 40.3 while.469
  3636.9 40.3 while.469
  3713.6 40.3 while.469
  3790.1 40.3 while.469
  3866.8 40.3 while.469
  3943.4 40.3 while.469
  4020.0 40.3 while.469
  4096.6 40.3 while.469
  4173.2 40.3 while.469
  4249.7 40.3 while.469
  4326.4 40.3 while.469
  4403.0 40.3 while.469
  4479.5 40.3 while.469
  4556.1 40.3 while.469
  4878.3 102.6 %all-reduce.39.cloned.1.call-done = (f32[72,2304]{1,0:T(8,128)}, f32[16,2304]{1,0:T(8,128)}) async-done(((f32[72,2304]{1,0:T(8,128)}, f32[16,2304]{1,0:T(8,128)}), (f32[72,2304]{1,0:T(8,128)}, f32[16,2304]{1,0:T(8,128)})) %all-reduce.39.cloned.1.call-update) | async-done | bytes 811024
  4983.9 99.2 %reduce-scatter.19.cloned.1.call-done = f32[72,104]{1,0:T(8,128)} async-done(((f32[2304,104]{1,0:T(8,128)}), f32[72,104]{1,0:T(8,128)}) %reduce-scatter.19.cloned.1.call-update) | async-done | bytes 29968
  5083.1 147.5 %reduce-scatter.21.cloned.1.call-done = f32[72,1152]{1,0:T(8,128)} async-done(((f32[2304,1152]{1,0:T(8,128)}), f32[72,1152]{1,0:T(8,128)}) %reduce-scatter.21.cloned.1.call-update) | async-done | bytes 331792
  5230.5 225.4 %reduce-scatter.13.cloned.1.call-done = f32[1152,144]{0,1:T(8,128)} async-done(((f32[1152,4608]{0,1:T(8,128)}), f32[1152,144]{0,1:T(8,128)}) %reduce-scatter.13.cloned.1.call-update) | async-done | bytes 663568 | tf_op jit(solution)/shard_map/reduce_scatter | solution.py:487
  5456.0 452.9 %reduce-scatter.15.cloned.1.call-done = f32[2,1152,384]{2,1,0:T(8,128)} async-done(((f32[2,1152,3072]{2,1,0:T(8,128)}), f32[2,1152,384]{2,1,0:T(8,128)}) %reduce-scatter.15.cloned.1.call-update) | async-done | bytes 3538960 | tf_op jit(solution)/shard_map/reduce_scatter | solution.py:498
  5908.9 452.1 %reduce-scatter.17.cloned.1.call-done = f32[2,384,1152]{2,1,0:T(8,128)} async-done(((f32[2,3072,1152]{2,1,0:T(8,128)}), f32[2,384,1152]{2,1,0:T(8,128)}) %reduce-scatter.17.cloned.1.call-update) | async-done | bytes 3538960 | tf_op jit(solution)/shard_map/reduce_scatter | solution.py:499
  (16878 shorter events, 6637.9 us)
Async XLA Ops:
  7.2 1730.0 %copy-start = (bf16[1152,8]{0,1:T(8,128)(2,1)S(1)}, bf16[1152,8]{0,1:T(8,128)(2,1)}, u32[]{:S(2)}) copy-start(bf16[1152,8]{0,1:T(8,128)(2,1)} %param.71) | copy-start | bytes 55300
  7.2 176.8 %copy-start.152 = (s32[4,256]{1,0:T(4,128)S(1)}, s32[4,256]{1,0:T(4,128)}, u32[]{:S(2)}) copy-start(s32[4,256]{1,0:T(4,128)} %param.56) | copy-start | bytes 12292
  7.2 223.3 %copy-start.48 = (bf16[4,256,1152]{2,1,0:T(8,128)(2,1)S(1)}, bf16[4,256,1152]{2,1,0:T(8,128)(2,1)}, u32[]{:S(2)}) copy-start(bf16[4,256,1152]{2,1,0:T(8,128)(2,1)} %param.55) | copy-start | bytes 7077892
  7.2 176.8 %copy-start.151 = (bf16[72,104]{1,0:T(8,128)(2,1)S(1)}, bf16[72,104]{1,0:T(8,128)(2,1)}, u32[]{:S(2)}) copy-start(bf16[72,104]{1,0:T(8,128)(2,1)} %param.64) | copy-start | bytes 44932
  7.2 223.2 %all-gather.17.cloned.1.call-start = ((), (), s32[]{:S(2)}) async-start(), calls=%async_computation.13 | async-start | bytes 10948608 | tf_op jit(solution)/shard_map/all_gather | solution.py:431
  8.0 394.5 %all-gather.19.cloned.1.call-start = ((), (), s32[]{:S(2)}) async-start(), calls=%async_computation.14 | async-start | bytes 1474560 | tf_op jit(solution)/shard_map/all_gather | solution.py:28
  8.8 214.8 %collective-permute-start.1 = (f32[2,3]{1,0:T(2,128)S(1)}, f32[2,3]{1,0:T(2,128)S(1)}, u32[]{:S(2)}, u32[]{:S(2)}) collective-permute-start(f32[2,3]{1,0:T(2,128)S(1)} %slice.297), channel_id=1, source_target_pairs={{0,4},{4,8},{8,12},{1,5},{5,9},{9,13},{2,6},{6,10},{10,14},{3,7},{... | collective-permute-start | bytes 80 | tf_op jit(solution)/shard_map/ppermute | solution.py:23
  13.8 210.1 %collective-permute-start.3 = (f32[2,3]{1,0:T(2,128)S(1)}, f32[2,3]{1,0:T(2,128)S(1)}, u32[]{:S(2)}, u32[]{:S(2)}) collective-permute-start(f32[2,3]{1,0:T(2,128)S(1)} %slice.322), channel_id=1, source_target_pairs={{0,4},{4,8},{8,12},{1,5},{5,9},{9,13},{2,6},{6,10},{10,14},{3,7},{... | collective-permute-start | bytes 80 | tf_op jit(solution)/shard_map/ppermute | solution.py:23
  18.0 223.1 %copy-start.85 = (f32[1152]{0:T(1024)}, f32[1152]{0:T(1024)S(1)}, u32[]{:S(2)}) copy-start(f32[1152]{0:T(1024)S(1)} %convert_element_type.282) | copy-start | bytes 13828
  239.8 17.7 collective-permute-start
  256.0 7.5 collective-permute-start.2
  262.6 1356.0 %copy-start.10 = (bf16[2,256,2304]{2,1,0:T(8,128)(2,1)}, bf16[2,256,2304]{2,1,0:T(8,128)(2,1)S(1)}, u32[]{:S(2)}) copy-start(bf16[2,256,2304]{2,1,0:T(8,128)(2,1)S(1)} %get-tuple-element.4194) | copy-start | bytes 7077892
  312.7 89.8 %all-gather.29.cloned.1.call-start = ((), (), s32[]{:S(2)}) async-start(), calls=%async_computation.22 | async-start | bytes 1474560 | tf_op jit(solution)/shard_map/all_gather | solution.py:28
  365.0 737.8 %all-gather.27.cloned.1.call-start = ((), (), s32[]{:S(2)}) async-start(), calls=%async_computation.18 | async-start | bytes 1474560 | tf_op jit(solution)/shard_map/all_gather | solution.py:28
  365.6 737.2 %all-gather.31.cloned.1.call-start = ((), (), s32[]{:S(2)}) async-start(), calls=%async_computation.23 | async-start | bytes 1474560 | tf_op jit(solution)/shard_map/all_gather | solution.py:28
  366.2 1262.5 %all-gather.21.cloned.1.call-start = ((), (), s32[]{:S(2)}) async-start(), calls=%async_computation.15 | async-start | bytes 5474304 | tf_op jit(solution)/shard_map/all_gather | solution.py:439
  366.8 1307.1 %all-gather.23.cloned.1.call-start = ((), (), s32[]{:S(2)}) async-start(), calls=%async_computation.16 | async-start | bytes 15925248 | tf_op jit(solution)/shard_map/all_gather | solution.py:442
  367.5 1320.2 %all-gather.25.cloned.1.call-start = ((), (), s32[]{:S(2)}) async-start(), calls=%async_computation.17 | async-start | bytes 15925248 | tf_op jit(solution)/shard_map/all_gather | solution.py:443
  369.2 1270.0 %copy-start.94 = (f32[1152]{0:T(1024)}, f32[1152]{0:T(1024)S(1)}, u32[]{:S(2)}) copy-start(f32[1152]{0:T(1024)S(1)} %convert_element_type.295) | copy-start | bytes 13828
  1643.3 25.7 all-to-all-start.2
  1669.0 33.6 all-to-all-start
  1702.6 30.0 all-to-all-start.3
  1732.6 26.8 all-to-all-start.1
  1738.2 271.1 %copy-start.135 = (f32[2,256]{1,0:T(2,128)}, f32[2,256]{1,0:T(2,128)S(1)}, u32[]{:S(2)}) copy-start(f32[2,256]{1,0:T(2,128)S(1)} %get-tuple-element.4319) | copy-start | bytes 6148
  1764.3 245.0 %copy-start.141 = (f32[2,256]{1,0:T(2,128)}, f32[2,256]{1,0:T(2,128)S(1)}, u32[]{:S(2)}) copy-start(f32[2,256]{1,0:T(2,128)S(1)} %get-tuple-element.4291) | copy-start | bytes 6148
  1764.3 246.2 %copy-start.133 = (f32[2,256]{1,0:T(2,128)}, f32[2,256]{1,0:T(2,128)S(1)}, u32[]{:S(2)}) copy-start(f32[2,256]{1,0:T(2,128)S(1)} %get-tuple-element.4286) | copy-start | bytes 6148
  1766.7 26.7 all-to-all-start.6
  1793.3 39.6 all-to-all-start.4
  1833.0 40.3 all-to-all-start.7
  1873.2 133.4 %all-to-all-start.5 = ((bf16[4,2,96,1152]{3,2,1,0:T(8,128)(2,1)}), bf16[4,2,96,1152]{3,2,1,0:T(8,128)(2,1)}, u32[]{:S(2)}, u32[]{:S(2)}) async-start(bf16[4,2,96,1152]{3,2,1,0:T(8,128)(2,1)} %copy.419), calls=%async_computation.5 | async-start | bytes 3538944 | tf_op jit(solution)/shard_map/all_to_all | solution.py:321
  1877.8 543.4 %all-gather.33.cloned.1.call-start = ((), (), s32[]{:S(2)}) async-start(), calls=%async_computation.24 | async-start | bytes 1474560 | tf_op jit(solution)/shard_map/all_gather | solution.py:28
  1880.5 123.7 %copy-start.122 = (f32[2,256,8]{1,2,0:T(8,128)S(1)}, f32[2,256,8]{1,2,0:T(8,128)}, u32[]{:S(2)}) copy-start(f32[2,256,8]{1,2,0:T(8,128)} %copy-done.120) | copy-start | bytes 49156
  2084.0 1274.0 %all-gather.35.cloned.1.call-start = ((), (), s32[]{:S(2)}) async-start(), calls=%async_computation.25 | async-start | bytes 1474560 | tf_op jit(solution)/shard_map/all_gather | solution.py:28
  2086.8 317.2 %copy-start.45 = (bf16[2,256,1152]{2,1,0:T(8,128)(2,1)S(1)}, bf16[2,256,1152]{2,1,0:T(8,128)(2,1)}, u32[]{:S(2)}) copy-start(bf16[2,256,1152]{2,1,0:T(8,128)(2,1)} %get-tuple-element.4284) | copy-start | bytes 3538948
  2086.8 317.2 %copy-start.134 = (f32[2,256]{1,0:T(2,128)S(1)}, f32[2,256]{1,0:T(2,128)}, u32[]{:S(2)}) copy-start(f32[2,256]{1,0:T(2,128)} %copy-done.133) | copy-start | bytes 6148
  2086.8 317.8 %copy-start.43 = (bf16[2,256,1152]{2,1,0:T(8,128)(2,1)S(1)}, bf16[2,256,1152]{2,1,0:T(8,128)(2,1)}, u32[]{:S(2)}) copy-start(bf16[2,256,1152]{2,1,0:T(8,128)(2,1)} %copy-done.42) | copy-start | bytes 3538948
  2086.9 317.8 %copy-start.136 = (f32[2,256]{1,0:T(2,128)S(1)}, f32[2,256]{1,0:T(2,128)}, u32[]{:S(2)}) copy-start(f32[2,256]{1,0:T(2,128)} %copy-done.135) | copy-start | bytes 6148
  2086.9 317.8 %copy-start.142 = (f32[2,256]{1,0:T(2,128)S(1)}, f32[2,256]{1,0:T(2,128)}, u32[]{:S(2)}) copy-start(f32[2,256]{1,0:T(2,128)} %copy-done.141) | copy-start | bytes 6148
  2419.9 2453.1 %all-reduce.37.cloned.1.call-start = ((), (), s32[]{:S(2)}) async-start(), calls=%async_computation.28 | async-start | bytes 253952 | tf_op jit(solution)/shard_map/psum | solution.py:501
  4654.2 41.6 collective-permute-start.5
  4693.2 6.5 collective-permute-start.4
  4719.1 261.8 %all-reduce.39.cloned.1.call-start = ((), (), s32[]{:S(2)}) async-start(), calls=%async_computation.29 | async-start | bytes 1622016
  4722.4 360.7 %reduce-scatter.19.cloned.1.call-start = ((), (), s32[]{:S(2)}) async-start(), calls=%async_computation.26 | async-start | bytes 1216512
  4727.2 503.3 %reduce-scatter.21.cloned.1.call-start = ((), (), s32[]{:S(2)}) async-start(), calls=%async_computation.27 | async-start | bytes 10948608
  4739.4 716.5 %reduce-scatter.13.cloned.1.call-start = ((), (), s32[]{:S(2)}) async-start(), calls=%async_computation.19 | async-start | bytes 21897216 | tf_op jit(solution)/shard_map/reduce_scatter | solution.py:487
  4775.8 1133.1 %reduce-scatter.15.cloned.1.call-start = ((), (), s32[]{:S(2)}) async-start(), calls=%async_computation.20 | async-start | bytes 31850496 | tf_op jit(solution)/shard_map/reduce_scatter | solution.py:498
  4816.1 1544.9 %reduce-scatter.17.cloned.1.call-start = ((), (), s32[]{:S(2)}) async-start(), calls=%async_computation.21 | async-start | bytes 31850496 | tf_op jit(solution)/shard_map/reduce_scatter | solution.py:499
  4870.6 1494.4 %copy-start.1 = (bf16[1152,8]{0,1:T(8,128)(2,1)S(1)}, bf16[1152,8]{0,1:T(8,128)(2,1)}, u32[]{:S(2)}) copy-start(bf16[1152,8]{0,1:T(8,128)(2,1)} %param.71) | copy-start | bytes 55300
  (190 other events, 2601.7 us)
Sparse Core Ops, SparseCore 0:
  11.0 90.3 all-gather.16
  312.8 27.8 all-gather.18
  365.2 27.8 all-gather.28
  395.0 29.5 all-gather.26
  426.0 29.5 all-gather.30
  458.3 64.7 all-gather.20
  525.1 194.6 all-gather.22
  721.9 193.8 all-gather.24
  2084.1 28.9 all-gather.32
  2420.1 28.9 all-gather.34
  4719.2 128.4 all-reduce.36
  4852.8 127.9 all-reduce.38
  4986.5 96.4 reduce-scatter.18
  5089.6 140.9 reduce-scatter.20
  5237.4 218.5 reduce-scatter.12
  5460.8 448.0 reduce-scatter.14
  5913.3 447.7 reduce-scatter.16
where the time goes:
time: 6470 us; the launch traced here: 6370 us
  other arithmetic  2470 us (38%)
  local copies, waits for them, and re-layouts  1600 us (25%)
  waiting for transfers between devices  1540 us (24%)
  matrix products  404 us (6%)
  blocking collectives  199 us (3%)
  loops' own time  93.3 us (1%)
    reduce_sum x512, other arithmetic, token_step(): (delta_t * xs_t)[:, :, None] * b_t[:, None, :]  795 us
    mul x1536, other arithmetic, token_step(): delta_t * xs_t  582 us
    dynamic_update_slice x512, other arithmetic, ssm_local(): lax.scan(jax.checkpoint(block_step), start_state, (arrange(xs_vals), arra...  558 us
    dynamic_update_slice x2560, local copies, waits for them, and re-layouts, block_step(): state_end, outs = lax.scan(token_step, state_now, ordered)  488 us
    reduce_scatter x1, waiting for transfers between devices, local(): lax.psum_scatter(expert_tot[0], ('dp', 'seq'), scatter_dimension=2, tiled...  453 us
    reduce_scatter x1, waiting for transfers between devices, local(): lax.psum_scatter(expert_tot[1], ('dp', 'seq'), scatter_dimension=1, tiled...  452 us
    dot_general x38, matrix products, low_dot(): jnp.einsum(formula, left_op, right_op, preferred_element_type=jnp.float32)  388 us
    unnamed x20, waiting for transfers between devices  353 us

commit v1 on v0

v1 whole, which is shorter than its diff:
```python
import functools

import jax
import jax.numpy as jnp
from jax import lax
from jax.experimental import pallas as pl
from jax.experimental.pallas import tpu as pltpu
from jax.sharding import PartitionSpec as P

D = 1152
DI = 2304
NSTATE = 16
DTR = 72
CONVK = 4
EXPERTS = 8
XW = DTR + 2 * NSTATE
HALVES = 2
LANES = 128
LN2 = 0.6931471805599453
SPLITS = 3
SUB = 8
PACK = 256
CHUNK = 16
BIG = 1e30
VMEM = 60 * 1024 * 1024

norm_eps = 1e-05
ALL = ("dp", "seq", "expert")


def shifted(value, axis, steps):
    count = lax.axis_size(axis)
    first, last = (max(0, -steps), min(count, count - steps))
    return lax.ppermute(value, axis, [(source, source + steps) for source in range(first, last)])


def dot(left, right, dims, out=jnp.float32):
    return lax.dot_general(left, right, (dims, ((), ())), preferred_element_type=out)


NN = ((1,), (0,))
NT = ((1,), (1,))
TN = ((0,), (0,))


def to_rows(value):
    seqs, length = value.shape[:2]
    rest = value.shape[2:]
    split = value.reshape((seqs, HALVES, length // HALVES) + rest)
    return jnp.moveaxis(split, 2, 0).reshape((seqs * length,) + rest)


def from_rows(value, seqs):
    rest = value.shape[1:]
    length = value.shape[0] // seqs
    split = value.reshape((length // HALVES, seqs, HALVES) + rest)
    return jnp.moveaxis(split, 0, 2).reshape((seqs, length) + rest)


def to_ext_rows(value, halo):
    seqs, length = value.shape[:2]
    rest = value.shape[2:]
    part = length // HALVES
    ext = jnp.concatenate([halo, value], axis=1)
    split = jnp.stack([ext[:, h * part : h * part + part + CONVK - 1] for h in range(HALVES)], axis=1)
    return jnp.moveaxis(split, 2, 0).reshape(((part + CONVK - 1) * seqs * HALVES,) + rest)


def decay_rates(alog_ref, a_s):
    rates = -(1.0 / LN2) * jnp.exp(alog_ref[...].astype(jnp.float32))
    for n in range(NSTATE):
        a_s[n] = jnp.broadcast_to(rates[n : n + 1, :], (SUB, LANES))


def spread(src_ref, dst, first):
    src = src_ref[...]
    high = src.astype(jnp.bfloat16)
    both = jnp.concatenate([high, (src - high.astype(jnp.float32)).astype(jnp.bfloat16)], axis=1)
    line = lax.broadcasted_iota(jnp.int32, (4 * NSTATE, LANES), 0)

    def body(n, carry):
        pick = (line == first + n) | (line == 2 * NSTATE + first + n)
        dst[n] = dot(both, jnp.where(pick, 1.0, 0.0).astype(jnp.bfloat16), NN)
        return carry

    lax.fori_loop(0, NSTATE, body, 0)


def tree_sum(parts):
    while len(parts) > 1:
        parts = [parts[i] + parts[i + 1] if i + 1 < len(parts) else parts[i] for i in range(0, len(parts), 2)]
    return parts[0]


UNROLL = 8


def unrolled(first, count, body, carry):
    def group(i, inner):
        for u in range(UNROLL):
            inner = body(first + i * UNROLL + u, inner)
        return inner

    return lax.fori_loop(0, count // UNROLL, group, carry)


def row_at(t):
    return pl.ds(pl.multiple_of(t * SUB, SUB), SUB)


def end_kernel(xs_ref, din_ref, dtw_ref, dtb_ref, alog_ref, bc_ref, cut_ref, delta_ref, end_ref, sum_ref, b_s, a_s, dx_s):
    steps = delta_ref.shape[0] // SUB

    @pl.when(pl.program_id(0) == 0)
    def _():
        spread(bc_ref, b_s, 0)

    decay_rates(alog_ref, a_s)
    pre = dot(din_ref[...], dtw_ref[...], NT) + dtb_ref[...].astype(jnp.float32)
    low = jnp.exp(-jnp.abs(pre))
    delta = jnp.maximum(pre, 0.0) + jnp.where(low < 0.01, low * (1.0 - low * (0.5 - low * (1.0 / 3.0))), jnp.log(1.0 + low))
    delta_ref[...] = delta
    dx_s[...] = delta * xs_ref[...].astype(jnp.float32)
    rates = [a_s[n] for n in range(NSTATE)]

    def body(t, carry):
        total, state = carry
        at = row_at(t)
        step = jnp.maximum(delta_ref[at, :], cut_ref[at, :])
        dx = dx_s[at, :]
        state = [jnp.exp2(step * rates[n]) * state[n] + dx * b_s[n, at, :] for n in range(NSTATE)]
        return (total + step, state)

    zero = jnp.zeros((SUB, LANES), jnp.float32)
    total, state = unrolled(0, steps, body, (zero, [zero] * NSTATE))
    sum_ref[...] = total
    for n in range(NSTATE):
        end_ref[n] = state[n]


def out_kernel(xs_ref, delta_ref, alog_ref, bc_ref, cut_ref, start_ref, z_ref, skip_ref, branch_ref, ssm_ref, held_ref, b_s, c_s, a_s, dx_s, y_s):
    steps = delta_ref.shape[0] // SUB

    @pl.when(pl.program_id(0) == 0)
    def _():
        spread(bc_ref, b_s, 0)
        spread(bc_ref, c_s, NSTATE)

    decay_rates(alog_ref, a_s)
    xs = xs_ref[...].astype(jnp.float32)
    dx_s[...] = delta_ref[...] * xs
    rates = [a_s[n] for n in range(NSTATE)]

    def body(t, state):
        at = row_at(t)
        step = jnp.maximum(delta_ref[at, :], cut_ref[at, :])
        dx = dx_s[at, :]
        state = [jnp.exp2(step * rates[n]) * state[n] + dx * b_s[n, at, :] for n in range(NSTATE)]
        y_s[at, :] = tree_sum([state[n] * c_s[n, at, :] for n in range(NSTATE)])
        return state

    def chunk(i, state):
        for n in range(NSTATE):
            held_ref[i, n] = state[n]
        return unrolled(i * CHUNK, CHUNK, body, state)

    lax.fori_loop(0, steps // CHUNK, chunk, [start_ref[n] for n in range(NSTATE)])
    ssm = y_s[...] + skip_ref[...].astype(jnp.float32) * xs
    z = z_ref[...]
    ssm_ref[...] = ssm.astype(jnp.bfloat16)
    branch_ref[...] = (ssm * (z / (1.0 + jnp.exp(-z)))).astype(jnp.bfloat16)


def first_kernel(delta_ref, alog_ref, bc_ref, cut_ref, gb_ref, z_ref, ssm_ref, lead_ref, gz_ref, g_s, c_s, a_s):
    steps = delta_ref.shape[0] // SUB

    @pl.when(pl.program_id(0) == 0)
    def _():
        spread(bc_ref, c_s, NSTATE)

    decay_rates(alog_ref, a_s)
    z = z_ref[...]
    grad = gb_ref[...]
    sig = 1.0 / (1.0 + jnp.exp(-z))
    g_s[...] = grad * (z * sig)
    gz_ref[...] = (grad * ssm_ref[...].astype(jnp.float32) * (sig * (1.0 + z * (1.0 - sig)))).astype(jnp.bfloat16)
    rates = [a_s[n] for n in range(NSTATE)]

    def body(k, lead):
        at = row_at(steps - 1 - k)
        step = jnp.maximum(delta_ref[at, :], cut_ref[at, :])
        g = g_s[at, :]
        return [jnp.exp2(step * rates[n]) * (lead[n] + g * c_s[n, at, :]) for n in range(NSTATE)]

    zero = jnp.zeros((SUB, LANES), jnp.float32)
    lead = unrolled(0, steps, body, [zero] * NSTATE)
    for n in range(NSTATE):
        lead_ref[n] = lead[n]


def back_kernel(
    xs_ref, delta_ref, alog_ref, bc_ref, cut_ref, g_ref, skip_ref, held_ref, last_ref,
    gxs_ref, gpre_ref, galog_ref, gvec_ref, gbc_ref,
    b_s, c_s, gb_s, gc_s, a_s, dx_s, x_s, gx_s, gd_s, hd_s, dec_s,
):
    steps = delta_ref.shape[0] // SUB

    @pl.when(pl.program_id(0) == 0)
    def _():
        spread(bc_ref, b_s, 0)
        spread(bc_ref, c_s, NSTATE)
        gb_s[...] = jnp.zeros_like(gb_s)
        gc_s[...] = jnp.zeros_like(gc_s)

    decay_rates(alog_ref, a_s)
    xs = xs_ref[...].astype(jnp.float32)
    x_s[...] = xs
    dx_s[...] = delta_ref[...] * xs

    def ahead(j, state, base):
        at = row_at(base + j)
        step = jnp.maximum(delta_ref[at, :], cut_ref[at, :])
        dx = dx_s[at, :]
        g = g_ref[at, :]
        new = []
        for n in range(NSTATE):
            dec = jnp.exp2(step * a_s[n])
            hd = dec * state[n]
            dec_s[j, n] = dec
            hd_s[j, n] = hd
            h = hd + dx * b_s[n, at, :]
            gc_s[n, at, :] = gc_s[n, at, :] + g * h
            new.append(h)
        return new

    def behind(k, carry, base):
        coming, rate_grad = carry
        j = CHUNK - 1 - k
        at = row_at(base + j)
        delta = delta_ref[at, :]
        dx = dx_s[at, :]
        g = g_ref[at, :]
        next_coming, next_rate, with_b, with_a = [], [], [], []
        for n in range(NSTATE):
            lam = coming[n] + g * c_s[n, at, :]
            with_b.append(lam * b_s[n, at, :])
            gb_s[n, at, :] = gb_s[n, at, :] + lam * dx
            q = lam * hd_s[j, n]
            with_a.append(q * a_s[n])
            next_rate.append(rate_grad[n] + delta * q)
            next_coming.append(lam * dec_s[j, n])
        by_b = tree_sum(with_b)
        gx_s[at, :] = by_b * delta
        gd_s[at, :] = by_b * x_s[at, :] + LN2 * tree_sum(with_a)
        return (next_coming, next_rate)

    chunks = steps // CHUNK

    def chunk(i, carry):
        c = chunks - 1 - i
        base = c * CHUNK
        unrolled(0, CHUNK, functools.partial(ahead, base=base), [held_ref[c, n] for n in range(NSTATE)])
        return unrolled(0, CHUNK, functools.partial(behind, base=base), carry)

    zero = jnp.zeros((SUB, LANES), jnp.float32)
    _, rate_grad = lax.fori_loop(0, chunks, chunk, ([last_ref[n] for n in range(NSTATE)], [zero] * NSTATE))
    for n in range(NSTATE):
        galog_ref[n : n + 1, :] = LN2 * jnp.sum(rate_grad[n] * a_s[n], axis=0, keepdims=True)
    skip = skip_ref[...].astype(jnp.float32)
    grad_ssm = g_ref[...]
    gxs_ref[...] = gx_s[...] + grad_ssm * skip
    delta = delta_ref[...]
    slope = jnp.where(delta < 0.01, delta * (1.0 - 0.5 * delta * (1.0 - delta * (1.0 / 3.0))), 1.0 - jnp.exp(-delta))
    gpre = gd_s[...] * slope
    gpre_ref[...] = gpre.astype(jnp.bfloat16)
    gvec_ref[0:1, :] = jnp.sum(gpre, axis=0, keepdims=True)
    gvec_ref[1:2, :] = jnp.sum(grad_ssm * xs, axis=0, keepdims=True)
    gvec_ref[2:SUB, :] = jnp.zeros((SUB - 2, LANES), jnp.float32)

    @pl.when(pl.program_id(0) == pl.num_programs(0) - 1)
    def _():
        lane = lax.broadcasted_iota(jnp.int32, (LANES, LANES), 1)
        gbc_ref[...] = jnp.zeros_like(gbc_ref)

        def gather(n, carry):
            for part, first in ((gb_s, 0), (gc_s, NSTATE)):
                pick = jnp.where(lane == first + n, 1.0, 0.0).astype(jnp.bfloat16)
                gbc_ref[...] += dot(part[n].astype(jnp.bfloat16), pick, NN)
            return carry

        lax.fori_loop(0, NSTATE, gather, 0)


def col_spec(rows):
    return pl.BlockSpec((rows, LANES), lambda c: (0, c))


def full_spec(shape):
    return pl.BlockSpec(shape, lambda c: (0,) * len(shape))


def state_spec():
    return pl.BlockSpec((NSTATE, SUB, LANES), lambda c: (0, 0, c))


def params():
    return pltpu.CompilerParams(vmem_limit_bytes=VMEM)


def f32s(*shape):
    return jax.ShapeDtypeStruct(shape, jnp.float32)


def b16s(*shape):
    return jax.ShapeDtypeStruct(shape, jnp.bfloat16)


def vm(*shape):
    return pltpu.VMEM(shape, jnp.float32)


def cost(rows, width, per_value):
    work = rows * width * NSTATE
    return pl.CostEstimate(flops=work * 8, bytes_accessed=work * per_value, transcendentals=work)


def run_end(xs, din, dtw, dtb, alog, bc, cut):
    rows = xs.shape[0]
    return pl.pallas_call(
        end_kernel,
        grid=(DI // LANES,),
        in_specs=[
            col_spec(rows), full_spec(din.shape), pl.BlockSpec((LANES, DTR), lambda c: (c, 0)),
            col_spec(1), col_spec(NSTATE), full_spec(bc.shape), full_spec(cut.shape),
        ],
        out_specs=[col_spec(rows), state_spec(), col_spec(SUB)],
        out_shape=[f32s(rows, DI), f32s(NSTATE, SUB, DI), f32s(SUB, DI)],
        scratch_shapes=[vm(NSTATE, rows, LANES), vm(NSTATE, SUB, LANES), vm(rows, LANES)],
        compiler_params=params(),
        cost_estimate=cost(rows, DI, 4),
        name="end",
    )(xs, din, dtw, dtb, alog, bc, cut)


def run_out(xs, delta, alog, bc, cut, start, z, skip):
    rows = xs.shape[0]
    chunks = rows // SUB // CHUNK
    return pl.pallas_call(
        out_kernel,
        grid=(DI // LANES,),
        in_specs=[
            col_spec(rows), col_spec(rows), col_spec(NSTATE), full_spec(bc.shape), full_spec(cut.shape),
            state_spec(), col_spec(rows), col_spec(1),
        ],
        out_specs=[
            col_spec(rows), col_spec(rows),
            pl.BlockSpec((chunks, NSTATE, SUB, LANES), lambda c: (0, 0, 0, c)),
        ],
        out_shape=[b16s(rows, DI), b16s(rows, DI), f32s(chunks, NSTATE, SUB, DI)],
        scratch_shapes=[
            vm(NSTATE, rows, LANES), vm(NSTATE, rows, LANES), vm(NSTATE, SUB, LANES), vm(rows, LANES), vm(rows, LANES),
        ],
        compiler_params=params(),
        cost_estimate=cost(rows, DI, 5),
        name="out",
    )(xs, delta, alog, bc, cut, start, z, skip)


def run_first(delta, alog, bc, cut, gbranch, z, ssm):
    rows = delta.shape[0]
    return pl.pallas_call(
        first_kernel,
        grid=(DI // LANES,),
        in_specs=[
            col_spec(rows), col_spec(NSTATE), full_spec(bc.shape), full_spec(cut.shape), col_spec(rows), col_spec(rows),
            col_spec(rows),
        ],
        out_specs=[state_spec(), col_spec(rows), col_spec(rows)],
        out_shape=[f32s(NSTATE, SUB, DI), b16s(rows, DI), f32s(rows, DI)],
        scratch_shapes=[vm(NSTATE, rows, LANES), vm(NSTATE, SUB, LANES)],
        compiler_params=params(),
        cost_estimate=cost(rows, DI, 4),
        name="first",
    )(delta, alog, bc, cut, gbranch, z, ssm)


def run_back(xs, delta, alog, bc, cut, grad_ssm, skip, held, last, part):
    rows = xs.shape[0]
    chunks = rows // SUB // CHUNK
    big = (NSTATE, rows, LANES)
    row = (rows, LANES)
    width = DI // SPLITS
    first = part * (width // LANES)

    def col(count):
        return pl.BlockSpec((count, LANES), lambda c: (0, c + first))

    return pl.pallas_call(
        back_kernel,
        grid=(width // LANES,),
        in_specs=[
            col(rows), col(rows), col(NSTATE), full_spec(bc.shape), full_spec(cut.shape), col(rows), col(1),
            pl.BlockSpec((chunks, NSTATE, SUB, LANES), lambda c: (0, 0, 0, c + first)),
            pl.BlockSpec((NSTATE, SUB, LANES), lambda c: (0, 0, c + first)),
        ],
        out_specs=[col_spec(rows), col_spec(rows), col_spec(NSTATE), col_spec(SUB), full_spec(row)],
        out_shape=[f32s(rows, width), b16s(rows, width), f32s(NSTATE, width), f32s(SUB, width), f32s(*row)],
        scratch_shapes=[
            vm(*big), vm(*big), vm(*big), vm(*big), vm(NSTATE, SUB, LANES),
            vm(*row), vm(*row), vm(*row), vm(*row),
            vm(CHUNK, NSTATE, SUB, LANES), vm(CHUNK, NSTATE, SUB, LANES),
        ],
        compiler_params=params(),
        cost_estimate=cost(rows, width, 17),
        name="back",
    )(xs, delta, alog, bc, cut, grad_ssm, skip, held, last)


def conv_kernel(gxs_ref, gproj_ref, xproj_ref, ext_ref, taps_ref, bias_ref, same_ref, gext_ref, gvec_ref, acc_s):
    rows = gxs_ref.shape[0]
    halo = CONVK - 1
    taps = taps_ref[...]
    bias = bias_ref[...]
    pieces = []
    conv = bias
    for k in range(CONVK):
        piece = ext_ref[k * SUB : k * SUB + rows, :]
        if k < halo:
            piece = piece * same_ref[k]
        pieces.append(piece)
        conv = conv + taps[k : k + 1, :] * piece
    sig = 1.0 / (1.0 + jnp.exp(-conv))
    grad = gxs_ref[...] + dot(gproj_ref[...], xproj_ref[...], NT)
    grad = grad * (sig * (1.0 + conv * (1.0 - sig)))
    acc_s[...] = jnp.zeros_like(acc_s)
    for k in range(CONVK):
        gvec_ref[k : k + 1, :] = jnp.sum(grad * pieces[k], axis=0, keepdims=True)
        part = taps[k : k + 1, :] * grad
        if k < halo:
            part = part * same_ref[k]
        acc_s[k * SUB : k * SUB + rows, :] += part
    gvec_ref[CONVK : CONVK + 1, :] = jnp.sum(grad, axis=0, keepdims=True)
    gvec_ref[CONVK + 1 : SUB, :] = jnp.zeros((SUB - CONVK - 1, LANES), jnp.float32)
    gext_ref[...] = acc_s[...].astype(jnp.bfloat16)


def run_conv(gxs, gproj, xproj, ext, taps, bias, same, part):
    rows, width = gxs.shape
    long = ext.shape[0]
    first = part * (width // LANES)

    def col(count):
        return pl.BlockSpec((count, LANES), lambda c: (0, c + first))

    return pl.pallas_call(
        conv_kernel,
        grid=(width // LANES,),
        in_specs=[
            col_spec(rows), full_spec(gproj.shape), pl.BlockSpec((LANES, XW), lambda c: (c + first, 0)), col(long),
            col(CONVK), col(1), full_spec(same.shape),
        ],
        out_specs=[col_spec(long), col_spec(SUB)],
        out_shape=[b16s(long, width), f32s(SUB, width)],
        scratch_shapes=[vm(long, LANES)],
        compiler_params=params(),
        cost_estimate=pl.CostEstimate(flops=rows * width * 260, bytes_accessed=rows * width * 10, transcendentals=rows * width),
        name="conv",
    )(gxs, gproj, xproj, ext, taps, bias, same)


def halves_of(value, seqs):
    split = value.reshape(value.shape[:-2] + (seqs, HALVES, value.shape[-1]))
    return split[..., 0, :], split[..., 1, :]


def join_halves(first, second):
    both = jnp.stack([first, second], axis=-2)
    return both.reshape(both.shape[:-3] + (both.shape[-3] * HALVES, both.shape[-1]))


def chained(own, decay, steps):
    start = jnp.zeros_like(own)
    carry = own
    for k in range(lax.axis_size("seq") - 1):
        start = shifted(carry.astype(jnp.bfloat16), "seq", steps).astype(jnp.float32)
        carry = own + decay * start
    return start


def start_states(ends, sums, rates, seqs):
    end_0, end_1 = halves_of(ends, seqs)
    sum_0, sum_1 = halves_of(sums, seqs)
    decay_0 = jnp.exp(rates * sum_0)
    decay_1 = jnp.exp(rates * sum_1)
    start = chained(decay_1 * end_0 + end_1, decay_0 * decay_1, 1)
    return join_halves(start, decay_0 * start + end_0), (decay_0, decay_1)


def last_grads(leads, decays, seqs):
    decay_0, decay_1 = decays
    lead_0, lead_1 = halves_of(leads, seqs)
    last = chained(lead_0 + decay_0 * lead_1, decay_0 * decay_1, -1)
    return join_halves(lead_1 + decay_1 * last, last)


def ring(value, axis, step):
    count = lax.axis_size(axis)
    return lax.ppermute(value, axis, [(i, (i + step) % count) for i in range(count)])


def partner(value, axis, bits):
    count = lax.axis_size(axis)
    return lax.ppermute(value, axis, [(i, i ^ bits) for i in range(count)])


def held_for(first, *others):
    flat, tree = jax.tree.flatten((first,) + others)
    return jax.tree.unflatten(tree, lax.optimization_barrier(flat))


class Gather:
    def __init__(self, own):
        self.here, self.there = [own], []

    def step(self):
        self.there.append(ring(self.here[len(self.there)], "dp", 1))
        if len(self.here) < lax.axis_size("seq"):
            self.here.append(ring(self.here[-1], "seq", 1))

    def hold(self, value):
        value, here, there = held_for(value, self.here[1:], self.there)
        self.here[1:], self.there = here, there
        return value

    def done(self):
        return len(self.there) == lax.axis_size("seq")


class Reduce:
    def __init__(self, here, there, x_first):
        self.peers = lax.axis_size("seq")
        here = here.reshape(self.peers, -1, D)
        there = there.reshape(self.peers, -1, D)
        self.x_first, self.k, self.total = x_first, self.peers, None
        self.blocks = [(here[k], there[k]) for k in range(self.peers)]
        if x_first:
            self.moving = ring(there, "dp", 1)
        else:
            self.advance()

    def term(self, k):
        if self.x_first:
            return self.blocks[k][0].astype(jnp.float32) + self.other[k].astype(jnp.float32)
        return jnp.stack(self.blocks[k]).astype(jnp.float32)

    def advance(self):
        self.k -= 1
        self.total = self.term(self.k) if self.total is None else self.term(self.k) + self.moving.astype(jnp.float32)
        if self.k > 0:
            self.moving = ring(self.total.astype(jnp.bfloat16), "seq", -1)
        elif self.x_first:
            self.moving = None
        else:
            self.moving = ring(self.total[1].astype(jnp.bfloat16), "dp", 1)

    def step(self):
        if self.moving is None:
            return
        if self.x_first and self.total is None:
            self.other = self.moving
            self.advance()
        elif self.k > 0:
            self.advance()
        else:
            self.total = self.total[0] + self.moving.astype(jnp.float32)
            self.moving = None

    def finish(self):
        while self.moving is not None:
            self.step()
        return self.total


def hold_all(value, reduces):
    live = [r for r in reduces if r.moving is not None]
    value, moved = held_for(value, [r.moving for r in live])
    for r, m in zip(live, moved):
        r.moving = m
        r.step()
    return value


def sum_everywhere(value):
    for axis in ALL:
        bits = 1
        while bits < lax.axis_size(axis):
            value = value + partner(value, axis, bits)
            bits *= 2
    return value


def exchange(blocks):
    return [blocks[0]] + [partner(blocks[d], "expert", d) for d in range(1, len(blocks))]


def gelu_pair(v):
    inner = 0.7978845608 * (v + 0.044715 * v * v * v)
    t = jnp.tanh(inner)
    value = 0.5 * v * (1.0 + t)
    slope = 0.5 * (1.0 + t) + 0.5 * v * (1.0 - t * t) * (0.7978845608 * (1.0 + 3.0 * 0.044715 * v * v))
    return value, slope


def local(
    tokens, segment_ids, routes, keep_mask, out_grad, norm_one, in_proj, conv_weight, conv_bias, x_proj,
    dt_proj, dt_bias, a_log, d_skip, out_proj, norm_two, router, expert_up, expert_down,
):
    seqs, length = tokens.shape[:2]
    rows = seqs * length
    steps = length // HALVES
    halo = CONVK - 1
    capacity = seqs * max(2, length * 3 // 16)
    f32, b16 = jnp.float32, jnp.bfloat16
    own = in_proj.shape[1]

    small = jnp.concatenate(
        [x_proj, dt_proj.T, conv_weight.T, conv_bias[:, None], dt_bias[:, None], a_log.T, d_skip[:, None]], axis=1
    )
    used = small.shape[1]
    small = jnp.pad(small, ((0, 0), (0, PACK - used)))
    entry = lax.all_gather(jnp.concatenate([in_proj.T, small.reshape(-1, D)], axis=0), ALL, axis=0, tiled=False)
    in_full = entry[:, :own].reshape(2 * DI, D)
    small = entry[:, own:].reshape(DI, PACK)
    out_full = lax.all_gather(out_proj, ALL, axis=0, tiled=True)
    local_experts = expert_up.shape[0]
    shard = jnp.stack([m for e in range(local_experts) for m in (expert_up[e].T, expert_down[e])])
    shard, in_full = held_for(shard, in_full)
    gather = Gather(shard)
    gather.step()

    xproj_full = small[:, :XW]
    dtw = small[:, XW : XW + DTR]
    at = XW + DTR
    rest = small[:, at:used].T
    conv_w = rest[:CONVK].astype(f32)
    cbias = rest[CONVK : CONVK + 1].astype(f32)
    dtb = rest[CONVK + 1 : CONVK + 2]
    alog = rest[CONVK + 2 : CONVK + 2 + NSTATE]
    skip = rest[CONVK + 2 + NSTATE :]

    halo_tokens = shifted(tokens[:, length - halo :], "seq", 1)
    halo_segs = shifted(segment_ids[:, length - halo :].astype(f32), "seq", 1)
    inputs = to_ext_rows(tokens, halo_tokens).astype(f32)
    seg_ext = to_ext_rows(segment_ids.astype(f32), halo_segs)
    drop = to_rows(keep_mask).astype(f32)
    route = to_rows(routes[..., 0])
    grad_low = to_rows(out_grad)
    grad_final = grad_low.astype(f32)
    skip_rows = halo * SUB
    seg = seg_ext[skip_rows:]
    same = [(seg_ext[k * SUB : k * SUB + rows] == seg).astype(f32)[:, None] for k in range(halo)]
    same_wide = jnp.broadcast_to(jnp.stack(same), (halo, rows, LANES))
    cut = jnp.broadcast_to((1.0 - same[halo - 1]) * BIG, (rows, LANES))

    onehot = (route[:, None] == jnp.arange(EXPERTS, dtype=jnp.int32)).astype(f32)
    order = jnp.arange(rows)
    below = (order[None, :] < order[:, None]).astype(b16)
    rank = jnp.sum(dot(below, onehot.astype(b16), NN) * onehot, axis=-1).astype(jnp.int32)
    peers = lax.axis_size("expert")
    target = (route // local_experts) ^ lax.axis_index("expert")
    slot = (target * local_experts + route % local_experts) * capacity + rank
    placing = (jnp.arange(EXPERTS * capacity, dtype=jnp.int32)[:, None] == slot[None, :]).astype(b16)

    def dispatch(values):
        sent = dot(placing, values, NN, b16).reshape(peers, local_experts, capacity, values.shape[1])
        return exchange([sent[d] for d in range(peers)])

    gain_one = norm_one.astype(f32)
    inv_one = lax.rsqrt(jnp.mean(inputs * inputs, axis=-1, keepdims=True) + norm_eps)
    normed_one = (inputs * inv_one * gain_one).astype(b16)
    ext = dot(normed_one, in_full[:DI], NT)
    gate_z = dot(normed_one[skip_rows:], in_full[DI:], NT)
    conv_out = cbias + conv_w[halo] * ext[skip_rows:]
    for k in range(halo):
        conv_out = conv_out + conv_w[k] * (same[k] * ext[k * SUB : k * SUB + rows])
    xs = jax.nn.silu(conv_out).astype(b16)
    proj = dot(xs, xproj_full, NN)
    delta_in = proj[:, :DTR].astype(b16)
    bc = proj[:, DTR:]
    grad_arrived = dispatch(grad_low)
    delta, ends, sums = run_end(xs, delta_in, dtw, dtb, alog, bc, cut)
    ends, grad_arrived = held_for(ends, grad_arrived)
    rates = -jnp.exp(alog.astype(f32))[:, None, :]
    starts, decays = start_states(ends, sums, rates, seqs)
    starts = gather.hold(starts)
    gather.step()
    branch, ssm, held = run_out(xs, delta, alog, bc, cut, starts, gate_z, skip)
    tokens_rows = inputs[skip_rows:]
    first_sum = tokens_rows + dot(branch, out_full, NN)

    gain_two = norm_two.astype(f32)
    inv_two = lax.rsqrt(jnp.mean(first_sum * first_sum, axis=-1, keepdims=True) + norm_eps)
    normed_two = (first_sum * inv_two * gain_two).astype(b16)
    probs = jax.nn.softmax(dot(normed_two, router, NN), axis=-1)
    gate_raw = jnp.sum(probs * onehot, axis=-1)
    gate = gate_raw * drop
    gate_high = lax.reduce_precision(gate, 8, 7)
    gate_mid = lax.reduce_precision(gate - gate_high, 8, 7)
    gate_low = gate - gate_high - gate_mid
    gates = jnp.stack([gate_high, gate_mid, gate_low], axis=1).astype(b16)
    message = jnp.concatenate([normed_two, jnp.pad(gates, ((0, 0), (0, LANES - 3)))], axis=1)
    message = gather.hold(message)
    gather.step()
    arrived = dispatch(message)
    arrived = gather.hold(arrived)
    while not gather.done():
        gather.step()

    def matrices(blocks):
        return [jnp.concatenate([block[m] for block in blocks], axis=0) for m in range(2 * local_experts)]

    rows_of = []
    for e in range(local_experts):
        here = jnp.concatenate([part[e] for part in arrived], axis=0)
        gate_rows = jnp.sum(here[:, D : D + 3].astype(f32), axis=1, keepdims=True)
        g_rows = (gate_rows * jnp.concatenate([part[e] for part in grad_arrived], axis=0).astype(f32)).astype(b16)
        rows_of.append((here[:, :D], g_rows))
    sides, produced, grad_in = [], [0.0] * local_experts, [0.0] * local_experts
    for side in range(2):
        mats = matrices(gather.here if side == 0 else gather.there)
        kept = []
        for e in range(local_experts):
            x_rows, g_rows = rows_of[e]
            value, slope = gelu_pair(dot(x_rows, mats[2 * e], NT))
            hidden = value.astype(b16)
            produced[e] = produced[e] + dot(hidden, mats[2 * e + 1], NN)
            grad_pre = (slope * dot(g_rows, mats[2 * e + 1], NT)).astype(b16)
            grad_in[e] = grad_in[e] + dot(grad_pre, mats[2 * e], NN)
            kept.append((hidden, grad_pre))
        sides.append(kept)
        if side == 0:
            produced, grad_in = held_for(produced, grad_in)
            rows_of, produced, grad_in = gather.hold((rows_of, produced, grad_in))

    def send_back(parts):
        return [exchange([part.astype(b16).reshape(peers, capacity, D)[d] for d in range(peers)]) for part in parts]

    returned_y = send_back(produced)
    returned_g = send_back(grad_in)
    weight_grads = []
    for e in range(local_experts):
        x_rows, g_rows = rows_of[e]
        for m in range(2):
            left, right = (1, x_rows) if m == 0 else (0, g_rows)
            weight_grads.append([dot(sides[side][e][left], right, TN, b16) for side in range(2)])
    count = len(weight_grads)
    returned_y, returned_g, weight_grads = held_for(returned_y, returned_g, weight_grads)
    reduces = [Reduce(g[0], g[1], i < count - 1) for i, g in enumerate(weight_grads)]
    early = [reduces[0], reduces[-1]]

    def collect(parts):
        back_rows = jnp.stack([jnp.stack(part) for part in parts], axis=1).reshape(EXPERTS * capacity, D)
        return dot(placing, back_rows, TN)

    expert_rows = collect(returned_y)
    grad_back = collect(returned_g)
    output = (first_sum + gate[:, None] * expert_rows).astype(b16)

    grad_gate = jnp.sum(grad_final * expert_rows, axis=-1) * drop
    grad_logits = (grad_gate * gate_raw)[:, None] * (onehot - probs)
    logits_low = grad_logits.astype(b16)
    router_grad = dot(normed_two, logits_low, TN)
    grad_two = grad_back + dot(logits_low, router, NT)
    gain_two_grad = jnp.sum(grad_two * (first_sum * inv_two), axis=0)
    scaled = grad_two * gain_two
    grad_first = (
        grad_final + inv_two * scaled
        - first_sum * (inv_two * inv_two * inv_two * jnp.mean(scaled * first_sum, axis=-1, keepdims=True))
    )
    grad_first = hold_all(grad_first, reduces[-1:])
    first_low = grad_first.astype(b16)
    out_grad_part = dot(branch, first_low, TN, b16)
    grad_branch = dot(first_low, out_full, NT)
    grad_branch, out_grad_part = held_for(grad_branch, out_grad_part)
    out_sum = lax.psum_scatter(out_grad_part, ALL, scatter_dimension=0, tiled=True)
    grad_branch = hold_all(grad_branch, early)

    leads, grad_z, grad_ssm = run_first(delta, alog, bc, cut, grad_branch, gate_z, ssm)
    last = last_grads(leads, decays, seqs)
    gate_part = dot(grad_z, normed_one[skip_rows:], TN, b16)
    grad_normed_z = dot(grad_z, in_full[DI:], NN)
    grad_ssm, gate_part, grad_normed_z = held_for(grad_ssm, gate_part, grad_normed_z)
    gate_own = lax.psum_scatter(gate_part, ("seq", "expert"), scatter_dimension=0, tiled=True)
    grad_delta_in, gbc, parts = 0.0, 0.0, []
    width = DI // SPLITS
    for part in range(SPLITS):
        if part == 1:
            last, out_sum = held_for(last, out_sum)
        last = hold_all(last, reduces[: 2 + part] + reduces[-1:] if 2 + part < count else reduces)
        gxs, gpre, galog, gvec, gbc_part = run_back(xs, delta, alog, bc, cut, grad_ssm, skip, held, last, part)
        grad_delta_in = grad_delta_in + dot(gpre, dtw[part * width : (part + 1) * width], NN)
        gbc = gbc + gbc_part[:, : 2 * NSTATE]
        dtproj_part = dot(gpre, delta_in, TN)
        last, gxs, dtproj_part, grad_delta_in, gbc, galog, gvec = held_for(
            last, gxs, dtproj_part, grad_delta_in, gbc, galog, gvec
        )
        parts.append((gxs, dtproj_part, galog, gvec))
    grad_proj = jnp.concatenate([grad_delta_in, gbc], axis=1).astype(b16)
    grad_proj, gate_own = held_for(hold_all(grad_proj, reduces), gate_own)
    xproj_grad = dot(xs, grad_proj, TN)
    zeros = jnp.zeros((CONVK + 1, DI), f32)
    vecs = jnp.concatenate([p[3] for p in parts], axis=1)
    small_grad = jnp.concatenate(
        [
            xproj_grad,
            jnp.concatenate([p[1] for p in parts], axis=0),
            zeros.T,
            vecs[0][:, None],
            jnp.concatenate([p[2] for p in parts], axis=1).T,
            vecs[1][:, None],
        ],
        axis=1,
    ).astype(b16)
    small_grad = jnp.pad(small_grad, ((0, 0), (0, PACK - used)))
    small_grad, grad_proj = held_for(small_grad, grad_proj)
    small_sum = lax.psum_scatter(small_grad, ALL, scatter_dimension=0, tiled=True).astype(f32)
    grad_normed, conv_parts, conv_grads = 0.0, [], []
    for part in range(SPLITS):
        gext, gvec = run_conv(parts[part][0], grad_proj, xproj_full, ext, conv_w, cbias, same_wide, part)
        if part == SPLITS - 1:
            gext, small_sum = held_for(hold_all(gext, reduces), small_sum)
        conv_parts.append(dot(gext, normed_one, TN, b16))
        grad_normed = grad_normed + dot(gext, in_full[part * width : (part + 1) * width], NN)
        conv_grads.append(gvec)
    conv_all, grad_normed = held_for(jnp.concatenate(conv_parts, axis=0), grad_normed)
    conv_own = lax.psum_scatter(conv_all, ("seq", "expert"), scatter_dimension=0, tiled=True)
    is_gate = lax.axis_index("dp") == 1
    in_sum = jnp.where(is_gate, gate_own, conv_own).astype(f32)
    in_sum = in_sum + ring(jnp.where(is_gate, conv_own, gate_own), "dp", 1).astype(f32)

    over = grad_normed[:skip_rows].reshape(halo, seqs, HALVES, D)
    from_next = shifted(over[:, :, 0], "seq", -1)
    edge = jnp.stack([over[:, :, 1], from_next], axis=2).reshape(skip_rows, D)
    grad_normed = grad_normed[skip_rows:] + grad_normed_z
    grad_normed = grad_normed + jnp.pad(edge, ((rows - skip_rows, 0), (0, 0)))
    inv_rows = inv_one[skip_rows:]
    gain_one_grad = jnp.sum(grad_normed * (tokens_rows * inv_rows), axis=0)
    scaled_one = grad_normed * gain_one
    grad_tokens = (
        grad_first + inv_rows * scaled_one
        - tokens_rows * (inv_rows * inv_rows * inv_rows * jnp.mean(scaled_one * tokens_rows, axis=-1, keepdims=True))
    )
    conv_grad = jnp.concatenate(conv_grads, axis=1)[: CONVK + 1]
    flat = jnp.concatenate([gain_one_grad, gain_two_grad, router_grad.reshape(-1), conv_grad.reshape(-1)])
    flat = sum_everywhere(flat.reshape(-1, LANES)).reshape(-1)
    gain_one_sum, gain_two_sum = flat[:D], flat[D : 2 * D]
    router_sum = flat[2 * D : (2 + EXPERTS) * D].reshape(D, EXPERTS)
    conv_sum = flat[(2 + EXPERTS) * D :].reshape(CONVK + 1, DI)
    place = (lax.axis_index("dp") * lax.axis_size("seq") + lax.axis_index("seq")) * peers + lax.axis_index("expert")
    channels = own // 2
    conv_sum = lax.dynamic_slice_in_dim(conv_sum, place * channels, channels, axis=1)

    small_sum = small_sum.T
    return (
        from_rows(output, seqs),
        from_rows(grad_tokens, seqs),
        gain_one_sum,
        in_sum.T,
        conv_sum[:CONVK],
        conv_sum[CONVK],
        small_sum[:XW].T,
        small_sum[XW : XW + DTR],
        small_sum[at + CONVK + 1],
        small_sum[at + CONVK + 2 : at + CONVK + 2 + NSTATE],
        small_sum[used - 1],
        out_sum.astype(f32),
        gain_two_sum,
        router_sum,
        jnp.stack([r.finish().T for r in reduces[0::2]]),
        jnp.stack([r.finish() for r in reduces[1::2]]),
    )


def solution(mesh):
    batch = ("dp", "expert")
    split = ("dp", "seq")
    return jax.shard_map(
        local,
        mesh=mesh,
        in_specs=(
            P(batch, "seq", None),
            P(batch, "seq"),
            P(batch, "seq", None),
            P(batch, "seq"),
            P(batch, "seq", None),
            P(),
            P(None, ALL),
            P(None, ALL),
            P(ALL),
            P(ALL, None),
            P(None, ALL),
            P(ALL),
            P(None, ALL),
            P(ALL),
            P(ALL, None),
            P(),
            P(),
            P("expert", None, split),
            P("expert", split, None),
        ),
        out_specs=(
            P(batch, "seq", None),
            P(batch, "seq", None),
            P(),
            P(None, ALL),
            P(None, ALL),
            P(ALL),
            P(ALL, None),
            P(None, ALL),
            P(ALL),
            P(None, ALL),
            P(ALL),
            P(ALL, None),
            P(),
            P(),
            P("expert", None, split),
            P("expert", split, None),
        ),
        check_vma=False,
    )
```

time: 6470 us -> 1520 us (0.23); the launches traced: 6370 us -> 1510 us
  other arithmetic: 2470 us -> 104 us
  local copies, waits for them, and re-layouts: 1600 us -> 167 us
  waiting for transfers between devices: 1540 us -> 436 us
  Pallas kernels: 0 us -> 381 us
  blocking collectives: 199 us -> 0 us
  loops' own time: 93.3 us -> 0 us
  matrix products: 404 us -> 312 us
    reduce_scatter x3 -> x2, waiting for transfers between devices: 1130 us -> 3.83 us  [the longest x1 3.81 us: local(): lax.psum_scatter(conv_all, ('seq', 'expert'), scatter_dimension=0, tiled=...]
    reduce_sum x1543 -> x6, other arithmetic: 1060 us -> 8.54 us  [the longest x1 7.6 us: local(): gain_one_grad = jnp.sum(grad_normed * (tokens_rows * inv_rows), axis=0)]
    dynamic_update_slice x2688 -> x0, local copies, waits for them, and re-layouts: 604 us -> none  [the longest x2560 488 us: block_step(): state_end, outs = lax.scan(token_step, state_now, ordered)]
    mul x1540 -> x4, other arithmetic: 588 us -> 0.03 us  [the longest x1 0.01 us: local(): inv_rows * inv_rows * inv_rows]
    dynamic_update_slice x1536 -> x0, other arithmetic: 587 us -> none  [the longest x512 558 us: ssm_local(): lax.scan(jax.checkpoint(block_step), start_state, (arrange(xs_vals), arra...]
    mul x6144 -> x1, local copies, waits for them, and re-layouts: 419 us -> 0.25 us  [local(): inv_rows * scaled_one]
    pallas_call x0 -> x9, Pallas kernels: none -> 381 us  [the longest x3 214 us: run_back(): pl.pallas_call(back_kernel, grid=(width // LANES,), in_specs=[col(rows),...]
    unnamed x20 -> x7, waiting for transfers between devices: 353 us -> 58.6 us
where the time goes in v1:
time: 1520 us; the launch traced here: 1510 us
  waiting for transfers between devices  436 us (29%)
  Pallas kernels  381 us (25%)
  matrix products  312 us (21%)
  local copies, waits for them, and re-layouts  167 us (11%)
  other arithmetic  104 us (7%)
  starting transfers between devices  91.3 us (6%)
  between operations  17 us (1%)
    dot_general x53, matrix products, dot(): lax.dot_general(left, right, (dims, ((), ())), preferred_element_type=out)  312 us
    pallas_call x3, Pallas kernels, run_back(): pl.pallas_call(back_kernel, grid=(width // LANES,), in_specs=[col(rows),...  214 us
    ppermute x9, waiting for transfers between devices, shifted(): lax.ppermute(value, axis, [(source, source + steps) for source in range(f...  117 us
    ppermute x23, waiting for transfers between devices, partner(): return lax.ppermute(value, axis, [(i, i ^ bits) for i in range(count)])  115 us
    ppermute x24, waiting for transfers between devices, ring(): lax.ppermute(value, axis, [(i, (i + step) % count) for i in range(count)])  98.1 us
    unnamed x7, waiting for transfers between devices  58.6 us
    pallas_call x1, Pallas kernels, run_out(): pl.pallas_call(out_kernel, grid=(DI // LANES,), in_specs=[col_spec(rows),...  55.6 us
    pallas_call x1, Pallas kernels, run_end(): pl.pallas_call(end_kernel, grid=(DI // LANES,), in_specs=[col_spec(rows),...  45.2 us
  transfers between devices with their start and end apart: 62, of which 30 were waited for; matrix products, arithmetic and copies ran while one was open for 28% of the time, Pallas kernels for 25%

profile of v1, /device:TPU:0, one launch (start us, length us, event | category | flops | bytes accessed | tf_op | source)
XLA Modules:
  0.0 1509.3 jit_solution(5366625352667929084)
XLA Ops:
  79.2 43.9 %all-gather.6.cloned.1.call-done = bf16[5120,1152]{1,0:T(8,128)(2,1)} async-done(((bf16[160,1152]{1,0:T(8,128)(2,1)}), bf16[5120,1152]{1,0:T(8,128)(2,1)}) %all-gather.6.cloned.1.call-update) | async-done | bytes 11796496 | tf_op jit(solution)/shard_map/all_gather | solution.py:631
  123.2 9.4 slice.833
  136.4 9.7 fusion.11.ext_ref
  146.2 7.1 multiply_convert_fusion.xs_ref
  160.7 45.2 %end.1 = (f32[1024,2304]{1,0:T(8,128)}, f32[16,8,2304]{2,1,0:T(8,128)}, f32[8,2304]{1,0:T(8,128)}) custom-call(bf16[1024,2304]{1,0:T(8,128)(2,1)} %copy-done.2, bf16[1024,72]{1,0:T(8,128)(2,1)} %copy.212.din_ref, bf16[2304,72]{1,0:T(8,128)(2,1)} %slice.848.dtw_ref, bf16[1,2304]{1,0:T(2,128)(2,1)} %get-tuple-element.499.dtb_ref, ...), custom_call_target="tpu_custom_call" | custom-call | flops 301989888 | bytes 150994944 | tf_op jit(solution)/shard_map/end/pallas_call | solution.py:329
  247.8 11.5 fusion.51.z_ref
  259.3 63.9 %collective-permute-done.7 = bf16[16,4,2304]{2,1,0:T(4,128)(2,1)S(1)} collective-permute-done((bf16[16,4,2304]{2,1,0:T(4,128)(2,1)S(1)}, bf16[16,4,2304]{2,1,0:T(4,128)(2,1)S(1)}, u32[]{:S(2)}, u32[]{:S(2)}) %collective-permute-start.7) | collective-permute-done | bytes 294944 | tf_op jit(solution)/shard_map/ppermute | solution.py:34
  330.5 55.6 %out.1 = (bf16[1024,2304]{1,0:T(8,128)(2,1)}, bf16[1024,2304]{1,0:T(8,128)(2,1)}, f32[8,16,8,2304]{3,2,1,0:T(8,128)}) custom-call(bf16[1024,2304]{1,0:T(8,128)(2,1)} %copy-done.2, f32[1024,2304]{1,0:T(8,128)} %get-tuple-element.170.delta_ref, bf16[16,2304]{1,0:T(8,128)(2,1)} %slice.850.alog_ref, f32[1024,32]{1,0:T(8,128)} %copy.213.bc_ref, ...), custom_call_target="tpu_custom_call" | custom-call | flops 301989888 | bytes 188743680 | tf_op jit(solution)/shard_map/out/pallas_call | solution.py:348
  386.1 10.6 multiply_reduce_fusion.4
  422.4 21.0 %collective-permute-done.13 = bf16[2,192,1280]{2,1,0:T(8,128)(2,1)S(1)} collective-permute-done((bf16[2,192,1280]{2,1,0:T(8,128)(2,1)S(1)}, bf16[2,192,1280]{2,1,0:T(8,128)(2,1)S(1)}, u32[]{:S(2)}, u32[]{:S(2)}) %collective-permute-start.13) | collective-permute-done | bytes 983072 | tf_op jit(solution)/shard_map/ppermute | solution.py:513
  443.5 20.2 %collective-permute-done.14 = bf16[2,192,1280]{2,1,0:T(8,128)(2,1)S(1)} collective-permute-done((bf16[2,192,1280]{2,1,0:T(8,128)(2,1)S(1)}, bf16[2,192,1280]{2,1,0:T(8,128)(2,1)S(1)}, u32[]{:S(2)}, u32[]{:S(2)}) %collective-permute-start.14) | collective-permute-done | bytes 983072 | tf_op jit(solution)/shard_map/ppermute | solution.py:513
  463.6 21.1 %collective-permute-done.15 = bf16[4,384,1152]{2,1,0:T(8,128)(2,1)} collective-permute-done((bf16[4,384,1152]{2,1,0:T(8,128)(2,1)}, bf16[4,384,1152]{2,1,0:T(8,128)(2,1)}, u32[]{:S(2)}, u32[]{:S(2)}) %collective-permute-start.15) | collective-permute-done | bytes 3538976 | tf_op jit(solution)/shard_map/ppermute | solution.py:508
  494.3 7.1 fusion.108
  501.9 12.4 fusion.26
  521.0 7.1 fusion.105
  528.5 11.6 fusion.32
  578.9 7.3 fusion.102
  592.6 12.5 fusion.42
  617.4 7.8 fusion.164
  635.3 7.2 fusion.99
  642.5 8.2 fusion.97
  650.7 12.4 fusion.48
  687.0 8.4 collective-permute-done.20
  697.5 8.3 collective-permute-done.22
  705.8 8.6 collective-permute-done.23
  724.8 8.6 collective-permute-done.26
  733.4 10.4 collective-permute-done.28
  743.7 8.6 collective-permute-done.29
  780.0 30.5 %collective-permute-done.30 = bf16[2,384,1152]{2,1,0:T(8,128)(2,1)S(1)} collective-permute-done((bf16[2,384,1152]{2,1,0:T(8,128)(2,1)S(1)}, bf16[2,384,1152]{2,1,0:T(8,128)(2,1)S(1)}, u32[]{:S(2)}, u32[]{:S(2)}) %collective-permute-start.30) | collective-permute-done | bytes 1769504 | tf_op jit(solution)/shard_map/ppermute | solution.py:508
  815.5 11.2 fusion.92.gb_ref
  826.7 8.1 fusion.90
  834.9 16.0 %collective-permute-done.31 = bf16[4,384,1152]{2,1,0:T(8,128)(2,1)} collective-permute-done((bf16[4,384,1152]{2,1,0:T(8,128)(2,1)}, bf16[4,384,1152]{2,1,0:T(8,128)(2,1)}, u32[]{:S(2)}, u32[]{:S(2)}) %collective-permute-start.31) | collective-permute-done | bytes 3538976 | tf_op jit(solution)/shard_map/ppermute | solution.py:508
  854.5 39.6 %first.1 = (f32[16,8,2304]{2,1,0:T(8,128)}, bf16[1024,2304]{1,0:T(8,128)(2,1)}, f32[1024,2304]{1,0:T(8,128)}) custom-call(f32[1024,2304]{1,0:T(8,128)} %get-tuple-element.170.delta_ref, bf16[16,2304]{1,0:T(8,128)(2,1)} %slice.850.alog_ref, f32[1024,32]{1,0:T(8,128)} %copy.213.bc_ref, f32[1024,128]{1,0:T(8,128)} %broadcast_in_dim.18.cut_ref, ...), custom_call_target="tpu_custom_call" | custom-call | flops 301989888 | bytes 150994944 | tf_op jit(solution)/shard_map/first/pallas_call | solution.py:371
  899.4 10.1 fusion.59
  909.6 11.2 fusion.49
  930.3 7.2 collective-permute-done.34
  946.4 38.9 %collective-permute-done.35 = bf16[16,4,2304]{2,1,0:T(4,128)(2,1)S(1)} collective-permute-done((bf16[16,4,2304]{2,1,0:T(4,128)(2,1)S(1)}, bf16[16,4,2304]{2,1,0:T(4,128)(2,1)S(1)}, u32[]{:S(2)}, u32[]{:S(2)}) %collective-permute-start.35) | collective-permute-done | bytes 294944 | tf_op jit(solution)/shard_map/ppermute | solution.py:34
  991.1 12.2 collective-permute-done.36
  1021.3 71.4 %back.3 = (f32[1024,768]{1,0:T(8,128)}, bf16[1024,768]{1,0:T(8,128)(2,1)}, f32[16,768]{1,0:T(8,128)}, f32[8,768]{1,0:T(8,128)}, f32[1024,128]{1,0:T(8,128)}) custom-call(bf16[1024,2304]{1,0:T(8,128)(2,1)} %copy-done.2, f32[1024,2304]{1,0:T(8,128)} %get-tuple-element.170.delta_ref, bf16[16,2304]{1,0:T(8,128)(2,1)} %slice.850.alog_ref, ...), custom_call_target="tpu_custom_call" | custom-call | flops 100663296 | bytes 213909504 | tf_op jit(solution)/shard_map/back/pallas_call | solution.py:398
  1118.2 71.5 %back.4 = (f32[1024,768]{1,0:T(8,128)}, bf16[1024,768]{1,0:T(8,128)(2,1)}, f32[16,768]{1,0:T(8,128)}, f32[8,768]{1,0:T(8,128)}, f32[1024,128]{1,0:T(8,128)}) custom-call(bf16[1024,2304]{1,0:T(8,128)(2,1)} %copy-done.2, f32[1024,2304]{1,0:T(8,128)} %get-tuple-element.170.delta_ref, bf16[16,2304]{1,0:T(8,128)(2,1)} %slice.850.alog_ref, ...), custom_call_target="tpu_custom_call" | custom-call | flops 100663296 | bytes 213909504 | tf_op jit(solution)/shard_map/back/pallas_call | solution.py:398
  1202.7 71.5 %back.5 = (f32[1024,768]{1,0:T(8,128)}, bf16[1024,768]{1,0:T(8,128)(2,1)}, f32[16,768]{1,0:T(8,128)}, f32[8,768]{1,0:T(8,128)}, f32[1024,128]{1,0:T(8,128)}) custom-call(bf16[1024,2304]{1,0:T(8,128)(2,1)} %copy-done.2, f32[1024,2304]{1,0:T(8,128)} %get-tuple-element.170.delta_ref, bf16[16,2304]{1,0:T(8,128)(2,1)} %slice.850.alog_ref, ...), custom_call_target="tpu_custom_call" | custom-call | flops 100663296 | bytes 213909504 | tf_op jit(solution)/shard_map/back/pallas_call | solution.py:398
  1287.2 8.8 conv.5
  1300.5 8.8 conv.4
  1309.4 9.0 conv.3
  1337.8 58.6 %reduce-scatter.13.cloned.1.call-done = bf16[72,256]{1,0:T(8,128)(2,1)} async-done(((bf16[2304,256]{1,0:T(8,128)(2,1)}), bf16[72,256]{1,0:T(8,128)(2,1)}) %reduce-scatter.13.cloned.1.call-update) | async-done | bytes 36880
  1430.4 7.6 multiply_reduce_fusion.1
  1452.9 8.4 collective-permute-done.52
  1467.1 8.0 multiply_subtract_fusion
  (645 shorter events, 517.6 us)
Async XLA Ops:
  7.2 116.0 %all-gather.6.cloned.1.call-start = ((), (), s32[]{:S(2)}) async-start(), calls=%async_computation.7 | async-start | bytes 12165120 | tf_op jit(solution)/shard_map/all_gather | solution.py:631
  14.6 371.5 %all-gather.4.cloned.1.call-start = ((), (), s32[]{:S(2)}) async-start(), calls=%async_computation.4 | async-start | bytes 5474304 | tf_op jit(solution)/shard_map/all_gather | solution.py:634
  15.6 42.7 %collective-permute-start = (bf16[4,3,1152]{2,1,0:T(4,128)(2,1)S(1)}, bf16[4,3,1152]{2,1,0:T(4,128)(2,1)S(1)}, u32[]{:S(2)}, u32[]{:S(2)}) collective-permute-start(bf16[4,3,1152]{2,1,0:T(4,128)(2,1)S(1)} %slice.633), channel_id=1, source_target_pairs={{0,4},{4,8},{8,12},{1,5},{5,9},{9,13},{2,6},{6,10},{10,14},{3,7},{... | collective-permute-start | bytes 82952 | tf_op jit(solution)/shard_map/ppermute | solution.py:34
  21.3 30.1 %collective-permute-start.1 = (f32[4,3]{1,0:T(4,128)S(1)}, f32[4,3]{1,0:T(4,128)S(1)}, u32[]{:S(2)}, u32[]{:S(2)}) collective-permute-start(f32[4,3]{1,0:T(4,128)S(1)} %slice_convert_fusion.4), channel_id=1, source_target_pairs={{0,4},{4,8},{8,12},{1,5},{5,9},{9,13},{2,6},{6,10},{10,14},{3,7},{... | collective-permute-start | bytes 152 | tf_op jit(solution)/shard_map/ppermute | solution.py:34
  40.2 165.8 %collective-permute-start.2 = (bf16[2,192,1152]{2,1,0:T(8,128)(2,1)}, bf16[2,192,1152]{2,1,0:T(8,128)(2,1)}, u32[]{:S(2)}, u32[]{:S(2)}) collective-permute-start(bf16[2,192,1152]{2,1,0:T(8,128)(2,1)} %bitcast.28), channel_id=1, source_target_pairs={{0,1},{1,0},{2,3},{3,2},{4,5},{5,4},{6,7},{7,6},{8,9},{9,8},{10,11... | collective-permute-start | bytes 2654216 | tf_op jit(solution)/shard_map/ppermute | solution.py:513
  40.2 165.8 %collective-permute-start.3 = (bf16[2,192,1152]{2,1,0:T(8,128)(2,1)}, bf16[2,192,1152]{2,1,0:T(8,128)(2,1)}, u32[]{:S(2)}, u32[]{:S(2)}) collective-permute-start(bf16[2,192,1152]{2,1,0:T(8,128)(2,1)} %bitcast.29), channel_id=1, source_target_pairs={{0,2},{1,3},{2,0},{3,1},{4,6},{5,7},{6,4},{7,5},{8,10},{9,11},{10,... | collective-permute-start | bytes 2654216 | tf_op jit(solution)/shard_map/ppermute | solution.py:513
  41.7 164.3 %collective-permute-start.4 = (bf16[2,192,1152]{2,1,0:T(8,128)(2,1)}, bf16[2,192,1152]{2,1,0:T(8,128)(2,1)}, u32[]{:S(2)}, u32[]{:S(2)}) collective-permute-start(bf16[2,192,1152]{2,1,0:T(8,128)(2,1)} %bitcast.30), channel_id=1, source_target_pairs={{0,3},{1,2},{2,1},{3,0},{4,7},{5,6},{6,5},{7,4},{8,11},{9,10},{10,... | collective-permute-start | bytes 2654216 | tf_op jit(solution)/shard_map/ppermute | solution.py:513
  42.1 1054.5 %reduce-scatter.15.cloned.1.call-start = ((), (), s32[]{:S(2)}) async-start(), calls=%async_computation.9 | async-start | bytes 5474304
  220.4 22.6 %collective-permute-start.6 = (bf16[16,4,2304]{2,1,0:T(4,128)(2,1)S(1)}, bf16[16,4,2304]{2,1,0:T(4,128)(2,1)S(1)}, u32[]{:S(2)}, u32[]{:S(2)}) collective-permute-start(bf16[16,4,2304]{2,1,0:T(4,128)(2,1)S(1)} %add_convert_fusion.10), channel_id=1, source_target_pairs={{0,4},{4,8},{8,12},{1,5},{5,9},{9,13},{2,6},{6,10},{10,14},{3,7},{... | collective-permute-start | bytes 884744 | tf_op jit(solution)/shard_map/ppermute | solution.py:34
  240.9 85.6 %collective-permute-start.8 = (bf16[4,384,1152]{2,1,0:T(8,128)(2,1)}, bf16[4,384,1152]{2,1,0:T(8,128)(2,1)}, u32[]{:S(2)}, u32[]{:S(2)}) collective-permute-start(bf16[4,384,1152]{2,1,0:T(8,128)(2,1)} %pad_maximum_fusion.1), channel_id=1, source_target_pairs={{0,4},{4,8},{8,12},{12,0},{1,5},{5,9},{9,13},{13,1},{2,6},{6,10},{... | collective-permute-start | bytes 10616840 | tf_op jit(solution)/shard_map/ppermute | solution.py:508
  241.6 85.0 %collective-permute-start.9 = (bf16[4,384,1152]{2,1,0:T(8,128)(2,1)}, bf16[4,384,1152]{2,1,0:T(8,128)(2,1)}, u32[]{:S(2)}, u32[]{:S(2)}) collective-permute-start(bf16[4,384,1152]{2,1,0:T(8,128)(2,1)} %pad_maximum_fusion.1), channel_id=1, source_target_pairs={{0,16},{16,0},{1,17},{17,1},{2,18},{18,2},{3,19},{19,3},{4,20},{20... | collective-permute-start | bytes 10616840 | tf_op jit(solution)/shard_map/ppermute | solution.py:508
  243.6 79.6 %collective-permute-start.7 = (bf16[16,4,2304]{2,1,0:T(4,128)(2,1)S(1)}, bf16[16,4,2304]{2,1,0:T(4,128)(2,1)S(1)}, u32[]{:S(2)}, u32[]{:S(2)}) collective-permute-start(bf16[16,4,2304]{2,1,0:T(4,128)(2,1)S(1)} %add_convert_fusion.9), channel_id=1, source_target_pairs={{0,4},{4,8},{8,12},{1,5},{5,9},{9,13},{2,6},{6,10},{10,14},{3,7},{... | collective-permute-start | bytes 884744 | tf_op jit(solution)/shard_map/ppermute | solution.py:34
  326.6 79.5 %collective-permute-start.10 = (bf16[4,384,1152]{2,1,0:T(8,128)(2,1)}, bf16[4,384,1152]{2,1,0:T(8,128)(2,1)}, u32[]{:S(2)}, u32[]{:S(2)}) collective-permute-start(bf16[4,384,1152]{2,1,0:T(8,128)(2,1)} %collective-permute-done.8), channel_id=1, source_target_pairs={{0,4},{4,8},{8,12},{12,0},{1,5},{5,9},{9,13},{13,1},{2,6},{6,10},{... | collective-permute-start | bytes 10616840 | tf_op jit(solution)/shard_map/ppermute | solution.py:508
  329.1 77.0 %collective-permute-start.11 = (bf16[4,384,1152]{2,1,0:T(8,128)(2,1)}, bf16[4,384,1152]{2,1,0:T(8,128)(2,1)}, u32[]{:S(2)}, u32[]{:S(2)}) collective-permute-start(bf16[4,384,1152]{2,1,0:T(8,128)(2,1)} %collective-permute-done.8), channel_id=1, source_target_pairs={{0,16},{16,0},{1,17},{17,1},{2,18},{18,2},{3,19},{19,3},{4,20},{20... | collective-permute-start | bytes 10616840 | tf_op jit(solution)/shard_map/ppermute | solution.py:508
  406.1 78.6 %collective-permute-start.15 = (bf16[4,384,1152]{2,1,0:T(8,128)(2,1)}, bf16[4,384,1152]{2,1,0:T(8,128)(2,1)}, u32[]{:S(2)}, u32[]{:S(2)}) collective-permute-start(bf16[4,384,1152]{2,1,0:T(8,128)(2,1)} %collective-permute-done.10), channel_id=1, source_target_pairs={{0,4},{4,8},{8,12},{12,0},{1,5},{5,9},{9,13},{13,1},{2,6},{6,10},{... | collective-permute-start | bytes 10616840 | tf_op jit(solution)/shard_map/ppermute | solution.py:508
  408.3 76.4 %collective-permute-start.16 = (bf16[4,384,1152]{2,1,0:T(8,128)(2,1)}, bf16[4,384,1152]{2,1,0:T(8,128)(2,1)}, u32[]{:S(2)}, u32[]{:S(2)}) collective-permute-start(bf16[4,384,1152]{2,1,0:T(8,128)(2,1)} %collective-permute-done.10), channel_id=1, source_target_pairs={{0,16},{16,0},{1,17},{17,1},{2,18},{18,2},{3,19},{19,3},{4,20},{20... | collective-permute-start | bytes 10616840 | tf_op jit(solution)/shard_map/ppermute | solution.py:508
  418.9 24.6 %collective-permute-start.13 = (bf16[2,192,1280]{2,1,0:T(8,128)(2,1)S(1)}, bf16[2,192,1280]{2,1,0:T(8,128)(2,1)S(1)}, u32[]{:S(2)}, u32[]{:S(2)}) collective-permute-start(bf16[2,192,1280]{2,1,0:T(8,128)(2,1)S(1)} %bitcast.443), channel_id=1, source_target_pairs={{0,2},{1,3},{2,0},{3,1},{4,6},{5,7},{6,4},{7,5},{8,10},{9,11},{10,... | collective-permute-start | bytes 2949128 | tf_op jit(solution)/shard_map/ppermute | solution.py:513
  420.4 43.2 %collective-permute-start.14 = (bf16[2,192,1280]{2,1,0:T(8,128)(2,1)S(1)}, bf16[2,192,1280]{2,1,0:T(8,128)(2,1)S(1)}, u32[]{:S(2)}, u32[]{:S(2)}) collective-permute-start(bf16[2,192,1280]{2,1,0:T(8,128)(2,1)S(1)} %bitcast.442), channel_id=1, source_target_pairs={{0,3},{1,2},{2,1},{3,0},{4,7},{5,6},{6,5},{7,4},{8,11},{9,10},{10,... | collective-permute-start | bytes 2949128 | tf_op jit(solution)/shard_map/ppermute | solution.py:513
  487.1 75.6 %collective-permute-start.17 = (bf16[4,384,1152]{2,1,0:T(8,128)(2,1)}, bf16[4,384,1152]{2,1,0:T(8,128)(2,1)S(1)}, u32[]{:S(2)}, u32[]{:S(2)}) collective-permute-start(bf16[4,384,1152]{2,1,0:T(8,128)(2,1)} %collective-permute-done.15), channel_id=1, source_target_pairs={{0,16},{16,0},{1,17},{17,1},{2,18},{18,2},{3,19},{19,3},{4,20},{20... | collective-permute-start | bytes 10616840 | tf_op jit(solution)/shard_map/ppermute | solution.py:508
  676.9 28.9 %collective-permute-start.22 = (bf16[192,1152]{1,0:T(8,128)(2,1)S(1)}, bf16[192,1152]{1,0:T(8,128)(2,1)S(1)}, u32[]{:S(2)}, u32[]{:S(2)}) collective-permute-start(bf16[192,1152]{1,0:T(8,128)(2,1)S(1)} %get-tuple-element.462), channel_id=1, source_target_pairs={{0,2},{1,3},{2,0},{3,1},{4,6},{5,7},{6,4},{7,5},{8,10},{9,11},{10,... | collective-permute-start | bytes 1327112 | tf_op jit(solution)/shard_map/ppermute | solution.py:513
  684.6 29.8 %collective-permute-start.23 = (bf16[192,1152]{1,0:T(8,128)(2,1)S(1)}, bf16[192,1152]{1,0:T(8,128)(2,1)S(1)}, u32[]{:S(2)}, u32[]{:S(2)}) collective-permute-start(bf16[192,1152]{1,0:T(8,128)(2,1)S(1)} %get-tuple-element.461), channel_id=1, source_target_pairs={{0,3},{1,2},{2,1},{3,0},{4,7},{5,6},{6,5},{7,4},{8,11},{9,10},{10,... | collective-permute-start | bytes 1327112 | tf_op jit(solution)/shard_map/ppermute | solution.py:513
  686.9 29.0 %collective-permute-start.24 = (bf16[192,1152]{1,0:T(8,128)(2,1)S(1)}, bf16[192,1152]{1,0:T(8,128)(2,1)S(1)}, u32[]{:S(2)}, u32[]{:S(2)}) collective-permute-start(bf16[192,1152]{1,0:T(8,128)(2,1)S(1)} %get-tuple-element.459), channel_id=1, source_target_pairs={{0,1},{1,0},{2,3},{3,2},{4,5},{5,4},{6,7},{7,6},{8,9},{9,8},{10,11... | collective-permute-start | bytes 1327112 | tf_op jit(solution)/shard_map/ppermute | solution.py:513
  695.4 29.3 %collective-permute-start.25 = (bf16[192,1152]{1,0:T(8,128)(2,1)S(1)}, bf16[192,1152]{1,0:T(8,128)(2,1)S(1)}, u32[]{:S(2)}, u32[]{:S(2)}) collective-permute-start(bf16[192,1152]{1,0:T(8,128)(2,1)S(1)} %get-tuple-element.458), channel_id=1, source_target_pairs={{0,2},{1,3},{2,0},{3,1},{4,6},{5,7},{6,4},{7,5},{8,10},{9,11},{10,... | collective-permute-start | bytes 1327112 | tf_op jit(solution)/shard_map/ppermute | solution.py:513
  697.0 36.4 %collective-permute-start.26 = (bf16[192,1152]{1,0:T(8,128)(2,1)S(1)}, bf16[192,1152]{1,0:T(8,128)(2,1)S(1)}, u32[]{:S(2)}, u32[]{:S(2)}) collective-permute-start(bf16[192,1152]{1,0:T(8,128)(2,1)S(1)} %get-tuple-element.457), channel_id=1, source_target_pairs={{0,3},{1,2},{2,1},{3,0},{4,7},{5,6},{6,5},{7,4},{8,11},{9,10},{10,... | collective-permute-start | bytes 1327112 | tf_op jit(solution)/shard_map/ppermute | solution.py:513
  705.8 27.5 %collective-permute-start.27 = (bf16[192,1152]{1,0:T(8,128)(2,1)S(1)}, bf16[192,1152]{1,0:T(8,128)(2,1)S(1)}, u32[]{:S(2)}, u32[]{:S(2)}) collective-permute-start(bf16[192,1152]{1,0:T(8,128)(2,1)S(1)} %get-tuple-element.455), channel_id=1, source_target_pairs={{0,1},{1,0},{2,3},{3,2},{4,5},{5,4},{6,7},{7,6},{8,9},{9,8},{10,11... | collective-permute-start | bytes 1327112 | tf_op jit(solution)/shard_map/ppermute | solution.py:513
  714.4 29.3 %collective-permute-start.28 = (bf16[192,1152]{1,0:T(8,128)(2,1)S(1)}, bf16[192,1152]{1,0:T(8,128)(2,1)S(1)}, u32[]{:S(2)}, u32[]{:S(2)}) collective-permute-start(bf16[192,1152]{1,0:T(8,128)(2,1)S(1)} %get-tuple-element.454), channel_id=1, source_target_pairs={{0,2},{1,3},{2,0},{3,1},{4,6},{5,7},{6,4},{7,5},{8,10},{9,11},{10,... | collective-permute-start | bytes 1327112 | tf_op jit(solution)/shard_map/ppermute | solution.py:513
  715.9 36.4 %collective-permute-start.29 = (bf16[192,1152]{1,0:T(8,128)(2,1)S(1)}, bf16[192,1152]{1,0:T(8,128)(2,1)S(1)}, u32[]{:S(2)}, u32[]{:S(2)}) collective-permute-start(bf16[192,1152]{1,0:T(8,128)(2,1)S(1)} %get-tuple-element.453), channel_id=1, source_target_pairs={{0,3},{1,2},{2,1},{3,0},{4,7},{5,6},{6,5},{7,4},{8,11},{9,10},{10,... | collective-permute-start | bytes 1327112 | tf_op jit(solution)/shard_map/ppermute | solution.py:513
  769.7 40.8 %collective-permute-start.30 = (bf16[2,384,1152]{2,1,0:T(8,128)(2,1)S(1)}, bf16[2,384,1152]{2,1,0:T(8,128)(2,1)S(1)}, u32[]{:S(2)}, u32[]{:S(2)}) collective-permute-start(bf16[2,384,1152]{2,1,0:T(8,128)(2,1)S(1)} %pad_maximum_fusion.17), channel_id=1, source_target_pairs={{0,12},{4,0},{8,4},{12,8},{1,13},{5,1},{9,5},{13,9},{2,14},{6,2},{... | collective-permute-start | bytes 5308424 | tf_op jit(solution)/shard_map/ppermute | solution.py:508
  771.2 79.7 %collective-permute-start.31 = (bf16[4,384,1152]{2,1,0:T(8,128)(2,1)}, bf16[4,384,1152]{2,1,0:T(8,128)(2,1)}, u32[]{:S(2)}, u32[]{:S(2)}) collective-permute-start(bf16[4,384,1152]{2,1,0:T(8,128)(2,1)} %bitcast.115), channel_id=1, source_target_pairs={{0,16},{16,0},{1,17},{17,1},{2,18},{18,2},{3,19},{19,3},{4,20},{20... | collective-permute-start | bytes 10616840 | tf_op jit(solution)/shard_map/ppermute | solution.py:508
  772.7 218.5 %collective-permute-start.37 = (bf16[4,384,1152]{2,1,0:T(8,128)(2,1)}, bf16[4,384,1152]{2,1,0:T(8,128)(2,1)}, u32[]{:S(2)}, u32[]{:S(2)}) collective-permute-start(bf16[4,384,1152]{2,1,0:T(8,128)(2,1)} %bitcast.122), channel_id=1, source_target_pairs={{0,16},{16,0},{1,17},{17,1},{2,18},{18,2},{3,19},{19,3},{4,20},{20... | collective-permute-start | bytes 10616840 | tf_op jit(solution)/shard_map/ppermute | solution.py:508
  773.2 323.4 %collective-permute-start.41 = (bf16[4,384,1152]{2,1,0:T(8,128)(2,1)}, bf16[4,384,1152]{2,1,0:T(8,128)(2,1)}, u32[]{:S(2)}, u32[]{:S(2)}) collective-permute-start(bf16[4,384,1152]{2,1,0:T(8,128)(2,1)} %bitcast.127), channel_id=1, source_target_pairs={{0,16},{16,0},{1,17},{17,1},{2,18},{18,2},{3,19},{19,3},{4,20},{20... | collective-permute-start | bytes 10616840 | tf_op jit(solution)/shard_map/ppermute | solution.py:508
  812.2 41.1 %collective-permute-start.32 = (bf16[2,384,1152]{2,1,0:T(8,128)(2,1)}, bf16[2,384,1152]{2,1,0:T(8,128)(2,1)S(1)}, u32[]{:S(2)}, u32[]{:S(2)}) collective-permute-start(bf16[2,384,1152]{2,1,0:T(8,128)(2,1)} %add_convert_fusion.2), channel_id=1, source_target_pairs={{0,12},{4,0},{8,4},{12,8},{1,13},{5,1},{9,5},{13,9},{2,14},{6,2},{... | collective-permute-start | bytes 5308424 | tf_op jit(solution)/shard_map/ppermute | solution.py:508
  834.8 446.5 %reduce-scatter.9.cloned.1.call-start = ((), (), s32[]{:S(2)}) async-start(), calls=%async_computation.5 | async-start | bytes 5640192 | tf_op jit(solution)/shard_map/reduce_scatter | solution.py:793
  898.1 22.7 %collective-permute-start.33 = (bf16[16,4,2304]{2,1,0:T(4,128)(2,1)}, bf16[16,4,2304]{2,1,0:T(4,128)(2,1)}, u32[]{:S(2)}, u32[]{:S(2)}) collective-permute-start(bf16[16,4,2304]{2,1,0:T(4,128)(2,1)} %fusion.163), channel_id=1, source_target_pairs={{4,0},{8,4},{12,8},{5,1},{9,5},{13,9},{6,2},{10,6},{14,10},{7,3},{... | collective-permute-start | bytes 884744 | tf_op jit(solution)/shard_map/ppermute | solution.py:34
  925.3 78.1 %collective-permute-start.38 = (bf16[2,384,1152]{2,1,0:T(8,128)(2,1)}, bf16[2,384,1152]{2,1,0:T(8,128)(2,1)}, u32[]{:S(2)}, u32[]{:S(2)}) collective-permute-start(bf16[2,384,1152]{2,1,0:T(8,128)(2,1)} %add_convert_fusion.1), channel_id=1, source_target_pairs={{0,12},{4,0},{8,4},{12,8},{1,13},{5,1},{9,5},{13,9},{2,14},{6,2},{... | collective-permute-start | bytes 5308424 | tf_op jit(solution)/shard_map/ppermute | solution.py:508
  938.0 47.3 %collective-permute-start.35 = (bf16[16,4,2304]{2,1,0:T(4,128)(2,1)S(1)}, bf16[16,4,2304]{2,1,0:T(4,128)(2,1)S(1)}, u32[]{:S(2)}, u32[]{:S(2)}) collective-permute-start(bf16[16,4,2304]{2,1,0:T(4,128)(2,1)S(1)} %add_convert_fusion.7), channel_id=1, source_target_pairs={{4,0},{8,4},{12,8},{5,1},{9,5},{13,9},{6,2},{10,6},{14,10},{7,3},{... | collective-permute-start | bytes 884744 | tf_op jit(solution)/shard_map/ppermute | solution.py:34
  942.0 61.4 %collective-permute-start.36 = (bf16[384,1152]{1,0:T(8,128)(2,1)}, bf16[384,1152]{1,0:T(8,128)(2,1)}, u32[]{:S(2)}, u32[]{:S(2)}) collective-permute-start(bf16[384,1152]{1,0:T(8,128)(2,1)} %fusion.84), channel_id=1, source_target_pairs={{0,12},{4,0},{8,4},{12,8},{1,13},{5,1},{9,5},{13,9},{2,14},{6,2},{... | collective-permute-start | bytes 2654216 | tf_op jit(solution)/shard_map/ppermute | solution.py:508
  946.3 450.0 %reduce-scatter.13.cloned.1.call-start = ((), (), s32[]{:S(2)}) async-start(), calls=%async_computation.8 | async-start | bytes 1216512
  1006.5 90.2 %collective-permute-start.39 = (bf16[384,1152]{1,0:T(8,128)(2,1)}, bf16[384,1152]{1,0:T(8,128)(2,1)}, u32[]{:S(2)}, u32[]{:S(2)}) collective-permute-start(bf16[384,1152]{1,0:T(8,128)(2,1)} %fusion.83), channel_id=1, source_target_pairs={{0,12},{4,0},{8,4},{12,8},{1,13},{5,1},{9,5},{13,9},{2,14},{6,2},{... | collective-permute-start | bytes 2654216 | tf_op jit(solution)/shard_map/ppermute | solution.py:508
  1010.3 86.4 %collective-permute-start.40 = (bf16[384,1152]{1,0:T(8,128)(2,1)}, bf16[384,1152]{1,0:T(8,128)(2,1)}, u32[]{:S(2)}, u32[]{:S(2)}) collective-permute-start(bf16[384,1152]{1,0:T(8,128)(2,1)} %fusion.81), channel_id=1, source_target_pairs={{0,12},{4,0},{8,4},{12,8},{1,13},{5,1},{9,5},{13,9},{2,14},{6,2},{... | collective-permute-start | bytes 2654216 | tf_op jit(solution)/shard_map/ppermute | solution.py:508
  1017.2 79.4 %collective-permute-start.42 = (bf16[384,1152]{1,0:T(8,128)(2,1)S(1)}, bf16[384,1152]{1,0:T(8,128)(2,1)}, u32[]{:S(2)}, u32[]{:S(2)}) collective-permute-start(bf16[384,1152]{1,0:T(8,128)(2,1)S(1)} %fusion.96), channel_id=1, source_target_pairs={{0,16},{16,0},{1,17},{17,1},{2,18},{18,2},{3,19},{19,3},{4,20},{20... | collective-permute-start | bytes 2654216 | tf_op jit(solution)/shard_map/ppermute | solution.py:508
  1099.7 94.5 %collective-permute-start.43 = (bf16[384,1152]{1,0:T(8,128)(2,1)}, bf16[384,1152]{1,0:T(8,128)(2,1)}, u32[]{:S(2)}, u32[]{:S(2)}) collective-permute-start(bf16[384,1152]{1,0:T(8,128)(2,1)} %fusion.80), channel_id=1, source_target_pairs={{0,12},{4,0},{8,4},{12,8},{1,13},{5,1},{9,5},{13,9},{2,14},{6,2},{... | collective-permute-start | bytes 2654216 | tf_op jit(solution)/shard_map/ppermute | solution.py:508
  1103.4 90.8 %collective-permute-start.44 = (bf16[384,1152]{1,0:T(8,128)(2,1)}, bf16[384,1152]{1,0:T(8,128)(2,1)}, u32[]{:S(2)}, u32[]{:S(2)}) collective-permute-start(bf16[384,1152]{1,0:T(8,128)(2,1)} %fusion.78), channel_id=1, source_target_pairs={{0,12},{4,0},{8,4},{12,8},{1,13},{5,1},{9,5},{13,9},{2,14},{6,2},{... | collective-permute-start | bytes 2654216 | tf_op jit(solution)/shard_map/ppermute | solution.py:508
  1106.6 87.6 %collective-permute-start.45 = (bf16[384,1152]{1,0:T(8,128)(2,1)}, bf16[384,1152]{1,0:T(8,128)(2,1)}, u32[]{:S(2)}, u32[]{:S(2)}) collective-permute-start(bf16[384,1152]{1,0:T(8,128)(2,1)} %fusion.76), channel_id=1, source_target_pairs={{0,12},{4,0},{8,4},{12,8},{1,13},{5,1},{9,5},{13,9},{2,14},{6,2},{... | collective-permute-start | bytes 2654216 | tf_op jit(solution)/shard_map/ppermute | solution.py:508
  1196.2 81.9 %collective-permute-start.46 = (bf16[384,1152]{1,0:T(8,128)(2,1)S(1)}, bf16[384,1152]{1,0:T(8,128)(2,1)}, u32[]{:S(2)}, u32[]{:S(2)}) collective-permute-start(bf16[384,1152]{1,0:T(8,128)(2,1)S(1)} %fusion.75), channel_id=1, source_target_pairs={{0,12},{4,0},{8,4},{12,8},{1,13},{5,1},{9,5},{13,9},{2,14},{6,2},{... | collective-permute-start | bytes 2654216 | tf_op jit(solution)/shard_map/ppermute | solution.py:508
  1201.9 76.3 %collective-permute-start.47 = (bf16[384,1152]{1,0:T(8,128)(2,1)}, bf16[384,1152]{1,0:T(8,128)(2,1)}, u32[]{:S(2)}, u32[]{:S(2)}) collective-permute-start(bf16[384,1152]{1,0:T(8,128)(2,1)} %fusion.73), channel_id=1, source_target_pairs={{0,12},{4,0},{8,4},{12,8},{1,13},{5,1},{9,5},{13,9},{2,14},{6,2},{... | collective-permute-start | bytes 2654216 | tf_op jit(solution)/shard_map/ppermute | solution.py:508
  1300.5 190.8 %reduce-scatter.11.cloned.1.call-start = ((), (), s32[]{:S(2)}) async-start(), calls=%async_computation.6 | async-start | bytes 5640192 | tf_op jit(solution)/shard_map/reduce_scatter | solution.py:836
  1462.7 24.6 %collective-permute-start.54 = (f32[180,128]{1,0:T(8,128)S(1)}, f32[180,128]{1,0:T(8,128)S(1)}, u32[]{:S(2)}, u32[]{:S(2)}) collective-permute-start(f32[180,128]{1,0:T(8,128)S(1)} %add.404), channel_id=1, source_target_pairs={{0,2},{1,3},{2,0},{3,1},{4,6},{5,7},{6,4},{7,5},{8,10},{9,11},{10,... | collective-permute-start | bytes 276488 | tf_op jit(solution)/shard_map/ppermute | solution.py:513
  (145 other events, 3315.6 us)
Sparse Core Ops, SparseCore 0:
  14.8 108.3 all-gather.5
  126.0 65.9 all-gather.3
  834.9 120.6 reduce-scatter.14
  959.5 130.6 reduce-scatter.8
  1300.6 95.7 reduce-scatter.12
  1410.9 80.2 reduce-scatter.10

commit v2 on v1

--- a/solution.py
+++ b/solution.py
@@ -468,6 +468,126 @@
     )(gxs, gproj, xproj, ext, taps, bias, same)
 
 
+def gelu_pair(v):
+    inner = 0.7978845608 * (v + 0.044715 * v * v * v)
+    t = jnp.tanh(inner)
+    value = 0.5 * v * (1.0 + t)
+    slope = 0.5 * (1.0 + t) + 0.5 * v * (1.0 - t * t) * (0.7978845608 * (1.0 + 3.0 * 0.044715 * v * v))
+    return value, slope
+
+
+def expert_kernel(blocks, peers, split_last, final, *refs):
+    count = blocks + (1 if split_last else 0)
+    weights, refs = refs[:count], refs[count:]
+    xs, gs, refs = refs[:peers], refs[peers : 2 * peers], refs[2 * peers :]
+    if final:
+        before, refs = refs[:2], refs[2:]
+    out_refs, (upg_ref, downg_ref), refs = refs[:2], refs[2:4], refs[4:]
+    x_s, g_s, up_s, down_s, hid_s, pre_s, acc_y, acc_g = refs
+    cap = xs[0].shape[1]
+    size = weights[0].shape[1]
+    expert, half = pl.program_id(0), pl.program_id(1)
+
+    @pl.when(half == 0)
+    def _():
+        for d in range(peers):
+            at = slice(d * cap, (d + 1) * cap)
+            piece = xs[d][0]
+            x_s[at, :] = piece[:, :D]
+            gate = jnp.sum(piece[:, D:].astype(jnp.float32), axis=1, keepdims=True)
+            g_s[at, :] = (gate * gs[d][0].astype(jnp.float32)).astype(jnp.bfloat16)
+        if final:
+            acc_y[...] = before[0][0].astype(jnp.float32)
+            acc_g[...] = before[1][0].astype(jnp.float32)
+        else:
+            acc_y[...] = jnp.zeros_like(acc_y)
+            acc_g[...] = jnp.zeros_like(acc_g)
+
+    def place(k, ref):
+        at = slice(k * size, (k + 1) * size)
+        up_s[at, :] = ref[0]
+        down_s[at, :] = ref[1]
+
+    for h in range(2):
+
+        @pl.when(half == h)
+        def _():
+            for k in range(blocks // 2):
+                block = h * (blocks // 2) + k
+                if split_last and block == blocks - 1:
+                    for e in range(2):
+                        pl.when(expert == e)(functools.partial(place, k, weights[block + e]))
+                else:
+                    place(k, weights[block])
+
+    rows = cap * peers
+    tile = rows // 3
+    cols = up_s.shape[0]
+
+    def body(r, carry):
+        at = pl.ds(pl.multiple_of(r * tile, tile), tile)
+        value, slope = gelu_pair(dot(x_s[at, :], up_s[...], NT))
+        hidden = value.astype(jnp.bfloat16)
+        grad_pre = (slope * dot(g_s[at, :], down_s[...], NT)).astype(jnp.bfloat16)
+        hid_s[at, :] = hidden
+        pre_s[at, :] = grad_pre
+        acc_y[at, :] += dot(hidden, down_s[...], NN)
+        acc_g[at, :] += dot(grad_pre, up_s[...], NN)
+        return carry
+
+    lax.fori_loop(0, 3, body, 0)
+    wide = cols // 3
+
+    def grads(c, carry):
+        at = pl.ds(pl.multiple_of(c * wide, wide), wide)
+        upg_ref[0, at, :] = dot(pre_s[:, at], x_s[...], TN).astype(jnp.bfloat16)
+        downg_ref[0, at, :] = dot(hid_s[:, at], g_s[...], TN).astype(jnp.bfloat16)
+        return carry
+
+    lax.fori_loop(0, 3, grads, 0)
+
+    @pl.when(half == 1)
+    def _():
+        out_refs[0][0] = acc_y[...].astype(jnp.bfloat16)
+        out_refs[1][0] = acc_g[...].astype(jnp.bfloat16)
+
+
+def run_experts(weights, split_last, xs, gs, before):
+    blocks = len(weights) - (1 if split_last else 0)
+    peers = len(xs)
+    count, cap = xs[0].shape[:2]
+    size = weights[0].shape[1]
+    rows, cols = peers * cap, blocks * size
+    final = before is not None
+
+    def pick(shape, **more):
+        return pl.BlockSpec((1,) + shape, lambda e, h: (e, 0, 0), **more)
+
+    once = dict(pipeline_mode=pl.Buffered(1))
+    pair = pl.BlockSpec((2, size, D), lambda e, h: (e, 0, 0))
+    half = pl.BlockSpec((2, size, D), lambda e, h: (0, 0, 0), **once)
+    in_specs = [pair] * (blocks - 1 if split_last else blocks) + ([half] * 2 if split_last else [])
+    in_specs += [pick(xs[0].shape[1:])] * peers + [pick(gs[0].shape[1:])] * peers
+    in_specs += [pick((rows, D), **once)] * (2 if final else 0)
+    low = functools.partial(pltpu.VMEM, dtype=jnp.bfloat16)
+    work = 12 * count * rows * cols * D
+    grads = pl.BlockSpec((1, cols // 2, D), lambda e, h: (e, h, 0))
+    return pl.pallas_call(
+        functools.partial(expert_kernel, blocks, peers, split_last, final),
+        grid=(count, 2),
+        in_specs=in_specs,
+        out_specs=[pick((rows, D))] * 2 + [grads] * 2,
+        out_shape=[b16s(count, rows, D)] * 2 + [b16s(count, cols, D)] * 2,
+        scratch_shapes=[
+            low((rows, D)), low((rows, D)), low((cols // 2, D)), low((cols // 2, D)),
+            low((rows, cols // 2)), low((rows, cols // 2)), vm(rows, D), vm(rows, D),
+        ],
+        compiler_params=params(),
+        cost_estimate=pl.CostEstimate(flops=work, bytes_accessed=count * (4 * cols + 8 * rows) * D * 2, transcendentals=count * rows * cols),
+        name="experts",
+    )(*weights, *xs, *gs, *(before or ()))
+
+
 def halves_of(value, seqs):
     split = value.reshape(value.shape[:-2] + (seqs, HALVES, value.shape[-1]))
     return split[..., 0, :], split[..., 1, :]
@@ -521,11 +641,17 @@
 class Gather:
     def __init__(self, own):
         self.here, self.there = [own], []
+        self.peers = lax.axis_size("seq")
 
     def step(self):
-        self.there.append(ring(self.here[len(self.there)], "dp", 1))
-        if len(self.here) < lax.axis_size("seq"):
-            self.here.append(ring(self.here[-1], "seq", 1))
+        at = len(self.there)
+        block = self.here[at]
+        if at < self.peers - 1:
+            self.there.append(ring(block, "dp", 1))
+            self.here.append(ring(block, "seq", 1))
+        else:
+            half = block.shape[0] // 2
+            self.there.append([ring(block[:half], "dp", 1), ring(self.there[-1][half:], "seq", 1)])
 
     def hold(self, value):
         value, here, there = held_for(value, self.here[1:], self.there)
@@ -533,7 +659,7 @@
         return value
 
     def done(self):
-        return len(self.there) == lax.axis_size("seq")
+        return len(self.there) == self.peers
 
 
 class Reduce:
@@ -581,6 +707,14 @@
         return self.total
 
 
+def settle(value, reduces):
+    live = [r for r in reduces if r.moving is not None]
+    value, moved = held_for(value, [r.moving for r in live])
+    for r, m in zip(live, moved):
+        r.moving = m
+    return value
+
+
 def hold_all(value, reduces):
     live = [r for r in reduces if r.moving is not None]
     value, moved = held_for(value, [r.moving for r in live])
@@ -590,6 +724,18 @@
     return value
 
 
+def halved(value, axis):
+    index, bits = lax.axis_index(axis), lax.axis_size(axis) // 2
+    while bits >= 1:
+        pair = value.reshape((2, bits) + value.shape[1:])
+        high = (index // bits) % 2 == 1
+        keep = jnp.where(high, pair[1], pair[0])
+        send = jnp.where(high, pair[0], pair[1])
+        value = keep.astype(jnp.float32) + partner(send.astype(jnp.bfloat16), axis, bits).astype(jnp.float32)
+        bits //= 2
+    return value[0]
+
+
 def sum_everywhere(value):
     for axis in ALL:
         bits = 1
@@ -601,14 +747,6 @@
 
 def exchange(blocks):
     return [blocks[0]] + [partner(blocks[d], "expert", d) for d in range(1, len(blocks))]
-
-
-def gelu_pair(v):
-    inner = 0.7978845608 * (v + 0.044715 * v * v * v)
-    t = jnp.tanh(inner)
-    value = 0.5 * v * (1.0 + t)
-    slope = 0.5 * (1.0 + t) + 0.5 * v * (1.0 - t * t) * (0.7978845608 * (1.0 + 3.0 * 0.044715 * v * v))
-    return value, slope
 
 
 def local(
@@ -689,7 +827,7 @@
     bc = proj[:, DTR:]
     grad_arrived = dispatch(grad_low)
     delta, ends, sums = run_end(xs, delta_in, dtw, dtb, alog, bc, cut)
-    ends, grad_arrived = held_for(ends, grad_arrived)
+    ends, grad_arrived = held_for(gather.hold(ends), grad_arrived)
     rates = -jnp.exp(alog.astype(f32))[:, None, :]
     starts, decays = start_states(ends, sums, rates, seqs)
     starts = gather.hold(starts)
@@ -715,55 +853,30 @@
     arrived = gather.hold(arrived)
     while not gather.done():
         gather.step()
-
-    def matrices(blocks):
-        return [jnp.concatenate([block[m] for block in blocks], axis=0) for m in range(2 * local_experts)]
-
-    rows_of = []
-    for e in range(local_experts):
-        here = jnp.concatenate([part[e] for part in arrived], axis=0)
-        gate_rows = jnp.sum(here[:, D : D + 3].astype(f32), axis=1, keepdims=True)
-        g_rows = (gate_rows * jnp.concatenate([part[e] for part in grad_arrived], axis=0).astype(f32)).astype(b16)
-        rows_of.append((here[:, :D], g_rows))
-    sides, produced, grad_in = [], [0.0] * local_experts, [0.0] * local_experts
-    for side in range(2):
-        mats = matrices(gather.here if side == 0 else gather.there)
-        kept = []
-        for e in range(local_experts):
-            x_rows, g_rows = rows_of[e]
-            value, slope = gelu_pair(dot(x_rows, mats[2 * e], NT))
-            hidden = value.astype(b16)
-            produced[e] = produced[e] + dot(hidden, mats[2 * e + 1], NN)
-            grad_pre = (slope * dot(g_rows, mats[2 * e + 1], NT)).astype(b16)
-            grad_in[e] = grad_in[e] + dot(grad_pre, mats[2 * e], NN)
-            kept.append((hidden, grad_pre))
-        sides.append(kept)
-        if side == 0:
-            produced, grad_in = held_for(produced, grad_in)
-            rows_of, produced, grad_in = gather.hold((rows_of, produced, grad_in))
-
-    def send_back(parts):
-        return [exchange([part.astype(b16).reshape(peers, capacity, D)[d] for d in range(peers)]) for part in parts]
-
-    returned_y = send_back(produced)
-    returned_g = send_back(grad_in)
+    sum_y, sum_g, up_here, down_here = run_experts(gather.here, False, arrived, grad_arrived, None)
+    sum_y = gather.hold(sum_y)
+    sum_y, sum_g, up_there, down_there = run_experts(
+        gather.there[:-1] + gather.there[-1], True, arrived, grad_arrived, (sum_y, sum_g)
+    )
     weight_grads = []
     for e in range(local_experts):
-        x_rows, g_rows = rows_of[e]
-        for m in range(2):
-            left, right = (1, x_rows) if m == 0 else (0, g_rows)
-            weight_grads.append([dot(sides[side][e][left], right, TN, b16) for side in range(2)])
+        weight_grads += [(up_here[e], up_there[e]), (down_here[e], down_there[e])]
     count = len(weight_grads)
-    returned_y, returned_g, weight_grads = held_for(returned_y, returned_g, weight_grads)
     reduces = [Reduce(g[0], g[1], i < count - 1) for i, g in enumerate(weight_grads)]
-    early = [reduces[0], reduces[-1]]
+
+    def send_back(parts):
+        parts = parts.reshape(local_experts, peers, capacity, D)
+        return exchange([parts[:, d] for d in range(peers)])
+
+    returned_y = send_back(sum_y)
+    returned_g = send_back(sum_g)
 
     def collect(parts):
-        back_rows = jnp.stack([jnp.stack(part) for part in parts], axis=1).reshape(EXPERTS * capacity, D)
+        back_rows = jnp.stack(parts).reshape(EXPERTS * capacity, D)
         return dot(placing, back_rows, TN)
 
     expert_rows = collect(returned_y)
-    grad_back = collect(returned_g)
+    grad_back = collect(hold_all(returned_g, reduces[-1:]))
     output = (first_sum + gate[:, None] * expert_rows).astype(b16)
 
     grad_gate = jnp.sum(grad_final * expert_rows, axis=-1) * drop
@@ -782,11 +895,13 @@
     out_grad_part = dot(branch, first_low, TN, b16)
     grad_branch = dot(first_low, out_full, NT)
     grad_branch, out_grad_part = held_for(grad_branch, out_grad_part)
+    grad_branch = hold_all(grad_branch, reduces[:1])
+
+    leads, grad_z, grad_ssm = run_first(delta, alog, bc, cut, grad_branch, gate_z, ssm)
+    leads = settle(leads, [reduces[0], reduces[1], reduces[-1]])
+    last = last_grads(leads, decays, seqs)
+    last, out_grad_part = held_for(last, out_grad_part)
     out_sum = lax.psum_scatter(out_grad_part, ALL, scatter_dimension=0, tiled=True)
-    grad_branch = hold_all(grad_branch, early)
-
-    leads, grad_z, grad_ssm = run_first(delta, alog, bc, cut, grad_branch, gate_z, ssm)
-    last = last_grads(leads, decays, seqs)
     gate_part = dot(grad_z, normed_one[skip_rows:], TN, b16)
     grad_normed_z = dot(grad_z, in_full[DI:], NN)
     grad_ssm, gate_part, grad_normed_z = held_for(grad_ssm, gate_part, grad_normed_z)
@@ -823,16 +938,20 @@
     ).astype(b16)
     small_grad = jnp.pad(small_grad, ((0, 0), (0, PACK - used)))
     small_grad, grad_proj = held_for(small_grad, grad_proj)
-    small_sum = lax.psum_scatter(small_grad, ALL, scatter_dimension=0, tiled=True).astype(f32)
-    grad_normed, conv_parts, conv_grads = 0.0, [], []
+    small_sum = small_grad.reshape(lax.axis_size("dp"), lax.axis_size("seq"), peers, own // 2, PACK)
+    small_sum = halved(small_sum, "dp")
+    small_sum = halved(small_sum.swapaxes(0, 1), "expert")
+    small_sum = halved(small_sum, "seq")
+    gexts, conv_parts, conv_grads = [], [], []
     for part in range(SPLITS):
         gext, gvec = run_conv(parts[part][0], grad_proj, xproj_full, ext, conv_w, cbias, same_wide, part)
         if part == SPLITS - 1:
-            gext, small_sum = held_for(hold_all(gext, reduces), small_sum)
+            gext = hold_all(gext, reduces)
         conv_parts.append(dot(gext, normed_one, TN, b16))
-        grad_normed = grad_normed + dot(gext, in_full[part * width : (part + 1) * width], NN)
+        gexts.append(gext)
         conv_grads.append(gvec)
-    conv_all, grad_normed = held_for(jnp.concatenate(conv_parts, axis=0), grad_normed)
+    conv_all, gexts = held_for(jnp.concatenate(conv_parts, axis=0), gexts)
+    grad_normed = sum(dot(gexts[k], in_full[k * width : (k + 1) * width], NN) for k in range(SPLITS))
     conv_own = lax.psum_scatter(conv_all, ("seq", "expert"), scatter_dimension=0, tiled=True)
     is_gate = lax.axis_index("dp") == 1
     in_sum = jnp.where(is_gate, gate_own, conv_own).astype(f32)

time: 1520 us -> 1290 us (0.85)
  matrix products: 312 us -> 145 us
  waiting for transfers between devices: 436 us -> 295 us
  Pallas kernels: 381 us -> 494 us
  starting transfers between devices: 91.3 us -> 70.8 us
    dot_general x53 -> x29, matrix products: 312 us -> 145 us  [dot(): lax.dot_general(left, right, (dims, ((), ())), preferred_element_type=out)]
    pallas_call x0 -> x2, Pallas kernels: none -> 113 us  [run_experts(): pl.pallas_call(functools.partial(expert_kernel, blocks, peers, split_last...]
    ppermute x9, waiting for transfers between devices: 117 us -> 43.9 us  [shifted(): lax.ppermute(value, axis, [(source, source + steps) for source in range(f...]
    unnamed x7 -> x5, waiting for transfers between devices: 58.6 us -> 0.08 us
    ppermute x24 -> x25, waiting for transfers between devices: 98.1 us -> 77.7 us  [ring(): lax.ppermute(value, axis, [(i, (i + step) % count) for i in range(count)])]
    squeeze x12 -> x1, local copies, waits for them, and re-layouts: 21.4 us -> 1.57 us  [send_back(): return exchange([parts[:, d] for d in range(peers)])]
    ppermute x23 -> x22, waiting for transfers between devices: 115 us -> 125 us  [partner(): return lax.ppermute(value, axis, [(i, i ^ bits) for i in range(count)])]
    ppermute x24 -> x25, starting transfers between devices: 43.1 us -> 35.5 us  [ring(): lax.ppermute(value, axis, [(i, (i + step) % count) for i in range(count)])]
  transfers between devices with their start and end apart: 62 -> 61, of which waited for: 30 -> 24; matrix products, arithmetic and copies ran while one was open for 28% -> 29% of each run, Pallas kernels for 25% -> 34%
where the time goes in v2:
time: 1290 us; the launch traced here: 1280 us
  Pallas kernels  494 us (38%)
  waiting for transfers between devices  295 us (23%)
  local copies, waits for them, and re-layouts  162 us (13%)
  matrix products  145 us (11%)
  other arithmetic  101 us (8%)
  starting transfers between devices  70.8 us (5%)
  between operations  16 us (1%)
    pallas_call x3, Pallas kernels, run_back(): pl.pallas_call(back_kernel, grid=(width // LANES,), in_specs=[col(rows),...  215 us
    dot_general x29, matrix products, dot(): lax.dot_general(left, right, (dims, ((), ())), preferred_element_type=out)  145 us
    ppermute x22, waiting for transfers between devices, partner(): return lax.ppermute(value, axis, [(i, i ^ bits) for i in range(count)])  125 us
    pallas_call x2, Pallas kernels, run_experts(): pl.pallas_call(functools.partial(expert_kernel, blocks, peers, split_last...  113 us
    ppermute x25, waiting for transfers between devices, ring(): lax.ppermute(value, axis, [(i, (i + step) % count) for i in range(count)])  77.7 us
    pallas_call x1, Pallas kernels, run_out(): pl.pallas_call(out_kernel, grid=(DI // LANES,), in_specs=[col_spec(rows),...  55.6 us
    all_gather x1, waiting for transfers between devices, local(): lax.all_gather(jnp.concatenate([in_proj.T, small.reshape(-1, D)], axis=0)...  48.7 us
    pallas_call x1, Pallas kernels, run_end(): pl.pallas_call(end_kernel, grid=(DI // LANES,), in_specs=[col_spec(rows),...  45.2 us
  transfers between devices with their start and end apart: 61, of which 24 were waited for; matrix products, arithmetic and copies ran while one was open for 29% of the time, Pallas kernels for 34%

profile of v2, /device:TPU:0, one launch (start us, length us, event | category | flops | bytes accessed | tf_op | source)
XLA Modules:
  0.0 1282.8 jit_solution(15316503320581970662)
XLA Ops:
  32.9 6.3 fusion.10
  56.9 5.9 copy.246
  62.8 7.1 convert_element_type.468
  75.5 48.7 %all-gather.6.cloned.1.call-done = bf16[5120,1152]{1,0:T(8,128)(2,1)} async-done(((bf16[160,1152]{1,0:T(8,128)(2,1)}), bf16[5120,1152]{1,0:T(8,128)(2,1)}) %all-gather.6.cloned.1.call-update) | async-done | bytes 11796496 | tf_op jit(solution)/shard_map/all_gather | solution.py:769
  124.2 9.4 slice.658
  140.0 9.8 fusion.11.ext_ref
  149.8 7.1 multiply_convert_fusion.xs_ref
  165.1 45.2 %end.1 = (f32[1024,2304]{1,0:T(8,128)}, f32[16,8,2304]{2,1,0:T(8,128)}, f32[8,2304]{1,0:T(8,128)}) custom-call(bf16[1024,2304]{1,0:T(8,128)(2,1)} %copy-done.3, bf16[1024,72]{1,0:T(8,128)(2,1)} %copy.304.din_ref, bf16[2304,72]{1,0:T(8,128)(2,1)} %slice.673.dtw_ref, bf16[1,2304]{1,0:T(2,128)(2,1)} %get-tuple-element.439.dtb_ref, ...), custom_call_target="tpu_custom_call" | custom-call | flops 301989888 | bytes 150994944 | tf_op jit(solution)/shard_map/end/pallas_call | solution.py:329
  211.3 8.1 collective-permute-done.2.refs_1_
  224.3 12.4 collective-permute-done.7
  245.6 5.8 copy.238
  251.5 6.8 slice.515
  260.7 11.7 fusion.20.z_ref
  282.2 55.6 %out.1 = (bf16[1024,2304]{1,0:T(8,128)(2,1)}, bf16[1024,2304]{1,0:T(8,128)(2,1)}, f32[8,16,8,2304]{3,2,1,0:T(8,128)}) custom-call(bf16[1024,2304]{1,0:T(8,128)(2,1)} %copy-done.3, f32[1024,2304]{1,0:T(8,128)} %get-tuple-element.157.delta_ref, bf16[16,2304]{1,0:T(8,128)(2,1)} %slice.675.alog_ref, f32[1024,32]{1,0:T(8,128)} %copy.305.bc_ref, ...), custom_call_target="tpu_custom_call" | custom-call | flops 301989888 | bytes 188743680 | tf_op jit(solution)/shard_map/out/pallas_call | solution.py:348
  337.8 10.6 multiply_reduce_fusion.4
  368.2 21.8 %collective-permute-done.13.refs_6_.refs_7_ = bf16[2,192,1280]{2,1,0:T(8,128)(2,1)} collective-permute-done((bf16[2,192,1280]{2,1,0:T(8,128)(2,1)S(1)}, bf16[2,192,1280]{2,1,0:T(8,128)(2,1)}, u32[]{:S(2)}, u32[]{:S(2)}) %collective-permute-start.13) | collective-permute-done | bytes 983072 | tf_op jit(solution)/shard_map/ppermute | solution.py:633
  389.9 20.3 %collective-permute-done.14.refs_7_.refs_8_ = bf16[2,192,1280]{2,1,0:T(8,128)(2,1)} collective-permute-done((bf16[2,192,1280]{2,1,0:T(8,128)(2,1)S(1)}, bf16[2,192,1280]{2,1,0:T(8,128)(2,1)}, u32[]{:S(2)}, u32[]{:S(2)}) %collective-permute-start.14) | collective-permute-done | bytes 983072 | tf_op jit(solution)/shard_map/ppermute | solution.py:633
  410.2 23.3 %collective-permute-done.15.refs_3_ = bf16[4,384,1152]{2,1,0:T(8,128)(2,1)} collective-permute-done((bf16[4,384,1152]{2,1,0:T(8,128)(2,1)}, bf16[4,384,1152]{2,1,0:T(8,128)(2,1)}, u32[]{:S(2)}, u32[]{:S(2)}) %collective-permute-start.15) | collective-permute-done | bytes 3538976 | tf_op jit(solution)/shard_map/ppermute | solution.py:628
  440.7 53.3 %experts.2 = (bf16[2,768,1152]{2,1,0:T(8,128)(2,1)}, bf16[2,768,1152]{2,1,0:T(8,128)(2,1)}, bf16[2,1536,1152]{2,1,0:T(8,128)(2,1)}, bf16[2,1536,1152]{2,1,0:T(8,128)(2,1)}) custom-call(bf16[4,384,1152]{2,1,0:T(8,128)(2,1)} %pad_maximum_fusion.1.refs_0_, bf16[4,384,1152]{2,1,0:T(8,128)(2,1)} %collective-permute-done.2.refs_1_, ...), custom_call_target="tpu_custom_call" | custom-call | flops 32614907904 | bytes 56623104 | tf_op jit(solution)/shard_map/experts/pallas_call | solution.py:575
  497.2 59.3 %experts.3 = (bf16[2,768,1152]{2,1,0:T(8,128)(2,1)}, bf16[2,768,1152]{2,1,0:T(8,128)(2,1)}, bf16[2,1536,1152]{2,1,0:T(8,128)(2,1)}, bf16[2,1536,1152]{2,1,0:T(8,128)(2,1)}) custom-call(bf16[4,384,1152]{2,1,0:T(8,128)(2,1)} %collective-permute-done.3.refs_0_, bf16[4,384,1152]{2,1,0:T(8,128)(2,1)} %collective-permute-done.11.refs_1_, ...), custom_call_target="tpu_custom_call" | custom-call | flops 32614907904 | bytes 56623104 | tf_op jit(solution)/shard_map/experts/pallas_call | solution.py:575
  578.8 13.7 %collective-permute-done.20 = bf16[2,192,1152]{2,1,0:T(8,128)(2,1)} collective-permute-done((bf16[2,192,1152]{2,1,0:T(8,128)(2,1)}, bf16[2,192,1152]{2,1,0:T(8,128)(2,1)}, u32[]{:S(2)}, u32[]{:S(2)}) %collective-permute-start.20) | collective-permute-done | bytes 884768 | tf_op jit(solution)/shard_map/ppermute | solution.py:633
  593.0 17.7 %collective-permute-done.21 = bf16[2,192,1152]{2,1,0:T(8,128)(2,1)} collective-permute-done((bf16[2,192,1152]{2,1,0:T(8,128)(2,1)}, bf16[2,192,1152]{2,1,0:T(8,128)(2,1)}, u32[]{:S(2)}, u32[]{:S(2)}) %collective-permute-start.21) | collective-permute-done | bytes 884768 | tf_op jit(solution)/shard_map/ppermute | solution.py:633
  620.6 9.8 collective-permute-done.23
  630.4 18.2 %collective-permute-done.24 = bf16[2,192,1152]{2,1,0:T(8,128)(2,1)S(1)} collective-permute-done((bf16[2,192,1152]{2,1,0:T(8,128)(2,1)S(1)}, bf16[2,192,1152]{2,1,0:T(8,128)(2,1)S(1)}, u32[]{:S(2)}, u32[]{:S(2)}) %collective-permute-start.24) | collective-permute-done | bytes 884768 | tf_op jit(solution)/shard_map/ppermute | solution.py:633
  662.0 30.2 %collective-permute-done.26 = bf16[2,384,1152]{2,1,0:T(8,128)(2,1)S(1)} collective-permute-done((bf16[2,384,1152]{2,1,0:T(8,128)(2,1)S(1)}, bf16[2,384,1152]{2,1,0:T(8,128)(2,1)S(1)}, u32[]{:S(2)}, u32[]{:S(2)}) %collective-permute-start.26) | collective-permute-done | bytes 1769504 | tf_op jit(solution)/shard_map/ppermute | solution.py:628
  696.1 9.8 fusion.47
  706.0 11.9 fusion.49.gb_ref
  720.4 39.2 %first.1 = (f32[16,8,2304]{2,1,0:T(8,128)}, bf16[1024,2304]{1,0:T(8,128)(2,1)}, f32[1024,2304]{1,0:T(8,128)}) custom-call(f32[1024,2304]{1,0:T(8,128)} %get-tuple-element.157.delta_ref, bf16[16,2304]{1,0:T(8,128)(2,1)} %slice.675.alog_ref, f32[1024,32]{1,0:T(8,128)} %copy.305.bc_ref, f32[1024,128]{1,0:T(8,128)} %broadcast_in_dim.18.cut_ref, ...), custom_call_target="tpu_custom_call" | custom-call | flops 301989888 | bytes 150994944 | tf_op jit(solution)/shard_map/first/pallas_call | solution.py:371
  759.6 6.3 collective-permute-done.29
  772.1 9.3 collective-permute-done.31
  783.3 8.5 collective-permute-done.32
  794.0 7.1 collective-permute-done.33
  818.6 9.9 fusion.28
  838.8 11.1 fusion.18
  850.0 71.5 %back.3 = (f32[1024,768]{1,0:T(8,128)}, bf16[1024,768]{1,0:T(8,128)(2,1)}, f32[16,768]{1,0:T(8,128)}, f32[8,768]{1,0:T(8,128)}, f32[1024,128]{1,0:T(8,128)}) custom-call(bf16[1024,2304]{1,0:T(8,128)(2,1)} %copy-done.3, f32[1024,2304]{1,0:T(8,128)} %get-tuple-element.157.delta_ref, bf16[16,2304]{1,0:T(8,128)(2,1)} %slice.675.alog_ref, ...), custom_call_target="tpu_custom_call" | custom-call | flops 100663296 | bytes 213909504 | tf_op jit(solution)/shard_map/back/pallas_call | solution.py:398
  939.6 71.8 %back.4 = (f32[1024,768]{1,0:T(8,128)}, bf16[1024,768]{1,0:T(8,128)(2,1)}, f32[16,768]{1,0:T(8,128)}, f32[8,768]{1,0:T(8,128)}, f32[1024,128]{1,0:T(8,128)}) custom-call(bf16[1024,2304]{1,0:T(8,128)(2,1)} %copy-done.3, f32[1024,2304]{1,0:T(8,128)} %get-tuple-element.157.delta_ref, bf16[16,2304]{1,0:T(8,128)(2,1)} %slice.675.alog_ref, ...), custom_call_target="tpu_custom_call" | custom-call | flops 100663296 | bytes 213909504 | tf_op jit(solution)/shard_map/back/pallas_call | solution.py:398
  1027.3 71.4 %back.5 = (f32[1024,768]{1,0:T(8,128)}, bf16[1024,768]{1,0:T(8,128)(2,1)}, f32[16,768]{1,0:T(8,128)}, f32[8,768]{1,0:T(8,128)}, f32[1024,128]{1,0:T(8,128)}) custom-call(bf16[1024,2304]{1,0:T(8,128)(2,1)} %copy-done.3, f32[1024,2304]{1,0:T(8,128)} %get-tuple-element.157.delta_ref, bf16[16,2304]{1,0:T(8,128)(2,1)} %slice.675.alog_ref, ...), custom_call_target="tpu_custom_call" | custom-call | flops 100663296 | bytes 213909504 | tf_op jit(solution)/shard_map/back/pallas_call | solution.py:398
  1125.8 8.8 conv.5
  1134.6 8.9 conv.3
  1143.5 6.1 fusion.118
  1149.6 8.8 conv.4
  1158.4 6.1 fusion.119
  1204.6 6.6 collective-permute-done.44
  1211.4 6.5 multiply_reduce_fusion.1
  1218.9 5.9 multiply_subtract_fusion
  1224.8 6.7 reshape.624
  1231.5 5.5 copy.284
  1237.2 10.1 collective-permute-done.54
  (497 shorter events, 341.2 us)
Async XLA Ops:
  7.2 117.0 %all-gather.6.cloned.1.call-start = ((), (), s32[]{:S(2)}) async-start(), calls=%async_computation.6 | async-start | bytes 12165120 | tf_op jit(solution)/shard_map/all_gather | solution.py:769
  14.6 323.1 %all-gather.4.cloned.1.call-start = ((), (), s32[]{:S(2)}) async-start(), calls=%async_computation.3 | async-start | bytes 5474304 | tf_op jit(solution)/shard_map/all_gather | solution.py:772
  15.6 38.0 %collective-permute-start = (bf16[4,3,1152]{2,1,0:T(4,128)(2,1)S(1)}, bf16[4,3,1152]{2,1,0:T(4,128)(2,1)S(1)}, u32[]{:S(2)}, u32[]{:S(2)}) collective-permute-start(bf16[4,3,1152]{2,1,0:T(4,128)(2,1)S(1)} %slice.511), channel_id=1, source_target_pairs={{0,4},{4,8},{8,12},{1,5},{5,9},{9,13},{2,6},{6,10},{10,14},{3,7},{... | collective-permute-start | bytes 82952 | tf_op jit(solution)/shard_map/ppermute | solution.py:34
  21.3 30.3 %collective-permute-start.1 = (f32[4,3]{1,0:T(4,128)S(1)}, f32[4,3]{1,0:T(4,128)S(1)}, u32[]{:S(2)}, u32[]{:S(2)}) collective-permute-start(f32[4,3]{1,0:T(4,128)S(1)} %slice_convert_fusion.4), channel_id=1, source_target_pairs={{0,4},{4,8},{8,12},{1,5},{5,9},{9,13},{2,6},{6,10},{10,14},{3,7},{... | collective-permute-start | bytes 152 | tf_op jit(solution)/shard_map/ppermute | solution.py:34
  41.1 178.3 %collective-permute-start.4 = (bf16[2,192,1152]{2,1,0:T(8,128)(2,1)}, bf16[2,192,1152]{2,1,0:T(8,128)(2,1)}, u32[]{:S(2)}, u32[]{:S(2)}) collective-permute-start(bf16[2,192,1152]{2,1,0:T(8,128)(2,1)} %bitcast.28), channel_id=1, source_target_pairs={{0,1},{1,0},{2,3},{3,2},{4,5},{5,4},{6,7},{7,6},{8,9},{9,8},{10,11... | collective-permute-start | bytes 2654216 | tf_op jit(solution)/shard_map/ppermute | solution.py:633
  41.1 178.3 %collective-permute-start.5 = (bf16[2,192,1152]{2,1,0:T(8,128)(2,1)}, bf16[2,192,1152]{2,1,0:T(8,128)(2,1)}, u32[]{:S(2)}, u32[]{:S(2)}) collective-permute-start(bf16[2,192,1152]{2,1,0:T(8,128)(2,1)} %bitcast.29), channel_id=1, source_target_pairs={{0,2},{1,3},{2,0},{3,1},{4,6},{5,7},{6,4},{7,5},{8,10},{9,11},{10,... | collective-permute-start | bytes 2654216 | tf_op jit(solution)/shard_map/ppermute | solution.py:633
  42.6 176.8 %collective-permute-start.6 = (bf16[2,192,1152]{2,1,0:T(8,128)(2,1)}, bf16[2,192,1152]{2,1,0:T(8,128)(2,1)}, u32[]{:S(2)}, u32[]{:S(2)}) collective-permute-start(bf16[2,192,1152]{2,1,0:T(8,128)(2,1)} %bitcast.30), channel_id=1, source_target_pairs={{0,3},{1,2},{2,1},{3,0},{4,7},{5,6},{6,5},{7,4},{8,11},{9,10},{10,... | collective-permute-start | bytes 2654216 | tf_op jit(solution)/shard_map/ppermute | solution.py:633
  43.0 883.3 %reduce-scatter.10.cloned.1.call-start = ((), (), s32[]{:S(2)}) async-start(), calls=%async_computation.7 | async-start | bytes 5474304
  135.0 84.4 %collective-permute-start.2 = (bf16[4,384,1152]{2,1,0:T(8,128)(2,1)}, bf16[4,384,1152]{2,1,0:T(8,128)(2,1)}, u32[]{:S(2)}, u32[]{:S(2)}) collective-permute-start(bf16[4,384,1152]{2,1,0:T(8,128)(2,1)} %pad_maximum_fusion.1.refs_0_), channel_id=1, source_target_pairs={{0,4},{4,8},{8,12},{12,0},{1,5},{5,9},{9,13},{13,1},{2,6},{6,10},{... | collective-permute-start | bytes 10616840 | tf_op jit(solution)/shard_map/ppermute | solution.py:628
  135.7 83.7 %collective-permute-start.3 = (bf16[4,384,1152]{2,1,0:T(8,128)(2,1)}, bf16[4,384,1152]{2,1,0:T(8,128)(2,1)}, u32[]{:S(2)}, u32[]{:S(2)}) collective-permute-start(bf16[4,384,1152]{2,1,0:T(8,128)(2,1)} %pad_maximum_fusion.1.refs_0_), channel_id=1, source_target_pairs={{0,16},{16,0},{1,17},{17,1},{2,18},{18,2},{3,19},{19,3},{4,20},{20... | collective-permute-start | bytes 10616840 | tf_op jit(solution)/shard_map/ppermute | solution.py:628
  222.7 14.0 %collective-permute-start.7 = (bf16[16,4,2304]{2,1,0:T(4,128)(2,1)S(1)}, bf16[16,4,2304]{2,1,0:T(4,128)(2,1)S(1)}, u32[]{:S(2)}, u32[]{:S(2)}) collective-permute-start(bf16[16,4,2304]{2,1,0:T(4,128)(2,1)S(1)} %fusion.94), channel_id=1, source_target_pairs={{0,4},{4,8},{8,12},{1,5},{5,9},{9,13},{2,6},{6,10},{10,14},{3,7},{... | collective-permute-start | bytes 884744 | tf_op jit(solution)/shard_map/ppermute | solution.py:34
  237.3 21.1 %collective-permute-start.8 = (bf16[16,4,2304]{2,1,0:T(4,128)(2,1)S(1)}, bf16[16,4,2304]{2,1,0:T(4,128)(2,1)S(1)}, u32[]{:S(2)}, u32[]{:S(2)}) collective-permute-start(bf16[16,4,2304]{2,1,0:T(4,128)(2,1)S(1)} %add_convert_fusion.9), channel_id=1, source_target_pairs={{0,4},{4,8},{8,12},{1,5},{5,9},{9,13},{2,6},{6,10},{10,14},{3,7},{... | collective-permute-start | bytes 884744 | tf_op jit(solution)/shard_map/ppermute | solution.py:34
  258.8 13.6 %collective-permute-start.9 = (bf16[16,4,2304]{2,1,0:T(4,128)(2,1)S(1)}, bf16[16,4,2304]{2,1,0:T(4,128)(2,1)S(1)}, u32[]{:S(2)}, u32[]{:S(2)}) collective-permute-start(bf16[16,4,2304]{2,1,0:T(4,128)(2,1)S(1)} %add_convert_fusion.8), channel_id=1, source_target_pairs={{0,4},{4,8},{8,12},{1,5},{5,9},{9,13},{2,6},{6,10},{10,14},{3,7},{... | collective-permute-start | bytes 884744 | tf_op jit(solution)/shard_map/ppermute | solution.py:34
  275.8 80.1 %collective-permute-start.10 = (bf16[4,384,1152]{2,1,0:T(8,128)(2,1)}, bf16[4,384,1152]{2,1,0:T(8,128)(2,1)}, u32[]{:S(2)}, u32[]{:S(2)}) collective-permute-start(bf16[4,384,1152]{2,1,0:T(8,128)(2,1)} %collective-permute-done.2.refs_1_), channel_id=1, source_target_pairs={{0,4},{4,8},{8,12},{12,0},{1,5},{5,9},{9,13},{13,1},{2,6},{6,10},{... | collective-permute-start | bytes 10616840 | tf_op jit(solution)/shard_map/ppermute | solution.py:628
  280.5 76.4 %collective-permute-start.11 = (bf16[4,384,1152]{2,1,0:T(8,128)(2,1)}, bf16[4,384,1152]{2,1,0:T(8,128)(2,1)}, u32[]{:S(2)}, u32[]{:S(2)}) collective-permute-start(bf16[4,384,1152]{2,1,0:T(8,128)(2,1)} %collective-permute-done.2.refs_1_), channel_id=1, source_target_pairs={{0,16},{16,0},{1,17},{17,1},{2,18},{18,2},{3,19},{19,3},{4,20},{20... | collective-permute-start | bytes 10616840 | tf_op jit(solution)/shard_map/ppermute | solution.py:628
  356.9 76.7 %collective-permute-start.15 = (bf16[4,384,1152]{2,1,0:T(8,128)(2,1)}, bf16[4,384,1152]{2,1,0:T(8,128)(2,1)}, u32[]{:S(2)}, u32[]{:S(2)}) collective-permute-start(bf16[4,384,1152]{2,1,0:T(8,128)(2,1)} %collective-permute-done.10.refs_2_), channel_id=1, source_target_pairs={{0,4},{4,8},{8,12},{12,0},{1,5},{5,9},{9,13},{13,1},{2,6},{6,10},{... | collective-permute-start | bytes 10616840 | tf_op jit(solution)/shard_map/ppermute | solution.py:628
  357.3 76.2 %collective-permute-start.16 = (bf16[4,384,1152]{2,1,0:T(8,128)(2,1)}, bf16[4,384,1152]{2,1,0:T(8,128)(2,1)}, u32[]{:S(2)}, u32[]{:S(2)}) collective-permute-start(bf16[4,384,1152]{2,1,0:T(8,128)(2,1)} %collective-permute-done.10.refs_2_), channel_id=1, source_target_pairs={{0,16},{16,0},{1,17},{17,1},{2,18},{18,2},{3,19},{19,3},{4,20},{20... | collective-permute-start | bytes 10616840 | tf_op jit(solution)/shard_map/ppermute | solution.py:628
  365.3 24.7 %collective-permute-start.13 = (bf16[2,192,1280]{2,1,0:T(8,128)(2,1)S(1)}, bf16[2,192,1280]{2,1,0:T(8,128)(2,1)}, u32[]{:S(2)}, u32[]{:S(2)}) collective-permute-start(bf16[2,192,1280]{2,1,0:T(8,128)(2,1)S(1)} %bitcast.358), channel_id=1, source_target_pairs={{0,2},{1,3},{2,0},{3,1},{4,6},{5,7},{6,4},{7,5},{8,10},{9,11},{10,... | collective-permute-start | bytes 2949128 | tf_op jit(solution)/shard_map/ppermute | solution.py:633
  366.9 43.3 %collective-permute-start.14 = (bf16[2,192,1280]{2,1,0:T(8,128)(2,1)S(1)}, bf16[2,192,1280]{2,1,0:T(8,128)(2,1)}, u32[]{:S(2)}, u32[]{:S(2)}) collective-permute-start(bf16[2,192,1280]{2,1,0:T(8,128)(2,1)S(1)} %bitcast.357), channel_id=1, source_target_pairs={{0,3},{1,2},{2,1},{3,0},{4,7},{5,6},{6,5},{7,4},{8,11},{9,10},{10,... | collective-permute-start | bytes 2949128 | tf_op jit(solution)/shard_map/ppermute | solution.py:633
  436.4 60.8 %collective-permute-start.17 = (bf16[2,384,1152]{2,1,0:T(8,128)(2,1)}, bf16[2,384,1152]{2,1,0:T(8,128)(2,1)}, u32[]{:S(2)}, u32[]{:S(2)}) collective-permute-start(bf16[2,384,1152]{2,1,0:T(8,128)(2,1)} %slice.562), channel_id=1, source_target_pairs={{0,16},{16,0},{1,17},{17,1},{2,18},{18,2},{3,19},{19,3},{4,20},{20... | collective-permute-start | bytes 5308424 | tf_op jit(solution)/shard_map/ppermute | solution.py:628
  440.6 56.6 %collective-permute-start.18 = (bf16[2,384,1152]{2,1,0:T(8,128)(2,1)}, bf16[2,384,1152]{2,1,0:T(8,128)(2,1)}, u32[]{:S(2)}, u32[]{:S(2)}) collective-permute-start(bf16[2,384,1152]{2,1,0:T(8,128)(2,1)} %slice.563), channel_id=1, source_target_pairs={{0,4},{4,8},{8,12},{12,0},{1,5},{5,9},{9,13},{13,1},{2,6},{6,10},{... | collective-permute-start | bytes 5308424 | tf_op jit(solution)/shard_map/ppermute | solution.py:628
  561.2 87.3 %collective-permute-start.25 = (bf16[2,384,1152]{2,1,0:T(8,128)(2,1)}, bf16[2,384,1152]{2,1,0:T(8,128)(2,1)}, u32[]{:S(2)}, u32[]{:S(2)}) collective-permute-start(bf16[2,384,1152]{2,1,0:T(8,128)(2,1)} %pad_maximum_fusion.7), channel_id=1, source_target_pairs={{0,12},{4,0},{8,4},{12,8},{1,13},{5,1},{9,5},{13,9},{2,14},{6,2},{... | collective-permute-start | bytes 5308424 | tf_op jit(solution)/shard_map/ppermute | solution.py:628
  566.8 52.3 %collective-permute-start.22 = (bf16[2,192,1152]{2,1,0:T(8,128)(2,1)}, bf16[2,192,1152]{2,1,0:T(8,128)(2,1)S(1)}, u32[]{:S(2)}, u32[]{:S(2)}) collective-permute-start(bf16[2,192,1152]{2,1,0:T(8,128)(2,1)} %get-tuple-element.412), channel_id=1, source_target_pairs={{0,1},{1,0},{2,3},{3,2},{4,5},{5,4},{6,7},{7,6},{8,9},{9,8},{10,11... | collective-permute-start | bytes 2654216 | tf_op jit(solution)/shard_map/ppermute | solution.py:633
  569.8 22.8 %collective-permute-start.20 = (bf16[2,192,1152]{2,1,0:T(8,128)(2,1)}, bf16[2,192,1152]{2,1,0:T(8,128)(2,1)}, u32[]{:S(2)}, u32[]{:S(2)}) collective-permute-start(bf16[2,192,1152]{2,1,0:T(8,128)(2,1)} %get-tuple-element.418), channel_id=1, source_target_pairs={{0,2},{1,3},{2,0},{3,1},{4,6},{5,7},{6,4},{7,5},{8,10},{9,11},{10,... | collective-permute-start | bytes 2654216 | tf_op jit(solution)/shard_map/ppermute | solution.py:633
  571.3 39.4 %collective-permute-start.21 = (bf16[2,192,1152]{2,1,0:T(8,128)(2,1)}, bf16[2,192,1152]{2,1,0:T(8,128)(2,1)}, u32[]{:S(2)}, u32[]{:S(2)}) collective-permute-start(bf16[2,192,1152]{2,1,0:T(8,128)(2,1)} %get-tuple-element.417), channel_id=1, source_target_pairs={{0,3},{1,2},{2,1},{3,0},{4,7},{5,6},{6,5},{7,4},{8,11},{9,10},{10,... | collective-permute-start | bytes 2654216 | tf_op jit(solution)/shard_map/ppermute | solution.py:633
  577.3 53.1 %collective-permute-start.23 = (bf16[2,192,1152]{2,1,0:T(8,128)(2,1)S(1)}, bf16[2,192,1152]{2,1,0:T(8,128)(2,1)S(1)}, u32[]{:S(2)}, u32[]{:S(2)}) collective-permute-start(bf16[2,192,1152]{2,1,0:T(8,128)(2,1)S(1)} %copy-done.43), channel_id=1, source_target_pairs={{0,2},{1,3},{2,0},{3,1},{4,6},{5,7},{6,4},{7,5},{8,10},{9,11},{10,... | collective-permute-start | bytes 2654216 | tf_op jit(solution)/shard_map/ppermute | solution.py:633
  592.6 56.0 %collective-permute-start.24 = (bf16[2,192,1152]{2,1,0:T(8,128)(2,1)S(1)}, bf16[2,192,1152]{2,1,0:T(8,128)(2,1)S(1)}, u32[]{:S(2)}, u32[]{:S(2)}) collective-permute-start(bf16[2,192,1152]{2,1,0:T(8,128)(2,1)S(1)} %copy-done.42), channel_id=1, source_target_pairs={{0,3},{1,2},{2,1},{3,0},{4,7},{5,6},{6,5},{7,4},{8,11},{9,10},{10,... | collective-permute-start | bytes 2654216 | tf_op jit(solution)/shard_map/ppermute | solution.py:633
  610.7 107.1 %collective-permute-start.27 = (bf16[4,384,1152]{2,1,0:T(8,128)(2,1)}, bf16[4,384,1152]{2,1,0:T(8,128)(2,1)}, u32[]{:S(2)}, u32[]{:S(2)}) collective-permute-start(bf16[4,384,1152]{2,1,0:T(8,128)(2,1)} %bitcast.62), channel_id=1, source_target_pairs={{0,16},{16,0},{1,17},{17,1},{2,18},{18,2},{3,19},{19,3},{4,20},{20... | collective-permute-start | bytes 10616840 | tf_op jit(solution)/shard_map/ppermute | solution.py:628
  619.2 146.8 %collective-permute-start.29 = (bf16[4,384,1152]{2,1,0:T(8,128)(2,1)}, bf16[4,384,1152]{2,1,0:T(8,128)(2,1)}, u32[]{:S(2)}, u32[]{:S(2)}) collective-permute-start(bf16[4,384,1152]{2,1,0:T(8,128)(2,1)} %bitcast.64), channel_id=1, source_target_pairs={{0,16},{16,0},{1,17},{17,1},{2,18},{18,2},{3,19},{19,3},{4,20},{20... | collective-permute-start | bytes 10616840 | tf_op jit(solution)/shard_map/ppermute | solution.py:628
  650.6 41.6 %collective-permute-start.26 = (bf16[2,384,1152]{2,1,0:T(8,128)(2,1)S(1)}, bf16[2,384,1152]{2,1,0:T(8,128)(2,1)S(1)}, u32[]{:S(2)}, u32[]{:S(2)}) collective-permute-start(bf16[2,384,1152]{2,1,0:T(8,128)(2,1)S(1)} %add_convert_fusion.2), channel_id=1, source_target_pairs={{0,12},{4,0},{8,4},{12,8},{1,13},{5,1},{9,5},{13,9},{2,14},{6,2},{... | collective-permute-start | bytes 5308424 | tf_op jit(solution)/shard_map/ppermute | solution.py:628
  693.9 72.0 %collective-permute-start.30 = (bf16[2,384,1152]{2,1,0:T(8,128)(2,1)}, bf16[2,384,1152]{2,1,0:T(8,128)(2,1)S(1)}, u32[]{:S(2)}, u32[]{:S(2)}) collective-permute-start(bf16[2,384,1152]{2,1,0:T(8,128)(2,1)} %add_convert_fusion.1), channel_id=1, source_target_pairs={{0,12},{4,0},{8,4},{12,8},{1,13},{5,1},{9,5},{13,9},{2,14},{6,2},{... | collective-permute-start | bytes 5308424 | tf_op jit(solution)/shard_map/ppermute | solution.py:628
  720.4 45.5 %collective-permute-start.28 = (bf16[384,1152]{1,0:T(8,128)(2,1)}, bf16[384,1152]{1,0:T(8,128)(2,1)S(1)}, u32[]{:S(2)}, u32[]{:S(2)}) collective-permute-start(bf16[384,1152]{1,0:T(8,128)(2,1)} %fusion.53), channel_id=1, source_target_pairs={{0,12},{4,0},{8,4},{12,8},{1,13},{5,1},{9,5},{13,9},{2,14},{6,2},{... | collective-permute-start | bytes 2654216 | tf_op jit(solution)/shard_map/ppermute | solution.py:628
  805.3 307.2 %reduce-scatter.6.cloned.1.call-start = ((), (), s32[]{:S(2)}) async-start(), calls=%async_computation.4 | async-start | bytes 5640192 | tf_op jit(solution)/shard_map/reduce_scatter | solution.py:908
  809.4 116.9 %collective-permute-start.36 = (bf16[4,384,1152]{2,1,0:T(8,128)(2,1)}, bf16[4,384,1152]{2,1,0:T(8,128)(2,1)}, u32[]{:S(2)}, u32[]{:S(2)}) collective-permute-start(bf16[4,384,1152]{2,1,0:T(8,128)(2,1)} %bitcast.328), channel_id=1, source_target_pairs={{0,16},{16,0},{1,17},{17,1},{2,18},{18,2},{3,19},{19,3},{4,20},{20... | collective-permute-start | bytes 10616840 | tf_op jit(solution)/shard_map/ppermute | solution.py:628
  831.7 94.6 %collective-permute-start.37 = (bf16[384,1152]{1,0:T(8,128)(2,1)}, bf16[384,1152]{1,0:T(8,128)(2,1)}, u32[]{:S(2)}, u32[]{:S(2)}) collective-permute-start(bf16[384,1152]{1,0:T(8,128)(2,1)} %fusion.56), channel_id=1, source_target_pairs={{0,16},{16,0},{1,17},{17,1},{2,18},{18,2},{3,19},{19,3},{4,20},{20... | collective-permute-start | bytes 2654216 | tf_op jit(solution)/shard_map/ppermute | solution.py:628
  835.8 90.5 %collective-permute-start.35 = (bf16[384,1152]{1,0:T(8,128)(2,1)}, bf16[384,1152]{1,0:T(8,128)(2,1)S(1)}, u32[]{:S(2)}, u32[]{:S(2)}) collective-permute-start(bf16[384,1152]{1,0:T(8,128)(2,1)} %fusion.54), channel_id=1, source_target_pairs={{0,12},{4,0},{8,4},{12,8},{1,13},{5,1},{9,5},{13,9},{2,14},{6,2},{... | collective-permute-start | bytes 2654216 | tf_op jit(solution)/shard_map/ppermute | solution.py:628
  838.5 87.8 %collective-permute-start.34 = (bf16[384,1152]{1,0:T(8,128)(2,1)}, bf16[384,1152]{1,0:T(8,128)(2,1)}, u32[]{:S(2)}, u32[]{:S(2)}) collective-permute-start(bf16[384,1152]{1,0:T(8,128)(2,1)} %fusion.41), channel_id=1, source_target_pairs={{0,12},{4,0},{8,4},{12,8},{1,13},{5,1},{9,5},{13,9},{2,14},{6,2},{... | collective-permute-start | bytes 2654216 | tf_op jit(solution)/shard_map/ppermute | solution.py:628
  849.9 414.4 %reduce-scatter.8.cloned.1.call-start = ((), (), s32[]{:S(2)}) async-start(), calls=%async_computation.5 | async-start | bytes 5640192 | tf_op jit(solution)/shard_map/reduce_scatter | solution.py:955
  928.9 90.3 %collective-permute-start.40 = (bf16[384,1152]{1,0:T(8,128)(2,1)}, bf16[384,1152]{1,0:T(8,128)(2,1)}, u32[]{:S(2)}, u32[]{:S(2)}) collective-permute-start(bf16[384,1152]{1,0:T(8,128)(2,1)} %fusion.55), channel_id=1, source_target_pairs={{0,12},{4,0},{8,4},{12,8},{1,13},{5,1},{9,5},{13,9},{2,14},{6,2},{... | collective-permute-start | bytes 2654216 | tf_op jit(solution)/shard_map/ppermute | solution.py:628
  933.9 85.2 %collective-permute-start.39 = (bf16[384,1152]{1,0:T(8,128)(2,1)}, bf16[384,1152]{1,0:T(8,128)(2,1)}, u32[]{:S(2)}, u32[]{:S(2)}) collective-permute-start(bf16[384,1152]{1,0:T(8,128)(2,1)} %fusion.39), channel_id=1, source_target_pairs={{0,12},{4,0},{8,4},{12,8},{1,13},{5,1},{9,5},{13,9},{2,14},{6,2},{... | collective-permute-start | bytes 2654216 | tf_op jit(solution)/shard_map/ppermute | solution.py:628
  939.6 79.6 %collective-permute-start.38 = (bf16[384,1152]{1,0:T(8,128)(2,1)}, bf16[384,1152]{1,0:T(8,128)(2,1)}, u32[]{:S(2)}, u32[]{:S(2)}) collective-permute-start(bf16[384,1152]{1,0:T(8,128)(2,1)} %fusion.40), channel_id=1, source_target_pairs={{0,12},{4,0},{8,4},{12,8},{1,13},{5,1},{9,5},{13,9},{2,14},{6,2},{... | collective-permute-start | bytes 2654216 | tf_op jit(solution)/shard_map/ppermute | solution.py:628
  1022.2 81.5 %collective-permute-start.42 = (bf16[384,1152]{1,0:T(8,128)(2,1)}, bf16[384,1152]{1,0:T(8,128)(2,1)}, u32[]{:S(2)}, u32[]{:S(2)}) collective-permute-start(bf16[384,1152]{1,0:T(8,128)(2,1)} %fusion.37), channel_id=1, source_target_pairs={{0,12},{4,0},{8,4},{12,8},{1,13},{5,1},{9,5},{13,9},{2,14},{6,2},{... | collective-permute-start | bytes 2654216 | tf_op jit(solution)/shard_map/ppermute | solution.py:628
  1025.1 78.6 %collective-permute-start.41 = (bf16[384,1152]{1,0:T(8,128)(2,1)}, bf16[384,1152]{1,0:T(8,128)(2,1)}, u32[]{:S(2)}, u32[]{:S(2)}) collective-permute-start(bf16[384,1152]{1,0:T(8,128)(2,1)} %fusion.38), channel_id=1, source_target_pairs={{0,12},{4,0},{8,4},{12,8},{1,13},{5,1},{9,5},{13,9},{2,14},{6,2},{... | collective-permute-start | bytes 2654216 | tf_op jit(solution)/shard_map/ppermute | solution.py:628
  1106.6 64.9 %collective-permute-start.43 = (bf16[384,1152]{1,0:T(8,128)(2,1)}, bf16[384,1152]{1,0:T(8,128)(2,1)}, u32[]{:S(2)}, u32[]{:S(2)}) collective-permute-start(bf16[384,1152]{1,0:T(8,128)(2,1)} %fusion.36), channel_id=1, source_target_pairs={{0,12},{4,0},{8,4},{12,8},{1,13},{5,1},{9,5},{13,9},{2,14},{6,2},{... | collective-permute-start | bytes 2654216 | tf_op jit(solution)/shard_map/ppermute | solution.py:628
  1121.9 46.6 %collective-permute-start.51 = (bf16[1,4,4,72,256]{4,3,2,1,0:T(8,128)(2,1)}, bf16[1,4,4,72,256]{4,3,2,1,0:T(8,128)(2,1)}, u32[]{:S(2)}, u32[]{:S(2)}) collective-permute-start(bf16[1,4,4,72,256]{4,3,2,1,0:T(8,128)(2,1)} %bitcast.369), channel_id=1, source_target_pairs={{0,16},{16,0},{1,17},{17,1},{2,18},{18,2},{3,19},{19,3},{4,20},{20... | collective-permute-start | bytes 1769480 | tf_op jit(solution)/shard_map/ppermute | solution.py:633
  1169.9 34.4 %collective-permute-start.52 = (bf16[2,4,72,256]{3,2,0,1:T(8,128)(2,1)S(1)}, bf16[2,4,72,256]{3,2,0,1:T(8,128)(2,1)S(1)}, u32[]{:S(2)}, u32[]{:S(2)}) collective-permute-start(bf16[2,4,72,256]{3,2,0,1:T(8,128)(2,1)S(1)} %select_convert_fusion), channel_id=1, source_target_pairs={{0,2},{1,3},{2,0},{3,1},{4,6},{5,7},{6,4},{7,5},{8,10},{9,11},{10,... | collective-permute-start | bytes 884744 | tf_op jit(solution)/shard_map/ppermute | solution.py:633
  1204.5 32.4 %collective-permute-start.53 = (bf16[1,4,72,256]{3,2,0,1:T(8,128)(2,1)S(1)}, bf16[1,4,72,256]{3,2,0,1:T(8,128)(2,1)S(1)}, u32[]{:S(2)}, u32[]{:S(2)}) collective-permute-start(bf16[1,4,72,256]{3,2,0,1:T(8,128)(2,1)S(1)} %select_convert_fusion.2), channel_id=1, source_target_pairs={{0,1},{1,0},{2,3},{3,2},{4,5},{5,4},{6,7},{7,6},{8,9},{9,8},{10,11... | collective-permute-start | bytes 442376 | tf_op jit(solution)/shard_map/ppermute | solution.py:633
  1217.9 19.2 %collective-permute-start.45 = (f32[180,128]{1,0:T(8,128)S(1)}, f32[180,128]{1,0:T(8,128)S(1)}, u32[]{:S(2)}, u32[]{:S(2)}) collective-permute-start(f32[180,128]{1,0:T(8,128)S(1)} %maximum_bitcast_fusion), channel_id=1, source_target_pairs={{0,16},{16,0},{1,17},{17,1},{2,18},{18,2},{3,19},{19,3},{4,20},{20... | collective-permute-start | bytes 276488 | tf_op jit(solution)/shard_map/ppermute | solution.py:633
  (92 other events, 1288.8 us)
Sparse Core Ops, SparseCore 0:
  14.8 109.3 all-gather.5
  127.0 137.6 all-gather.3
  805.4 120.2 reduce-scatter.9
  929.6 96.3 reduce-scatter.5
  1177.6 80.2 reduce-scatter.7

commit v3 on v2

--- a/solution.py
+++ b/solution.py
@@ -76,14 +76,18 @@
     src = src_ref[...]
     high = src.astype(jnp.bfloat16)
     both = jnp.concatenate([high, (src - high.astype(jnp.float32)).astype(jnp.bfloat16)], axis=1)
-    line = lax.broadcasted_iota(jnp.int32, (4 * NSTATE, LANES), 0)
+    line = lax.broadcasted_iota(jnp.int32, (4 * NSTATE, 2 * LANES), 0)
+    shift = jnp.where(lax.broadcasted_iota(jnp.int32, (4 * NSTATE, 2 * LANES), 1) < LANES, 0, NSTATE // 2)
 
     def body(n, carry):
-        pick = (line == first + n) | (line == 2 * NSTATE + first + n)
-        dst[n] = dot(both, jnp.where(pick, 1.0, 0.0).astype(jnp.bfloat16), NN)
+        wanted = shift + (first + n)
+        pick = (line == wanted) | (line == wanted + 2 * NSTATE)
+        wide = dot(both, jnp.where(pick, 1.0, 0.0).astype(jnp.bfloat16), NN)
+        dst[n] = wide[:, :LANES]
+        dst[n + NSTATE // 2] = wide[:, LANES:]
         return carry
 
-    lax.fori_loop(0, NSTATE, body, 0)
+    lax.fori_loop(0, NSTATE // 2, body, 0)
 
 
 def tree_sum(parts):
@@ -217,6 +221,8 @@
     x_s[...] = xs
     dx_s[...] = delta_ref[...] * xs
 
+    rates = [a_s[n] for n in range(NSTATE)]
+
     def ahead(j, state, base):
         at = row_at(base + j)
         step = jnp.maximum(delta_ref[at, :], cut_ref[at, :])
@@ -224,7 +230,7 @@
         g = g_ref[at, :]
         new = []
         for n in range(NSTATE):
-            dec = jnp.exp2(step * a_s[n])
+            dec = jnp.exp2(step * rates[n])
             hd = dec * state[n]
             dec_s[j, n] = dec
             hd_s[j, n] = hd
@@ -279,13 +285,14 @@
 
     @pl.when(pl.program_id(0) == pl.num_programs(0) - 1)
     def _():
-        lane = lax.broadcasted_iota(jnp.int32, (LANES, LANES), 1)
+        lane = lax.broadcasted_iota(jnp.int32, (2 * LANES, LANES), 1)
+        line = lax.broadcasted_iota(jnp.int32, (2 * LANES, LANES), 0)
         gbc_ref[...] = jnp.zeros_like(gbc_ref)
 
         def gather(n, carry):
-            for part, first in ((gb_s, 0), (gc_s, NSTATE)):
-                pick = jnp.where(lane == first + n, 1.0, 0.0).astype(jnp.bfloat16)
-                gbc_ref[...] += dot(part[n].astype(jnp.bfloat16), pick, NN)
+            pick = jnp.where(lane == jnp.where(line < LANES, n, NSTATE + n), 1.0, 0.0).astype(jnp.bfloat16)
+            both = jnp.concatenate([gb_s[n].astype(jnp.bfloat16), gc_s[n].astype(jnp.bfloat16)], axis=1)
+            gbc_ref[...] += dot(both, pick, NN)
             return carry
 
         lax.fori_loop(0, NSTATE, gather, 0)
@@ -476,116 +483,108 @@
     return value, slope
 
 
-def expert_kernel(blocks, peers, split_last, final, *refs):
-    count = blocks + (1 if split_last else 0)
-    weights, refs = refs[:count], refs[count:]
+QUARTERS = 4
+
+
+def expert_kernel(blocks, peers, *refs):
+    weights, refs = refs[:blocks], refs[blocks:]
     xs, gs, refs = refs[:peers], refs[peers : 2 * peers], refs[2 * peers :]
-    if final:
-        before, refs = refs[:2], refs[2:]
-    out_refs, (upg_ref, downg_ref), refs = refs[:2], refs[2:4], refs[4:]
-    x_s, g_s, up_s, down_s, hid_s, pre_s, acc_y, acc_g = refs
+    out_ref, x_ref, g_ref, hid_ref, pre_ref, up_s, down_s, acc_y, acc_g = refs
     cap = xs[0].shape[1]
     size = weights[0].shape[1]
-    expert, half = pl.program_id(0), pl.program_id(1)
-
-    @pl.when(half == 0)
+    step = pl.program_id(0)
+
+    @pl.when(step == 0)
     def _():
         for d in range(peers):
             at = slice(d * cap, (d + 1) * cap)
             piece = xs[d][0]
-            x_s[at, :] = piece[:, :D]
+            x_ref[at, :] = piece[:, :D]
             gate = jnp.sum(piece[:, D:].astype(jnp.float32), axis=1, keepdims=True)
-            g_s[at, :] = (gate * gs[d][0].astype(jnp.float32)).astype(jnp.bfloat16)
-        if final:
-            acc_y[...] = before[0][0].astype(jnp.float32)
-            acc_g[...] = before[1][0].astype(jnp.float32)
-        else:
-            acc_y[...] = jnp.zeros_like(acc_y)
-            acc_g[...] = jnp.zeros_like(acc_g)
-
-    def place(k, ref):
-        at = slice(k * size, (k + 1) * size)
-        up_s[at, :] = ref[0]
-        down_s[at, :] = ref[1]
-
-    for h in range(2):
-
-        @pl.when(half == h)
+            g_ref[at, :] = (gate * gs[d][0].astype(jnp.float32)).astype(jnp.bfloat16)
+        acc_y[...] = jnp.zeros_like(acc_y)
+        acc_g[...] = jnp.zeros_like(acc_g)
+
+    each = blocks // QUARTERS
+    for h in range(QUARTERS):
+
+        @pl.when(step == h)
         def _():
-            for k in range(blocks // 2):
-                block = h * (blocks // 2) + k
-                if split_last and block == blocks - 1:
-                    for e in range(2):
-                        pl.when(expert == e)(functools.partial(place, k, weights[block + e]))
-                else:
-                    place(k, weights[block])
-
-    rows = cap * peers
-    tile = rows // 3
-    cols = up_s.shape[0]
+            for k in range(each):
+                at = slice(k * size, (k + 1) * size)
+                up_s[at, :] = weights[h * each + k][0]
+                down_s[at, :] = weights[h * each + k][1]
+
+    tile = cap * peers // 3
 
     def body(r, carry):
         at = pl.ds(pl.multiple_of(r * tile, tile), tile)
-        value, slope = gelu_pair(dot(x_s[at, :], up_s[...], NT))
+        value, slope = gelu_pair(dot(x_ref[at, :], up_s[...], NT))
         hidden = value.astype(jnp.bfloat16)
-        grad_pre = (slope * dot(g_s[at, :], down_s[...], NT)).astype(jnp.bfloat16)
-        hid_s[at, :] = hidden
-        pre_s[at, :] = grad_pre
+        grad_pre = (slope * dot(g_ref[at, :], down_s[...], NT)).astype(jnp.bfloat16)
+        hid_ref[at, :] = hidden
+        pre_ref[at, :] = grad_pre
         acc_y[at, :] += dot(hidden, down_s[...], NN)
         acc_g[at, :] += dot(grad_pre, up_s[...], NN)
         return carry
 
     lax.fori_loop(0, 3, body, 0)
-    wide = cols // 3
-
-    def grads(c, carry):
-        at = pl.ds(pl.multiple_of(c * wide, wide), wide)
-        upg_ref[0, at, :] = dot(pre_s[:, at], x_s[...], TN).astype(jnp.bfloat16)
-        downg_ref[0, at, :] = dot(hid_s[:, at], g_s[...], TN).astype(jnp.bfloat16)
-        return carry
-
-    lax.fori_loop(0, 3, grads, 0)
-
-    @pl.when(half == 1)
+
+    @pl.when(step == QUARTERS - 1)
     def _():
-        out_refs[0][0] = acc_y[...].astype(jnp.bfloat16)
-        out_refs[1][0] = acc_g[...].astype(jnp.bfloat16)
-
-
-def run_experts(weights, split_last, xs, gs, before):
-    blocks = len(weights) - (1 if split_last else 0)
-    peers = len(xs)
-    count, cap = xs[0].shape[:2]
+        out_ref[:, :D] = acc_y[...].astype(jnp.bfloat16)
+        out_ref[:, D:] = acc_g[...].astype(jnp.bfloat16)
+
+
+def run_expert(weights, xs, gs, e):
+    blocks, peers = len(weights), len(xs)
+    cap = xs[0].shape[1]
     size = weights[0].shape[1]
     rows, cols = peers * cap, blocks * size
-    final = before is not None
-
-    def pick(shape, **more):
-        return pl.BlockSpec((1,) + shape, lambda e, h: (e, 0, 0), **more)
-
+    part = cols // QUARTERS
     once = dict(pipeline_mode=pl.Buffered(1))
-    pair = pl.BlockSpec((2, size, D), lambda e, h: (e, 0, 0))
-    half = pl.BlockSpec((2, size, D), lambda e, h: (0, 0, 0), **once)
-    in_specs = [pair] * (blocks - 1 if split_last else blocks) + ([half] * 2 if split_last else [])
+
+    def pick(shape):
+        return pl.BlockSpec((1,) + shape, lambda h: (e, 0, 0), **once)
+
+    in_specs = [pl.BlockSpec((2, size, D), lambda h: (e, 0, 0), **once)] * blocks
     in_specs += [pick(xs[0].shape[1:])] * peers + [pick(gs[0].shape[1:])] * peers
-    in_specs += [pick((rows, D), **once)] * (2 if final else 0)
-    low = functools.partial(pltpu.VMEM, dtype=jnp.bfloat16)
-    work = 12 * count * rows * cols * D
-    grads = pl.BlockSpec((1, cols // 2, D), lambda e, h: (e, h, 0))
+    column = pl.BlockSpec((rows, part), lambda h: (0, h))
     return pl.pallas_call(
-        functools.partial(expert_kernel, blocks, peers, split_last, final),
-        grid=(count, 2),
+        functools.partial(expert_kernel, blocks, peers),
+        grid=(QUARTERS,),
         in_specs=in_specs,
-        out_specs=[pick((rows, D))] * 2 + [grads] * 2,
-        out_shape=[b16s(count, rows, D)] * 2 + [b16s(count, cols, D)] * 2,
+        out_specs=[full_spec((rows, 2 * D)), full_spec((rows, D)), full_spec((rows, D)), column, column],
+        out_shape=[b16s(rows, 2 * D), b16s(rows, D), b16s(rows, D), b16s(rows, cols), b16s(rows, cols)],
         scratch_shapes=[
-            low((rows, D)), low((rows, D)), low((cols // 2, D)), low((cols // 2, D)),
-            low((rows, cols // 2)), low((rows, cols // 2)), vm(rows, D), vm(rows, D),
+            pltpu.VMEM((part, D), jnp.bfloat16), pltpu.VMEM((part, D), jnp.bfloat16), vm(rows, D), vm(rows, D),
         ],
         compiler_params=params(),
-        cost_estimate=pl.CostEstimate(flops=work, bytes_accessed=count * (4 * cols + 8 * rows) * D * 2, transcendentals=count * rows * cols),
-        name="experts",
-    )(*weights, *xs, *gs, *(before or ()))
+        cost_estimate=pl.CostEstimate(flops=1000, bytes_accessed=1000, transcendentals=0),
+        name="expert",
+    )(*weights, *xs, *gs)
+
+
+def weight_kernel(hid_ref, pre_ref, x_ref, g_ref, up_ref, down_ref):
+    up_ref[...] = dot(pre_ref[...], x_ref[...], TN).astype(jnp.bfloat16)
+    down_ref[...] = dot(hid_ref[...], g_ref[...], TN).astype(jnp.bfloat16)
+
+
+def run_weight(hid, pre, x, g):
+    rows, cols = hid.shape
+    part = cols // 12
+    column = pl.BlockSpec((rows, part), lambda c: (0, c))
+    out = pl.BlockSpec((part, D), lambda c: (c, 0))
+    return pl.pallas_call(
+        weight_kernel,
+        grid=(12,),
+        in_specs=[column, column, full_spec((rows, D)), full_spec((rows, D))],
+        out_specs=[out, out],
+        out_shape=[b16s(cols, D), b16s(cols, D)],
+        compiler_params=params(),
+        cost_estimate=pl.CostEstimate(flops=1000, bytes_accessed=1000, transcendentals=0),
+        name="weight",
+    )(hid, pre, x, g)
 
 
 def halves_of(value, seqs):
@@ -598,28 +597,31 @@
     return both.reshape(both.shape[:-3] + (both.shape[-3] * HALVES, both.shape[-1]))
 
 
-def chained(own, decay, steps):
+def chained(own, decay, steps, beside):
     start = jnp.zeros_like(own)
     carry = own
     for k in range(lax.axis_size("seq") - 1):
-        start = shifted(carry.astype(jnp.bfloat16), "seq", steps).astype(jnp.float32)
+        start = shifted(carry.astype(jnp.bfloat16), "seq", steps)
+        if k < len(beside):
+            start, beside[k] = held_for(start, beside[k])
+        start = start.astype(jnp.float32)
         carry = own + decay * start
     return start
 
 
-def start_states(ends, sums, rates, seqs):
+def start_states(ends, sums, rates, seqs, beside):
     end_0, end_1 = halves_of(ends, seqs)
     sum_0, sum_1 = halves_of(sums, seqs)
     decay_0 = jnp.exp(rates * sum_0)
     decay_1 = jnp.exp(rates * sum_1)
-    start = chained(decay_1 * end_0 + end_1, decay_0 * decay_1, 1)
+    start = chained(decay_1 * end_0 + end_1, decay_0 * decay_1, 1, beside)
     return join_halves(start, decay_0 * start + end_0), (decay_0, decay_1)
 
 
-def last_grads(leads, decays, seqs):
+def last_grads(leads, decays, seqs, beside):
     decay_0, decay_1 = decays
     lead_0, lead_1 = halves_of(leads, seqs)
-    last = chained(lead_0 + decay_0 * lead_1, decay_0 * decay_1, -1)
+    last = chained(lead_0 + decay_0 * lead_1, decay_0 * decay_1, -1, beside)
     return join_halves(lead_1 + decay_1 * last, last)
 
 
@@ -724,16 +726,34 @@
     return value
 
 
-def halved(value, axis):
-    index, bits = lax.axis_index(axis), lax.axis_size(axis) // 2
-    while bits >= 1:
-        pair = value.reshape((2, bits) + value.shape[1:])
-        high = (index // bits) % 2 == 1
-        keep = jnp.where(high, pair[1], pair[0])
-        send = jnp.where(high, pair[0], pair[1])
-        value = keep.astype(jnp.float32) + partner(send.astype(jnp.bfloat16), axis, bits).astype(jnp.float32)
-        bits //= 2
-    return value[0]
+class Halving:
+    def __init__(self, value, axes, near_first):
+        self.dims = [(axis, 1 << k) for axis in axes for k in reversed(range(lax.axis_size(axis).bit_length() - 1))]
+        self.plan = [d for d in self.dims if near_first and d == ("expert", 1)]
+        self.plan += [d for d in self.dims if d[0] == "expert" and d not in self.plan]
+        self.plan += [d for d in self.dims if d not in self.plan]
+        self.value = value.reshape((2,) * len(self.plan) + value.shape[1:])
+        self.start()
+
+    def start(self):
+        axis, bit = self.plan.pop(0)
+        dim = self.dims.index((axis, bit))
+        self.dims.pop(dim)
+        low, high = (lax.index_in_dim(self.value, k, dim, False) for k in range(2))
+        upper = (lax.axis_index(axis) // bit) % 2 == 1
+        self.keep = jnp.where(upper, high, low)
+        self.moving = partner(jnp.where(upper, low, high).astype(jnp.bfloat16), axis, bit)
+
+    def step(self):
+        self.value = self.keep.astype(jnp.float32) + self.moving.astype(jnp.float32)
+        self.moving = None
+        if self.plan:
+            self.start()
+
+    def finish(self):
+        while self.moving is not None:
+            self.step()
+        return self.value
 
 
 def sum_everywhere(value):
@@ -767,13 +787,16 @@
     used = small.shape[1]
     small = jnp.pad(small, ((0, 0), (0, PACK - used)))
     entry = lax.all_gather(jnp.concatenate([in_proj.T, small.reshape(-1, D)], axis=0), ALL, axis=0, tiled=False)
-    in_full = entry[:, :own].reshape(2 * DI, D)
+    middle = entry.shape[0] // 2
+    conv_full = entry[:middle, :own].reshape(DI, D)
+    gate_full = entry[middle:, :own].reshape(DI, D)
     small = entry[:, own:].reshape(DI, PACK)
     out_full = lax.all_gather(out_proj, ALL, axis=0, tiled=True)
     local_experts = expert_up.shape[0]
     shard = jnp.stack([m for e in range(local_experts) for m in (expert_up[e].T, expert_down[e])])
-    shard, in_full = held_for(shard, in_full)
     gather = Gather(shard)
+    gather.step()
+    conv_full = gather.hold(conv_full)
     gather.step()
 
     xproj_full = small[:, :XW]
@@ -816,8 +839,8 @@
     gain_one = norm_one.astype(f32)
     inv_one = lax.rsqrt(jnp.mean(inputs * inputs, axis=-1, keepdims=True) + norm_eps)
     normed_one = (inputs * inv_one * gain_one).astype(b16)
-    ext = dot(normed_one, in_full[:DI], NT)
-    gate_z = dot(normed_one[skip_rows:], in_full[DI:], NT)
+    ext = dot(normed_one, conv_full, NT)
+    gate_z = dot(normed_one[skip_rows:], gate_full, NT)
     conv_out = cbias + conv_w[halo] * ext[skip_rows:]
     for k in range(halo):
         conv_out = conv_out + conv_w[k] * (same[k] * ext[k * SUB : k * SUB + rows])
@@ -829,7 +852,9 @@
     delta, ends, sums = run_end(xs, delta_in, dtw, dtb, alog, bc, cut)
     ends, grad_arrived = held_for(gather.hold(ends), grad_arrived)
     rates = -jnp.exp(alog.astype(f32))[:, None, :]
-    starts, decays = start_states(ends, sums, rates, seqs)
+    beside = [gate_z]
+    starts, decays = start_states(ends, sums, rates, seqs, beside)
+    gate_z = beside[0]
     starts = gather.hold(starts)
     gather.step()
     branch, ssm, held = run_out(xs, delta, alog, bc, cut, starts, gate_z, skip)
@@ -849,34 +874,30 @@
     message = jnp.concatenate([normed_two, jnp.pad(gates, ((0, 0), (0, LANES - 3)))], axis=1)
     message = gather.hold(message)
     gather.step()
-    arrived = dispatch(message)
-    arrived = gather.hold(arrived)
     while not gather.done():
         gather.step()
-    sum_y, sum_g, up_here, down_here = run_experts(gather.here, False, arrived, grad_arrived, None)
-    sum_y = gather.hold(sum_y)
-    sum_y, sum_g, up_there, down_there = run_experts(
-        gather.there[:-1] + gather.there[-1], True, arrived, grad_arrived, (sum_y, sum_g)
-    )
+    arrived = gather.hold(dispatch(message))
+    blocks = gather.here + gather.there[:-1] + [jnp.concatenate(gather.there[-1], axis=0)]
+    returned, for_weights = [], []
+    for e in range(local_experts):
+        done, *rest = run_expert(blocks, arrived, grad_arrived, e)
+        for_weights.append(rest)
+        if e > 0:
+            done, returned = held_for(done, returned)
+        returned.append(exchange([part for part in done.reshape(peers, capacity, 2 * D)]))
     weight_grads = []
     for e in range(local_experts):
-        weight_grads += [(up_here[e], up_there[e]), (down_here[e], down_there[e])]
+        x_rows, g_rows, hid, pre = for_weights[e]
+        weight_grads += run_weight(hid, pre, x_rows, g_rows)
+    returned[-1], weight_grads = held_for(returned[-1], weight_grads)
     count = len(weight_grads)
-    reduces = [Reduce(g[0], g[1], i < count - 1) for i, g in enumerate(weight_grads)]
-
-    def send_back(parts):
-        parts = parts.reshape(local_experts, peers, capacity, D)
-        return exchange([parts[:, d] for d in range(peers)])
-
-    returned_y = send_back(sum_y)
-    returned_g = send_back(sum_g)
-
-    def collect(parts):
-        back_rows = jnp.stack(parts).reshape(EXPERTS * capacity, D)
-        return dot(placing, back_rows, TN)
-
-    expert_rows = collect(returned_y)
-    grad_back = collect(hold_all(returned_g, reduces[-1:]))
+    middle = weight_grads[0].shape[0] // 2
+    reduces = [Reduce(g[:middle], g[middle:], i < count - 1) for i, g in enumerate(weight_grads)]
+    returned = [jnp.stack([returned[e][d] for e in range(local_experts)]) for d in range(peers)]
+
+    back_rows = jnp.stack(returned).reshape(EXPERTS * capacity, 2 * D)
+    combined = dot(placing, back_rows, TN)
+    expert_rows, grad_back = combined[:, :D], combined[:, D:]
     output = (first_sum + gate[:, None] * expert_rows).astype(b16)
 
     grad_gate = jnp.sum(grad_final * expert_rows, axis=-1) * drop
@@ -899,12 +920,13 @@
 
     leads, grad_z, grad_ssm = run_first(delta, alog, bc, cut, grad_branch, gate_z, ssm)
     leads = settle(leads, [reduces[0], reduces[1], reduces[-1]])
-    last = last_grads(leads, decays, seqs)
-    last, out_grad_part = held_for(last, out_grad_part)
+    gate_part = dot(grad_z, normed_one[skip_rows:], TN, b16)
+    grad_normed_z = dot(grad_z, gate_full, NN)
+    beside = [gate_part, grad_normed_z, router_grad]
+    last = last_grads(leads, decays, seqs, beside)
+    gate_part, grad_normed_z, router_grad = beside
+    last, out_grad_part, gate_part = held_for(last, out_grad_part, gate_part)
     out_sum = lax.psum_scatter(out_grad_part, ALL, scatter_dimension=0, tiled=True)
-    gate_part = dot(grad_z, normed_one[skip_rows:], TN, b16)
-    grad_normed_z = dot(grad_z, in_full[DI:], NN)
-    grad_ssm, gate_part, grad_normed_z = held_for(grad_ssm, gate_part, grad_normed_z)
     gate_own = lax.psum_scatter(gate_part, ("seq", "expert"), scatter_dimension=0, tiled=True)
     grad_delta_in, gbc, parts = 0.0, 0.0, []
     width = DI // SPLITS
@@ -938,10 +960,7 @@
     ).astype(b16)
     small_grad = jnp.pad(small_grad, ((0, 0), (0, PACK - used)))
     small_grad, grad_proj = held_for(small_grad, grad_proj)
-    small_sum = small_grad.reshape(lax.axis_size("dp"), lax.axis_size("seq"), peers, own // 2, PACK)
-    small_sum = halved(small_sum, "dp")
-    small_sum = halved(small_sum.swapaxes(0, 1), "expert")
-    small_sum = halved(small_sum, "seq")
+    small_half = Halving(small_grad.reshape(-1, own // 2, PACK), ALL, True)
     gexts, conv_parts, conv_grads = [], [], []
     for part in range(SPLITS):
         gext, gvec = run_conv(parts[part][0], grad_proj, xproj_full, ext, conv_w, cbias, same_wide, part)
@@ -951,12 +970,14 @@
         gexts.append(gext)
         conv_grads.append(gvec)
     conv_all, gexts = held_for(jnp.concatenate(conv_parts, axis=0), gexts)
-    grad_normed = sum(dot(gexts[k], in_full[k * width : (k + 1) * width], NN) for k in range(SPLITS))
-    conv_own = lax.psum_scatter(conv_all, ("seq", "expert"), scatter_dimension=0, tiled=True)
-    is_gate = lax.axis_index("dp") == 1
-    in_sum = jnp.where(is_gate, gate_own, conv_own).astype(f32)
-    in_sum = in_sum + ring(jnp.where(is_gate, conv_own, gate_own), "dp", 1).astype(f32)
-
+    third = D // 3
+    conv_own = []
+    for k in range(3):
+        piece = conv_all[:, k * third : (k + 1) * third].reshape(-1, own, third)
+        conv_own.append(Halving(piece, ("seq", "expert"), True))
+    gexts = hold_all(gexts, conv_own + [small_half])
+    grad_normed = sum(dot(gexts[k], conv_full[k * width : (k + 1) * width], NN) for k in range(SPLITS))
+    grad_normed = hold_all(grad_normed, conv_own + [small_half])
     over = grad_normed[:skip_rows].reshape(halo, seqs, HALVES, D)
     from_next = shifted(over[:, :, 0], "seq", -1)
     edge = jnp.stack([over[:, :, 1], from_next], axis=2).reshape(skip_rows, D)
@@ -971,7 +992,14 @@
     )
     conv_grad = jnp.concatenate(conv_grads, axis=1)[: CONVK + 1]
     flat = jnp.concatenate([gain_one_grad, gain_two_grad, router_grad.reshape(-1), conv_grad.reshape(-1)])
+    flat = hold_all(flat, conv_own + [small_half])
     flat = sum_everywhere(flat.reshape(-1, LANES)).reshape(-1)
+    small_sum = small_half.finish()
+    is_gate = lax.axis_index("dp") == 1
+    gate_own = gate_own.astype(f32)
+    conv_own = jnp.concatenate([part.finish() for part in conv_own], axis=1)
+    in_sum = jnp.where(is_gate, gate_own, conv_own)
+    in_sum = in_sum + ring(jnp.where(is_gate, conv_own, gate_own).astype(b16), "dp", 1).astype(f32)
     gain_one_sum, gain_two_sum = flat[:D], flat[D : 2 * D]
     router_sum = flat[2 * D : (2 + EXPERTS) * D].reshape(D, EXPERTS)
     conv_sum = flat[(2 + EXPERTS) * D :].reshape(CONVK + 1, DI)

time: 1290 us -> 1420 us (1.10)
  waiting for transfers between devices: 295 us -> 376 us
  starting transfers between devices: 70.8 us -> 95.4 us
  local copies, waits for them, and re-layouts: 162 us -> 182 us
  other arithmetic: 101 us -> 116 us
    ppermute x9, waiting for transfers between devices: 43.9 us -> 122 us  [shifted(): lax.ppermute(value, axis, [(source, source + steps) for source in range(f...]
    ppermute x25, waiting for transfers between devices: 77.7 us -> 130 us  [ring(): lax.ppermute(value, axis, [(i, (i + step) % count) for i in range(count)])]
    all_gather x1, waiting for transfers between devices: 48.7 us -> 0.01 us  [local(): lax.all_gather(jnp.concatenate([in_proj.T, small.reshape(-1, D)], axis=0)...]
    ppermute x22 -> x34, waiting for transfers between devices: 125 us -> 77.6 us  [partner(): return lax.ppermute(value, axis, [(i, i ^ bits) for i in range(count)])]
    optimization_barrier x1, waiting for transfers between devices: 0.02 us -> 46 us  [held_for(): return jax.tree.unflatten(tree, lax.optimization_barrier(flat))]
    ppermute x22 -> x34, starting transfers between devices: 12.8 us -> 31.3 us  [partner(): return lax.ppermute(value, axis, [(i, i ^ bits) for i in range(count)])]
    dot_general x29 -> x28, matrix products: 145 us -> 133 us  [dot(): lax.dot_general(left, right, (dims, ((), ())), preferred_element_type=out)]
    unnamed x172 -> x239, local copies, waits for them, and re-layouts: 24.3 us -> 34.2 us
  transfers between devices with their start and end apart: 61 -> 72, of which waited for: 24 -> 23; matrix products, arithmetic and copies ran while one was open for 29% -> 24% of each run, Pallas kernels for 34% -> 32%
where the time goes in v3:
time: 1420 us; the launch traced here: 1410 us
  Pallas kernels  487 us (34%)
  waiting for transfers between devices  376 us (26%)
  local copies, waits for them, and re-layouts  182 us (13%)
  matrix products  133 us (9%)
  other arithmetic  116 us (8%)
  starting transfers between devices  95.4 us (7%)
  between operations  16.4 us (1%)
    pallas_call x3, Pallas kernels, run_back(): pl.pallas_call(back_kernel, grid=(width // LANES,), in_specs=[col(rows),...  207 us
    dot_general x28, matrix products, dot(): lax.dot_general(left, right, (dims, ((), ())), preferred_element_type=out)  133 us
    ppermute x25, waiting for transfers between devices, ring(): lax.ppermute(value, axis, [(i, (i + step) % count) for i in range(count)])  130 us
    ppermute x9, waiting for transfers between devices, shifted(): lax.ppermute(value, axis, [(source, source + steps) for source in range(f...  122 us
    pallas_call x2, Pallas kernels, run_expert(): pl.pallas_call(functools.partial(expert_kernel, blocks, peers), grid=(QUA...  80.5 us
    ppermute x34, waiting for transfers between devices, partner(): return lax.ppermute(value, axis, [(i, i ^ bits) for i in range(count)])  77.6 us
    pallas_call x1, Pallas kernels, run_out(): pl.pallas_call(out_kernel, grid=(DI // LANES,), in_specs=[col_spec(rows),...  53.4 us
    optimization_barrier x1, waiting for transfers between devices, held_for(): return jax.tree.unflatten(tree, lax.optimization_barrier(flat))  46 us
  transfers between devices with their start and end apart: 72, of which 23 were waited for; matrix products, arithmetic and copies ran while one was open for 24% of the time, Pallas kernels for 32%

profile of v3, /device:TPU:0, one launch (start us, length us, event | category | flops | bytes accessed | tf_op | source)
XLA Modules:
  0.0 1405.0 jit_solution(589826881706106657)
XLA Ops:
  38.1 5.0 reshape.633
  51.0 105.4 %collective-permute-done.3 = f32[4,3]{1,0:T(4,128)S(1)} collective-permute-done((f32[4,3]{1,0:T(4,128)S(1)}, f32[4,3]{1,0:T(4,128)S(1)}, u32[]{:S(2)}, u32[]{:S(2)}) %collective-permute-start.3) | collective-permute-done | bytes 80 | tf_op jit(solution)/shard_map/ppermute | solution.py:34
  164.9 5.9 copy.249
  170.8 7.1 convert_element_type.583
  184.7 8.8 fusion.120
  200.3 9.7 fusion.142.ext_ref
  210.0 7.1 multiply_convert_fusion.xs_ref
  225.4 44.0 %end.1 = (f32[1024,2304]{1,0:T(8,128)}, f32[16,8,2304]{2,1,0:T(8,128)}, f32[8,2304]{1,0:T(8,128)}) custom-call(bf16[1024,2304]{1,0:T(8,128)(2,1)} %copy-done.3, bf16[1024,72]{1,0:T(8,128)(2,1)} %copy.309.din_ref, bf16[2304,72]{1,0:T(8,128)(2,1)} %slice.764.dtw_ref, bf16[1,2304]{1,0:T(2,128)(2,1)} %get-tuple-element.526.dtb_ref, ...), custom_call_target="tpu_custom_call" | custom-call | flops 301989888 | bytes 150994944 | tf_op jit(solution)/shard_map/end/pallas_call | solution.py:336
  270.5 22.9 %collective-permute-done.4.refs_2_ = bf16[4,384,1152]{2,1,0:T(8,128)(2,1)} collective-permute-done((bf16[4,384,1152]{2,1,0:T(8,128)(2,1)}, bf16[4,384,1152]{2,1,0:T(8,128)(2,1)}, u32[]{:S(2)}, u32[]{:S(2)}) %collective-permute-start.4) | collective-permute-done | bytes 3538976 | tf_op jit(solution)/shard_map/ppermute | solution.py:630
  298.7 11.3 fusion.22.z_ref
  313.4 6.2 collective-permute-done.10
  327.8 5.8 copy.241
  333.7 7.0 slice.578
  346.7 53.4 %out.1 = (bf16[1024,2304]{1,0:T(8,128)(2,1)}, bf16[1024,2304]{1,0:T(8,128)(2,1)}, f32[8,16,8,2304]{3,2,1,0:T(8,128)}) custom-call(bf16[1024,2304]{1,0:T(8,128)(2,1)} %copy-done.3, f32[1024,2304]{1,0:T(8,128)} %get-tuple-element.198.delta_ref, bf16[16,2304]{1,0:T(8,128)(2,1)} %slice.766.alog_ref, f32[1024,32]{1,0:T(8,128)} %copy.310.bc_ref, ...), custom_call_target="tpu_custom_call" | custom-call | flops 301989888 | bytes 188743680 | tf_op jit(solution)/shard_map/out/pallas_call | solution.py:355
  400.2 10.7 multiply_reduce_fusion.4
  414.5 8.8 collective-permute-done.12.refs_3_
  436.8 22.0 %collective-permute-done.15.refs_10_ = bf16[2,192,1280]{2,1,0:T(8,128)(2,1)S(1)} collective-permute-done((bf16[2,192,1280]{2,1,0:T(8,128)(2,1)S(1)}, bf16[2,192,1280]{2,1,0:T(8,128)(2,1)S(1)}, u32[]{:S(2)}, u32[]{:S(2)}) %collective-permute-start.15) | collective-permute-done | bytes 983072 | tf_op jit(solution)/shard_map/ppermute | solution.py:635
  458.8 20.3 %collective-permute-done.16.refs_11_ = bf16[2,192,1280]{2,1,0:T(8,128)(2,1)S(1)} collective-permute-done((bf16[2,192,1280]{2,1,0:T(8,128)(2,1)S(1)}, bf16[2,192,1280]{2,1,0:T(8,128)(2,1)S(1)}, u32[]{:S(2)}, u32[]{:S(2)}) %collective-permute-start.16) | collective-permute-done | bytes 983072 | tf_op jit(solution)/shard_map/ppermute | solution.py:635
  482.3 40.3 %expert.3 = (bf16[768,2304]{1,0:T(8,128)(2,1)}, bf16[768,1152]{1,0:T(8,128)(2,1)}, bf16[768,1152]{1,0:T(8,128)(2,1)}, bf16[768,3072]{1,0:T(8,128)(2,1)}, bf16[768,3072]{1,0:T(8,128)(2,1)}) custom-call(bf16[4,384,1152]{2,1,0:T(8,128)(2,1)} %pad_maximum_fusion.2.refs_0_, bf16[4,384,1152]{2,1,0:T(8,128)(2,1)} %collective-permute-done.1.refs_1_, ...), custom_call_target="tpu_custom_call" | custom-call | flops 1000 | bytes 1000 | tf_op jit(solution)/shard_map/expert/pallas_call | solution.py:553
  528.0 40.2 %expert.2 = (bf16[768,2304]{1,0:T(8,128)(2,1)}, bf16[768,1152]{1,0:T(8,128)(2,1)}, bf16[768,1152]{1,0:T(8,128)(2,1)}, bf16[768,3072]{1,0:T(8,128)(2,1)}, bf16[768,3072]{1,0:T(8,128)(2,1)}) custom-call(bf16[4,384,1152]{2,1,0:T(8,128)(2,1)} %pad_maximum_fusion.2.refs_0_, bf16[4,384,1152]{2,1,0:T(8,128)(2,1)} %collective-permute-done.1.refs_1_, ...), custom_call_target="tpu_custom_call" | custom-call | flops 1000 | bytes 1000 | tf_op jit(solution)/shard_map/expert/pallas_call | solution.py:553
  574.8 18.5 %weight.2 = (bf16[3072,1152]{1,0:T(8,128)(2,1)}, bf16[3072,1152]{1,0:T(8,128)(2,1)}) custom-call(bf16[768,3072]{1,0:T(8,128)(2,1)} %get-tuple-element.244.hid_ref, bf16[768,3072]{1,0:T(8,128)(2,1)} %get-tuple-element.245.pre_ref, bf16[768,1152]{1,0:T(8,128)(2,1)} %get-tuple-element.246.x_ref, bf16[768,1152]{1,0:T(8,128)(2,1)} %get-tuple-element.247.g_ref), custom_call_target="tpu_custom_call" | custom-call | flops 1000 | bytes 1000 | tf_op jit(solution)/shard_map/weight/pallas_call | solution.py:578
  593.3 18.5 %weight.3 = (bf16[3072,1152]{1,0:T(8,128)(2,1)}, bf16[3072,1152]{1,0:T(8,128)(2,1)}) custom-call(bf16[768,3072]{1,0:T(8,128)(2,1)} %get-tuple-element.250.hid_ref, bf16[768,3072]{1,0:T(8,128)(2,1)} %get-tuple-element.251.pre_ref, bf16[768,1152]{1,0:T(8,128)(2,1)} %get-tuple-element.252.x_ref, bf16[768,1152]{1,0:T(8,128)(2,1)} %get-tuple-element.253.g_ref), custom_call_target="tpu_custom_call" | custom-call | flops 1000 | bytes 1000 | tf_op jit(solution)/shard_map/weight/pallas_call | solution.py:578
  619.0 7.8 fusion.8
  651.9 25.1 %collective-permute-done.25 = bf16[2,384,1152]{2,1,0:T(8,128)(2,1)S(1)} collective-permute-done((bf16[2,384,1152]{2,1,0:T(8,128)(2,1)S(1)}, bf16[2,384,1152]{2,1,0:T(8,128)(2,1)S(1)}, u32[]{:S(2)}, u32[]{:S(2)}) %collective-permute-start.25) | collective-permute-done | bytes 1769504 | tf_op jit(solution)/shard_map/ppermute | solution.py:630
  678.3 9.8 fusion.53
  695.7 11.2 fusion.55.gb_ref
  706.9 15.0 %collective-permute-done.26 = bf16[4,384,1152]{2,1,0:T(8,128)(2,1)} collective-permute-done((bf16[4,384,1152]{2,1,0:T(8,128)(2,1)}, bf16[4,384,1152]{2,1,0:T(8,128)(2,1)}, u32[]{:S(2)}, u32[]{:S(2)}) %collective-permute-start.26) | collective-permute-done | bytes 3538976 | tf_op jit(solution)/shard_map/ppermute | solution.py:630
  724.6 38.1 %first.1 = (f32[16,8,2304]{2,1,0:T(8,128)}, bf16[1024,2304]{1,0:T(8,128)(2,1)}, f32[1024,2304]{1,0:T(8,128)}) custom-call(f32[1024,2304]{1,0:T(8,128)} %get-tuple-element.198.delta_ref, bf16[16,2304]{1,0:T(8,128)(2,1)} %slice.766.alog_ref, f32[1024,32]{1,0:T(8,128)} %copy.310.bc_ref, f32[1024,128]{1,0:T(8,128)} %broadcast_in_dim.18.cut_ref, ...), custom_call_target="tpu_custom_call" | custom-call | flops 301989888 | bytes 150994944 | tf_op jit(solution)/shard_map/first/pallas_call | solution.py:378
  762.8 34.6 %collective-permute-done.28 = bf16[4,384,1152]{2,1,0:T(8,128)(2,1)} collective-permute-done((bf16[4,384,1152]{2,1,0:T(8,128)(2,1)}, bf16[4,384,1152]{2,1,0:T(8,128)(2,1)}, u32[]{:S(2)}, u32[]{:S(2)}) %collective-permute-start.28) | collective-permute-done | bytes 3538976 | tf_op jit(solution)/shard_map/ppermute | solution.py:630
  804.5 9.7 fusion.20
  816.2 11.0 fusion.143
  829.5 10.1 collective-permute-done.32
  861.7 69.2 %back.3 = (f32[1024,768]{1,0:T(8,128)}, bf16[1024,768]{1,0:T(8,128)(2,1)}, f32[16,768]{1,0:T(8,128)}, f32[8,768]{1,0:T(8,128)}, f32[1024,128]{1,0:T(8,128)}) custom-call(bf16[1024,2304]{1,0:T(8,128)(2,1)} %copy-done.3, f32[1024,2304]{1,0:T(8,128)} %get-tuple-element.198.delta_ref, bf16[16,2304]{1,0:T(8,128)(2,1)} %slice.766.alog_ref, ...), custom_call_target="tpu_custom_call" | custom-call | flops 100663296 | bytes 213909504 | tf_op jit(solution)/shard_map/back/pallas_call | solution.py:405
  936.2 46.0 %reduce-scatter.7.cloned.1.call-done = bf16[72,1152]{1,0:T(8,128)(2,1)} async-done(((bf16[2304,1152]{1,0:T(8,128)(2,1)}), bf16[72,1152]{1,0:T(8,128)(2,1)}) %reduce-scatter.7.cloned.1.call-update) | async-done | bytes 165904 | tf_op jit(solution)/shard_map/optimization_barrier | solution.py:640
  1004.2 5.9 reshape.638
  1015.0 69.0 %back.4 = (f32[1024,768]{1,0:T(8,128)}, bf16[1024,768]{1,0:T(8,128)(2,1)}, f32[16,768]{1,0:T(8,128)}, f32[8,768]{1,0:T(8,128)}, f32[1024,128]{1,0:T(8,128)}) custom-call(bf16[1024,2304]{1,0:T(8,128)(2,1)} %copy-done.3, f32[1024,2304]{1,0:T(8,128)} %get-tuple-element.198.delta_ref, bf16[16,2304]{1,0:T(8,128)(2,1)} %slice.766.alog_ref, ...), custom_call_target="tpu_custom_call" | custom-call | flops 100663296 | bytes 213909504 | tf_op jit(solution)/shard_map/back/pallas_call | solution.py:405
  1088.5 69.0 %back.5 = (f32[1024,768]{1,0:T(8,128)}, bf16[1024,768]{1,0:T(8,128)(2,1)}, f32[16,768]{1,0:T(8,128)}, f32[8,768]{1,0:T(8,128)}, f32[1024,128]{1,0:T(8,128)}) custom-call(bf16[1024,2304]{1,0:T(8,128)(2,1)} %copy-done.3, f32[1024,2304]{1,0:T(8,128)} %get-tuple-element.198.delta_ref, bf16[16,2304]{1,0:T(8,128)(2,1)} %slice.766.alog_ref, ...), custom_call_target="tpu_custom_call" | custom-call | flops 100663296 | bytes 213909504 | tf_op jit(solution)/shard_map/back/pallas_call | solution.py:405
  1175.4 10.5 collective-permute-done.41
  1186.9 13.5 collective-permute-done.42
  1216.2 8.8 conv.5
  1225.0 8.8 conv.4
  1233.8 6.1 fusion.145
  1239.9 8.9 conv.3
  1274.2 5.3 copy.301
  1303.0 23.6 %collective-permute-done.51 = bf16[2,2,2,72,256]{4,3,2,1,0:T(8,128)(2,1)S(1)} collective-permute-done((bf16[2,2,2,72,256]{4,3,2,1,0:T(8,128)(2,1)S(1)}, bf16[2,2,2,72,256]{4,3,2,1,0:T(8,128)(2,1)S(1)}, u32[]{:S(2)}, u32[]{:S(2)}) %collective-permute-start.51) | collective-permute-done | bytes 294944 | tf_op jit(solution)/shard_map/ppermute | solution.py:635
  1339.4 6.6 multiply_reduce_fusion.1
  1350.6 6.7 reshape.647
  1357.3 5.5 copy.294
  (620 shorter events, 373.7 us)
Async XLA Ops:
  7.2 176.1 %all-gather.6.cloned.1.call-start = ((), (), s32[]{:S(2)}) async-start(), calls=%async_computation.4 | async-start | bytes 12165120 | tf_op jit(solution)/shard_map/all_gather | solution.py:789
  14.6 385.6 %all-gather.4.cloned.1.call-start = ((), (), s32[]{:S(2)}) async-start(), calls=%async_computation.2 | async-start | bytes 5474304 | tf_op jit(solution)/shard_map/all_gather | solution.py:794
  21.8 171.7 %collective-permute-start.1 = (bf16[4,384,1152]{2,1,0:T(8,128)(2,1)}, bf16[4,384,1152]{2,1,0:T(8,128)(2,1)}, u32[]{:S(2)}, u32[]{:S(2)}) collective-permute-start(bf16[4,384,1152]{2,1,0:T(8,128)(2,1)} %pad_maximum_fusion.2.refs_0_), channel_id=1, source_target_pairs={{0,4},{4,8},{8,12},{12,0},{1,5},{5,9},{9,13},{13,1},{2,6},{6,10},{... | collective-permute-start | bytes 10616840 | tf_op jit(solution)/shard_map/ppermute | solution.py:630
  24.8 168.7 %collective-permute-start.2 = (bf16[4,384,1152]{2,1,0:T(8,128)(2,1)}, bf16[4,384,1152]{2,1,0:T(8,128)(2,1)}, u32[]{:S(2)}, u32[]{:S(2)}) collective-permute-start(bf16[4,384,1152]{2,1,0:T(8,128)(2,1)} %pad_maximum_fusion.2.refs_0_), channel_id=1, source_target_pairs={{0,16},{16,0},{1,17},{17,1},{2,18},{18,2},{3,19},{19,3},{4,20},{20... | collective-permute-start | bytes 10616840 | tf_op jit(solution)/shard_map/ppermute | solution.py:630
  27.2 132.8 %collective-permute-start = (bf16[4,3,1152]{2,1,0:T(4,128)(2,1)S(1)}, bf16[4,3,1152]{2,1,0:T(4,128)(2,1)S(1)}, u32[]{:S(2)}, u32[]{:S(2)}) collective-permute-start(bf16[4,3,1152]{2,1,0:T(4,128)(2,1)S(1)} %slice.574), channel_id=1, source_target_pairs={{0,4},{4,8},{8,12},{1,5},{5,9},{9,13},{2,6},{6,10},{10,14},{3,7},{... | collective-permute-start | bytes 82952 | tf_op jit(solution)/shard_map/ppermute | solution.py:34
  30.8 125.6 %collective-permute-start.3 = (f32[4,3]{1,0:T(4,128)S(1)}, f32[4,3]{1,0:T(4,128)S(1)}, u32[]{:S(2)}, u32[]{:S(2)}) collective-permute-start(f32[4,3]{1,0:T(4,128)S(1)} %slice_convert_fusion.4), channel_id=1, source_target_pairs={{0,4},{4,8},{8,12},{1,5},{5,9},{9,13},{2,6},{6,10},{10,14},{3,7},{... | collective-permute-start | bytes 152 | tf_op jit(solution)/shard_map/ppermute | solution.py:34
  50.7 242.7 %collective-permute-start.6 = (bf16[2,192,1152]{2,1,0:T(8,128)(2,1)}, bf16[2,192,1152]{2,1,0:T(8,128)(2,1)S(1)}, u32[]{:S(2)}, u32[]{:S(2)}) collective-permute-start(bf16[2,192,1152]{2,1,0:T(8,128)(2,1)} %bitcast.28), channel_id=1, source_target_pairs={{0,1},{1,0},{2,3},{3,2},{4,5},{5,4},{6,7},{7,6},{8,9},{9,8},{10,11... | collective-permute-start | bytes 2654216 | tf_op jit(solution)/shard_map/ppermute | solution.py:635
  50.7 931.5 %reduce-scatter.7.cloned.1.call-start = ((), (), s32[]{:S(2)}) async-start(), calls=%async_computation.5 | async-start | bytes 5474304
  156.4 137.0 %collective-permute-start.7 = (bf16[2,192,1152]{2,1,0:T(8,128)(2,1)}, bf16[2,192,1152]{2,1,0:T(8,128)(2,1)}, u32[]{:S(2)}, u32[]{:S(2)}) collective-permute-start(bf16[2,192,1152]{2,1,0:T(8,128)(2,1)} %bitcast.437), channel_id=1, source_target_pairs={{0,2},{1,3},{2,0},{3,1},{4,6},{5,7},{6,4},{7,5},{8,10},{9,11},{10,... | collective-permute-start | bytes 2654216 | tf_op jit(solution)/shard_map/ppermute | solution.py:635
  160.0 133.4 %collective-permute-start.8 = (bf16[2,192,1152]{2,1,0:T(8,128)(2,1)}, bf16[2,192,1152]{2,1,0:T(8,128)(2,1)}, u32[]{:S(2)}, u32[]{:S(2)}) collective-permute-start(bf16[2,192,1152]{2,1,0:T(8,128)(2,1)} %bitcast.436), channel_id=1, source_target_pairs={{0,3},{1,2},{2,1},{3,0},{4,7},{5,6},{6,5},{7,4},{8,11},{9,10},{10,... | collective-permute-start | bytes 2654216 | tf_op jit(solution)/shard_map/ppermute | solution.py:635
  193.5 99.9 %collective-permute-start.4 = (bf16[4,384,1152]{2,1,0:T(8,128)(2,1)}, bf16[4,384,1152]{2,1,0:T(8,128)(2,1)}, u32[]{:S(2)}, u32[]{:S(2)}) collective-permute-start(bf16[4,384,1152]{2,1,0:T(8,128)(2,1)} %collective-permute-done.1.refs_1_), channel_id=1, source_target_pairs={{0,4},{4,8},{8,12},{12,0},{1,5},{5,9},{9,13},{13,1},{2,6},{6,10},{... | collective-permute-start | bytes 10616840 | tf_op jit(solution)/shard_map/ppermute | solution.py:630
  196.4 97.0 %collective-permute-start.5 = (bf16[4,384,1152]{2,1,0:T(8,128)(2,1)}, bf16[4,384,1152]{2,1,0:T(8,128)(2,1)}, u32[]{:S(2)}, u32[]{:S(2)}) collective-permute-start(bf16[4,384,1152]{2,1,0:T(8,128)(2,1)} %collective-permute-done.1.refs_1_), channel_id=1, source_target_pairs={{0,16},{16,0},{1,17},{17,1},{2,18},{18,2},{3,19},{19,3},{4,20},{20... | collective-permute-start | bytes 10616840 | tf_op jit(solution)/shard_map/ppermute | solution.py:630
  344.1 79.2 %collective-permute-start.12 = (bf16[4,384,1152]{2,1,0:T(8,128)(2,1)}, bf16[4,384,1152]{2,1,0:T(8,128)(2,1)}, u32[]{:S(2)}, u32[]{:S(2)}) collective-permute-start(bf16[4,384,1152]{2,1,0:T(8,128)(2,1)} %collective-permute-done.4.refs_2_), channel_id=1, source_target_pairs={{0,4},{4,8},{8,12},{12,0},{1,5},{5,9},{9,13},{13,1},{2,6},{6,10},{... | collective-permute-start | bytes 10616840 | tf_op jit(solution)/shard_map/ppermute | solution.py:630
  345.3 78.0 %collective-permute-start.13 = (bf16[4,384,1152]{2,1,0:T(8,128)(2,1)}, bf16[4,384,1152]{2,1,0:T(8,128)(2,1)}, u32[]{:S(2)}, u32[]{:S(2)}) collective-permute-start(bf16[4,384,1152]{2,1,0:T(8,128)(2,1)} %collective-permute-done.4.refs_2_), channel_id=1, source_target_pairs={{0,16},{16,0},{1,17},{17,1},{2,18},{18,2},{3,19},{19,3},{4,20},{20... | collective-permute-start | bytes 10616840 | tf_op jit(solution)/shard_map/ppermute | solution.py:630
  424.9 54.2 %collective-permute-start.17 = (bf16[2,384,1152]{2,1,0:T(8,128)(2,1)S(1)}, bf16[2,384,1152]{2,1,0:T(8,128)(2,1)S(1)}, u32[]{:S(2)}, u32[]{:S(2)}) collective-permute-start(bf16[2,384,1152]{2,1,0:T(8,128)(2,1)S(1)} %slice.624), channel_id=1, source_target_pairs={{0,16},{16,0},{1,17},{17,1},{2,18},{18,2},{3,19},{19,3},{4,20},{20... | collective-permute-start | bytes 5308424 | tf_op jit(solution)/shard_map/ppermute | solution.py:630
  428.0 51.0 %collective-permute-start.18 = (bf16[2,384,1152]{2,1,0:T(8,128)(2,1)S(1)}, bf16[2,384,1152]{2,1,0:T(8,128)(2,1)S(1)}, u32[]{:S(2)}, u32[]{:S(2)}) collective-permute-start(bf16[2,384,1152]{2,1,0:T(8,128)(2,1)S(1)} %slice.625), channel_id=1, source_target_pairs={{0,4},{4,8},{8,12},{12,0},{1,5},{5,9},{9,13},{13,1},{2,6},{6,10},{... | collective-permute-start | bytes 5308424 | tf_op jit(solution)/shard_map/ppermute | solution.py:630
  434.2 24.6 %collective-permute-start.15 = (bf16[2,192,1280]{2,1,0:T(8,128)(2,1)S(1)}, bf16[2,192,1280]{2,1,0:T(8,128)(2,1)S(1)}, u32[]{:S(2)}, u32[]{:S(2)}) collective-permute-start(bf16[2,192,1280]{2,1,0:T(8,128)(2,1)S(1)} %bitcast.427), channel_id=1, source_target_pairs={{0,2},{1,3},{2,0},{3,1},{4,6},{5,7},{6,4},{7,5},{8,10},{9,11},{10,... | collective-permute-start | bytes 2949128 | tf_op jit(solution)/shard_map/ppermute | solution.py:635
  434.9 44.2 %collective-permute-start.16 = (bf16[2,192,1280]{2,1,0:T(8,128)(2,1)S(1)}, bf16[2,192,1280]{2,1,0:T(8,128)(2,1)S(1)}, u32[]{:S(2)}, u32[]{:S(2)}) collective-permute-start(bf16[2,192,1280]{2,1,0:T(8,128)(2,1)S(1)} %bitcast.426), channel_id=1, source_target_pairs={{0,3},{1,2},{2,1},{3,0},{4,7},{5,6},{6,5},{7,4},{8,11},{9,10},{10,... | collective-permute-start | bytes 2949128 | tf_op jit(solution)/shard_map/ppermute | solution.py:635
  526.1 42.1 %collective-permute-start.19 = (bf16[192,2304]{1,0:T(8,128)(2,1)}, bf16[192,2304]{1,0:T(8,128)(2,1)S(1)}, u32[]{:S(2)}, u32[]{:S(2)}) collective-permute-start(bf16[192,2304]{1,0:T(8,128)(2,1)} %get-tuple-element.500), channel_id=1, source_target_pairs={{0,1},{1,0},{2,3},{3,2},{4,5},{5,4},{6,7},{7,6},{8,9},{9,8},{10,11... | collective-permute-start | bytes 2654216 | tf_op jit(solution)/shard_map/ppermute | solution.py:635
  526.3 41.9 %collective-permute-start.20 = (bf16[192,2304]{1,0:T(8,128)(2,1)}, bf16[192,2304]{1,0:T(8,128)(2,1)S(1)}, u32[]{:S(2)}, u32[]{:S(2)}) collective-permute-start(bf16[192,2304]{1,0:T(8,128)(2,1)} %get-tuple-element.499), channel_id=1, source_target_pairs={{0,2},{1,3},{2,0},{3,1},{4,6},{5,7},{6,4},{7,5},{8,10},{9,11},{10,... | collective-permute-start | bytes 2654216 | tf_op jit(solution)/shard_map/ppermute | solution.py:635
  527.0 41.3 %collective-permute-start.21 = (bf16[192,2304]{1,0:T(8,128)(2,1)}, bf16[192,2304]{1,0:T(8,128)(2,1)}, u32[]{:S(2)}, u32[]{:S(2)}) collective-permute-start(bf16[192,2304]{1,0:T(8,128)(2,1)} %get-tuple-element.498), channel_id=1, source_target_pairs={{0,3},{1,2},{2,1},{3,0},{4,7},{5,6},{6,5},{7,4},{8,11},{9,10},{10,... | collective-permute-start | bytes 2654216 | tf_op jit(solution)/shard_map/ppermute | solution.py:635
  572.7 39.1 %collective-permute-start.22 = (bf16[192,2304]{1,0:T(8,128)(2,1)}, bf16[192,2304]{1,0:T(8,128)(2,1)}, u32[]{:S(2)}, u32[]{:S(2)}) collective-permute-start(bf16[192,2304]{1,0:T(8,128)(2,1)} %get-tuple-element.496), channel_id=1, source_target_pairs={{0,1},{1,0},{2,3},{3,2},{4,5},{5,4},{6,7},{7,6},{8,9},{9,8},{10,11... | collective-permute-start | bytes 2654216 | tf_op jit(solution)/shard_map/ppermute | solution.py:635
  573.2 38.6 %collective-permute-start.23 = (bf16[192,2304]{1,0:T(8,128)(2,1)}, bf16[192,2304]{1,0:T(8,128)(2,1)}, u32[]{:S(2)}, u32[]{:S(2)}) collective-permute-start(bf16[192,2304]{1,0:T(8,128)(2,1)} %get-tuple-element.495), channel_id=1, source_target_pairs={{0,2},{1,3},{2,0},{3,1},{4,6},{5,7},{6,4},{7,5},{8,10},{9,11},{10,... | collective-permute-start | bytes 2654216 | tf_op jit(solution)/shard_map/ppermute | solution.py:635
  573.8 39.3 %collective-permute-start.24 = (bf16[192,2304]{1,0:T(8,128)(2,1)}, bf16[192,2304]{1,0:T(8,128)(2,1)}, u32[]{:S(2)}, u32[]{:S(2)}) collective-permute-start(bf16[192,2304]{1,0:T(8,128)(2,1)} %get-tuple-element.494), channel_id=1, source_target_pairs={{0,3},{1,2},{2,1},{3,0},{4,7},{5,6},{6,5},{7,4},{8,11},{9,10},{10,... | collective-permute-start | bytes 2654216 | tf_op jit(solution)/shard_map/ppermute | solution.py:635
  634.2 42.8 %collective-permute-start.25 = (bf16[2,384,1152]{2,1,0:T(8,128)(2,1)S(1)}, bf16[2,384,1152]{2,1,0:T(8,128)(2,1)S(1)}, u32[]{:S(2)}, u32[]{:S(2)}) collective-permute-start(bf16[2,384,1152]{2,1,0:T(8,128)(2,1)S(1)} %pad_maximum_fusion.6), channel_id=1, source_target_pairs={{0,12},{4,0},{8,4},{12,8},{1,13},{5,1},{9,5},{13,9},{2,14},{6,2},{... | collective-permute-start | bytes 5308424 | tf_op jit(solution)/shard_map/ppermute | solution.py:630
  642.3 79.6 %collective-permute-start.26 = (bf16[4,384,1152]{2,1,0:T(8,128)(2,1)}, bf16[4,384,1152]{2,1,0:T(8,128)(2,1)}, u32[]{:S(2)}, u32[]{:S(2)}) collective-permute-start(bf16[4,384,1152]{2,1,0:T(8,128)(2,1)} %bitcast.59), channel_id=1, source_target_pairs={{0,16},{16,0},{1,17},{17,1},{2,18},{18,2},{3,19},{19,3},{4,20},{20... | collective-permute-start | bytes 10616840 | tf_op jit(solution)/shard_map/ppermute | solution.py:630
  646.9 150.4 %collective-permute-start.28 = (bf16[4,384,1152]{2,1,0:T(8,128)(2,1)}, bf16[4,384,1152]{2,1,0:T(8,128)(2,1)}, u32[]{:S(2)}, u32[]{:S(2)}) collective-permute-start(bf16[4,384,1152]{2,1,0:T(8,128)(2,1)} %bitcast.61), channel_id=1, source_target_pairs={{0,16},{16,0},{1,17},{17,1},{2,18},{18,2},{3,19},{19,3},{4,20},{20... | collective-permute-start | bytes 10616840 | tf_op jit(solution)/shard_map/ppermute | solution.py:630
  691.4 106.0 %collective-permute-start.29 = (bf16[2,384,1152]{2,1,0:T(8,128)(2,1)}, bf16[2,384,1152]{2,1,0:T(8,128)(2,1)S(1)}, u32[]{:S(2)}, u32[]{:S(2)}) collective-permute-start(bf16[2,384,1152]{2,1,0:T(8,128)(2,1)} %add_convert_fusion.2), channel_id=1, source_target_pairs={{0,12},{4,0},{8,4},{12,8},{1,13},{5,1},{9,5},{13,9},{2,14},{6,2},{... | collective-permute-start | bytes 5308424 | tf_op jit(solution)/shard_map/ppermute | solution.py:630
  724.5 72.8 %collective-permute-start.27 = (bf16[384,1152]{1,0:T(8,128)(2,1)}, bf16[384,1152]{1,0:T(8,128)(2,1)S(1)}, u32[]{:S(2)}, u32[]{:S(2)}) collective-permute-start(bf16[384,1152]{1,0:T(8,128)(2,1)} %fusion.46), channel_id=1, source_target_pairs={{0,12},{4,0},{8,4},{12,8},{1,13},{5,1},{9,5},{13,9},{2,14},{6,2},{... | collective-permute-start | bytes 2654216 | tf_op jit(solution)/shard_map/ppermute | solution.py:630
  843.8 357.5 %reduce-scatter.5.cloned.1.call-start = ((), (), s32[]{:S(2)}) async-start(), calls=%async_computation.3 | async-start | bytes 5640192 | tf_op jit(solution)/shard_map/reduce_scatter | solution.py:930
  848.1 134.1 %collective-permute-start.35 = (bf16[4,384,1152]{2,1,0:T(8,128)(2,1)}, bf16[4,384,1152]{2,1,0:T(8,128)(2,1)}, u32[]{:S(2)}, u32[]{:S(2)}) collective-permute-start(bf16[4,384,1152]{2,1,0:T(8,128)(2,1)} %bitcast.69), channel_id=1, source_target_pairs={{0,16},{16,0},{1,17},{17,1},{2,18},{18,2},{3,19},{19,3},{4,20},{20... | collective-permute-start | bytes 10616840 | tf_op jit(solution)/shard_map/ppermute | solution.py:630
  850.3 131.9 %collective-permute-start.36 = (bf16[2,384,1152]{2,1,0:T(8,128)(2,1)}, bf16[2,384,1152]{2,1,0:T(8,128)(2,1)}, u32[]{:S(2)}, u32[]{:S(2)}) collective-permute-start(bf16[2,384,1152]{2,1,0:T(8,128)(2,1)} %add_convert_fusion.1), channel_id=1, source_target_pairs={{0,12},{4,0},{8,4},{12,8},{1,13},{5,1},{9,5},{13,9},{2,14},{6,2},{... | collective-permute-start | bytes 5308424 | tf_op jit(solution)/shard_map/ppermute | solution.py:630
  854.9 127.2 %collective-permute-start.33 = (bf16[384,1152]{1,0:T(8,128)(2,1)}, bf16[384,1152]{1,0:T(8,128)(2,1)}, u32[]{:S(2)}, u32[]{:S(2)}) collective-permute-start(bf16[384,1152]{1,0:T(8,128)(2,1)} %fusion.45), channel_id=1, source_target_pairs={{0,12},{4,0},{8,4},{12,8},{1,13},{5,1},{9,5},{13,9},{2,14},{6,2},{... | collective-permute-start | bytes 2654216 | tf_op jit(solution)/shard_map/ppermute | solution.py:630
  860.0 122.1 %collective-permute-start.34 = (bf16[384,1152]{1,0:T(8,128)(2,1)}, bf16[384,1152]{1,0:T(8,128)(2,1)S(1)}, u32[]{:S(2)}, u32[]{:S(2)}) collective-permute-start(bf16[384,1152]{1,0:T(8,128)(2,1)} %fusion.43), channel_id=1, source_target_pairs={{0,12},{4,0},{8,4},{12,8},{1,13},{5,1},{9,5},{13,9},{2,14},{6,2},{... | collective-permute-start | bytes 2654216 | tf_op jit(solution)/shard_map/ppermute | solution.py:630
  986.0 102.5 %collective-permute-start.37 = (bf16[384,1152]{1,0:T(8,128)(2,1)}, bf16[384,1152]{1,0:T(8,128)(2,1)}, u32[]{:S(2)}, u32[]{:S(2)}) collective-permute-start(bf16[384,1152]{1,0:T(8,128)(2,1)} %fusion.42), channel_id=1, source_target_pairs={{0,12},{4,0},{8,4},{12,8},{1,13},{5,1},{9,5},{13,9},{2,14},{6,2},{... | collective-permute-start | bytes 2654216 | tf_op jit(solution)/shard_map/ppermute | solution.py:630
  991.2 97.3 %collective-permute-start.38 = (bf16[384,1152]{1,0:T(8,128)(2,1)}, bf16[384,1152]{1,0:T(8,128)(2,1)}, u32[]{:S(2)}, u32[]{:S(2)}) collective-permute-start(bf16[384,1152]{1,0:T(8,128)(2,1)} %fusion.40), channel_id=1, source_target_pairs={{0,12},{4,0},{8,4},{12,8},{1,13},{5,1},{9,5},{13,9},{2,14},{6,2},{... | collective-permute-start | bytes 2654216 | tf_op jit(solution)/shard_map/ppermute | solution.py:630
  994.7 93.8 %collective-permute-start.39 = (bf16[384,1152]{1,0:T(8,128)(2,1)}, bf16[384,1152]{1,0:T(8,128)(2,1)}, u32[]{:S(2)}, u32[]{:S(2)}) collective-permute-start(bf16[384,1152]{1,0:T(8,128)(2,1)} %fusion.38), channel_id=1, source_target_pairs={{0,12},{4,0},{8,4},{12,8},{1,13},{5,1},{9,5},{13,9},{2,14},{6,2},{... | collective-permute-start | bytes 2654216 | tf_op jit(solution)/shard_map/ppermute | solution.py:630
  1001.0 87.5 %collective-permute-start.40 = (bf16[384,1152]{1,0:T(8,128)(2,1)}, bf16[384,1152]{1,0:T(8,128)(2,1)}, u32[]{:S(2)}, u32[]{:S(2)}) collective-permute-start(bf16[384,1152]{1,0:T(8,128)(2,1)} %fusion.59), channel_id=1, source_target_pairs={{0,16},{16,0},{1,17},{17,1},{2,18},{18,2},{3,19},{19,3},{4,20},{20... | collective-permute-start | bytes 2654216 | tf_op jit(solution)/shard_map/ppermute | solution.py:630
  1166.0 34.4 %collective-permute-start.42 = (bf16[384,1152]{1,0:T(8,128)(2,1)S(1)}, bf16[384,1152]{1,0:T(8,128)(2,1)S(1)}, u32[]{:S(2)}, u32[]{:S(2)}) collective-permute-start(bf16[384,1152]{1,0:T(8,128)(2,1)S(1)} %fusion.35), channel_id=1, source_target_pairs={{0,12},{4,0},{8,4},{12,8},{1,13},{5,1},{9,5},{13,9},{2,14},{6,2},{... | collective-permute-start | bytes 2654216 | tf_op jit(solution)/shard_map/ppermute | solution.py:630
  1211.8 48.0 %collective-permute-start.43 = (bf16[384,1152]{1,0:T(8,128)(2,1)}, bf16[384,1152]{1,0:T(8,128)(2,1)}, u32[]{:S(2)}, u32[]{:S(2)}) collective-permute-start(bf16[384,1152]{1,0:T(8,128)(2,1)} %fusion.33), channel_id=1, source_target_pairs={{0,12},{4,0},{8,4},{12,8},{1,13},{5,1},{9,5},{13,9},{2,14},{6,2},{... | collective-permute-start | bytes 2654216 | tf_op jit(solution)/shard_map/ppermute | solution.py:630
  1251.3 28.1 %collective-permute-start.47 = (bf16[2,2,2,2,72,256]{5,4,3,2,1,0:T(8,128)(2,1)}, bf16[2,2,2,2,72,256]{5,4,3,2,1,0:T(8,128)(2,1)}, u32[]{:S(2)}, u32[]{:S(2)}) collective-permute-start(bf16[2,2,2,2,72,256]{5,4,3,2,1,0:T(8,128)(2,1)} %fusion.67), channel_id=1, source_target_pairs={{0,1},{1,0},{2,3},{3,2},{4,5},{5,4},{6,7},{7,6},{8,9},{9,8},{10,11... | collective-permute-start | bytes 1769480 | tf_op jit(solution)/shard_map/ppermute | solution.py:635
  1289.0 37.6 %collective-permute-start.48 = (bf16[2,2,144,384]{3,2,1,0:T(8,128)(2,1)S(1)}, bf16[2,2,144,384]{3,2,1,0:T(8,128)(2,1)S(1)}, u32[]{:S(2)}, u32[]{:S(2)}) collective-permute-start(bf16[2,2,144,384]{3,2,1,0:T(8,128)(2,1)S(1)} %fusion.71), channel_id=1, source_target_pairs={{0,2},{1,3},{2,0},{3,1},{4,6},{5,7},{6,4},{7,5},{8,10},{9,11},{10,... | collective-permute-start | bytes 1327112 | tf_op jit(solution)/shard_map/ppermute | solution.py:635
  1291.9 34.7 %collective-permute-start.49 = (bf16[2,2,144,384]{3,2,1,0:T(8,128)(2,1)S(1)}, bf16[2,2,144,384]{3,2,1,0:T(8,128)(2,1)}, u32[]{:S(2)}, u32[]{:S(2)}) collective-permute-start(bf16[2,2,144,384]{3,2,1,0:T(8,128)(2,1)S(1)} %fusion.72), channel_id=1, source_target_pairs={{0,2},{1,3},{2,0},{3,1},{4,6},{5,7},{6,4},{7,5},{8,10},{9,11},{10,... | collective-permute-start | bytes 1327112 | tf_op jit(solution)/shard_map/ppermute | solution.py:635
  1294.3 33.0 %collective-permute-start.50 = (bf16[2,2,144,384]{3,2,1,0:T(8,128)(2,1)S(1)}, bf16[2,2,144,384]{3,2,1,0:T(8,128)(2,1)}, u32[]{:S(2)}, u32[]{:S(2)}) collective-permute-start(bf16[2,2,144,384]{3,2,1,0:T(8,128)(2,1)S(1)} %fusion.73), channel_id=1, source_target_pairs={{0,2},{1,3},{2,0},{3,1},{4,6},{5,7},{6,4},{7,5},{8,10},{9,11},{10,... | collective-permute-start | bytes 1327112 | tf_op jit(solution)/shard_map/ppermute | solution.py:635
  1298.0 28.6 %collective-permute-start.51 = (bf16[2,2,2,72,256]{4,3,2,1,0:T(8,128)(2,1)S(1)}, bf16[2,2,2,72,256]{4,3,2,1,0:T(8,128)(2,1)S(1)}, u32[]{:S(2)}, u32[]{:S(2)}) collective-permute-start(bf16[2,2,2,72,256]{4,3,2,1,0:T(8,128)(2,1)S(1)} %fusion.74), channel_id=1, source_target_pairs={{0,2},{1,3},{2,0},{3,1},{4,6},{5,7},{6,4},{7,5},{8,10},{9,11},{10,... | collective-permute-start | bytes 884744 | tf_op jit(solution)/shard_map/ppermute | solution.py:635
  1329.0 33.8 %collective-permute-start.53 = (bf16[2,144,384]{2,1,0:T(8,128)(2,1)S(1)}, bf16[2,144,384]{2,1,0:T(8,128)(2,1)}, u32[]{:S(2)}, u32[]{:S(2)}) collective-permute-start(bf16[2,144,384]{2,1,0:T(8,128)(2,1)S(1)} %fusion.75), channel_id=1, source_target_pairs={{0,8},{4,12},{8,0},{12,4},{1,9},{5,13},{9,1},{13,5},{2,10},{6,14},... | collective-permute-start | bytes 663560 | tf_op jit(solution)/shard_map/ppermute | solution.py:635
  1332.8 29.9 %collective-permute-start.54 = (bf16[2,144,384]{2,1,0:T(8,128)(2,1)}, bf16[2,144,384]{2,1,0:T(8,128)(2,1)}, u32[]{:S(2)}, u32[]{:S(2)}) collective-permute-start(bf16[2,144,384]{2,1,0:T(8,128)(2,1)} %fusion.76), channel_id=1, source_target_pairs={{0,8},{4,12},{8,0},{12,4},{1,9},{5,13},{9,1},{13,5},{2,10},{6,14},... | collective-permute-start | bytes 663560 | tf_op jit(solution)/shard_map/ppermute | solution.py:635
  1336.5 26.3 %collective-permute-start.55 = (bf16[2,144,384]{2,1,0:T(8,128)(2,1)}, bf16[2,144,384]{2,1,0:T(8,128)(2,1)}, u32[]{:S(2)}, u32[]{:S(2)}) collective-permute-start(bf16[2,144,384]{2,1,0:T(8,128)(2,1)} %fusion.77), channel_id=1, source_target_pairs={{0,8},{4,12},{8,0},{12,4},{1,9},{5,13},{9,1},{13,5},{2,10},{6,14},... | collective-permute-start | bytes 663560 | tf_op jit(solution)/shard_map/ppermute | solution.py:635
  (136 other events, 1840.4 us)
Sparse Core Ops, SparseCore 0:
  14.8 146.3 all-gather.5
  164.0 82.7 all-gather.3
  843.9 138.1 reduce-scatter.6
  986.0 95.7 reduce-scatter.4

commit v4 on v3

--- a/solution.py
+++ b/solution.py
@@ -386,7 +386,7 @@
         out_shape=[f32s(NSTATE, SUB, DI), b16s(rows, DI), f32s(rows, DI)],
         scratch_shapes=[vm(NSTATE, rows, LANES), vm(NSTATE, SUB, LANES)],
         compiler_params=params(),
-        cost_estimate=cost(rows, DI, 4),
+        cost_estimate=pl.CostEstimate(flops=1000, bytes_accessed=1000, transcendentals=0),
         name="first",
     )(delta, alog, bc, cut, gbranch, z, ssm)
 
@@ -483,30 +483,39 @@
     return value, slope
 
 
-QUARTERS = 4
-
-
-def expert_kernel(blocks, peers, *refs):
+PARTS = 2
+
+
+def expert_kernel(blocks, peers, final, *refs):
     weights, refs = refs[:blocks], refs[blocks:]
-    xs, gs, refs = refs[:peers], refs[peers : 2 * peers], refs[2 * peers :]
-    out_ref, x_ref, g_ref, hid_ref, pre_ref, up_s, down_s, acc_y, acc_g = refs
-    cap = xs[0].shape[1]
+    step = pl.program_id(0)
+    if final:
+        x_ref, g_ref, before, out_ref, hid_ref, pre_ref, up_s, down_s, acc_y, acc_g = refs
+
+        @pl.when(step == 0)
+        def _():
+            acc_y[...] = before[:, :D].astype(jnp.float32)
+            acc_g[...] = before[:, D:].astype(jnp.float32)
+
+    else:
+        xs, gs, refs = refs[:peers], refs[peers : 2 * peers], refs[2 * peers :]
+        out_ref, x_ref, g_ref, hid_ref, pre_ref, up_s, down_s, acc_y, acc_g = refs
+        cap = xs[0].shape[1]
+
+        @pl.when(step == 0)
+        def _():
+            for d in range(peers):
+                at = slice(d * cap, (d + 1) * cap)
+                piece = xs[d][0]
+                x_ref[at, :] = piece[:, :D]
+                gate = jnp.sum(piece[:, D:].astype(jnp.float32), axis=1, keepdims=True)
+                g_ref[at, :] = (gate * gs[d][0].astype(jnp.float32)).astype(jnp.bfloat16)
+            acc_y[...] = jnp.zeros_like(acc_y)
+            acc_g[...] = jnp.zeros_like(acc_g)
+
     size = weights[0].shape[1]
-    step = pl.program_id(0)
-
-    @pl.when(step == 0)
-    def _():
-        for d in range(peers):
-            at = slice(d * cap, (d + 1) * cap)
-            piece = xs[d][0]
-            x_ref[at, :] = piece[:, :D]
-            gate = jnp.sum(piece[:, D:].astype(jnp.float32), axis=1, keepdims=True)
-            g_ref[at, :] = (gate * gs[d][0].astype(jnp.float32)).astype(jnp.bfloat16)
-        acc_y[...] = jnp.zeros_like(acc_y)
-        acc_g[...] = jnp.zeros_like(acc_g)
-
-    each = blocks // QUARTERS
-    for h in range(QUARTERS):
+    each = blocks // PARTS
+    for h in range(PARTS):
 
         @pl.when(step == h)
         def _():
@@ -515,7 +524,7 @@
                 up_s[at, :] = weights[h * each + k][0]
                 down_s[at, :] = weights[h * each + k][1]
 
-    tile = cap * peers // 3
+    tile = x_ref.shape[0] // 3
 
     def body(r, carry):
         at = pl.ds(pl.multiple_of(r * tile, tile), tile)
@@ -530,39 +539,49 @@
 
     lax.fori_loop(0, 3, body, 0)
 
-    @pl.when(step == QUARTERS - 1)
+    @pl.when(step == PARTS - 1)
     def _():
         out_ref[:, :D] = acc_y[...].astype(jnp.bfloat16)
         out_ref[:, D:] = acc_g[...].astype(jnp.bfloat16)
 
 
-def run_expert(weights, xs, gs, e):
-    blocks, peers = len(weights), len(xs)
-    cap = xs[0].shape[1]
+def run_expert(weights, e, xs, gs, before):
+    blocks = len(weights)
+    final = before is not None
     size = weights[0].shape[1]
-    rows, cols = peers * cap, blocks * size
-    part = cols // QUARTERS
+    peers = 1 if final else len(xs)
+    rows = xs.shape[0] if final else peers * xs[0].shape[1]
+    cols = blocks * size
+    part = cols // PARTS
     once = dict(pipeline_mode=pl.Buffered(1))
 
     def pick(shape):
         return pl.BlockSpec((1,) + shape, lambda h: (e, 0, 0), **once)
 
     in_specs = [pl.BlockSpec((2, size, D), lambda h: (e, 0, 0), **once)] * blocks
-    in_specs += [pick(xs[0].shape[1:])] * peers + [pick(gs[0].shape[1:])] * peers
     column = pl.BlockSpec((rows, part), lambda h: (0, h))
+    kept_specs, kept = [column, column], [b16s(rows, cols), b16s(rows, cols)]
+    if final:
+        operands = [xs, gs, before]
+        in_specs += [full_spec(v.shape) for v in operands]
+    else:
+        operands = [*xs, *gs]
+        in_specs += [pick(v.shape[1:]) for v in operands]
+        kept_specs = [full_spec((rows, D))] * 2 + kept_specs
+        kept = [b16s(rows, D)] * 2 + kept
     return pl.pallas_call(
-        functools.partial(expert_kernel, blocks, peers),
-        grid=(QUARTERS,),
+        functools.partial(expert_kernel, blocks, peers, final),
+        grid=(PARTS,),
         in_specs=in_specs,
-        out_specs=[full_spec((rows, 2 * D)), full_spec((rows, D)), full_spec((rows, D)), column, column],
-        out_shape=[b16s(rows, 2 * D), b16s(rows, D), b16s(rows, D), b16s(rows, cols), b16s(rows, cols)],
+        out_specs=[full_spec((rows, 2 * D))] + kept_specs,
+        out_shape=[b16s(rows, 2 * D)] + kept,
         scratch_shapes=[
             pltpu.VMEM((part, D), jnp.bfloat16), pltpu.VMEM((part, D), jnp.bfloat16), vm(rows, D), vm(rows, D),
         ],
         compiler_params=params(),
         cost_estimate=pl.CostEstimate(flops=1000, bytes_accessed=1000, transcendentals=0),
         name="expert",
-    )(*weights, *xs, *gs)
+    )(*weights, *operands)
 
 
 def weight_kernel(hid_ref, pre_ref, x_ref, g_ref, up_ref, down_ref):
@@ -572,12 +591,12 @@
 
 def run_weight(hid, pre, x, g):
     rows, cols = hid.shape
-    part = cols // 12
+    part = cols // 6
     column = pl.BlockSpec((rows, part), lambda c: (0, c))
     out = pl.BlockSpec((part, D), lambda c: (c, 0))
     return pl.pallas_call(
         weight_kernel,
-        grid=(12,),
+        grid=(6,),
         in_specs=[column, column, full_spec((rows, D)), full_spec((rows, D))],
         out_specs=[out, out],
         out_shape=[b16s(cols, D), b16s(cols, D)],
@@ -794,9 +813,8 @@
     out_full = lax.all_gather(out_proj, ALL, axis=0, tiled=True)
     local_experts = expert_up.shape[0]
     shard = jnp.stack([m for e in range(local_experts) for m in (expert_up[e].T, expert_down[e])])
+    shard, conv_full = held_for(shard, conv_full)
     gather = Gather(shard)
-    gather.step()
-    conv_full = gather.hold(conv_full)
     gather.step()
 
     xproj_full = small[:, :XW]
@@ -811,11 +829,11 @@
 
     halo_tokens = shifted(tokens[:, length - halo :], "seq", 1)
     halo_segs = shifted(segment_ids[:, length - halo :].astype(f32), "seq", 1)
-    inputs = to_ext_rows(tokens, halo_tokens).astype(f32)
+    inputs = lax.optimization_barrier(to_ext_rows(tokens, halo_tokens)).astype(f32)
     seg_ext = to_ext_rows(segment_ids.astype(f32), halo_segs)
     drop = to_rows(keep_mask).astype(f32)
     route = to_rows(routes[..., 0])
-    grad_low = to_rows(out_grad)
+    grad_low = lax.optimization_barrier(to_rows(out_grad))
     grad_final = grad_low.astype(f32)
     skip_rows = halo * SUB
     seg = seg_ext[skip_rows:]
@@ -874,25 +892,31 @@
     message = jnp.concatenate([normed_two, jnp.pad(gates, ((0, 0), (0, LANES - 3)))], axis=1)
     message = gather.hold(message)
     gather.step()
+    arrived = gather.hold(dispatch(message))
     while not gather.done():
         gather.step()
-    arrived = gather.hold(dispatch(message))
-    blocks = gather.here + gather.there[:-1] + [jnp.concatenate(gather.there[-1], axis=0)]
-    returned, for_weights = [], []
+    partial, for_weights = [], []
     for e in range(local_experts):
-        done, *rest = run_expert(blocks, arrived, grad_arrived, e)
+        done, *rest = run_expert(gather.here, e, arrived, grad_arrived, None)
+        partial.append(done)
         for_weights.append(rest)
+    partial = gather.hold(partial)
+    theirs = gather.there[:-1] + [jnp.concatenate(gather.there[-1], axis=0)]
+    returned = []
+    for e in range(local_experts):
+        done, *rest = run_expert(theirs, e, *for_weights[e][:2], partial[e])
+        for_weights[e] += rest
         if e > 0:
             done, returned = held_for(done, returned)
         returned.append(exchange([part for part in done.reshape(peers, capacity, 2 * D)]))
     weight_grads = []
     for e in range(local_experts):
-        x_rows, g_rows, hid, pre = for_weights[e]
-        weight_grads += run_weight(hid, pre, x_rows, g_rows)
+        x_rows, g_rows, *kept = for_weights[e]
+        sides = [run_weight(kept[2 * k], kept[2 * k + 1], x_rows, g_rows) for k in range(2)]
+        weight_grads += [(sides[0][m], sides[1][m]) for m in range(2)]
     returned[-1], weight_grads = held_for(returned[-1], weight_grads)
     count = len(weight_grads)
-    middle = weight_grads[0].shape[0] // 2
-    reduces = [Reduce(g[:middle], g[middle:], i < count - 1) for i, g in enumerate(weight_grads)]
+    reduces = [Reduce(g[0], g[1], i < count - 1) for i, g in enumerate(weight_grads)]
     returned = [jnp.stack([returned[e][d] for e in range(local_experts)]) for d in range(peers)]
 
     back_rows = jnp.stack(returned).reshape(EXPERTS * capacity, 2 * D)
@@ -911,15 +935,14 @@
         grad_final + inv_two * scaled
         - first_sum * (inv_two * inv_two * inv_two * jnp.mean(scaled * first_sum, axis=-1, keepdims=True))
     )
-    grad_first = hold_all(grad_first, reduces[-1:])
     first_low = grad_first.astype(b16)
     out_grad_part = dot(branch, first_low, TN, b16)
     grad_branch = dot(first_low, out_full, NT)
     grad_branch, out_grad_part = held_for(grad_branch, out_grad_part)
-    grad_branch = hold_all(grad_branch, reduces[:1])
+    grad_branch = hold_all(grad_branch, reduces[-1:])
 
     leads, grad_z, grad_ssm = run_first(delta, alog, bc, cut, grad_branch, gate_z, ssm)
-    leads = settle(leads, [reduces[0], reduces[1], reduces[-1]])
+    leads = settle(leads, [reduces[0], reduces[-1]])
     gate_part = dot(grad_z, normed_one[skip_rows:], TN, b16)
     grad_normed_z = dot(grad_z, gate_full, NN)
     beside = [gate_part, grad_normed_z, router_grad]
@@ -931,9 +954,9 @@
     grad_delta_in, gbc, parts = 0.0, 0.0, []
     width = DI // SPLITS
     for part in range(SPLITS):
-        if part == 1:
+        if part == SPLITS - 1:
             last, out_sum = held_for(last, out_sum)
-        last = hold_all(last, reduces[: 2 + part] + reduces[-1:] if 2 + part < count else reduces)
+        last = hold_all(last, reduces[: 1 + part] + reduces[-1:] if 1 + part < count else reduces)
         gxs, gpre, galog, gvec, gbc_part = run_back(xs, delta, alog, bc, cut, grad_ssm, skip, held, last, part)
         grad_delta_in = grad_delta_in + dot(gpre, dtw[part * width : (part + 1) * width], NN)
         gbc = gbc + gbc_part[:, : 2 * NSTATE]
@@ -970,14 +993,8 @@
         gexts.append(gext)
         conv_grads.append(gvec)
     conv_all, gexts = held_for(jnp.concatenate(conv_parts, axis=0), gexts)
-    third = D // 3
-    conv_own = []
-    for k in range(3):
-        piece = conv_all[:, k * third : (k + 1) * third].reshape(-1, own, third)
-        conv_own.append(Halving(piece, ("seq", "expert"), True))
-    gexts = hold_all(gexts, conv_own + [small_half])
+    conv_own = lax.psum_scatter(conv_all, ("seq", "expert"), scatter_dimension=0, tiled=True).astype(f32)
     grad_normed = sum(dot(gexts[k], conv_full[k * width : (k + 1) * width], NN) for k in range(SPLITS))
-    grad_normed = hold_all(grad_normed, conv_own + [small_half])
     over = grad_normed[:skip_rows].reshape(halo, seqs, HALVES, D)
     from_next = shifted(over[:, :, 0], "seq", -1)
     edge = jnp.stack([over[:, :, 1], from_next], axis=2).reshape(skip_rows, D)
@@ -992,12 +1009,10 @@
     )
     conv_grad = jnp.concatenate(conv_grads, axis=1)[: CONVK + 1]
     flat = jnp.concatenate([gain_one_grad, gain_two_grad, router_grad.reshape(-1), conv_grad.reshape(-1)])
-    flat = hold_all(flat, conv_own + [small_half])
     flat = sum_everywhere(flat.reshape(-1, LANES)).reshape(-1)
     small_sum = small_half.finish()
     is_gate = lax.axis_index("dp") == 1
     gate_own = gate_own.astype(f32)
-    conv_own = jnp.concatenate([part.finish() for part in conv_own], axis=1)
     in_sum = jnp.where(is_gate, gate_own, conv_own)
     in_sum = in_sum + ring(jnp.where(is_gate, conv_own, gate_own).astype(b16), "dp", 1).astype(f32)
     gain_one_sum, gain_two_sum = flat[:D], flat[D : 2 * D]

time: 1420 us -> 1290 us (0.908)
  waiting for transfers between devices: 376 us -> 229 us
  local copies, waits for them, and re-layouts: 182 us -> 151 us
  starting transfers between devices: 95.4 us -> 124 us
  Pallas kernels: 487 us -> 505 us
    ppermute x9, waiting for transfers between devices: 122 us -> 24.3 us  [shifted(): lax.ppermute(value, axis, [(source, source + steps) for source in range(f...]
    ppermute x25, waiting for transfers between devices: 130 us -> 56.9 us  [ring(): lax.ppermute(value, axis, [(i, (i + step) % count) for i in range(count)])]
    all_gather x1, waiting for transfers between devices: 0.01 us -> 58.9 us  [local(): lax.all_gather(jnp.concatenate([in_proj.T, small.reshape(-1, D)], axis=0)...]
    optimization_barrier x1, waiting for transfers between devices: 46 us -> 0.02 us  [held_for(): return jax.tree.unflatten(tree, lax.optimization_barrier(flat))]
    ppermute x25, starting transfers between devices: 42.5 us -> 80.6 us  [ring(): lax.ppermute(value, axis, [(i, (i + step) % count) for i in range(count)])]
    slice x10 -> x0, local copies, waits for them, and re-layouts: 29 us -> none  [the longest x3 15.6 us: local(): tokens_rows = inputs[skip_rows:]]
    pallas_call x4 -> x8, Pallas kernels: 118 us -> 136 us  [the longest x4 92.9 us: run_expert(): pl.pallas_call(functools.partial(expert_kernel, blocks, peers, final), gr...]
    ppermute x34 -> x22, starting transfers between devices: 31.3 us -> 16.5 us  [partner(): return lax.ppermute(value, axis, [(i, i ^ bits) for i in range(count)])]
  transfers between devices with their start and end apart: 72 -> 61, of which waited for: 23 -> 23; matrix products, arithmetic and copies ran while one was open for 24% -> 26% of each run, Pallas kernels for 32% -> 38%
where the time goes in v4:
time: 1290 us; the launch traced here: 1280 us
  Pallas kernels  505 us (39%)
  waiting for transfers between devices  229 us (18%)
  local copies, waits for them, and re-layouts  151 us (12%)
  matrix products  132 us (10%)
  starting transfers between devices  124 us (10%)
  other arithmetic  120 us (9%)
  between operations  15.9 us (1%)
    pallas_call x3, Pallas kernels, run_back(): pl.pallas_call(back_kernel, grid=(width // LANES,), in_specs=[col(rows),...  207 us
    dot_general x28, matrix products, dot(): lax.dot_general(left, right, (dims, ((), ())), preferred_element_type=out)  132 us
    pallas_call x4, Pallas kernels, run_expert(): pl.pallas_call(functools.partial(expert_kernel, blocks, peers, final), gr...  92.9 us
    ppermute x25, starting transfers between devices, ring(): lax.ppermute(value, axis, [(i, (i + step) % count) for i in range(count)])  80.6 us
    ppermute x22, waiting for transfers between devices, partner(): return lax.ppermute(value, axis, [(i, i ^ bits) for i in range(count)])  80.5 us
    all_gather x1, waiting for transfers between devices, local(): lax.all_gather(jnp.concatenate([in_proj.T, small.reshape(-1, D)], axis=0)...  58.9 us
    ppermute x25, waiting for transfers between devices, ring(): lax.ppermute(value, axis, [(i, (i + step) % count) for i in range(count)])  56.9 us
    pallas_call x1, Pallas kernels, run_out(): pl.pallas_call(out_kernel, grid=(DI // LANES,), in_specs=[col_spec(rows),...  53.5 us
  transfers between devices with their start and end apart: 61, of which 23 were waited for; matrix products, arithmetic and copies ran while one was open for 26% of the time, Pallas kernels for 38%

profile of v4, /device:TPU:0, one launch (start us, length us, event | category | flops | bytes accessed | tf_op | source)
XLA Modules:
  0.0 1275.9 jit_solution(2782544873429880889)
XLA Ops:
  25.9 5.6 copy.328
  67.6 58.9 %all-gather.6.cloned.1.call-done = bf16[5120,1152]{1,0:T(8,128)(2,1)} async-done(((bf16[160,1152]{1,0:T(8,128)(2,1)}), bf16[5120,1152]{1,0:T(8,128)(2,1)}) %all-gather.6.cloned.1.call-update) | async-done | bytes 11796496 | tf_op jit(solution)/shard_map/all_gather | solution.py:808
  126.6 8.8 fusion.111
  145.9 9.8 fusion.129.ext_ref
  155.7 7.2 multiply_convert_fusion.xs_ref
  171.1 44.0 %end.1 = (f32[1024,2304]{1,0:T(8,128)}, f32[16,8,2304]{2,1,0:T(8,128)}, f32[8,2304]{1,0:T(8,128)}) custom-call(bf16[1024,2304]{1,0:T(8,128)(2,1)} %copy-done.3, bf16[1024,72]{1,0:T(8,128)(2,1)} %copy.275.din_ref, bf16[2304,72]{1,0:T(8,128)(2,1)} %slice.615.dtw_ref, bf16[1,2304]{1,0:T(2,128)(2,1)} %get-tuple-element.501.dtb_ref, ...), custom_call_target="tpu_custom_call" | custom-call | flops 301989888 | bytes 150994944 | tf_op jit(solution)/shard_map/end/pallas_call | solution.py:336
  216.2 5.2 collective-permute-done.2.refs_1_
  229.3 11.4 fusion.21.z_ref
  244.5 13.1 %collective-permute-done.8 = bf16[16,4,2304]{2,1,0:T(4,128)(2,1)S(1)} collective-permute-done((bf16[16,4,2304]{2,1,0:T(4,128)(2,1)S(1)}, bf16[16,4,2304]{2,1,0:T(4,128)(2,1)S(1)}, u32[]{:S(2)}, u32[]{:S(2)}) %collective-permute-start.8) | collective-permute-done | bytes 294944 | tf_op jit(solution)/shard_map/ppermute | solution.py:34
  258.9 7.7 collective-permute-start.9
  281.9 53.5 %out.1 = (bf16[1024,2304]{1,0:T(8,128)(2,1)}, bf16[1024,2304]{1,0:T(8,128)(2,1)}, f32[8,16,8,2304]{3,2,1,0:T(8,128)}) custom-call(bf16[1024,2304]{1,0:T(8,128)(2,1)} %copy-done.3, f32[1024,2304]{1,0:T(8,128)} %get-tuple-element.190.delta_ref, bf16[16,2304]{1,0:T(8,128)(2,1)} %slice.617.alog_ref, f32[1024,32]{1,0:T(8,128)} %copy.276.bc_ref, ...), custom_call_target="tpu_custom_call" | custom-call | flops 301989888 | bytes 188743680 | tf_op jit(solution)/shard_map/out/pallas_call | solution.py:355
  335.5 10.6 multiply_reduce_fusion.5
  349.9 5.7 collective-permute-done.10.refs_2_
  369.2 22.0 %collective-permute-done.13.refs_6_ = bf16[2,192,1280]{2,1,0:T(8,128)(2,1)S(1)} collective-permute-done((bf16[2,192,1280]{2,1,0:T(8,128)(2,1)S(1)}, bf16[2,192,1280]{2,1,0:T(8,128)(2,1)S(1)}, u32[]{:S(2)}, u32[]{:S(2)}) %collective-permute-start.13) | collective-permute-done | bytes 983072 | tf_op jit(solution)/shard_map/ppermute | solution.py:654
  391.2 20.3 %collective-permute-done.14.refs_7_ = bf16[2,192,1280]{2,1,0:T(8,128)(2,1)S(1)} collective-permute-done((bf16[2,192,1280]{2,1,0:T(8,128)(2,1)S(1)}, bf16[2,192,1280]{2,1,0:T(8,128)(2,1)S(1)}, u32[]{:S(2)}, u32[]{:S(2)}) %collective-permute-start.14) | collective-permute-done | bytes 983072 | tf_op jit(solution)/shard_map/ppermute | solution.py:654
  411.5 21.2 %collective-permute-done.15.refs_3_ = bf16[4,384,1152]{2,1,0:T(8,128)(2,1)S(1)} collective-permute-done((bf16[4,384,1152]{2,1,0:T(8,128)(2,1)}, bf16[4,384,1152]{2,1,0:T(8,128)(2,1)S(1)}, u32[]{:S(2)}, u32[]{:S(2)}) %collective-permute-start.15) | collective-permute-done | bytes 3538976 | tf_op jit(solution)/shard_map/ppermute | solution.py:649
  439.6 23.5 %expert.5 = (bf16[768,2304]{1,0:T(8,128)(2,1)}, bf16[768,1152]{1,0:T(8,128)(2,1)}, bf16[768,1152]{1,0:T(8,128)(2,1)}, bf16[768,1536]{1,0:T(8,128)(2,1)}, bf16[768,1536]{1,0:T(8,128)(2,1)}) custom-call(bf16[4,384,1152]{2,1,0:T(8,128)(2,1)} %pad_maximum_fusion.2.refs_0_, bf16[4,384,1152]{2,1,0:T(8,128)(2,1)} %collective-permute-done.2.refs_1_, ...), custom_call_target="tpu_custom_call" | custom-call | flops 1000 | bytes 1000 | tf_op jit(solution)/shard_map/expert/pallas_call | solution.py:572
  463.1 23.3 %expert.4 = (bf16[768,2304]{1,0:T(8,128)(2,1)}, bf16[768,1152]{1,0:T(8,128)(2,1)}, bf16[768,1152]{1,0:T(8,128)(2,1)}, bf16[768,1536]{1,0:T(8,128)(2,1)}, bf16[768,1536]{1,0:T(8,128)(2,1)}) custom-call(bf16[4,384,1152]{2,1,0:T(8,128)(2,1)} %pad_maximum_fusion.2.refs_0_, bf16[4,384,1152]{2,1,0:T(8,128)(2,1)} %collective-permute-done.2.refs_1_, ...), custom_call_target="tpu_custom_call" | custom-call | flops 1000 | bytes 1000 | tf_op jit(solution)/shard_map/expert/pallas_call | solution.py:572
  492.1 22.9 %expert.7 = (bf16[768,2304]{1,0:T(8,128)(2,1)}, bf16[768,1536]{1,0:T(8,128)(2,1)}, bf16[768,1536]{1,0:T(8,128)(2,1)}) custom-call(bf16[4,384,1152]{2,1,0:T(8,128)(2,1)} %collective-permute-done.3.refs_0_, bf16[4,384,1152]{2,1,0:T(8,128)(2,1)} %collective-permute-done.11.refs_1_, bf16[4,384,1152]{2,1,0:T(8,128)(2,1)} %copy-done.5, ...), custom_call_target="tpu_custom_call" | custom-call | flops 1000 | bytes 1000 | tf_op jit(solution)/shard_map/expert/pallas_call | solution.py:572
  520.3 23.2 %expert.6 = (bf16[768,2304]{1,0:T(8,128)(2,1)}, bf16[768,1536]{1,0:T(8,128)(2,1)}, bf16[768,1536]{1,0:T(8,128)(2,1)}) custom-call(bf16[4,384,1152]{2,1,0:T(8,128)(2,1)} %collective-permute-done.3.refs_0_, bf16[4,384,1152]{2,1,0:T(8,128)(2,1)} %collective-permute-done.11.refs_1_, bf16[4,384,1152]{2,1,0:T(8,128)(2,1)} %copy-done.5, ...), custom_call_target="tpu_custom_call" | custom-call | flops 1000 | bytes 1000 | tf_op jit(solution)/shard_map/expert/pallas_call | solution.py:572
  543.5 15.9 %collective-permute-done.21 = bf16[192,2304]{1,0:T(8,128)(2,1)} collective-permute-done((bf16[192,2304]{1,0:T(8,128)(2,1)}, bf16[192,2304]{1,0:T(8,128)(2,1)}, u32[]{:S(2)}, u32[]{:S(2)}) %collective-permute-start.21) | collective-permute-done | bytes 884768 | tf_op jit(solution)/shard_map/ppermute | solution.py:654
  566.7 10.7 weight.6
  577.4 10.7 weight.4
  588.2 10.7 weight.7
  598.9 10.7 weight.5
  617.0 7.8 fusion.7
  643.2 8.1 fusion.51
  652.4 11.9 fusion.53.gb_ref
  664.4 11.7 collective-permute-done.25
  683.5 38.2 %first.1 = (f32[16,8,2304]{2,1,0:T(8,128)}, bf16[1024,2304]{1,0:T(8,128)(2,1)}, f32[1024,2304]{1,0:T(8,128)}) custom-call(f32[1024,2304]{1,0:T(8,128)} %get-tuple-element.190.delta_ref, bf16[16,2304]{1,0:T(8,128)(2,1)} %slice.617.alog_ref, f32[1024,32]{1,0:T(8,128)} %copy.276.bc_ref, f32[1024,128]{1,0:T(8,128)} %broadcast_in_dim.18.cut_ref, ...), custom_call_target="tpu_custom_call" | custom-call | flops 1000 | bytes 1000 | tf_op jit(solution)/shard_map/first/pallas_call | solution.py:378
  721.7 8.5 collective-permute-done.26
  739.1 10.3 fusion.19
  752.6 11.1 fusion.130
  765.9 9.7 collective-permute-done.30
  793.5 69.1 %back.3 = (f32[1024,768]{1,0:T(8,128)}, bf16[1024,768]{1,0:T(8,128)(2,1)}, f32[16,768]{1,0:T(8,128)}, f32[8,768]{1,0:T(8,128)}, f32[1024,128]{1,0:T(8,128)}) custom-call(bf16[1024,2304]{1,0:T(8,128)(2,1)} %copy-done.3, f32[1024,2304]{1,0:T(8,128)} %get-tuple-element.190.delta_ref, bf16[16,2304]{1,0:T(8,128)(2,1)} %slice.617.alog_ref, ...), custom_call_target="tpu_custom_call" | custom-call | flops 100663296 | bytes 213909504 | tf_op jit(solution)/shard_map/back/pallas_call | solution.py:405
  886.8 5.9 reshape.565
  897.5 69.0 %back.4 = (f32[1024,768]{1,0:T(8,128)}, bf16[1024,768]{1,0:T(8,128)(2,1)}, f32[16,768]{1,0:T(8,128)}, f32[8,768]{1,0:T(8,128)}, f32[1024,128]{1,0:T(8,128)}) custom-call(bf16[1024,2304]{1,0:T(8,128)(2,1)} %copy-done.3, f32[1024,2304]{1,0:T(8,128)} %get-tuple-element.190.delta_ref, bf16[16,2304]{1,0:T(8,128)(2,1)} %slice.617.alog_ref, ...), custom_call_target="tpu_custom_call" | custom-call | flops 100663296 | bytes 213909504 | tf_op jit(solution)/shard_map/back/pallas_call | solution.py:405
  981.9 69.0 %back.5 = (f32[1024,768]{1,0:T(8,128)}, bf16[1024,768]{1,0:T(8,128)(2,1)}, f32[16,768]{1,0:T(8,128)}, f32[8,768]{1,0:T(8,128)}, f32[1024,128]{1,0:T(8,128)}) custom-call(bf16[1024,2304]{1,0:T(8,128)(2,1)} %copy-done.3, f32[1024,2304]{1,0:T(8,128)} %get-tuple-element.190.delta_ref, bf16[16,2304]{1,0:T(8,128)(2,1)} %slice.617.alog_ref, ...), custom_call_target="tpu_custom_call" | custom-call | flops 100663296 | bytes 213909504 | tf_op jit(solution)/shard_map/back/pallas_call | solution.py:405
  1081.0 8.8 conv.5
  1089.8 8.8 conv.3
  1098.6 6.1 fusion.131
  1104.7 8.8 conv.4
  1124.6 36.4 %collective-permute-start.55 = (bf16[384,1152]{1,0:T(8,128)(2,1)}, bf16[384,1152]{1,0:T(8,128)(2,1)}, u32[]{:S(2)}, u32[]{:S(2)}) collective-permute-start(bf16[384,1152]{1,0:T(8,128)(2,1)} %fusion.28), channel_id=1, source_target_pairs={{0,12},{4,0},{8,4},{12,8},{1,13},{5,1},{9,5},{13,9},{2,14},{6,2},{... | collective-permute-start | bytes 2654216 | tf_op jit(solution)/shard_map/ppermute | solution.py:649
  1189.1 6.8 multiply_reduce_fusion.2
  1201.4 6.7 reshape.574
  1208.1 5.5 copy.253
  1230.1 5.2 collective-permute-done.46
  1239.1 5.2 collective-permute-done.48
  (528 shorter events, 374.6 us)
Async XLA Ops:
  7.2 119.4 %all-gather.6.cloned.1.call-start = ((), (), s32[]{:S(2)}) async-start(), calls=%async_computation.6 | async-start | bytes 12165120 | tf_op jit(solution)/shard_map/all_gather | solution.py:808
  14.6 320.8 %all-gather.4.cloned.1.call-start = ((), (), s32[]{:S(2)}) async-start(), calls=%async_computation.3 | async-start | bytes 5474304 | tf_op jit(solution)/shard_map/all_gather | solution.py:813
  15.6 40.0 %collective-permute-start = (bf16[4,3,1152]{2,1,0:T(4,128)(2,1)S(1)}, bf16[4,3,1152]{2,1,0:T(4,128)(2,1)S(1)}, u32[]{:S(2)}, u32[]{:S(2)}) collective-permute-start(bf16[4,3,1152]{2,1,0:T(4,128)(2,1)S(1)} %slice.456), channel_id=1, source_target_pairs={{0,4},{4,8},{8,12},{1,5},{5,9},{9,13},{2,6},{6,10},{10,14},{3,7},{... | collective-permute-start | bytes 82952 | tf_op jit(solution)/shard_map/ppermute | solution.py:34
  21.3 32.3 %collective-permute-start.1 = (f32[4,3]{1,0:T(4,128)S(1)}, f32[4,3]{1,0:T(4,128)S(1)}, u32[]{:S(2)}, u32[]{:S(2)}) collective-permute-start(f32[4,3]{1,0:T(4,128)S(1)} %slice_convert_fusion.4), channel_id=1, source_target_pairs={{0,4},{4,8},{8,12},{1,5},{5,9},{9,13},{2,6},{6,10},{10,14},{3,7},{... | collective-permute-start | bytes 152 | tf_op jit(solution)/shard_map/ppermute | solution.py:34
  43.6 177.8 %collective-permute-start.4 = (bf16[2,192,1152]{2,1,0:T(8,128)(2,1)}, bf16[2,192,1152]{2,1,0:T(8,128)(2,1)}, u32[]{:S(2)}, u32[]{:S(2)}) collective-permute-start(bf16[2,192,1152]{2,1,0:T(8,128)(2,1)} %bitcast.27), channel_id=1, source_target_pairs={{0,1},{1,0},{2,3},{3,2},{4,5},{5,4},{6,7},{7,6},{8,9},{9,8},{10,11... | collective-permute-start | bytes 2654216 | tf_op jit(solution)/shard_map/ppermute | solution.py:654
  43.6 177.8 %collective-permute-start.5 = (bf16[2,192,1152]{2,1,0:T(8,128)(2,1)}, bf16[2,192,1152]{2,1,0:T(8,128)(2,1)}, u32[]{:S(2)}, u32[]{:S(2)}) collective-permute-start(bf16[2,192,1152]{2,1,0:T(8,128)(2,1)} %bitcast.28), channel_id=1, source_target_pairs={{0,2},{1,3},{2,0},{3,1},{4,6},{5,7},{6,4},{7,5},{8,10},{9,11},{10,... | collective-permute-start | bytes 2654216 | tf_op jit(solution)/shard_map/ppermute | solution.py:654
  45.1 176.4 %collective-permute-start.6 = (bf16[2,192,1152]{2,1,0:T(8,128)(2,1)}, bf16[2,192,1152]{2,1,0:T(8,128)(2,1)}, u32[]{:S(2)}, u32[]{:S(2)}) collective-permute-start(bf16[2,192,1152]{2,1,0:T(8,128)(2,1)} %bitcast.29), channel_id=1, source_target_pairs={{0,3},{1,2},{2,1},{3,0},{4,7},{5,6},{6,5},{7,4},{8,11},{9,10},{10,... | collective-permute-start | bytes 2654216 | tf_op jit(solution)/shard_map/ppermute | solution.py:654
  45.5 924.8 %reduce-scatter.10.cloned.1.call-start = ((), (), s32[]{:S(2)}) async-start(), calls=%async_computation.7 | async-start | bytes 5474304
  137.8 83.6 %collective-permute-start.2 = (bf16[4,384,1152]{2,1,0:T(8,128)(2,1)}, bf16[4,384,1152]{2,1,0:T(8,128)(2,1)}, u32[]{:S(2)}, u32[]{:S(2)}) collective-permute-start(bf16[4,384,1152]{2,1,0:T(8,128)(2,1)} %pad_maximum_fusion.2.refs_0_), channel_id=1, source_target_pairs={{0,4},{4,8},{8,12},{12,0},{1,5},{5,9},{9,13},{13,1},{2,6},{6,10},{... | collective-permute-start | bytes 10616840 | tf_op jit(solution)/shard_map/ppermute | solution.py:649
  138.7 82.7 %collective-permute-start.3 = (bf16[4,384,1152]{2,1,0:T(8,128)(2,1)}, bf16[4,384,1152]{2,1,0:T(8,128)(2,1)}, u32[]{:S(2)}, u32[]{:S(2)}) collective-permute-start(bf16[4,384,1152]{2,1,0:T(8,128)(2,1)} %pad_maximum_fusion.2.refs_0_), channel_id=1, source_target_pairs={{0,16},{16,0},{1,17},{17,1},{2,18},{18,2},{3,19},{19,3},{4,20},{20... | collective-permute-start | bytes 10616840 | tf_op jit(solution)/shard_map/ppermute | solution.py:649
  241.3 16.3 %collective-permute-start.8 = (bf16[16,4,2304]{2,1,0:T(4,128)(2,1)S(1)}, bf16[16,4,2304]{2,1,0:T(4,128)(2,1)S(1)}, u32[]{:S(2)}, u32[]{:S(2)}) collective-permute-start(bf16[16,4,2304]{2,1,0:T(4,128)(2,1)S(1)} %add_convert_fusion.6), channel_id=1, source_target_pairs={{0,4},{4,8},{8,12},{1,5},{5,9},{9,13},{2,6},{6,10},{10,14},{3,7},{... | collective-permute-start | bytes 884744 | tf_op jit(solution)/shard_map/ppermute | solution.py:34
  276.5 79.2 %collective-permute-start.10 = (bf16[4,384,1152]{2,1,0:T(8,128)(2,1)}, bf16[4,384,1152]{2,1,0:T(8,128)(2,1)}, u32[]{:S(2)}, u32[]{:S(2)}) collective-permute-start(bf16[4,384,1152]{2,1,0:T(8,128)(2,1)} %collective-permute-done.2.refs_1_), channel_id=1, source_target_pairs={{0,4},{4,8},{8,12},{12,0},{1,5},{5,9},{9,13},{13,1},{2,6},{6,10},{... | collective-permute-start | bytes 10616840 | tf_op jit(solution)/shard_map/ppermute | solution.py:649
  279.4 76.5 %collective-permute-start.11 = (bf16[4,384,1152]{2,1,0:T(8,128)(2,1)}, bf16[4,384,1152]{2,1,0:T(8,128)(2,1)}, u32[]{:S(2)}, u32[]{:S(2)}) collective-permute-start(bf16[4,384,1152]{2,1,0:T(8,128)(2,1)} %collective-permute-done.2.refs_1_), channel_id=1, source_target_pairs={{0,16},{16,0},{1,17},{17,1},{2,18},{18,2},{3,19},{19,3},{4,20},{20... | collective-permute-start | bytes 10616840 | tf_op jit(solution)/shard_map/ppermute | solution.py:649
  355.9 76.8 %collective-permute-start.15 = (bf16[4,384,1152]{2,1,0:T(8,128)(2,1)}, bf16[4,384,1152]{2,1,0:T(8,128)(2,1)S(1)}, u32[]{:S(2)}, u32[]{:S(2)}) collective-permute-start(bf16[4,384,1152]{2,1,0:T(8,128)(2,1)} %collective-permute-done.10.refs_2_), channel_id=1, source_target_pairs={{0,4},{4,8},{8,12},{12,0},{1,5},{5,9},{9,13},{13,1},{2,6},{6,10},{... | collective-permute-start | bytes 10616840 | tf_op jit(solution)/shard_map/ppermute | solution.py:649
  359.1 74.1 %collective-permute-start.16 = (bf16[4,384,1152]{2,1,0:T(8,128)(2,1)}, bf16[4,384,1152]{2,1,0:T(8,128)(2,1)S(1)}, u32[]{:S(2)}, u32[]{:S(2)}) collective-permute-start(bf16[4,384,1152]{2,1,0:T(8,128)(2,1)} %collective-permute-done.10.refs_2_), channel_id=1, source_target_pairs={{0,16},{16,0},{1,17},{17,1},{2,18},{18,2},{3,19},{19,3},{4,20},{20... | collective-permute-start | bytes 10616840 | tf_op jit(solution)/shard_map/ppermute | solution.py:649
  366.7 24.6 %collective-permute-start.13 = (bf16[2,192,1280]{2,1,0:T(8,128)(2,1)S(1)}, bf16[2,192,1280]{2,1,0:T(8,128)(2,1)S(1)}, u32[]{:S(2)}, u32[]{:S(2)}) collective-permute-start(bf16[2,192,1280]{2,1,0:T(8,128)(2,1)S(1)} %bitcast.375), channel_id=1, source_target_pairs={{0,2},{1,3},{2,0},{3,1},{4,6},{5,7},{6,4},{7,5},{8,10},{9,11},{10,... | collective-permute-start | bytes 2949128 | tf_op jit(solution)/shard_map/ppermute | solution.py:654
  366.7 44.8 %collective-permute-start.14 = (bf16[2,192,1280]{2,1,0:T(8,128)(2,1)S(1)}, bf16[2,192,1280]{2,1,0:T(8,128)(2,1)S(1)}, u32[]{:S(2)}, u32[]{:S(2)}) collective-permute-start(bf16[2,192,1280]{2,1,0:T(8,128)(2,1)S(1)} %bitcast.374), channel_id=1, source_target_pairs={{0,3},{1,2},{2,1},{3,0},{4,7},{5,6},{6,5},{7,4},{8,11},{9,10},{10,... | collective-permute-start | bytes 2949128 | tf_op jit(solution)/shard_map/ppermute | solution.py:654
  435.0 51.4 %collective-permute-start.17 = (bf16[2,384,1152]{2,1,0:T(8,128)(2,1)}, bf16[2,384,1152]{2,1,0:T(8,128)(2,1)}, u32[]{:S(2)}, u32[]{:S(2)}) collective-permute-start(bf16[2,384,1152]{2,1,0:T(8,128)(2,1)} %slice.505), channel_id=1, source_target_pairs={{0,16},{16,0},{1,17},{17,1},{2,18},{18,2},{3,19},{19,3},{4,20},{20... | collective-permute-start | bytes 5308424 | tf_op jit(solution)/shard_map/ppermute | solution.py:649
  437.8 48.6 %collective-permute-start.18 = (bf16[2,384,1152]{2,1,0:T(8,128)(2,1)}, bf16[2,384,1152]{2,1,0:T(8,128)(2,1)}, u32[]{:S(2)}, u32[]{:S(2)}) collective-permute-start(bf16[2,384,1152]{2,1,0:T(8,128)(2,1)} %slice.506), channel_id=1, source_target_pairs={{0,4},{4,8},{8,12},{12,0},{1,5},{5,9},{9,13},{13,1},{2,6},{6,10},{... | collective-permute-start | bytes 5308424 | tf_op jit(solution)/shard_map/ppermute | solution.py:649
  518.5 25.1 %collective-permute-start.19 = (bf16[192,2304]{1,0:T(8,128)(2,1)}, bf16[192,2304]{1,0:T(8,128)(2,1)}, u32[]{:S(2)}, u32[]{:S(2)}) collective-permute-start(bf16[192,2304]{1,0:T(8,128)(2,1)} %get-tuple-element.481), channel_id=1, source_target_pairs={{0,1},{1,0},{2,3},{3,2},{4,5},{5,4},{6,7},{7,6},{8,9},{9,8},{10,11... | collective-permute-start | bytes 2654216 | tf_op jit(solution)/shard_map/ppermute | solution.py:654
  518.5 25.1 %collective-permute-start.20 = (bf16[192,2304]{1,0:T(8,128)(2,1)}, bf16[192,2304]{1,0:T(8,128)(2,1)}, u32[]{:S(2)}, u32[]{:S(2)}) collective-permute-start(bf16[192,2304]{1,0:T(8,128)(2,1)} %get-tuple-element.480), channel_id=1, source_target_pairs={{0,2},{1,3},{2,0},{3,1},{4,6},{5,7},{6,4},{7,5},{8,10},{9,11},{10,... | collective-permute-start | bytes 2654216 | tf_op jit(solution)/shard_map/ppermute | solution.py:654
  519.8 39.7 %collective-permute-start.21 = (bf16[192,2304]{1,0:T(8,128)(2,1)}, bf16[192,2304]{1,0:T(8,128)(2,1)}, u32[]{:S(2)}, u32[]{:S(2)}) collective-permute-start(bf16[192,2304]{1,0:T(8,128)(2,1)} %get-tuple-element.479), channel_id=1, source_target_pairs={{0,3},{1,2},{2,1},{3,0},{4,7},{5,6},{6,5},{7,4},{8,11},{9,10},{10,... | collective-permute-start | bytes 2654216 | tf_op jit(solution)/shard_map/ppermute | solution.py:654
  563.3 46.4 %collective-permute-start.22 = (bf16[192,2304]{1,0:T(8,128)(2,1)}, bf16[192,2304]{1,0:T(8,128)(2,1)}, u32[]{:S(2)}, u32[]{:S(2)}) collective-permute-start(bf16[192,2304]{1,0:T(8,128)(2,1)} %get-tuple-element.477), channel_id=1, source_target_pairs={{0,1},{1,0},{2,3},{3,2},{4,5},{5,4},{6,7},{7,6},{8,9},{9,8},{10,11... | collective-permute-start | bytes 2654216 | tf_op jit(solution)/shard_map/ppermute | solution.py:654
  563.5 46.1 %collective-permute-start.23 = (bf16[192,2304]{1,0:T(8,128)(2,1)}, bf16[192,2304]{1,0:T(8,128)(2,1)}, u32[]{:S(2)}, u32[]{:S(2)}) collective-permute-start(bf16[192,2304]{1,0:T(8,128)(2,1)} %get-tuple-element.476), channel_id=1, source_target_pairs={{0,2},{1,3},{2,0},{3,1},{4,6},{5,7},{6,4},{7,5},{8,10},{9,11},{10,... | collective-permute-start | bytes 2654216 | tf_op jit(solution)/shard_map/ppermute | solution.py:654
  564.8 44.9 %collective-permute-start.24 = (bf16[192,2304]{1,0:T(8,128)(2,1)}, bf16[192,2304]{1,0:T(8,128)(2,1)}, u32[]{:S(2)}, u32[]{:S(2)}) collective-permute-start(bf16[192,2304]{1,0:T(8,128)(2,1)} %get-tuple-element.475), channel_id=1, source_target_pairs={{0,3},{1,2},{2,1},{3,0},{4,7},{5,6},{6,5},{7,4},{8,11},{9,10},{10,... | collective-permute-start | bytes 2654216 | tf_op jit(solution)/shard_map/ppermute | solution.py:654
  633.7 42.3 %collective-permute-start.25 = (bf16[2,384,1152]{2,1,0:T(8,128)(2,1)}, bf16[2,384,1152]{2,1,0:T(8,128)(2,1)}, u32[]{:S(2)}, u32[]{:S(2)}) collective-permute-start(bf16[2,384,1152]{2,1,0:T(8,128)(2,1)} %pad_maximum_fusion.5), channel_id=1, source_target_pairs={{0,12},{4,0},{8,4},{12,8},{1,13},{5,1},{9,5},{13,9},{2,14},{6,2},{... | collective-permute-start | bytes 5308424 | tf_op jit(solution)/shard_map/ppermute | solution.py:649
  651.3 78.9 %collective-permute-start.26 = (bf16[4,384,1152]{2,1,0:T(8,128)(2,1)}, bf16[4,384,1152]{2,1,0:T(8,128)(2,1)}, u32[]{:S(2)}, u32[]{:S(2)}) collective-permute-start(bf16[4,384,1152]{2,1,0:T(8,128)(2,1)} %bitcast.401), channel_id=1, source_target_pairs={{0,16},{16,0},{1,17},{17,1},{2,18},{18,2},{3,19},{19,3},{4,20},{20... | collective-permute-start | bytes 10616840 | tf_op jit(solution)/shard_map/ppermute | solution.py:649
  679.3 50.9 %collective-permute-start.27 = (bf16[2,384,1152]{2,1,0:T(8,128)(2,1)}, bf16[2,384,1152]{2,1,0:T(8,128)(2,1)}, u32[]{:S(2)}, u32[]{:S(2)}) collective-permute-start(bf16[2,384,1152]{2,1,0:T(8,128)(2,1)} %add_convert_fusion.2), channel_id=1, source_target_pairs={{0,12},{4,0},{8,4},{12,8},{1,13},{5,1},{9,5},{13,9},{2,14},{6,2},{... | collective-permute-start | bytes 5308424 | tf_op jit(solution)/shard_map/ppermute | solution.py:649
  779.8 289.9 %reduce-scatter.6.cloned.1.call-start = ((), (), s32[]{:S(2)}) async-start(), calls=%async_computation.4 | async-start | bytes 5640192 | tf_op jit(solution)/shard_map/reduce_scatter | solution.py:953
  779.8 91.7 %collective-permute-start.32 = (bf16[4,384,1152]{2,1,0:T(8,128)(2,1)}, bf16[4,384,1152]{2,1,0:T(8,128)(2,1)}, u32[]{:S(2)}, u32[]{:S(2)}) collective-permute-start(bf16[4,384,1152]{2,1,0:T(8,128)(2,1)} %bitcast.400), channel_id=1, source_target_pairs={{0,16},{16,0},{1,17},{17,1},{2,18},{18,2},{3,19},{19,3},{4,20},{20... | collective-permute-start | bytes 10616840 | tf_op jit(solution)/shard_map/ppermute | solution.py:649
  784.2 87.3 %collective-permute-start.33 = (bf16[2,384,1152]{2,1,0:T(8,128)(2,1)}, bf16[2,384,1152]{2,1,0:T(8,128)(2,1)}, u32[]{:S(2)}, u32[]{:S(2)}) collective-permute-start(bf16[2,384,1152]{2,1,0:T(8,128)(2,1)} %add_convert_fusion.1), channel_id=1, source_target_pairs={{0,12},{4,0},{8,4},{12,8},{1,13},{5,1},{9,5},{13,9},{2,14},{6,2},{... | collective-permute-start | bytes 5308424 | tf_op jit(solution)/shard_map/ppermute | solution.py:649
  788.8 82.8 %collective-permute-start.31 = (bf16[384,1152]{1,0:T(8,128)(2,1)}, bf16[384,1152]{1,0:T(8,128)(2,1)}, u32[]{:S(2)}, u32[]{:S(2)}) collective-permute-start(bf16[384,1152]{1,0:T(8,128)(2,1)} %fusion.45), channel_id=1, source_target_pairs={{0,12},{4,0},{8,4},{12,8},{1,13},{5,1},{9,5},{13,9},{2,14},{6,2},{... | collective-permute-start | bytes 2654216 | tf_op jit(solution)/shard_map/ppermute | solution.py:649
  792.6 177.7 %collective-permute-start.36 = (bf16[4,384,1152]{2,1,0:T(8,128)(2,1)}, bf16[4,384,1152]{2,1,0:T(8,128)(2,1)}, u32[]{:S(2)}, u32[]{:S(2)}) collective-permute-start(bf16[4,384,1152]{2,1,0:T(8,128)(2,1)} %bitcast.399), channel_id=1, source_target_pairs={{0,16},{16,0},{1,17},{17,1},{2,18},{18,2},{3,19},{19,3},{4,20},{20... | collective-permute-start | bytes 10616840 | tf_op jit(solution)/shard_map/ppermute | solution.py:649
  867.7 387.9 %reduce-scatter.8.cloned.1.call-start = ((), (), s32[]{:S(2)}) async-start(), calls=%async_computation.5 | async-start | bytes 5640192 | tf_op jit(solution)/shard_map/reduce_scatter | solution.py:996
  874.7 95.6 %collective-permute-start.37 = (bf16[384,1152]{1,0:T(8,128)(2,1)}, bf16[384,1152]{1,0:T(8,128)(2,1)}, u32[]{:S(2)}, u32[]{:S(2)}) collective-permute-start(bf16[384,1152]{1,0:T(8,128)(2,1)} %fusion.57), channel_id=1, source_target_pairs={{0,16},{16,0},{1,17},{17,1},{2,18},{18,2},{3,19},{19,3},{4,20},{20... | collective-permute-start | bytes 2654216 | tf_op jit(solution)/shard_map/ppermute | solution.py:649
  878.5 91.9 %collective-permute-start.35 = (bf16[384,1152]{1,0:T(8,128)(2,1)}, bf16[384,1152]{1,0:T(8,128)(2,1)}, u32[]{:S(2)}, u32[]{:S(2)}) collective-permute-start(bf16[384,1152]{1,0:T(8,128)(2,1)} %fusion.42), channel_id=1, source_target_pairs={{0,12},{4,0},{8,4},{12,8},{1,13},{5,1},{9,5},{13,9},{2,14},{6,2},{... | collective-permute-start | bytes 2654216 | tf_op jit(solution)/shard_map/ppermute | solution.py:649
  883.3 87.0 %collective-permute-start.34 = (bf16[384,1152]{1,0:T(8,128)(2,1)}, bf16[384,1152]{1,0:T(8,128)(2,1)}, u32[]{:S(2)}, u32[]{:S(2)}) collective-permute-start(bf16[384,1152]{1,0:T(8,128)(2,1)} %fusion.44), channel_id=1, source_target_pairs={{0,12},{4,0},{8,4},{12,8},{1,13},{5,1},{9,5},{13,9},{2,14},{6,2},{... | collective-permute-start | bytes 2654216 | tf_op jit(solution)/shard_map/ppermute | solution.py:649
  972.9 85.6 %collective-permute-start.40 = (bf16[384,1152]{1,0:T(8,128)(2,1)}, bf16[384,1152]{1,0:T(8,128)(2,1)}, u32[]{:S(2)}, u32[]{:S(2)}) collective-permute-start(bf16[384,1152]{1,0:T(8,128)(2,1)} %fusion.37), channel_id=1, source_target_pairs={{0,12},{4,0},{8,4},{12,8},{1,13},{5,1},{9,5},{13,9},{2,14},{6,2},{... | collective-permute-start | bytes 2654216 | tf_op jit(solution)/shard_map/ppermute | solution.py:649
  976.6 81.9 %collective-permute-start.39 = (bf16[384,1152]{1,0:T(8,128)(2,1)}, bf16[384,1152]{1,0:T(8,128)(2,1)}, u32[]{:S(2)}, u32[]{:S(2)}) collective-permute-start(bf16[384,1152]{1,0:T(8,128)(2,1)} %fusion.39), channel_id=1, source_target_pairs={{0,12},{4,0},{8,4},{12,8},{1,13},{5,1},{9,5},{13,9},{2,14},{6,2},{... | collective-permute-start | bytes 2654216 | tf_op jit(solution)/shard_map/ppermute | solution.py:649
  979.8 78.7 %collective-permute-start.38 = (bf16[384,1152]{1,0:T(8,128)(2,1)}, bf16[384,1152]{1,0:T(8,128)(2,1)}, u32[]{:S(2)}, u32[]{:S(2)}) collective-permute-start(bf16[384,1152]{1,0:T(8,128)(2,1)} %fusion.41), channel_id=1, source_target_pairs={{0,12},{4,0},{8,4},{12,8},{1,13},{5,1},{9,5},{13,9},{2,14},{6,2},{... | collective-permute-start | bytes 2654216 | tf_op jit(solution)/shard_map/ppermute | solution.py:649
  1061.5 59.9 %collective-permute-start.42 = (bf16[384,1152]{1,0:T(8,128)(2,1)}, bf16[384,1152]{1,0:T(8,128)(2,1)}, u32[]{:S(2)}, u32[]{:S(2)}) collective-permute-start(bf16[384,1152]{1,0:T(8,128)(2,1)} %fusion.34), channel_id=1, source_target_pairs={{0,12},{4,0},{8,4},{12,8},{1,13},{5,1},{9,5},{13,9},{2,14},{6,2},{... | collective-permute-start | bytes 2654216 | tf_op jit(solution)/shard_map/ppermute | solution.py:649
  1066.7 54.7 %collective-permute-start.41 = (bf16[384,1152]{1,0:T(8,128)(2,1)}, bf16[384,1152]{1,0:T(8,128)(2,1)}, u32[]{:S(2)}, u32[]{:S(2)}) collective-permute-start(bf16[384,1152]{1,0:T(8,128)(2,1)} %fusion.36), channel_id=1, source_target_pairs={{0,12},{4,0},{8,4},{12,8},{1,13},{5,1},{9,5},{13,9},{2,14},{6,2},{... | collective-permute-start | bytes 2654216 | tf_op jit(solution)/shard_map/ppermute | solution.py:649
  1079.3 39.9 %collective-permute-start.50 = (bf16[2,2,2,2,72,256]{5,4,3,2,1,0:T(8,128)(2,1)}, bf16[2,2,2,2,72,256]{5,4,3,2,1,0:T(8,128)(2,1)}, u32[]{:S(2)}, u32[]{:S(2)}) collective-permute-start(bf16[2,2,2,2,72,256]{5,4,3,2,1,0:T(8,128)(2,1)} %fusion.63), channel_id=1, source_target_pairs={{0,1},{1,0},{2,3},{3,2},{4,5},{5,4},{6,7},{7,6},{8,9},{9,8},{10,11... | collective-permute-start | bytes 1769480 | tf_op jit(solution)/shard_map/ppermute | solution.py:654
  1120.6 40.4 %collective-permute-start.51 = (bf16[2,2,2,72,256]{4,3,2,1,0:T(8,128)(2,1)S(1)}, bf16[2,2,2,72,256]{4,3,2,1,0:T(8,128)(2,1)S(1)}, u32[]{:S(2)}, u32[]{:S(2)}) collective-permute-start(bf16[2,2,2,72,256]{4,3,2,1,0:T(8,128)(2,1)S(1)} %fusion.70), channel_id=1, source_target_pairs={{0,2},{1,3},{2,0},{3,1},{4,6},{5,7},{6,4},{7,5},{8,10},{9,11},{10,... | collective-permute-start | bytes 884744 | tf_op jit(solution)/shard_map/ppermute | solution.py:654
  1124.6 122.6 %collective-permute-start.55 = (bf16[384,1152]{1,0:T(8,128)(2,1)}, bf16[384,1152]{1,0:T(8,128)(2,1)}, u32[]{:S(2)}, u32[]{:S(2)}) collective-permute-start(bf16[384,1152]{1,0:T(8,128)(2,1)} %fusion.28), channel_id=1, source_target_pairs={{0,12},{4,0},{8,4},{12,8},{1,13},{5,1},{9,5},{13,9},{2,14},{6,2},{... | collective-permute-start | bytes 2654216 | tf_op jit(solution)/shard_map/ppermute | solution.py:649
  1162.6 51.0 %collective-permute-start.52 = (bf16[2,2,72,256]{3,2,1,0:T(8,128)(2,1)}, bf16[2,2,72,256]{3,2,1,0:T(8,128)(2,1)S(1)}, u32[]{:S(2)}, u32[]{:S(2)}) collective-permute-start(bf16[2,2,72,256]{3,2,1,0:T(8,128)(2,1)} %fusion.75), channel_id=1, source_target_pairs={{0,16},{16,0},{1,17},{17,1},{2,18},{18,2},{3,19},{19,3},{4,20},{20... | collective-permute-start | bytes 442376 | tf_op jit(solution)/shard_map/ppermute | solution.py:654
  1195.9 19.3 %collective-permute-start.44 = (f32[180,128]{1,0:T(8,128)S(1)}, f32[180,128]{1,0:T(8,128)S(1)}, u32[]{:S(2)}, u32[]{:S(2)}) collective-permute-start(f32[180,128]{1,0:T(8,128)S(1)} %maximum_bitcast_fusion.5), channel_id=1, source_target_pairs={{0,16},{16,0},{1,17},{17,1},{2,18},{18,2},{3,19},{19,3},{4,20},{20... | collective-permute-start | bytes 276488 | tf_op jit(solution)/shard_map/ppermute | solution.py:654
  1215.2 13.0 %collective-permute-start.45 = (f32[180,128]{1,0:T(8,128)S(1)}, f32[180,128]{1,0:T(8,128)S(1)}, u32[]{:S(2)}, u32[]{:S(2)}) collective-permute-start(f32[180,128]{1,0:T(8,128)S(1)} %fusion.169), channel_id=1, source_target_pairs={{0,4},{4,0},{8,12},{12,8},{1,5},{5,1},{9,13},{13,9},{2,6},{6,2},{1... | collective-permute-start | bytes 276488 | tf_op jit(solution)/shard_map/ppermute | solution.py:654
  (105 other events, 1925.1 us)
Sparse Core Ops, SparseCore 0:
  14.8 111.7 all-gather.5
  129.4 137.7 all-gather.3
  779.9 153.6 reduce-scatter.9
  937.5 132.1 reduce-scatter.5
  1169.8 85.6 reduce-scatter.7

commit v5 on v4

--- a/solution.py
+++ b/solution.py
@@ -806,14 +806,14 @@
     used = small.shape[1]
     small = jnp.pad(small, ((0, 0), (0, PACK - used)))
     entry = lax.all_gather(jnp.concatenate([in_proj.T, small.reshape(-1, D)], axis=0), ALL, axis=0, tiled=False)
+    shard = jnp.stack([m for e in range(expert_up.shape[0]) for m in (expert_up[e].T, expert_down[e])])
+    shard, entry = held_for(shard, entry)
     middle = entry.shape[0] // 2
     conv_full = entry[:middle, :own].reshape(DI, D)
     gate_full = entry[middle:, :own].reshape(DI, D)
     small = entry[:, own:].reshape(DI, PACK)
     out_full = lax.all_gather(out_proj, ALL, axis=0, tiled=True)
     local_experts = expert_up.shape[0]
-    shard = jnp.stack([m for e in range(local_experts) for m in (expert_up[e].T, expert_down[e])])
-    shard, conv_full = held_for(shard, conv_full)
     gather = Gather(shard)
     gather.step()
 
@@ -907,7 +907,7 @@
         done, *rest = run_expert(theirs, e, *for_weights[e][:2], partial[e])
         for_weights[e] += rest
         if e > 0:
-            done, returned = held_for(done, returned)
+            for_weights[e], returned = held_for(for_weights[e], returned)
         returned.append(exchange([part for part in done.reshape(peers, capacity, 2 * D)]))
     weight_grads = []
     for e in range(local_experts):
@@ -966,7 +966,7 @@
         )
         parts.append((gxs, dtproj_part, galog, gvec))
     grad_proj = jnp.concatenate([grad_delta_in, gbc], axis=1).astype(b16)
-    grad_proj, gate_own = held_for(hold_all(grad_proj, reduces), gate_own)
+    grad_proj = hold_all(grad_proj, reduces)
     xproj_grad = dot(xs, grad_proj, TN)
     zeros = jnp.zeros((CONVK + 1, DI), f32)
     vecs = jnp.concatenate([p[3] for p in parts], axis=1)
@@ -987,13 +987,12 @@
     gexts, conv_parts, conv_grads = [], [], []
     for part in range(SPLITS):
         gext, gvec = run_conv(parts[part][0], grad_proj, xproj_full, ext, conv_w, cbias, same_wide, part)
-        if part == SPLITS - 1:
-            gext = hold_all(gext, reduces)
         conv_parts.append(dot(gext, normed_one, TN, b16))
         gexts.append(gext)
         conv_grads.append(gvec)
-    conv_all, gexts = held_for(jnp.concatenate(conv_parts, axis=0), gexts)
+    conv_all, gexts, gate_own = held_for(jnp.concatenate(conv_parts, axis=0), gexts, gate_own)
     conv_own = lax.psum_scatter(conv_all, ("seq", "expert"), scatter_dimension=0, tiled=True).astype(f32)
+    gexts = hold_all(gexts, reduces)
     grad_normed = sum(dot(gexts[k], conv_full[k * width : (k + 1) * width], NN) for k in range(SPLITS))
     over = grad_normed[:skip_rows].reshape(halo, seqs, HALVES, D)
     from_next = shifted(over[:, :, 0], "seq", -1)

time: 1290 us -> 1230 us (0.953)
  starting transfers between devices: 124 us -> 86.7 us
    ppermute x25, starting transfers between devices: 80.6 us -> 38.7 us  [ring(): lax.ppermute(value, axis, [(i, (i + step) % count) for i in range(count)])]
    ppermute x25, waiting for transfers between devices: 56.9 us -> 81.1 us  [ring(): lax.ppermute(value, axis, [(i, (i + step) % count) for i in range(count)])]
    ppermute x22, waiting for transfers between devices: 80.5 us -> 65 us  [partner(): return lax.ppermute(value, axis, [(i, i ^ bits) for i in range(count)])]
    unnamed x199 -> x205, local copies, waits for them, and re-layouts: 26 us -> 25.3 us
  transfers between devices with their start and end apart: 61 -> 61, of which waited for: 23 -> 20; matrix products, arithmetic and copies ran while one was open for 26% -> 26% of each run, Pallas kernels for 38% -> 39%
where the time goes in v5:
time: 1230 us; the launch traced here: 1220 us
  Pallas kernels  506 us (41%)
  waiting for transfers between devices  226 us (18%)
  local copies, waits for them, and re-layouts  148 us (12%)
  matrix products  125 us (10%)
  other arithmetic  117 us (10%)
  starting transfers between devices  86.7 us (7%)
  between operations  16.1 us (1%)
    pallas_call x3, Pallas kernels, run_back(): pl.pallas_call(back_kernel, grid=(width // LANES,), in_specs=[col(rows),...  207 us
    dot_general x28, matrix products, dot(): lax.dot_general(left, right, (dims, ((), ())), preferred_element_type=out)  125 us
    pallas_call x4, Pallas kernels, run_expert(): pl.pallas_call(functools.partial(expert_kernel, blocks, peers, final), gr...  93.4 us
    ppermute x25, waiting for transfers between devices, ring(): lax.ppermute(value, axis, [(i, (i + step) % count) for i in range(count)])  81.1 us
    ppermute x22, waiting for transfers between devices, partner(): return lax.ppermute(value, axis, [(i, i ^ bits) for i in range(count)])  65 us
    all_gather x1, waiting for transfers between devices, local(): lax.all_gather(jnp.concatenate([in_proj.T, small.reshape(-1, D)], axis=0)...  58.9 us
    pallas_call x1, Pallas kernels, run_out(): pl.pallas_call(out_kernel, grid=(DI // LANES,), in_specs=[col_spec(rows),...  53.5 us
    pallas_call x1, Pallas kernels, run_end(): pl.pallas_call(end_kernel, grid=(DI // LANES,), in_specs=[col_spec(rows),...  44 us
  transfers between devices with their start and end apart: 61, of which 20 were waited for; matrix products, arithmetic and copies ran while one was open for 26% of the time, Pallas kernels for 39%

profile of v5, /device:TPU:0, one launch (start us, length us, event | category | flops | bytes accessed | tf_op | source)
XLA Modules:
  0.0 1224.7 jit_solution(1218798589832136689)
XLA Ops:
  15.6 4.9 collective-permute-start
  25.9 5.6 copy.328
  31.5 5.0 reshape.560
  59.8 5.1 reshape.553
  67.6 58.9 %all-gather.6.cloned.1.call-done = bf16[5120,1152]{1,0:T(8,128)(2,1)} async-done(((bf16[160,1152]{1,0:T(8,128)(2,1)}), bf16[5120,1152]{1,0:T(8,128)(2,1)}) %all-gather.6.cloned.1.call-update) | async-done | bytes 11796496 | tf_op jit(solution)/shard_map/all_gather | solution.py:808
  129.0 8.9 fusion.113
  145.9 9.8 fusion.131.ext_ref
  155.7 7.2 multiply_convert_fusion.xs_ref
  171.1 44.0 %end.1 = (f32[1024,2304]{1,0:T(8,128)}, f32[16,8,2304]{2,1,0:T(8,128)}, f32[8,2304]{1,0:T(8,128)}) custom-call(bf16[1024,2304]{1,0:T(8,128)(2,1)} %copy-done.3, bf16[1024,72]{1,0:T(8,128)(2,1)} %copy.275.din_ref, bf16[2304,72]{1,0:T(8,128)(2,1)} %slice.613.dtw_ref, bf16[1,2304]{1,0:T(2,128)(2,1)} %get-tuple-element.513.dtb_ref, ...), custom_call_target="tpu_custom_call" | custom-call | flops 301989888 | bytes 150994944 | tf_op jit(solution)/shard_map/end/pallas_call | solution.py:336
  216.2 26.5 %collective-permute-done.2.refs_1_ = bf16[4,384,1152]{2,1,0:T(8,128)(2,1)} collective-permute-done((bf16[4,384,1152]{2,1,0:T(8,128)(2,1)}, bf16[4,384,1152]{2,1,0:T(8,128)(2,1)}, u32[]{:S(2)}, u32[]{:S(2)}) %collective-permute-start.2) | collective-permute-done | bytes 3538976 | tf_op jit(solution)/shard_map/ppermute | solution.py:649
  250.7 11.4 fusion.22.z_ref
  265.2 6.2 collective-permute-done.8
  272.6 5.1 collective-permute-start.9
  292.1 53.5 %out.1 = (bf16[1024,2304]{1,0:T(8,128)(2,1)}, bf16[1024,2304]{1,0:T(8,128)(2,1)}, f32[8,16,8,2304]{3,2,1,0:T(8,128)}) custom-call(bf16[1024,2304]{1,0:T(8,128)(2,1)} %copy-done.3, f32[1024,2304]{1,0:T(8,128)} %get-tuple-element.196.delta_ref, bf16[16,2304]{1,0:T(8,128)(2,1)} %slice.615.alog_ref, f32[1024,32]{1,0:T(8,128)} %copy.276.bc_ref, ...), custom_call_target="tpu_custom_call" | custom-call | flops 301989888 | bytes 188743680 | tf_op jit(solution)/shard_map/out/pallas_call | solution.py:355
  345.6 10.6 multiply_reduce_fusion.5
  360.1 6.5 collective-permute-done.10.refs_2_
  377.4 22.5 %collective-permute-done.13.refs_6_ = bf16[2,192,1280]{2,1,0:T(8,128)(2,1)S(1)} collective-permute-done((bf16[2,192,1280]{2,1,0:T(8,128)(2,1)S(1)}, bf16[2,192,1280]{2,1,0:T(8,128)(2,1)S(1)}, u32[]{:S(2)}, u32[]{:S(2)}) %collective-permute-start.13) | collective-permute-done | bytes 983072 | tf_op jit(solution)/shard_map/ppermute | solution.py:654
  399.8 20.7 %collective-permute-done.14.refs_7_ = bf16[2,192,1280]{2,1,0:T(8,128)(2,1)S(1)} collective-permute-done((bf16[2,192,1280]{2,1,0:T(8,128)(2,1)S(1)}, bf16[2,192,1280]{2,1,0:T(8,128)(2,1)S(1)}, u32[]{:S(2)}, u32[]{:S(2)}) %collective-permute-start.14) | collective-permute-done | bytes 983072 | tf_op jit(solution)/shard_map/ppermute | solution.py:654
  420.5 23.7 %collective-permute-done.15.refs_3_ = bf16[4,384,1152]{2,1,0:T(8,128)(2,1)S(1)} collective-permute-done((bf16[4,384,1152]{2,1,0:T(8,128)(2,1)}, bf16[4,384,1152]{2,1,0:T(8,128)(2,1)S(1)}, u32[]{:S(2)}, u32[]{:S(2)}) %collective-permute-start.15) | collective-permute-done | bytes 3538976 | tf_op jit(solution)/shard_map/ppermute | solution.py:649
  448.7 23.8 %expert.4 = (bf16[768,2304]{1,0:T(8,128)(2,1)}, bf16[768,1152]{1,0:T(8,128)(2,1)}, bf16[768,1152]{1,0:T(8,128)(2,1)}, bf16[768,1536]{1,0:T(8,128)(2,1)}, bf16[768,1536]{1,0:T(8,128)(2,1)}) custom-call(bf16[4,384,1152]{2,1,0:T(8,128)(2,1)} %pad_maximum_fusion.2.refs_0_, bf16[4,384,1152]{2,1,0:T(8,128)(2,1)} %collective-permute-done.2.refs_1_, ...), custom_call_target="tpu_custom_call" | custom-call | flops 1000 | bytes 1000 | tf_op jit(solution)/shard_map/expert/pallas_call | solution.py:572
  472.5 23.3 %expert.5 = (bf16[768,2304]{1,0:T(8,128)(2,1)}, bf16[768,1152]{1,0:T(8,128)(2,1)}, bf16[768,1152]{1,0:T(8,128)(2,1)}, bf16[768,1536]{1,0:T(8,128)(2,1)}, bf16[768,1536]{1,0:T(8,128)(2,1)}) custom-call(bf16[4,384,1152]{2,1,0:T(8,128)(2,1)} %pad_maximum_fusion.2.refs_0_, bf16[4,384,1152]{2,1,0:T(8,128)(2,1)} %collective-permute-done.2.refs_1_, ...), custom_call_target="tpu_custom_call" | custom-call | flops 1000 | bytes 1000 | tf_op jit(solution)/shard_map/expert/pallas_call | solution.py:572
  501.5 23.0 %expert.7 = (bf16[768,2304]{1,0:T(8,128)(2,1)}, bf16[768,1536]{1,0:T(8,128)(2,1)}, bf16[768,1536]{1,0:T(8,128)(2,1)}) custom-call(bf16[4,384,1152]{2,1,0:T(8,128)(2,1)} %collective-permute-done.3.refs_0_, bf16[4,384,1152]{2,1,0:T(8,128)(2,1)} %collective-permute-done.11.refs_1_, bf16[4,384,1152]{2,1,0:T(8,128)(2,1)} %copy-done.6, ...), custom_call_target="tpu_custom_call" | custom-call | flops 1000 | bytes 1000 | tf_op jit(solution)/shard_map/expert/pallas_call | solution.py:572
  530.1 23.3 %expert.6 = (bf16[768,2304]{1,0:T(8,128)(2,1)}, bf16[768,1536]{1,0:T(8,128)(2,1)}, bf16[768,1536]{1,0:T(8,128)(2,1)}) custom-call(bf16[4,384,1152]{2,1,0:T(8,128)(2,1)} %collective-permute-done.3.refs_0_, bf16[4,384,1152]{2,1,0:T(8,128)(2,1)} %collective-permute-done.11.refs_1_, bf16[4,384,1152]{2,1,0:T(8,128)(2,1)} %copy-done.6, ...), custom_call_target="tpu_custom_call" | custom-call | flops 1000 | bytes 1000 | tf_op jit(solution)/shard_map/expert/pallas_call | solution.py:572
  560.8 10.7 weight.4
  571.5 10.8 weight.5
  582.3 10.8 weight.7
  593.1 10.8 weight.6
  614.5 7.8 fusion.8
  641.0 8.1 fusion.53
  650.3 11.9 fusion.55.gb_ref
  662.2 11.3 collective-permute-done.25
  681.0 38.1 %first.1 = (f32[16,8,2304]{2,1,0:T(8,128)}, bf16[1024,2304]{1,0:T(8,128)(2,1)}, f32[1024,2304]{1,0:T(8,128)}) custom-call(f32[1024,2304]{1,0:T(8,128)} %get-tuple-element.196.delta_ref, bf16[16,2304]{1,0:T(8,128)(2,1)} %slice.615.alog_ref, f32[1024,32]{1,0:T(8,128)} %copy.276.bc_ref, f32[1024,128]{1,0:T(8,128)} %broadcast_in_dim.18.cut_ref, ...), custom_call_target="tpu_custom_call" | custom-call | flops 1000 | bytes 1000 | tf_op jit(solution)/shard_map/first/pallas_call | solution.py:378
  719.1 8.6 collective-permute-done.26
  736.6 10.3 fusion.20
  750.1 11.1 fusion.132
  763.4 9.3 collective-permute-done.30
  790.6 69.1 %back.3 = (f32[1024,768]{1,0:T(8,128)}, bf16[1024,768]{1,0:T(8,128)(2,1)}, f32[16,768]{1,0:T(8,128)}, f32[8,768]{1,0:T(8,128)}, f32[1024,128]{1,0:T(8,128)}) custom-call(bf16[1024,2304]{1,0:T(8,128)(2,1)} %copy-done.3, f32[1024,2304]{1,0:T(8,128)} %get-tuple-element.196.delta_ref, bf16[16,2304]{1,0:T(8,128)(2,1)} %slice.615.alog_ref, ...), custom_call_target="tpu_custom_call" | custom-call | flops 100663296 | bytes 213909504 | tf_op jit(solution)/shard_map/back/pallas_call | solution.py:405
  882.2 5.9 reshape.565
  892.4 69.0 %back.4 = (f32[1024,768]{1,0:T(8,128)}, bf16[1024,768]{1,0:T(8,128)(2,1)}, f32[16,768]{1,0:T(8,128)}, f32[8,768]{1,0:T(8,128)}, f32[1024,128]{1,0:T(8,128)}) custom-call(bf16[1024,2304]{1,0:T(8,128)(2,1)} %copy-done.3, f32[1024,2304]{1,0:T(8,128)} %get-tuple-element.196.delta_ref, bf16[16,2304]{1,0:T(8,128)(2,1)} %slice.615.alog_ref, ...), custom_call_target="tpu_custom_call" | custom-call | flops 100663296 | bytes 213909504 | tf_op jit(solution)/shard_map/back/pallas_call | solution.py:405
  976.6 68.9 %back.5 = (f32[1024,768]{1,0:T(8,128)}, bf16[1024,768]{1,0:T(8,128)(2,1)}, f32[16,768]{1,0:T(8,128)}, f32[8,768]{1,0:T(8,128)}, f32[1024,128]{1,0:T(8,128)}) custom-call(bf16[1024,2304]{1,0:T(8,128)(2,1)} %copy-done.3, f32[1024,2304]{1,0:T(8,128)} %get-tuple-element.196.delta_ref, bf16[16,2304]{1,0:T(8,128)(2,1)} %slice.615.alog_ref, ...), custom_call_target="tpu_custom_call" | custom-call | flops 100663296 | bytes 213909504 | tf_op jit(solution)/shard_map/back/pallas_call | solution.py:405
  1067.2 8.9 conv.3
  1076.1 8.8 conv.4
  1084.9 8.9 conv.5
  1144.0 6.6 multiply_reduce_fusion.2
  1155.2 6.7 reshape.574
  1162.0 5.5 copy.253
  1183.2 7.4 collective-permute-done.46
  1210.7 5.2 copy.267
  (535 shorter events, 348.6 us)
Async XLA Ops:
  7.2 119.4 %all-gather.6.cloned.1.call-start = ((), (), s32[]{:S(2)}) async-start(), calls=%async_computation.6 | async-start | bytes 12165120 | tf_op jit(solution)/shard_map/all_gather | solution.py:808
  14.6 331.0 %all-gather.4.cloned.1.call-start = ((), (), s32[]{:S(2)}) async-start(), calls=%async_computation.3 | async-start | bytes 5474304 | tf_op jit(solution)/shard_map/all_gather | solution.py:815
  15.6 40.0 %collective-permute-start = (bf16[4,3,1152]{2,1,0:T(4,128)(2,1)S(1)}, bf16[4,3,1152]{2,1,0:T(4,128)(2,1)S(1)}, u32[]{:S(2)}, u32[]{:S(2)}) collective-permute-start(bf16[4,3,1152]{2,1,0:T(4,128)(2,1)S(1)} %slice.456), channel_id=1, source_target_pairs={{0,4},{4,8},{8,12},{1,5},{5,9},{9,13},{2,6},{6,10},{10,14},{3,7},{... | collective-permute-start | bytes 82952 | tf_op jit(solution)/shard_map/ppermute | solution.py:34
  21.3 32.3 %collective-permute-start.1 = (f32[4,3]{1,0:T(4,128)S(1)}, f32[4,3]{1,0:T(4,128)S(1)}, u32[]{:S(2)}, u32[]{:S(2)}) collective-permute-start(f32[4,3]{1,0:T(4,128)S(1)} %slice_convert_fusion.4), channel_id=1, source_target_pairs={{0,4},{4,8},{8,12},{1,5},{5,9},{9,13},{2,6},{6,10},{10,14},{3,7},{... | collective-permute-start | bytes 152 | tf_op jit(solution)/shard_map/ppermute | solution.py:34
  43.6 199.2 %collective-permute-start.4 = (bf16[2,192,1152]{2,1,0:T(8,128)(2,1)}, bf16[2,192,1152]{2,1,0:T(8,128)(2,1)}, u32[]{:S(2)}, u32[]{:S(2)}) collective-permute-start(bf16[2,192,1152]{2,1,0:T(8,128)(2,1)} %bitcast.27), channel_id=1, source_target_pairs={{0,1},{1,0},{2,3},{3,2},{4,5},{5,4},{6,7},{7,6},{8,9},{9,8},{10,11... | collective-permute-start | bytes 2654216 | tf_op jit(solution)/shard_map/ppermute | solution.py:654
  43.6 199.2 %collective-permute-start.5 = (bf16[2,192,1152]{2,1,0:T(8,128)(2,1)}, bf16[2,192,1152]{2,1,0:T(8,128)(2,1)}, u32[]{:S(2)}, u32[]{:S(2)}) collective-permute-start(bf16[2,192,1152]{2,1,0:T(8,128)(2,1)} %bitcast.28), channel_id=1, source_target_pairs={{0,2},{1,3},{2,0},{3,1},{4,6},{5,7},{6,4},{7,5},{8,10},{9,11},{10,... | collective-permute-start | bytes 2654216 | tf_op jit(solution)/shard_map/ppermute | solution.py:654
  45.1 197.7 %collective-permute-start.6 = (bf16[2,192,1152]{2,1,0:T(8,128)(2,1)}, bf16[2,192,1152]{2,1,0:T(8,128)(2,1)}, u32[]{:S(2)}, u32[]{:S(2)}) collective-permute-start(bf16[2,192,1152]{2,1,0:T(8,128)(2,1)} %bitcast.29), channel_id=1, source_target_pairs={{0,3},{1,2},{2,1},{3,0},{4,7},{5,6},{6,5},{7,4},{8,11},{9,10},{10,... | collective-permute-start | bytes 2654216 | tf_op jit(solution)/shard_map/ppermute | solution.py:654
  45.5 919.8 %reduce-scatter.10.cloned.1.call-start = ((), (), s32[]{:S(2)}) async-start(), calls=%async_computation.7 | async-start | bytes 5474304
  137.9 104.8 %collective-permute-start.2 = (bf16[4,384,1152]{2,1,0:T(8,128)(2,1)}, bf16[4,384,1152]{2,1,0:T(8,128)(2,1)}, u32[]{:S(2)}, u32[]{:S(2)}) collective-permute-start(bf16[4,384,1152]{2,1,0:T(8,128)(2,1)} %pad_maximum_fusion.2.refs_0_), channel_id=1, source_target_pairs={{0,4},{4,8},{8,12},{12,0},{1,5},{5,9},{9,13},{13,1},{2,6},{6,10},{... | collective-permute-start | bytes 10616840 | tf_op jit(solution)/shard_map/ppermute | solution.py:649
  138.8 104.0 %collective-permute-start.3 = (bf16[4,384,1152]{2,1,0:T(8,128)(2,1)}, bf16[4,384,1152]{2,1,0:T(8,128)(2,1)}, u32[]{:S(2)}, u32[]{:S(2)}) collective-permute-start(bf16[4,384,1152]{2,1,0:T(8,128)(2,1)} %pad_maximum_fusion.2.refs_0_), channel_id=1, source_target_pairs={{0,16},{16,0},{1,17},{17,1},{2,18},{18,2},{3,19},{19,3},{4,20},{20... | collective-permute-start | bytes 10616840 | tf_op jit(solution)/shard_map/ppermute | solution.py:649
  249.3 12.8 %collective-permute-start.7 = (bf16[16,4,2304]{2,1,0:T(4,128)(2,1)S(1)}, bf16[16,4,2304]{2,1,0:T(4,128)(2,1)S(1)}, u32[]{:S(2)}, u32[]{:S(2)}) collective-permute-start(bf16[16,4,2304]{2,1,0:T(4,128)(2,1)S(1)} %fusion.107), channel_id=1, source_target_pairs={{0,4},{4,8},{8,12},{1,5},{5,9},{9,13},{2,6},{6,10},{10,14},{3,7},{... | collective-permute-start | bytes 884744 | tf_op jit(solution)/shard_map/ppermute | solution.py:34
  288.0 78.6 %collective-permute-start.10 = (bf16[4,384,1152]{2,1,0:T(8,128)(2,1)}, bf16[4,384,1152]{2,1,0:T(8,128)(2,1)}, u32[]{:S(2)}, u32[]{:S(2)}) collective-permute-start(bf16[4,384,1152]{2,1,0:T(8,128)(2,1)} %collective-permute-done.2.refs_1_), channel_id=1, source_target_pairs={{0,4},{4,8},{8,12},{12,0},{1,5},{5,9},{9,13},{13,1},{2,6},{6,10},{... | collective-permute-start | bytes 10616840 | tf_op jit(solution)/shard_map/ppermute | solution.py:649
  290.5 76.5 %collective-permute-start.11 = (bf16[4,384,1152]{2,1,0:T(8,128)(2,1)}, bf16[4,384,1152]{2,1,0:T(8,128)(2,1)}, u32[]{:S(2)}, u32[]{:S(2)}) collective-permute-start(bf16[4,384,1152]{2,1,0:T(8,128)(2,1)} %collective-permute-done.2.refs_1_), channel_id=1, source_target_pairs={{0,16},{16,0},{1,17},{17,1},{2,18},{18,2},{3,19},{19,3},{4,20},{20... | collective-permute-start | bytes 10616840 | tf_op jit(solution)/shard_map/ppermute | solution.py:649
  367.0 77.3 %collective-permute-start.15 = (bf16[4,384,1152]{2,1,0:T(8,128)(2,1)}, bf16[4,384,1152]{2,1,0:T(8,128)(2,1)S(1)}, u32[]{:S(2)}, u32[]{:S(2)}) collective-permute-start(bf16[4,384,1152]{2,1,0:T(8,128)(2,1)} %collective-permute-done.10.refs_2_), channel_id=1, source_target_pairs={{0,4},{4,8},{8,12},{12,0},{1,5},{5,9},{9,13},{13,1},{2,6},{6,10},{... | collective-permute-start | bytes 10616840 | tf_op jit(solution)/shard_map/ppermute | solution.py:649
  367.3 77.0 %collective-permute-start.16 = (bf16[4,384,1152]{2,1,0:T(8,128)(2,1)}, bf16[4,384,1152]{2,1,0:T(8,128)(2,1)S(1)}, u32[]{:S(2)}, u32[]{:S(2)}) collective-permute-start(bf16[4,384,1152]{2,1,0:T(8,128)(2,1)} %collective-permute-done.10.refs_2_), channel_id=1, source_target_pairs={{0,16},{16,0},{1,17},{17,1},{2,18},{18,2},{3,19},{19,3},{4,20},{20... | collective-permute-start | bytes 10616840 | tf_op jit(solution)/shard_map/ppermute | solution.py:649
  374.7 25.1 %collective-permute-start.13 = (bf16[2,192,1280]{2,1,0:T(8,128)(2,1)S(1)}, bf16[2,192,1280]{2,1,0:T(8,128)(2,1)S(1)}, u32[]{:S(2)}, u32[]{:S(2)}) collective-permute-start(bf16[2,192,1280]{2,1,0:T(8,128)(2,1)S(1)} %bitcast.377), channel_id=1, source_target_pairs={{0,2},{1,3},{2,0},{3,1},{4,6},{5,7},{6,4},{7,5},{8,10},{9,11},{10,... | collective-permute-start | bytes 2949128 | tf_op jit(solution)/shard_map/ppermute | solution.py:654
  377.2 43.3 %collective-permute-start.14 = (bf16[2,192,1280]{2,1,0:T(8,128)(2,1)S(1)}, bf16[2,192,1280]{2,1,0:T(8,128)(2,1)S(1)}, u32[]{:S(2)}, u32[]{:S(2)}) collective-permute-start(bf16[2,192,1280]{2,1,0:T(8,128)(2,1)S(1)} %bitcast.376), channel_id=1, source_target_pairs={{0,3},{1,2},{2,1},{3,0},{4,7},{5,6},{6,5},{7,4},{8,11},{9,10},{10,... | collective-permute-start | bytes 2949128 | tf_op jit(solution)/shard_map/ppermute | solution.py:654
  445.8 50.1 %collective-permute-start.17 = (bf16[2,384,1152]{2,1,0:T(8,128)(2,1)}, bf16[2,384,1152]{2,1,0:T(8,128)(2,1)}, u32[]{:S(2)}, u32[]{:S(2)}) collective-permute-start(bf16[2,384,1152]{2,1,0:T(8,128)(2,1)} %slice.505), channel_id=1, source_target_pairs={{0,16},{16,0},{1,17},{17,1},{2,18},{18,2},{3,19},{19,3},{4,20},{20... | collective-permute-start | bytes 5308424 | tf_op jit(solution)/shard_map/ppermute | solution.py:649
  448.7 47.2 %collective-permute-start.18 = (bf16[2,384,1152]{2,1,0:T(8,128)(2,1)}, bf16[2,384,1152]{2,1,0:T(8,128)(2,1)}, u32[]{:S(2)}, u32[]{:S(2)}) collective-permute-start(bf16[2,384,1152]{2,1,0:T(8,128)(2,1)} %slice.506), channel_id=1, source_target_pairs={{0,4},{4,8},{8,12},{12,0},{1,5},{5,9},{9,13},{13,1},{2,6},{6,10},{... | collective-permute-start | bytes 5308424 | tf_op jit(solution)/shard_map/ppermute | solution.py:649
  528.1 31.2 %collective-permute-start.19 = (bf16[192,2304]{1,0:T(8,128)(2,1)}, bf16[192,2304]{1,0:T(8,128)(2,1)}, u32[]{:S(2)}, u32[]{:S(2)}) collective-permute-start(bf16[192,2304]{1,0:T(8,128)(2,1)} %get-tuple-element.489), channel_id=1, source_target_pairs={{0,1},{1,0},{2,3},{3,2},{4,5},{5,4},{6,7},{7,6},{8,9},{9,8},{10,11... | collective-permute-start | bytes 2654216 | tf_op jit(solution)/shard_map/ppermute | solution.py:654
  528.1 54.2 %collective-permute-start.20 = (bf16[192,2304]{1,0:T(8,128)(2,1)}, bf16[192,2304]{1,0:T(8,128)(2,1)}, u32[]{:S(2)}, u32[]{:S(2)}) collective-permute-start(bf16[192,2304]{1,0:T(8,128)(2,1)} %get-tuple-element.488), channel_id=1, source_target_pairs={{0,2},{1,3},{2,0},{3,1},{4,6},{5,7},{6,4},{7,5},{8,10},{9,11},{10,... | collective-permute-start | bytes 2654216 | tf_op jit(solution)/shard_map/ppermute | solution.py:654
  530.0 52.3 %collective-permute-start.21 = (bf16[192,2304]{1,0:T(8,128)(2,1)}, bf16[192,2304]{1,0:T(8,128)(2,1)}, u32[]{:S(2)}, u32[]{:S(2)}) collective-permute-start(bf16[192,2304]{1,0:T(8,128)(2,1)} %get-tuple-element.487), channel_id=1, source_target_pairs={{0,3},{1,2},{2,1},{3,0},{4,7},{5,6},{6,5},{7,4},{8,11},{9,10},{10,... | collective-permute-start | bytes 2654216 | tf_op jit(solution)/shard_map/ppermute | solution.py:654
  557.3 46.6 %collective-permute-start.22 = (bf16[192,2304]{1,0:T(8,128)(2,1)}, bf16[192,2304]{1,0:T(8,128)(2,1)}, u32[]{:S(2)}, u32[]{:S(2)}) collective-permute-start(bf16[192,2304]{1,0:T(8,128)(2,1)} %get-tuple-element.493), channel_id=1, source_target_pairs={{0,1},{1,0},{2,3},{3,2},{4,5},{5,4},{6,7},{7,6},{8,9},{9,8},{10,11... | collective-permute-start | bytes 2654216 | tf_op jit(solution)/shard_map/ppermute | solution.py:654
  557.4 46.4 %collective-permute-start.23 = (bf16[192,2304]{1,0:T(8,128)(2,1)}, bf16[192,2304]{1,0:T(8,128)(2,1)}, u32[]{:S(2)}, u32[]{:S(2)}) collective-permute-start(bf16[192,2304]{1,0:T(8,128)(2,1)} %get-tuple-element.492), channel_id=1, source_target_pairs={{0,2},{1,3},{2,0},{3,1},{4,6},{5,7},{6,4},{7,5},{8,10},{9,11},{10,... | collective-permute-start | bytes 2654216 | tf_op jit(solution)/shard_map/ppermute | solution.py:654
  559.3 47.9 %collective-permute-start.24 = (bf16[192,2304]{1,0:T(8,128)(2,1)}, bf16[192,2304]{1,0:T(8,128)(2,1)}, u32[]{:S(2)}, u32[]{:S(2)}) collective-permute-start(bf16[192,2304]{1,0:T(8,128)(2,1)} %get-tuple-element.491), channel_id=1, source_target_pairs={{0,3},{1,2},{2,1},{3,0},{4,7},{5,6},{6,5},{7,4},{8,11},{9,10},{10,... | collective-permute-start | bytes 2654216 | tf_op jit(solution)/shard_map/ppermute | solution.py:654
  631.3 42.2 %collective-permute-start.25 = (bf16[2,384,1152]{2,1,0:T(8,128)(2,1)}, bf16[2,384,1152]{2,1,0:T(8,128)(2,1)}, u32[]{:S(2)}, u32[]{:S(2)}) collective-permute-start(bf16[2,384,1152]{2,1,0:T(8,128)(2,1)} %pad_maximum_fusion.5), channel_id=1, source_target_pairs={{0,12},{4,0},{8,4},{12,8},{1,13},{5,1},{9,5},{13,9},{2,14},{6,2},{... | collective-permute-start | bytes 5308424 | tf_op jit(solution)/shard_map/ppermute | solution.py:649
  649.1 78.6 %collective-permute-start.26 = (bf16[4,384,1152]{2,1,0:T(8,128)(2,1)}, bf16[4,384,1152]{2,1,0:T(8,128)(2,1)}, u32[]{:S(2)}, u32[]{:S(2)}) collective-permute-start(bf16[4,384,1152]{2,1,0:T(8,128)(2,1)} %bitcast.403), channel_id=1, source_target_pairs={{0,16},{16,0},{1,17},{17,1},{2,18},{18,2},{3,19},{19,3},{4,20},{20... | collective-permute-start | bytes 10616840 | tf_op jit(solution)/shard_map/ppermute | solution.py:649
  676.7 42.4 %collective-permute-start.27 = (bf16[2,384,1152]{2,1,0:T(8,128)(2,1)}, bf16[2,384,1152]{2,1,0:T(8,128)(2,1)}, u32[]{:S(2)}, u32[]{:S(2)}) collective-permute-start(bf16[2,384,1152]{2,1,0:T(8,128)(2,1)} %add_convert_fusion.2), channel_id=1, source_target_pairs={{0,12},{4,0},{8,4},{12,8},{1,13},{5,1},{9,5},{13,9},{2,14},{6,2},{... | collective-permute-start | bytes 5308424 | tf_op jit(solution)/shard_map/ppermute | solution.py:649
  735.3 11.6 collective-permute-start.28
  748.7 12.5 %collective-permute-start.29 = (bf16[16,4,2304]{2,1,0:T(4,128)(2,1)S(1)}, bf16[16,4,2304]{2,1,0:T(4,128)(2,1)S(1)}, u32[]{:S(2)}, u32[]{:S(2)}) collective-permute-start(bf16[16,4,2304]{2,1,0:T(4,128)(2,1)S(1)} %add_convert_fusion.4), channel_id=1, source_target_pairs={{4,0},{8,4},{12,8},{5,1},{9,5},{13,9},{6,2},{10,6},{14,10},{7,3},{... | collective-permute-start | bytes 884744 | tf_op jit(solution)/shard_map/ppermute | solution.py:34
  776.9 330.0 %reduce-scatter.6.cloned.1.call-start = ((), (), s32[]{:S(2)}) async-start(), calls=%async_computation.4 | async-start | bytes 5640192 | tf_op jit(solution)/shard_map/reduce_scatter | solution.py:953
  776.9 91.7 %collective-permute-start.32 = (bf16[4,384,1152]{2,1,0:T(8,128)(2,1)}, bf16[4,384,1152]{2,1,0:T(8,128)(2,1)}, u32[]{:S(2)}, u32[]{:S(2)}) collective-permute-start(bf16[4,384,1152]{2,1,0:T(8,128)(2,1)} %bitcast.402), channel_id=1, source_target_pairs={{0,16},{16,0},{1,17},{17,1},{2,18},{18,2},{3,19},{19,3},{4,20},{20... | collective-permute-start | bytes 10616840 | tf_op jit(solution)/shard_map/ppermute | solution.py:649
  781.4 87.3 %collective-permute-start.33 = (bf16[2,384,1152]{2,1,0:T(8,128)(2,1)}, bf16[2,384,1152]{2,1,0:T(8,128)(2,1)S(1)}, u32[]{:S(2)}, u32[]{:S(2)}) collective-permute-start(bf16[2,384,1152]{2,1,0:T(8,128)(2,1)} %add_convert_fusion.1), channel_id=1, source_target_pairs={{0,12},{4,0},{8,4},{12,8},{1,13},{5,1},{9,5},{13,9},{2,14},{6,2},{... | collective-permute-start | bytes 5308424 | tf_op jit(solution)/shard_map/ppermute | solution.py:649
  785.9 82.8 %collective-permute-start.31 = (bf16[384,1152]{1,0:T(8,128)(2,1)}, bf16[384,1152]{1,0:T(8,128)(2,1)}, u32[]{:S(2)}, u32[]{:S(2)}) collective-permute-start(bf16[384,1152]{1,0:T(8,128)(2,1)} %fusion.51), channel_id=1, source_target_pairs={{0,12},{4,0},{8,4},{12,8},{1,13},{5,1},{9,5},{13,9},{2,14},{6,2},{... | collective-permute-start | bytes 2654216 | tf_op jit(solution)/shard_map/ppermute | solution.py:649
  789.7 175.6 %collective-permute-start.36 = (bf16[4,384,1152]{2,1,0:T(8,128)(2,1)}, bf16[4,384,1152]{2,1,0:T(8,128)(2,1)}, u32[]{:S(2)}, u32[]{:S(2)}) collective-permute-start(bf16[4,384,1152]{2,1,0:T(8,128)(2,1)} %bitcast.401), channel_id=1, source_target_pairs={{0,16},{16,0},{1,17},{17,1},{2,18},{18,2},{3,19},{19,3},{4,20},{20... | collective-permute-start | bytes 10616840 | tf_op jit(solution)/shard_map/ppermute | solution.py:649
  870.2 95.2 %collective-permute-start.37 = (bf16[384,1152]{1,0:T(8,128)(2,1)}, bf16[384,1152]{1,0:T(8,128)(2,1)}, u32[]{:S(2)}, u32[]{:S(2)}) collective-permute-start(bf16[384,1152]{1,0:T(8,128)(2,1)} %fusion.59), channel_id=1, source_target_pairs={{0,16},{16,0},{1,17},{17,1},{2,18},{18,2},{3,19},{19,3},{4,20},{20... | collective-permute-start | bytes 2654216 | tf_op jit(solution)/shard_map/ppermute | solution.py:649
  873.9 91.4 %collective-permute-start.35 = (bf16[384,1152]{1,0:T(8,128)(2,1)}, bf16[384,1152]{1,0:T(8,128)(2,1)}, u32[]{:S(2)}, u32[]{:S(2)}) collective-permute-start(bf16[384,1152]{1,0:T(8,128)(2,1)} %fusion.48), channel_id=1, source_target_pairs={{0,12},{4,0},{8,4},{12,8},{1,13},{5,1},{9,5},{13,9},{2,14},{6,2},{... | collective-permute-start | bytes 2654216 | tf_op jit(solution)/shard_map/ppermute | solution.py:649
  878.7 86.6 %collective-permute-start.34 = (bf16[384,1152]{1,0:T(8,128)(2,1)}, bf16[384,1152]{1,0:T(8,128)(2,1)}, u32[]{:S(2)}, u32[]{:S(2)}) collective-permute-start(bf16[384,1152]{1,0:T(8,128)(2,1)} %fusion.50), channel_id=1, source_target_pairs={{0,12},{4,0},{8,4},{12,8},{1,13},{5,1},{9,5},{13,9},{2,14},{6,2},{... | collective-permute-start | bytes 2654216 | tf_op jit(solution)/shard_map/ppermute | solution.py:649
  892.3 311.8 %reduce-scatter.8.cloned.1.call-start = ((), (), s32[]{:S(2)}) async-start(), calls=%async_computation.5 | async-start | bytes 5640192 | tf_op jit(solution)/shard_map/reduce_scatter | solution.py:994
  967.9 86.9 %collective-permute-start.40 = (bf16[384,1152]{1,0:T(8,128)(2,1)}, bf16[384,1152]{1,0:T(8,128)(2,1)}, u32[]{:S(2)}, u32[]{:S(2)}) collective-permute-start(bf16[384,1152]{1,0:T(8,128)(2,1)} %fusion.43), channel_id=1, source_target_pairs={{0,12},{4,0},{8,4},{12,8},{1,13},{5,1},{9,5},{13,9},{2,14},{6,2},{... | collective-permute-start | bytes 2654216 | tf_op jit(solution)/shard_map/ppermute | solution.py:649
  971.8 83.0 %collective-permute-start.39 = (bf16[384,1152]{1,0:T(8,128)(2,1)}, bf16[384,1152]{1,0:T(8,128)(2,1)}, u32[]{:S(2)}, u32[]{:S(2)}) collective-permute-start(bf16[384,1152]{1,0:T(8,128)(2,1)} %fusion.45), channel_id=1, source_target_pairs={{0,12},{4,0},{8,4},{12,8},{1,13},{5,1},{9,5},{13,9},{2,14},{6,2},{... | collective-permute-start | bytes 2654216 | tf_op jit(solution)/shard_map/ppermute | solution.py:649
  975.2 79.6 %collective-permute-start.38 = (bf16[384,1152]{1,0:T(8,128)(2,1)}, bf16[384,1152]{1,0:T(8,128)(2,1)}, u32[]{:S(2)}, u32[]{:S(2)}) collective-permute-start(bf16[384,1152]{1,0:T(8,128)(2,1)} %fusion.47), channel_id=1, source_target_pairs={{0,12},{4,0},{8,4},{12,8},{1,13},{5,1},{9,5},{13,9},{2,14},{6,2},{... | collective-permute-start | bytes 2654216 | tf_op jit(solution)/shard_map/ppermute | solution.py:649
  1057.8 56.4 %collective-permute-start.42 = (bf16[384,1152]{1,0:T(8,128)(2,1)}, bf16[384,1152]{1,0:T(8,128)(2,1)}, u32[]{:S(2)}, u32[]{:S(2)}) collective-permute-start(bf16[384,1152]{1,0:T(8,128)(2,1)} %fusion.40), channel_id=1, source_target_pairs={{0,12},{4,0},{8,4},{12,8},{1,13},{5,1},{9,5},{13,9},{2,14},{6,2},{... | collective-permute-start | bytes 2654216 | tf_op jit(solution)/shard_map/ppermute | solution.py:649
  1063.2 51.0 %collective-permute-start.41 = (bf16[384,1152]{1,0:T(8,128)(2,1)}, bf16[384,1152]{1,0:T(8,128)(2,1)}, u32[]{:S(2)}, u32[]{:S(2)}) collective-permute-start(bf16[384,1152]{1,0:T(8,128)(2,1)} %fusion.42), channel_id=1, source_target_pairs={{0,12},{4,0},{8,4},{12,8},{1,13},{5,1},{9,5},{13,9},{2,14},{6,2},{... | collective-permute-start | bytes 2654216 | tf_op jit(solution)/shard_map/ppermute | solution.py:649
  1117.3 83.6 %collective-permute-start.55 = (bf16[384,1152]{1,0:T(8,128)(2,1)}, bf16[384,1152]{1,0:T(8,128)(2,1)}, u32[]{:S(2)}, u32[]{:S(2)}) collective-permute-start(bf16[384,1152]{1,0:T(8,128)(2,1)} %fusion.34), channel_id=1, source_target_pairs={{0,12},{4,0},{8,4},{12,8},{1,13},{5,1},{9,5},{13,9},{2,14},{6,2},{... | collective-permute-start | bytes 2654216 | tf_op jit(solution)/shard_map/ppermute | solution.py:649
  1121.9 45.6 %collective-permute-start.52 = (bf16[2,2,72,256]{3,2,1,0:T(8,128)(2,1)S(1)}, bf16[2,2,72,256]{3,2,1,0:T(8,128)(2,1)S(1)}, u32[]{:S(2)}, u32[]{:S(2)}) collective-permute-start(bf16[2,2,72,256]{3,2,1,0:T(8,128)(2,1)S(1)} %fusion.77), channel_id=1, source_target_pairs={{0,16},{16,0},{1,17},{17,1},{2,18},{18,2},{3,19},{19,3},{4,20},{20... | collective-permute-start | bytes 442376 | tf_op jit(solution)/shard_map/ppermute | solution.py:654
  1150.6 20.1 %collective-permute-start.44 = (f32[180,128]{1,0:T(8,128)S(1)}, f32[180,128]{1,0:T(8,128)S(1)}, u32[]{:S(2)}, u32[]{:S(2)}) collective-permute-start(f32[180,128]{1,0:T(8,128)S(1)} %maximum_bitcast_fusion.5), channel_id=1, source_target_pairs={{0,16},{16,0},{1,17},{17,1},{2,18},{18,2},{3,19},{19,3},{4,20},{20... | collective-permute-start | bytes 276488 | tf_op jit(solution)/shard_map/ppermute | solution.py:654
  1179.4 11.1 collective-permute-start.46
  (108 other events, 1894.1 us)
Sparse Core Ops, SparseCore 0:
  14.8 111.7 all-gather.5
  129.4 88.4 all-gather.3
  777.0 153.0 reduce-scatter.9
  934.0 132.0 reduce-scatter.5
  1108.7 82.7 reduce-scatter.7

commit v6 on v5

--- a/solution.py
+++ b/solution.py
@@ -50,11 +50,24 @@
     return jnp.moveaxis(split, 2, 0).reshape((seqs * length,) + rest)
 
 
-def from_rows(value, seqs):
-    rest = value.shape[1:]
-    length = value.shape[0] // seqs
-    split = value.reshape((length // HALVES, seqs, HALVES) + rest)
-    return jnp.moveaxis(split, 0, 2).reshape((seqs, length) + rest)
+def from_rows_kernel(rows_ref, out_ref):
+    steps = out_ref.shape[1]
+    for s in range(SUB):
+        out_ref[s] = rows_ref[pl.ds(s, steps, stride=SUB), :].astype(out_ref.dtype)
+
+
+def from_rows(value, seqs, dtype):
+    rows = value.shape[0]
+    steps = rows // SUB
+    out = pl.pallas_call(
+        from_rows_kernel,
+        grid=(D // LANES,),
+        in_specs=[pl.BlockSpec((rows, LANES), lambda c: (0, c))],
+        out_specs=pl.BlockSpec((SUB, steps, LANES), lambda c: (0, 0, c)),
+        out_shape=jax.ShapeDtypeStruct((SUB, steps, D), dtype),
+        name="positions",
+    )(value)
+    return out.reshape(seqs, HALVES * steps, D)
 
 
 def to_ext_rows(value, halo):
@@ -777,8 +790,12 @@
 
 def sum_everywhere(value):
     for axis in ALL:
+        size = lax.axis_size(axis)
+        if size <= 4:
+            value = tree_sum([value] + [partner(value, axis, d) for d in range(1, size)])
+            continue
         bits = 1
-        while bits < lax.axis_size(axis):
+        while bits < size:
             value = value + partner(value, axis, bits)
             bits *= 2
     return value
@@ -922,7 +939,7 @@
     back_rows = jnp.stack(returned).reshape(EXPERTS * capacity, 2 * D)
     combined = dot(placing, back_rows, TN)
     expert_rows, grad_back = combined[:, :D], combined[:, D:]
-    output = (first_sum + gate[:, None] * expert_rows).astype(b16)
+    output = from_rows(first_sum + gate[:, None] * expert_rows, seqs, b16)
 
     grad_gate = jnp.sum(grad_final * expert_rows, axis=-1) * drop
     grad_logits = (grad_gate * gate_raw)[:, None] * (onehot - probs)
@@ -992,8 +1009,8 @@
         conv_grads.append(gvec)
     conv_all, gexts, gate_own = held_for(jnp.concatenate(conv_parts, axis=0), gexts, gate_own)
     conv_own = lax.psum_scatter(conv_all, ("seq", "expert"), scatter_dimension=0, tiled=True).astype(f32)
-    gexts = hold_all(gexts, reduces)
     grad_normed = sum(dot(gexts[k], conv_full[k * width : (k + 1) * width], NN) for k in range(SPLITS))
+    grad_normed = hold_all(grad_normed, reduces)
     over = grad_normed[:skip_rows].reshape(halo, seqs, HALVES, D)
     from_next = shifted(over[:, :, 0], "seq", -1)
     edge = jnp.stack([over[:, :, 1], from_next], axis=2).reshape(skip_rows, D)
@@ -1009,12 +1026,12 @@
     conv_grad = jnp.concatenate(conv_grads, axis=1)[: CONVK + 1]
     flat = jnp.concatenate([gain_one_grad, gain_two_grad, router_grad.reshape(-1), conv_grad.reshape(-1)])
     flat = sum_everywhere(flat.reshape(-1, LANES)).reshape(-1)
+    gain_one_sum, gain_two_sum = flat[:D], flat[D : 2 * D]
     small_sum = small_half.finish()
     is_gate = lax.axis_index("dp") == 1
     gate_own = gate_own.astype(f32)
     in_sum = jnp.where(is_gate, gate_own, conv_own)
     in_sum = in_sum + ring(jnp.where(is_gate, conv_own, gate_own).astype(b16), "dp", 1).astype(f32)
-    gain_one_sum, gain_two_sum = flat[:D], flat[D : 2 * D]
     router_sum = flat[2 * D : (2 + EXPERTS) * D].reshape(D, EXPERTS)
     conv_sum = flat[(2 + EXPERTS) * D :].reshape(CONVK + 1, DI)
     place = (lax.axis_index("dp") * lax.axis_size("seq") + lax.axis_index("seq")) * peers + lax.axis_index("expert")
@@ -1023,8 +1040,8 @@
 
     small_sum = small_sum.T
     return (
-        from_rows(output, seqs),
-        from_rows(grad_tokens, seqs),
+        output,
+        from_rows(grad_tokens, seqs, f32),
         gain_one_sum,
         in_sum.T,
         conv_sum[:CONVK],

time: 1230 us -> 1250 us (1.016)
  local copies, waits for them, and re-layouts: 148 us -> 130 us
  Pallas kernels: 506 us -> 520 us
    ppermute x9, waiting for transfers between devices: 21.1 us -> 53.3 us  [shifted(): lax.ppermute(value, axis, [(source, source + steps) for source in range(f...]
    ppermute x25, waiting for transfers between devices: 81.1 us -> 62.5 us  [ring(): lax.ppermute(value, axis, [(i, (i + step) % count) for i in range(count)])]
    pallas_call x0 -> x2, Pallas kernels: none -> 14.7 us  [from_rows(): pl.pallas_call(from_rows_kernel, grid=(D // LANES,), in_specs=[pl.BlockSp...]
    reshape x2 -> x0, local copies, waits for them, and re-layouts: 12.6 us -> none  [from_rows(): split = value.reshape((length // HALVES, seqs, HALVES) + rest)]
    ppermute x22 -> x24, waiting for transfers between devices: 65 us -> 56.6 us  [partner(): return lax.ppermute(value, axis, [(i, i ^ bits) for i in range(count)])]
  transfers between devices with their start and end apart: 61 -> 63, of which waited for: 20 -> 20; matrix products, arithmetic and copies ran while one was open for 26% -> 25% of each run, Pallas kernels for 39% -> 40%
where the time goes in v6:
time: 1250 us; the launch traced here: 1240 us
  Pallas kernels  520 us (42%)
  waiting for transfers between devices  232 us (19%)
  matrix products  134 us (11%)
  local copies, waits for them, and re-layouts  130 us (10%)
  other arithmetic  118 us (9%)
  starting transfers between devices  89.8 us (7%)
  between operations  16.1 us (1%)
    pallas_call x3, Pallas kernels, run_back(): pl.pallas_call(back_kernel, grid=(width // LANES,), in_specs=[col(rows),...  207 us
    dot_general x28, matrix products, dot(): lax.dot_general(left, right, (dims, ((), ())), preferred_element_type=out)  134 us
    pallas_call x4, Pallas kernels, run_expert(): pl.pallas_call(functools.partial(expert_kernel, blocks, peers, final), gr...  93.2 us
    ppermute x25, waiting for transfers between devices, ring(): lax.ppermute(value, axis, [(i, (i + step) % count) for i in range(count)])  62.5 us
    all_gather x1, waiting for transfers between devices, local(): lax.all_gather(jnp.concatenate([in_proj.T, small.reshape(-1, D)], axis=0)...  59 us
    ppermute x24, waiting for transfers between devices, partner(): return lax.ppermute(value, axis, [(i, i ^ bits) for i in range(count)])  56.6 us
    pallas_call x1, Pallas kernels, run_out(): pl.pallas_call(out_kernel, grid=(DI // LANES,), in_specs=[col_spec(rows),...  53.6 us
    ppermute x9, waiting for transfers between devices, shifted(): lax.ppermute(value, axis, [(source, source + steps) for source in range(f...  53.3 us
  transfers between devices with their start and end apart: 63, of which 20 were waited for; matrix products, arithmetic and copies ran while one was open for 25% of the time, Pallas kernels for 40%

profile of v6, /device:TPU:0, one launch (start us, length us, event | category | flops | bytes accessed | tf_op | source)
XLA Modules:
  0.0 1239.7 jit_solution(4287190764986974910)
XLA Ops:
  25.9 5.6 copy.318
  31.5 5.0 reshape.554
  59.8 5.1 reshape.547
  67.6 59.0 %all-gather.6.cloned.1.call-done = bf16[5120,1152]{1,0:T(8,128)(2,1)} async-done(((bf16[160,1152]{1,0:T(8,128)(2,1)}), bf16[5120,1152]{1,0:T(8,128)(2,1)}) %all-gather.6.cloned.1.call-update) | async-done | bytes 11796496 | tf_op jit(solution)/shard_map/all_gather | solution.py:825
  128.9 8.9 fusion.109
  145.9 9.8 fusion.127.ext_ref
  155.6 7.2 multiply_convert_fusion.xs_ref
  171.1 44.0 %end.1 = (f32[1024,2304]{1,0:T(8,128)}, f32[16,8,2304]{2,1,0:T(8,128)}, f32[8,2304]{1,0:T(8,128)}) custom-call(bf16[1024,2304]{1,0:T(8,128)(2,1)} %copy-done.3, bf16[1024,72]{1,0:T(8,128)(2,1)} %copy.265.din_ref, bf16[2304,72]{1,0:T(8,128)(2,1)} %slice.613.dtw_ref, bf16[1,2304]{1,0:T(2,128)(2,1)} %get-tuple-element.509.dtb_ref, ...), custom_call_target="tpu_custom_call" | custom-call | flops 301989888 | bytes 150994944 | tf_op jit(solution)/shard_map/end/pallas_call | solution.py:349
  216.2 5.2 collective-permute-done.2.refs_1_
  229.3 11.4 fusion.20.z_ref
  243.9 13.2 %collective-permute-done.8 = bf16[16,4,2304]{2,1,0:T(4,128)(2,1)S(1)} collective-permute-done((bf16[16,4,2304]{2,1,0:T(4,128)(2,1)S(1)}, bf16[16,4,2304]{2,1,0:T(4,128)(2,1)S(1)}, u32[]{:S(2)}, u32[]{:S(2)}) %collective-permute-start.8) | collective-permute-done | bytes 294944 | tf_op jit(solution)/shard_map/ppermute | solution.py:34
  258.4 9.0 collective-permute-start.9
  281.6 53.6 %out.1 = (bf16[1024,2304]{1,0:T(8,128)(2,1)}, bf16[1024,2304]{1,0:T(8,128)(2,1)}, f32[8,16,8,2304]{3,2,1,0:T(8,128)}) custom-call(bf16[1024,2304]{1,0:T(8,128)(2,1)} %copy-done.3, f32[1024,2304]{1,0:T(8,128)} %get-tuple-element.194.delta_ref, bf16[16,2304]{1,0:T(8,128)(2,1)} %slice.615.alog_ref, f32[1024,32]{1,0:T(8,128)} %copy.266.bc_ref, ...), custom_call_target="tpu_custom_call" | custom-call | flops 301989888 | bytes 188743680 | tf_op jit(solution)/shard_map/out/pallas_call | solution.py:368
  335.2 10.6 multiply_reduce_fusion.5
  349.7 8.9 collective-permute-done.10.refs_2_
  369.7 22.0 %collective-permute-done.13.refs_6_ = bf16[2,192,1280]{2,1,0:T(8,128)(2,1)S(1)} collective-permute-done((bf16[2,192,1280]{2,1,0:T(8,128)(2,1)S(1)}, bf16[2,192,1280]{2,1,0:T(8,128)(2,1)S(1)}, u32[]{:S(2)}, u32[]{:S(2)}) %collective-permute-start.13) | collective-permute-done | bytes 983072 | tf_op jit(solution)/shard_map/ppermute | solution.py:667
  391.7 20.3 %collective-permute-done.14.refs_7_ = bf16[2,192,1280]{2,1,0:T(8,128)(2,1)S(1)} collective-permute-done((bf16[2,192,1280]{2,1,0:T(8,128)(2,1)S(1)}, bf16[2,192,1280]{2,1,0:T(8,128)(2,1)S(1)}, u32[]{:S(2)}, u32[]{:S(2)}) %collective-permute-start.14) | collective-permute-done | bytes 983072 | tf_op jit(solution)/shard_map/ppermute | solution.py:667
  412.0 24.3 %collective-permute-done.15.refs_3_ = bf16[4,384,1152]{2,1,0:T(8,128)(2,1)S(1)} collective-permute-done((bf16[4,384,1152]{2,1,0:T(8,128)(2,1)}, bf16[4,384,1152]{2,1,0:T(8,128)(2,1)S(1)}, u32[]{:S(2)}, u32[]{:S(2)}) %collective-permute-start.15) | collective-permute-done | bytes 3538976 | tf_op jit(solution)/shard_map/ppermute | solution.py:662
  442.2 23.7 %expert.4 = (bf16[768,2304]{1,0:T(8,128)(2,1)}, bf16[768,1152]{1,0:T(8,128)(2,1)}, bf16[768,1152]{1,0:T(8,128)(2,1)}, bf16[768,1536]{1,0:T(8,128)(2,1)}, bf16[768,1536]{1,0:T(8,128)(2,1)}) custom-call(bf16[4,384,1152]{2,1,0:T(8,128)(2,1)} %pad_maximum_fusion.2.refs_0_, bf16[4,384,1152]{2,1,0:T(8,128)(2,1)} %collective-permute-done.2.refs_1_, ...), custom_call_target="tpu_custom_call" | custom-call | flops 1000 | bytes 1000 | tf_op jit(solution)/shard_map/expert/pallas_call | solution.py:585
  465.9 23.3 %expert.5 = (bf16[768,2304]{1,0:T(8,128)(2,1)}, bf16[768,1152]{1,0:T(8,128)(2,1)}, bf16[768,1152]{1,0:T(8,128)(2,1)}, bf16[768,1536]{1,0:T(8,128)(2,1)}, bf16[768,1536]{1,0:T(8,128)(2,1)}) custom-call(bf16[4,384,1152]{2,1,0:T(8,128)(2,1)} %pad_maximum_fusion.2.refs_0_, bf16[4,384,1152]{2,1,0:T(8,128)(2,1)} %collective-permute-done.2.refs_1_, ...), custom_call_target="tpu_custom_call" | custom-call | flops 1000 | bytes 1000 | tf_op jit(solution)/shard_map/expert/pallas_call | solution.py:585
  494.9 22.9 %expert.7 = (bf16[768,2304]{1,0:T(8,128)(2,1)}, bf16[768,1536]{1,0:T(8,128)(2,1)}, bf16[768,1536]{1,0:T(8,128)(2,1)}) custom-call(bf16[4,384,1152]{2,1,0:T(8,128)(2,1)} %collective-permute-done.3.refs_0_, bf16[4,384,1152]{2,1,0:T(8,128)(2,1)} %collective-permute-done.11.refs_1_, bf16[4,384,1152]{2,1,0:T(8,128)(2,1)} %copy-done.5, ...), custom_call_target="tpu_custom_call" | custom-call | flops 1000 | bytes 1000 | tf_op jit(solution)/shard_map/expert/pallas_call | solution.py:585
  523.2 23.3 %expert.6 = (bf16[768,2304]{1,0:T(8,128)(2,1)}, bf16[768,1536]{1,0:T(8,128)(2,1)}, bf16[768,1536]{1,0:T(8,128)(2,1)}) custom-call(bf16[4,384,1152]{2,1,0:T(8,128)(2,1)} %collective-permute-done.3.refs_0_, bf16[4,384,1152]{2,1,0:T(8,128)(2,1)} %collective-permute-done.11.refs_1_, bf16[4,384,1152]{2,1,0:T(8,128)(2,1)} %copy-done.5, ...), custom_call_target="tpu_custom_call" | custom-call | flops 1000 | bytes 1000 | tf_op jit(solution)/shard_map/expert/pallas_call | solution.py:585
  553.7 10.7 weight.4
  564.4 10.7 weight.5
  575.2 10.7 weight.7
  585.9 10.8 weight.6
  607.5 7.8 fusion.7
  639.5 8.1 fusion.50
  648.8 11.8 fusion.52.gb_ref
  660.6 11.3 collective-permute-done.25
  679.5 38.1 %first.1 = (f32[16,8,2304]{2,1,0:T(8,128)}, bf16[1024,2304]{1,0:T(8,128)(2,1)}, f32[1024,2304]{1,0:T(8,128)}) custom-call(f32[1024,2304]{1,0:T(8,128)} %get-tuple-element.194.delta_ref, bf16[16,2304]{1,0:T(8,128)(2,1)} %slice.615.alog_ref, f32[1024,32]{1,0:T(8,128)} %copy.266.bc_ref, f32[1024,128]{1,0:T(8,128)} %broadcast_in_dim.18.cut_ref, ...), custom_call_target="tpu_custom_call" | custom-call | flops 1000 | bytes 1000 | tf_op jit(solution)/shard_map/first/pallas_call | solution.py:391
  717.5 8.8 collective-permute-done.26
  735.2 10.3 fusion.18
  748.7 11.1 fusion.128
  761.9 9.4 collective-permute-done.30
  789.3 69.1 %back.3 = (f32[1024,768]{1,0:T(8,128)}, bf16[1024,768]{1,0:T(8,128)(2,1)}, f32[16,768]{1,0:T(8,128)}, f32[8,768]{1,0:T(8,128)}, f32[1024,128]{1,0:T(8,128)}) custom-call(bf16[1024,2304]{1,0:T(8,128)(2,1)} %copy-done.3, f32[1024,2304]{1,0:T(8,128)} %get-tuple-element.194.delta_ref, bf16[16,2304]{1,0:T(8,128)(2,1)} %slice.615.alog_ref, ...), custom_call_target="tpu_custom_call" | custom-call | flops 100663296 | bytes 213909504 | tf_op jit(solution)/shard_map/back/pallas_call | solution.py:418
  881.0 7.0 positions.2
  888.8 69.0 %back.4 = (f32[1024,768]{1,0:T(8,128)}, bf16[1024,768]{1,0:T(8,128)(2,1)}, f32[16,768]{1,0:T(8,128)}, f32[8,768]{1,0:T(8,128)}, f32[1024,128]{1,0:T(8,128)}) custom-call(bf16[1024,2304]{1,0:T(8,128)(2,1)} %copy-done.3, f32[1024,2304]{1,0:T(8,128)} %get-tuple-element.194.delta_ref, bf16[16,2304]{1,0:T(8,128)(2,1)} %slice.615.alog_ref, ...), custom_call_target="tpu_custom_call" | custom-call | flops 100663296 | bytes 213909504 | tf_op jit(solution)/shard_map/back/pallas_call | solution.py:418
  974.0 69.0 %back.5 = (f32[1024,768]{1,0:T(8,128)}, bf16[1024,768]{1,0:T(8,128)(2,1)}, f32[16,768]{1,0:T(8,128)}, f32[8,768]{1,0:T(8,128)}, f32[1024,128]{1,0:T(8,128)}) custom-call(bf16[1024,2304]{1,0:T(8,128)(2,1)} %copy-done.3, f32[1024,2304]{1,0:T(8,128)} %get-tuple-element.194.delta_ref, bf16[16,2304]{1,0:T(8,128)(2,1)} %slice.615.alog_ref, ...), custom_call_target="tpu_custom_call" | custom-call | flops 100663296 | bytes 213909504 | tf_op jit(solution)/shard_map/back/pallas_call | solution.py:418
  1063.2 8.8 conv.3
  1072.1 8.8 conv.4
  1080.9 9.0 conv.5
  1103.0 6.4 fusion.26
  1111.7 5.3 convolution_add_fusion.1
  1144.4 29.8 %collective-permute-done.43 = f32[3,4,1152]{2,1,0:T(4,128)S(1)} collective-permute-done((f32[3,4,1152]{2,1,0:T(4,128)S(1)}, f32[3,4,1152]{2,1,0:T(4,128)S(1)}, u32[]{:S(2)}, u32[]{:S(2)}) %collective-permute-start.43) | collective-permute-done | bytes 55328 | tf_op jit(solution)/shard_map/ppermute | solution.py:34
  1174.5 6.6 multiply_reduce_fusion.2
  1187.0 7.7 positions.3
  1225.8 5.2 copy.257
  (535 shorter events, 346.2 us)
Async XLA Ops:
  7.2 119.4 %all-gather.6.cloned.1.call-start = ((), (), s32[]{:S(2)}) async-start(), calls=%async_computation.6 | async-start | bytes 12165120 | tf_op jit(solution)/shard_map/all_gather | solution.py:825
  14.6 320.5 %all-gather.4.cloned.1.call-start = ((), (), s32[]{:S(2)}) async-start(), calls=%async_computation.3 | async-start | bytes 5474304 | tf_op jit(solution)/shard_map/all_gather | solution.py:832
  15.6 40.0 %collective-permute-start = (bf16[4,3,1152]{2,1,0:T(4,128)(2,1)S(1)}, bf16[4,3,1152]{2,1,0:T(4,128)(2,1)S(1)}, u32[]{:S(2)}, u32[]{:S(2)}) collective-permute-start(bf16[4,3,1152]{2,1,0:T(4,128)(2,1)S(1)} %slice.456), channel_id=1, source_target_pairs={{0,4},{4,8},{8,12},{1,5},{5,9},{9,13},{2,6},{6,10},{10,14},{3,7},{... | collective-permute-start | bytes 82952 | tf_op jit(solution)/shard_map/ppermute | solution.py:34
  21.3 32.3 %collective-permute-start.1 = (f32[4,3]{1,0:T(4,128)S(1)}, f32[4,3]{1,0:T(4,128)S(1)}, u32[]{:S(2)}, u32[]{:S(2)}) collective-permute-start(f32[4,3]{1,0:T(4,128)S(1)} %slice_convert_fusion.4), channel_id=1, source_target_pairs={{0,4},{4,8},{8,12},{1,5},{5,9},{9,13},{2,6},{6,10},{10,14},{3,7},{... | collective-permute-start | bytes 152 | tf_op jit(solution)/shard_map/ppermute | solution.py:34
  43.6 177.8 %collective-permute-start.4 = (bf16[2,192,1152]{2,1,0:T(8,128)(2,1)}, bf16[2,192,1152]{2,1,0:T(8,128)(2,1)}, u32[]{:S(2)}, u32[]{:S(2)}) collective-permute-start(bf16[2,192,1152]{2,1,0:T(8,128)(2,1)} %bitcast.27), channel_id=1, source_target_pairs={{0,1},{1,0},{2,3},{3,2},{4,5},{5,4},{6,7},{7,6},{8,9},{9,8},{10,11... | collective-permute-start | bytes 2654216 | tf_op jit(solution)/shard_map/ppermute | solution.py:667
  43.6 177.8 %collective-permute-start.5 = (bf16[2,192,1152]{2,1,0:T(8,128)(2,1)}, bf16[2,192,1152]{2,1,0:T(8,128)(2,1)}, u32[]{:S(2)}, u32[]{:S(2)}) collective-permute-start(bf16[2,192,1152]{2,1,0:T(8,128)(2,1)} %bitcast.28), channel_id=1, source_target_pairs={{0,2},{1,3},{2,0},{3,1},{4,6},{5,7},{6,4},{7,5},{8,10},{9,11},{10,... | collective-permute-start | bytes 2654216 | tf_op jit(solution)/shard_map/ppermute | solution.py:667
  45.1 176.4 %collective-permute-start.6 = (bf16[2,192,1152]{2,1,0:T(8,128)(2,1)}, bf16[2,192,1152]{2,1,0:T(8,128)(2,1)}, u32[]{:S(2)}, u32[]{:S(2)}) collective-permute-start(bf16[2,192,1152]{2,1,0:T(8,128)(2,1)} %bitcast.29), channel_id=1, source_target_pairs={{0,3},{1,2},{2,1},{3,0},{4,7},{5,6},{6,5},{7,4},{8,11},{9,10},{10,... | collective-permute-start | bytes 2654216 | tf_op jit(solution)/shard_map/ppermute | solution.py:667
  45.5 916.3 %reduce-scatter.10.cloned.1.call-start = ((), (), s32[]{:S(2)}) async-start(), calls=%async_computation.7 | async-start | bytes 5474304
  137.9 83.6 %collective-permute-start.2 = (bf16[4,384,1152]{2,1,0:T(8,128)(2,1)}, bf16[4,384,1152]{2,1,0:T(8,128)(2,1)}, u32[]{:S(2)}, u32[]{:S(2)}) collective-permute-start(bf16[4,384,1152]{2,1,0:T(8,128)(2,1)} %pad_maximum_fusion.2.refs_0_), channel_id=1, source_target_pairs={{0,4},{4,8},{8,12},{12,0},{1,5},{5,9},{9,13},{13,1},{2,6},{6,10},{... | collective-permute-start | bytes 10616840 | tf_op jit(solution)/shard_map/ppermute | solution.py:662
  138.8 82.7 %collective-permute-start.3 = (bf16[4,384,1152]{2,1,0:T(8,128)(2,1)}, bf16[4,384,1152]{2,1,0:T(8,128)(2,1)}, u32[]{:S(2)}, u32[]{:S(2)}) collective-permute-start(bf16[4,384,1152]{2,1,0:T(8,128)(2,1)} %pad_maximum_fusion.2.refs_0_), channel_id=1, source_target_pairs={{0,16},{16,0},{1,17},{17,1},{2,18},{18,2},{3,19},{19,3},{4,20},{20... | collective-permute-start | bytes 10616840 | tf_op jit(solution)/shard_map/ppermute | solution.py:662
  241.3 15.8 %collective-permute-start.8 = (bf16[16,4,2304]{2,1,0:T(4,128)(2,1)S(1)}, bf16[16,4,2304]{2,1,0:T(4,128)(2,1)S(1)}, u32[]{:S(2)}, u32[]{:S(2)}) collective-permute-start(bf16[16,4,2304]{2,1,0:T(4,128)(2,1)S(1)} %add_convert_fusion.5), channel_id=1, source_target_pairs={{0,4},{4,8},{8,12},{1,5},{5,9},{9,13},{2,6},{6,10},{10,14},{3,7},{... | collective-permute-start | bytes 884744 | tf_op jit(solution)/shard_map/ppermute | solution.py:34
  258.4 12.8 %collective-permute-start.9 = (bf16[16,4,2304]{2,1,0:T(4,128)(2,1)}, bf16[16,4,2304]{2,1,0:T(4,128)(2,1)}, u32[]{:S(2)}, u32[]{:S(2)}) collective-permute-start(bf16[16,4,2304]{2,1,0:T(4,128)(2,1)} %add_convert_fusion.4), channel_id=1, source_target_pairs={{0,4},{4,8},{8,12},{1,5},{5,9},{9,13},{2,6},{6,10},{10,14},{3,7},{... | collective-permute-start | bytes 884744 | tf_op jit(solution)/shard_map/ppermute | solution.py:34
  276.5 82.1 %collective-permute-start.10 = (bf16[4,384,1152]{2,1,0:T(8,128)(2,1)}, bf16[4,384,1152]{2,1,0:T(8,128)(2,1)}, u32[]{:S(2)}, u32[]{:S(2)}) collective-permute-start(bf16[4,384,1152]{2,1,0:T(8,128)(2,1)} %collective-permute-done.2.refs_1_), channel_id=1, source_target_pairs={{0,4},{4,8},{8,12},{12,0},{1,5},{5,9},{9,13},{13,1},{2,6},{6,10},{... | collective-permute-start | bytes 10616840 | tf_op jit(solution)/shard_map/ppermute | solution.py:662
  279.8 78.7 %collective-permute-start.11 = (bf16[4,384,1152]{2,1,0:T(8,128)(2,1)}, bf16[4,384,1152]{2,1,0:T(8,128)(2,1)}, u32[]{:S(2)}, u32[]{:S(2)}) collective-permute-start(bf16[4,384,1152]{2,1,0:T(8,128)(2,1)} %collective-permute-done.2.refs_1_), channel_id=1, source_target_pairs={{0,16},{16,0},{1,17},{17,1},{2,18},{18,2},{3,19},{19,3},{4,20},{20... | collective-permute-start | bytes 10616840 | tf_op jit(solution)/shard_map/ppermute | solution.py:662
  358.6 77.7 %collective-permute-start.15 = (bf16[4,384,1152]{2,1,0:T(8,128)(2,1)}, bf16[4,384,1152]{2,1,0:T(8,128)(2,1)S(1)}, u32[]{:S(2)}, u32[]{:S(2)}) collective-permute-start(bf16[4,384,1152]{2,1,0:T(8,128)(2,1)} %collective-permute-done.10.refs_2_), channel_id=1, source_target_pairs={{0,4},{4,8},{8,12},{12,0},{1,5},{5,9},{9,13},{13,1},{2,6},{6,10},{... | collective-permute-start | bytes 10616840 | tf_op jit(solution)/shard_map/ppermute | solution.py:662
  359.5 76.8 %collective-permute-start.16 = (bf16[4,384,1152]{2,1,0:T(8,128)(2,1)}, bf16[4,384,1152]{2,1,0:T(8,128)(2,1)S(1)}, u32[]{:S(2)}, u32[]{:S(2)}) collective-permute-start(bf16[4,384,1152]{2,1,0:T(8,128)(2,1)} %collective-permute-done.10.refs_2_), channel_id=1, source_target_pairs={{0,16},{16,0},{1,17},{17,1},{2,18},{18,2},{3,19},{19,3},{4,20},{20... | collective-permute-start | bytes 10616840 | tf_op jit(solution)/shard_map/ppermute | solution.py:662
  367.1 24.6 %collective-permute-start.13 = (bf16[2,192,1280]{2,1,0:T(8,128)(2,1)S(1)}, bf16[2,192,1280]{2,1,0:T(8,128)(2,1)S(1)}, u32[]{:S(2)}, u32[]{:S(2)}) collective-permute-start(bf16[2,192,1280]{2,1,0:T(8,128)(2,1)S(1)} %bitcast.371), channel_id=1, source_target_pairs={{0,2},{1,3},{2,0},{3,1},{4,6},{5,7},{6,4},{7,5},{8,10},{9,11},{10,... | collective-permute-start | bytes 2949128 | tf_op jit(solution)/shard_map/ppermute | solution.py:667
  368.4 43.5 %collective-permute-start.14 = (bf16[2,192,1280]{2,1,0:T(8,128)(2,1)S(1)}, bf16[2,192,1280]{2,1,0:T(8,128)(2,1)S(1)}, u32[]{:S(2)}, u32[]{:S(2)}) collective-permute-start(bf16[2,192,1280]{2,1,0:T(8,128)(2,1)S(1)} %bitcast.370), channel_id=1, source_target_pairs={{0,3},{1,2},{2,1},{3,0},{4,7},{5,6},{6,5},{7,4},{8,11},{9,10},{10,... | collective-permute-start | bytes 2949128 | tf_op jit(solution)/shard_map/ppermute | solution.py:667
  437.7 51.5 %collective-permute-start.17 = (bf16[2,384,1152]{2,1,0:T(8,128)(2,1)}, bf16[2,384,1152]{2,1,0:T(8,128)(2,1)}, u32[]{:S(2)}, u32[]{:S(2)}) collective-permute-start(bf16[2,384,1152]{2,1,0:T(8,128)(2,1)} %slice.505), channel_id=1, source_target_pairs={{0,16},{16,0},{1,17},{17,1},{2,18},{18,2},{3,19},{19,3},{4,20},{20... | collective-permute-start | bytes 5308424 | tf_op jit(solution)/shard_map/ppermute | solution.py:662
  442.2 47.1 %collective-permute-start.18 = (bf16[2,384,1152]{2,1,0:T(8,128)(2,1)}, bf16[2,384,1152]{2,1,0:T(8,128)(2,1)}, u32[]{:S(2)}, u32[]{:S(2)}) collective-permute-start(bf16[2,384,1152]{2,1,0:T(8,128)(2,1)} %slice.506), channel_id=1, source_target_pairs={{0,4},{4,8},{8,12},{12,0},{1,5},{5,9},{9,13},{13,1},{2,6},{6,10},{... | collective-permute-start | bytes 5308424 | tf_op jit(solution)/shard_map/ppermute | solution.py:662
  521.4 30.7 %collective-permute-start.19 = (bf16[192,2304]{1,0:T(8,128)(2,1)}, bf16[192,2304]{1,0:T(8,128)(2,1)}, u32[]{:S(2)}, u32[]{:S(2)}) collective-permute-start(bf16[192,2304]{1,0:T(8,128)(2,1)} %get-tuple-element.485), channel_id=1, source_target_pairs={{0,1},{1,0},{2,3},{3,2},{4,5},{5,4},{6,7},{7,6},{8,9},{9,8},{10,11... | collective-permute-start | bytes 2654216 | tf_op jit(solution)/shard_map/ppermute | solution.py:667
  521.4 53.8 %collective-permute-start.20 = (bf16[192,2304]{1,0:T(8,128)(2,1)}, bf16[192,2304]{1,0:T(8,128)(2,1)}, u32[]{:S(2)}, u32[]{:S(2)}) collective-permute-start(bf16[192,2304]{1,0:T(8,128)(2,1)} %get-tuple-element.484), channel_id=1, source_target_pairs={{0,2},{1,3},{2,0},{3,1},{4,6},{5,7},{6,4},{7,5},{8,10},{9,11},{10,... | collective-permute-start | bytes 2654216 | tf_op jit(solution)/shard_map/ppermute | solution.py:667
  522.8 52.4 %collective-permute-start.21 = (bf16[192,2304]{1,0:T(8,128)(2,1)}, bf16[192,2304]{1,0:T(8,128)(2,1)}, u32[]{:S(2)}, u32[]{:S(2)}) collective-permute-start(bf16[192,2304]{1,0:T(8,128)(2,1)} %get-tuple-element.483), channel_id=1, source_target_pairs={{0,3},{1,2},{2,1},{3,0},{4,7},{5,6},{6,5},{7,4},{8,11},{9,10},{10,... | collective-permute-start | bytes 2654216 | tf_op jit(solution)/shard_map/ppermute | solution.py:667
  550.3 46.4 %collective-permute-start.22 = (bf16[192,2304]{1,0:T(8,128)(2,1)}, bf16[192,2304]{1,0:T(8,128)(2,1)}, u32[]{:S(2)}, u32[]{:S(2)}) collective-permute-start(bf16[192,2304]{1,0:T(8,128)(2,1)} %get-tuple-element.489), channel_id=1, source_target_pairs={{0,1},{1,0},{2,3},{3,2},{4,5},{5,4},{6,7},{7,6},{8,9},{9,8},{10,11... | collective-permute-start | bytes 2654216 | tf_op jit(solution)/shard_map/ppermute | solution.py:667
  550.6 46.1 %collective-permute-start.23 = (bf16[192,2304]{1,0:T(8,128)(2,1)}, bf16[192,2304]{1,0:T(8,128)(2,1)}, u32[]{:S(2)}, u32[]{:S(2)}) collective-permute-start(bf16[192,2304]{1,0:T(8,128)(2,1)} %get-tuple-element.488), channel_id=1, source_target_pairs={{0,2},{1,3},{2,0},{3,1},{4,6},{5,7},{6,4},{7,5},{8,10},{9,11},{10,... | collective-permute-start | bytes 2654216 | tf_op jit(solution)/shard_map/ppermute | solution.py:667
  552.0 48.2 %collective-permute-start.24 = (bf16[192,2304]{1,0:T(8,128)(2,1)}, bf16[192,2304]{1,0:T(8,128)(2,1)}, u32[]{:S(2)}, u32[]{:S(2)}) collective-permute-start(bf16[192,2304]{1,0:T(8,128)(2,1)} %get-tuple-element.487), channel_id=1, source_target_pairs={{0,3},{1,2},{2,1},{3,0},{4,7},{5,6},{6,5},{7,4},{8,11},{9,10},{10,... | collective-permute-start | bytes 2654216 | tf_op jit(solution)/shard_map/ppermute | solution.py:667
  629.6 42.3 %collective-permute-start.25 = (bf16[2,384,1152]{2,1,0:T(8,128)(2,1)}, bf16[2,384,1152]{2,1,0:T(8,128)(2,1)}, u32[]{:S(2)}, u32[]{:S(2)}) collective-permute-start(bf16[2,384,1152]{2,1,0:T(8,128)(2,1)} %pad_maximum_fusion.5), channel_id=1, source_target_pairs={{0,12},{4,0},{8,4},{12,8},{1,13},{5,1},{9,5},{13,9},{2,14},{6,2},{... | collective-permute-start | bytes 5308424 | tf_op jit(solution)/shard_map/ppermute | solution.py:662
  647.6 78.7 %collective-permute-start.26 = (bf16[4,384,1152]{2,1,0:T(8,128)(2,1)}, bf16[4,384,1152]{2,1,0:T(8,128)(2,1)}, u32[]{:S(2)}, u32[]{:S(2)}) collective-permute-start(bf16[4,384,1152]{2,1,0:T(8,128)(2,1)} %bitcast.397), channel_id=1, source_target_pairs={{0,16},{16,0},{1,17},{17,1},{2,18},{18,2},{3,19},{19,3},{4,20},{20... | collective-permute-start | bytes 10616840 | tf_op jit(solution)/shard_map/ppermute | solution.py:662
  675.2 42.3 %collective-permute-start.27 = (bf16[2,384,1152]{2,1,0:T(8,128)(2,1)}, bf16[2,384,1152]{2,1,0:T(8,128)(2,1)}, u32[]{:S(2)}, u32[]{:S(2)}) collective-permute-start(bf16[2,384,1152]{2,1,0:T(8,128)(2,1)} %add_convert_fusion.1), channel_id=1, source_target_pairs={{0,12},{4,0},{8,4},{12,8},{1,13},{5,1},{9,5},{13,9},{2,14},{6,2},{... | collective-permute-start | bytes 5308424 | tf_op jit(solution)/shard_map/ppermute | solution.py:662
  775.6 327.5 %reduce-scatter.6.cloned.1.call-start = ((), (), s32[]{:S(2)}) async-start(), calls=%async_computation.4 | async-start | bytes 5640192 | tf_op jit(solution)/shard_map/reduce_scatter | solution.py:970
  775.6 91.7 %collective-permute-start.32 = (bf16[4,384,1152]{2,1,0:T(8,128)(2,1)}, bf16[4,384,1152]{2,1,0:T(8,128)(2,1)}, u32[]{:S(2)}, u32[]{:S(2)}) collective-permute-start(bf16[4,384,1152]{2,1,0:T(8,128)(2,1)} %bitcast.396), channel_id=1, source_target_pairs={{0,16},{16,0},{1,17},{17,1},{2,18},{18,2},{3,19},{19,3},{4,20},{20... | collective-permute-start | bytes 10616840 | tf_op jit(solution)/shard_map/ppermute | solution.py:662
  780.1 87.2 %collective-permute-start.33 = (bf16[2,384,1152]{2,1,0:T(8,128)(2,1)}, bf16[2,384,1152]{2,1,0:T(8,128)(2,1)S(1)}, u32[]{:S(2)}, u32[]{:S(2)}) collective-permute-start(bf16[2,384,1152]{2,1,0:T(8,128)(2,1)} %add_convert_fusion), channel_id=1, source_target_pairs={{0,12},{4,0},{8,4},{12,8},{1,13},{5,1},{9,5},{13,9},{2,14},{6,2},{... | collective-permute-start | bytes 5308424 | tf_op jit(solution)/shard_map/ppermute | solution.py:662
  784.6 82.7 %collective-permute-start.31 = (bf16[384,1152]{1,0:T(8,128)(2,1)}, bf16[384,1152]{1,0:T(8,128)(2,1)}, u32[]{:S(2)}, u32[]{:S(2)}) collective-permute-start(bf16[384,1152]{1,0:T(8,128)(2,1)} %fusion.48), channel_id=1, source_target_pairs={{0,12},{4,0},{8,4},{12,8},{1,13},{5,1},{9,5},{13,9},{2,14},{6,2},{... | collective-permute-start | bytes 2654216 | tf_op jit(solution)/shard_map/ppermute | solution.py:662
  788.4 173.4 %collective-permute-start.36 = (bf16[4,384,1152]{2,1,0:T(8,128)(2,1)}, bf16[4,384,1152]{2,1,0:T(8,128)(2,1)}, u32[]{:S(2)}, u32[]{:S(2)}) collective-permute-start(bf16[4,384,1152]{2,1,0:T(8,128)(2,1)} %bitcast.395), channel_id=1, source_target_pairs={{0,16},{16,0},{1,17},{17,1},{2,18},{18,2},{3,19},{19,3},{4,20},{20... | collective-permute-start | bytes 10616840 | tf_op jit(solution)/shard_map/ppermute | solution.py:662
  868.9 92.9 %collective-permute-start.37 = (bf16[384,1152]{1,0:T(8,128)(2,1)}, bf16[384,1152]{1,0:T(8,128)(2,1)}, u32[]{:S(2)}, u32[]{:S(2)}) collective-permute-start(bf16[384,1152]{1,0:T(8,128)(2,1)} %fusion.56), channel_id=1, source_target_pairs={{0,16},{16,0},{1,17},{17,1},{2,18},{18,2},{3,19},{19,3},{4,20},{20... | collective-permute-start | bytes 2654216 | tf_op jit(solution)/shard_map/ppermute | solution.py:662
  872.7 89.1 %collective-permute-start.35 = (bf16[384,1152]{1,0:T(8,128)(2,1)}, bf16[384,1152]{1,0:T(8,128)(2,1)}, u32[]{:S(2)}, u32[]{:S(2)}) collective-permute-start(bf16[384,1152]{1,0:T(8,128)(2,1)} %fusion.45), channel_id=1, source_target_pairs={{0,12},{4,0},{8,4},{12,8},{1,13},{5,1},{9,5},{13,9},{2,14},{6,2},{... | collective-permute-start | bytes 2654216 | tf_op jit(solution)/shard_map/ppermute | solution.py:662
  877.5 84.3 %collective-permute-start.34 = (bf16[384,1152]{1,0:T(8,128)(2,1)}, bf16[384,1152]{1,0:T(8,128)(2,1)}, u32[]{:S(2)}, u32[]{:S(2)}) collective-permute-start(bf16[384,1152]{1,0:T(8,128)(2,1)} %fusion.47), channel_id=1, source_target_pairs={{0,12},{4,0},{8,4},{12,8},{1,13},{5,1},{9,5},{13,9},{2,14},{6,2},{... | collective-permute-start | bytes 2654216 | tf_op jit(solution)/shard_map/ppermute | solution.py:662
  888.8 330.6 %reduce-scatter.8.cloned.1.call-start = ((), (), s32[]{:S(2)}) async-start(), calls=%async_computation.5 | async-start | bytes 5640192 | tf_op jit(solution)/shard_map/reduce_scatter | solution.py:1011
  964.3 87.9 %collective-permute-start.40 = (bf16[384,1152]{1,0:T(8,128)(2,1)}, bf16[384,1152]{1,0:T(8,128)(2,1)}, u32[]{:S(2)}, u32[]{:S(2)}) collective-permute-start(bf16[384,1152]{1,0:T(8,128)(2,1)} %fusion.40), channel_id=1, source_target_pairs={{0,12},{4,0},{8,4},{12,8},{1,13},{5,1},{9,5},{13,9},{2,14},{6,2},{... | collective-permute-start | bytes 2654216 | tf_op jit(solution)/shard_map/ppermute | solution.py:662
  967.4 84.8 %collective-permute-start.39 = (bf16[384,1152]{1,0:T(8,128)(2,1)}, bf16[384,1152]{1,0:T(8,128)(2,1)}, u32[]{:S(2)}, u32[]{:S(2)}) collective-permute-start(bf16[384,1152]{1,0:T(8,128)(2,1)} %fusion.42), channel_id=1, source_target_pairs={{0,12},{4,0},{8,4},{12,8},{1,13},{5,1},{9,5},{13,9},{2,14},{6,2},{... | collective-permute-start | bytes 2654216 | tf_op jit(solution)/shard_map/ppermute | solution.py:662
  973.1 79.1 %collective-permute-start.38 = (bf16[384,1152]{1,0:T(8,128)(2,1)}, bf16[384,1152]{1,0:T(8,128)(2,1)}, u32[]{:S(2)}, u32[]{:S(2)}) collective-permute-start(bf16[384,1152]{1,0:T(8,128)(2,1)} %fusion.44), channel_id=1, source_target_pairs={{0,12},{4,0},{8,4},{12,8},{1,13},{5,1},{9,5},{13,9},{2,14},{6,2},{... | collective-permute-start | bytes 2654216 | tf_op jit(solution)/shard_map/ppermute | solution.py:662
  1055.2 72.6 %collective-permute-start.42 = (bf16[384,1152]{1,0:T(8,128)(2,1)}, bf16[384,1152]{1,0:T(8,128)(2,1)}, u32[]{:S(2)}, u32[]{:S(2)}) collective-permute-start(bf16[384,1152]{1,0:T(8,128)(2,1)} %fusion.37), channel_id=1, source_target_pairs={{0,12},{4,0},{8,4},{12,8},{1,13},{5,1},{9,5},{13,9},{2,14},{6,2},{... | collective-permute-start | bytes 2654216 | tf_op jit(solution)/shard_map/ppermute | solution.py:662
  1059.7 68.0 %collective-permute-start.41 = (bf16[384,1152]{1,0:T(8,128)(2,1)}, bf16[384,1152]{1,0:T(8,128)(2,1)}, u32[]{:S(2)}, u32[]{:S(2)}) collective-permute-start(bf16[384,1152]{1,0:T(8,128)(2,1)} %fusion.39), channel_id=1, source_target_pairs={{0,12},{4,0},{8,4},{12,8},{1,13},{5,1},{9,5},{13,9},{2,14},{6,2},{... | collective-permute-start | bytes 2654216 | tf_op jit(solution)/shard_map/ppermute | solution.py:662
  1110.9 13.9 %collective-permute-start.52 = (bf16[2,2,2,2,72,256]{5,4,3,2,1,0:T(8,128)(2,1)}, bf16[2,2,2,2,72,256]{5,4,3,2,1,0:T(8,128)(2,1)}, u32[]{:S(2)}, u32[]{:S(2)}) collective-permute-start(bf16[2,2,2,2,72,256]{5,4,3,2,1,0:T(8,128)(2,1)} %fusion.62), channel_id=1, source_target_pairs={{0,1},{1,0},{2,3},{3,2},{4,5},{5,4},{6,7},{7,6},{8,9},{9,8},{10,11... | collective-permute-start | bytes 1769480 | tf_op jit(solution)/shard_map/ppermute | solution.py:667
  1130.8 85.4 %collective-permute-start.57 = (bf16[384,1152]{1,0:T(8,128)(2,1)}, bf16[384,1152]{1,0:T(8,128)(2,1)}, u32[]{:S(2)}, u32[]{:S(2)}) collective-permute-start(bf16[384,1152]{1,0:T(8,128)(2,1)} %fusion.31), channel_id=1, source_target_pairs={{0,12},{4,0},{8,4},{12,8},{1,13},{5,1},{9,5},{13,9},{2,14},{6,2},{... | collective-permute-start | bytes 2654216 | tf_op jit(solution)/shard_map/ppermute | solution.py:662
  1136.0 58.6 %collective-permute-start.54 = (bf16[2,2,72,256]{3,2,1,0:T(8,128)(2,1)S(1)}, bf16[2,2,72,256]{3,2,1,0:T(8,128)(2,1)S(1)}, u32[]{:S(2)}, u32[]{:S(2)}) collective-permute-start(bf16[2,2,72,256]{3,2,1,0:T(8,128)(2,1)S(1)} %fusion.74), channel_id=1, source_target_pairs={{0,16},{16,0},{1,17},{17,1},{2,18},{18,2},{3,19},{19,3},{4,20},{20... | collective-permute-start | bytes 442376 | tf_op jit(solution)/shard_map/ppermute | solution.py:667
  1137.5 36.8 %collective-permute-start.43 = (f32[3,4,1152]{2,1,0:T(4,128)S(1)}, f32[3,4,1152]{2,1,0:T(4,128)S(1)}, u32[]{:S(2)}, u32[]{:S(2)}) collective-permute-start(f32[3,4,1152]{2,1,0:T(4,128)S(1)} %bitcast.383), channel_id=1, source_target_pairs={{4,0},{8,4},{12,8},{5,1},{9,5},{13,9},{6,2},{10,6},{14,10},{7,3},{... | collective-permute-start | bytes 165896 | tf_op jit(solution)/shard_map/ppermute | solution.py:34
  1181.2 13.6 %collective-permute-start.44 = (f32[180,128]{1,0:T(8,128)S(1)}, f32[180,128]{1,0:T(8,128)S(1)}, u32[]{:S(2)}, u32[]{:S(2)}) collective-permute-start(f32[180,128]{1,0:T(8,128)S(1)} %maximum_bitcast_fusion.5), channel_id=1, source_target_pairs={{0,16},{16,0},{1,17},{17,1},{2,18},{18,2},{3,19},{19,3},{4,20},{20... | collective-permute-start | bytes 276488 | tf_op jit(solution)/shard_map/ppermute | solution.py:667
  (110 other events, 1988.3 us)
Sparse Core Ops, SparseCore 0:
  14.8 111.7 all-gather.5
  129.4 136.0 all-gather.3
  775.7 152.6 reduce-scatter.9
  932.3 132.4 reduce-scatter.5
  1111.1 88.2 reduce-scatter.7

commit v7 on v6

--- a/solution.py
+++ b/solution.py
@@ -1009,8 +1009,8 @@
         conv_grads.append(gvec)
     conv_all, gexts, gate_own = held_for(jnp.concatenate(conv_parts, axis=0), gexts, gate_own)
     conv_own = lax.psum_scatter(conv_all, ("seq", "expert"), scatter_dimension=0, tiled=True).astype(f32)
+    gexts = hold_all(gexts, reduces)
     grad_normed = sum(dot(gexts[k], conv_full[k * width : (k + 1) * width], NN) for k in range(SPLITS))
-    grad_normed = hold_all(grad_normed, reduces)
     over = grad_normed[:skip_rows].reshape(halo, seqs, HALVES, D)
     from_next = shifted(over[:, :, 0], "seq", -1)
     edge = jnp.stack([over[:, :, 1], from_next], axis=2).reshape(skip_rows, D)

time: 1250 us -> 1220 us (0.976)
  waiting for transfers between devices: 232 us -> 211 us
    ppermute x9, waiting for transfers between devices: 53.3 us -> 24.1 us  [shifted(): lax.ppermute(value, axis, [(source, source + steps) for source in range(f...]
  transfers between devices with their start and end apart: 63 -> 63, of which waited for: 20 -> 22; matrix products, arithmetic and copies ran while one was open for 25% -> 25% of each run, Pallas kernels for 40% -> 41%
where the time goes in v7:
time: 1220 us; the launch traced here: 1210 us
  Pallas kernels  520 us (43%)
  waiting for transfers between devices  211 us (17%)
  local copies, waits for them, and re-layouts  126 us (10%)
  matrix products  125 us (10%)
  other arithmetic  117 us (10%)
  starting transfers between devices  91.7 us (8%)
  between operations  16 us (1%)
    pallas_call x3, Pallas kernels, run_back(): pl.pallas_call(back_kernel, grid=(width // LANES,), in_specs=[col(rows),...  207 us
    dot_general x28, matrix products, dot(): lax.dot_general(left, right, (dims, ((), ())), preferred_element_type=out)  125 us
    pallas_call x4, Pallas kernels, run_expert(): pl.pallas_call(functools.partial(expert_kernel, blocks, peers, final), gr...  92.8 us
    ppermute x25, waiting for transfers between devices, ring(): lax.ppermute(value, axis, [(i, (i + step) % count) for i in range(count)])  62.8 us
    ppermute x24, waiting for transfers between devices, partner(): return lax.ppermute(value, axis, [(i, i ^ bits) for i in range(count)])  62.3 us
    all_gather x1, waiting for transfers between devices, local(): lax.all_gather(jnp.concatenate([in_proj.T, small.reshape(-1, D)], axis=0)...  58.6 us
    pallas_call x1, Pallas kernels, run_out(): pl.pallas_call(out_kernel, grid=(DI // LANES,), in_specs=[col_spec(rows),...  53.8 us
    pallas_call x1, Pallas kernels, run_end(): pl.pallas_call(end_kernel, grid=(DI // LANES,), in_specs=[col_spec(rows),...  44 us
  transfers between devices with their start and end apart: 63, of which 22 were waited for; matrix products, arithmetic and copies ran while one was open for 25% of the time, Pallas kernels for 41%

profile of v7, /device:TPU:0, one launch (start us, length us, event | category | flops | bytes accessed | tf_op | source)
XLA Modules:
  0.0 1207.0 jit_solution(8184203657546452877)
XLA Ops:
  15.6 4.9 collective-permute-start
  25.9 5.6 copy.318
  31.5 5.0 reshape.554
  37.0 4.7 fusion.10
  60.1 5.1 reshape.547
  67.9 58.6 %all-gather.6.cloned.1.call-done = bf16[5120,1152]{1,0:T(8,128)(2,1)} async-done(((bf16[160,1152]{1,0:T(8,128)(2,1)}), bf16[5120,1152]{1,0:T(8,128)(2,1)}) %all-gather.6.cloned.1.call-update) | async-done | bytes 11796496 | tf_op jit(solution)/shard_map/all_gather | solution.py:825
  128.9 8.9 fusion.113
  145.8 9.8 fusion.131.ext_ref
  155.6 7.2 multiply_convert_fusion.xs_ref
  171.0 44.0 %end.1 = (f32[1024,2304]{1,0:T(8,128)}, f32[16,8,2304]{2,1,0:T(8,128)}, f32[8,2304]{1,0:T(8,128)}) custom-call(bf16[1024,2304]{1,0:T(8,128)(2,1)} %copy-done.3, bf16[1024,72]{1,0:T(8,128)(2,1)} %copy.265.din_ref, bf16[2304,72]{1,0:T(8,128)(2,1)} %slice.613.dtw_ref, bf16[1,2304]{1,0:T(2,128)(2,1)} %get-tuple-element.513.dtb_ref, ...), custom_call_target="tpu_custom_call" | custom-call | flops 301989888 | bytes 150994944 | tf_op jit(solution)/shard_map/end/pallas_call | solution.py:349
  216.1 5.3 collective-permute-done.2.refs_1_
  229.1 11.4 fusion.22.z_ref
  243.6 13.2 %collective-permute-done.8 = bf16[16,4,2304]{2,1,0:T(4,128)(2,1)S(1)} collective-permute-done((bf16[16,4,2304]{2,1,0:T(4,128)(2,1)S(1)}, bf16[16,4,2304]{2,1,0:T(4,128)(2,1)S(1)}, u32[]{:S(2)}, u32[]{:S(2)}) %collective-permute-start.8) | collective-permute-done | bytes 294944 | tf_op jit(solution)/shard_map/ppermute | solution.py:34
  258.0 9.2 collective-permute-start.9
  281.5 53.8 %out.1 = (bf16[1024,2304]{1,0:T(8,128)(2,1)}, bf16[1024,2304]{1,0:T(8,128)(2,1)}, f32[8,16,8,2304]{3,2,1,0:T(8,128)}) custom-call(bf16[1024,2304]{1,0:T(8,128)(2,1)} %copy-done.3, f32[1024,2304]{1,0:T(8,128)} %get-tuple-element.196.delta_ref, bf16[16,2304]{1,0:T(8,128)(2,1)} %slice.615.alog_ref, f32[1024,32]{1,0:T(8,128)} %copy.266.bc_ref, ...), custom_call_target="tpu_custom_call" | custom-call | flops 301989888 | bytes 188743680 | tf_op jit(solution)/shard_map/out/pallas_call | solution.py:368
  335.3 10.6 multiply_reduce_fusion.5
  349.8 8.6 collective-permute-done.10.refs_2_
  369.0 22.0 %collective-permute-done.13.refs_6_ = bf16[2,192,1280]{2,1,0:T(8,128)(2,1)S(1)} collective-permute-done((bf16[2,192,1280]{2,1,0:T(8,128)(2,1)S(1)}, bf16[2,192,1280]{2,1,0:T(8,128)(2,1)S(1)}, u32[]{:S(2)}, u32[]{:S(2)}) %collective-permute-start.13) | collective-permute-done | bytes 983072 | tf_op jit(solution)/shard_map/ppermute | solution.py:667
  391.0 20.3 %collective-permute-done.14.refs_7_ = bf16[2,192,1280]{2,1,0:T(8,128)(2,1)S(1)} collective-permute-done((bf16[2,192,1280]{2,1,0:T(8,128)(2,1)S(1)}, bf16[2,192,1280]{2,1,0:T(8,128)(2,1)S(1)}, u32[]{:S(2)}, u32[]{:S(2)}) %collective-permute-start.14) | collective-permute-done | bytes 983072 | tf_op jit(solution)/shard_map/ppermute | solution.py:667
  411.3 24.8 %collective-permute-done.15.refs_3_ = bf16[4,384,1152]{2,1,0:T(8,128)(2,1)S(1)} collective-permute-done((bf16[4,384,1152]{2,1,0:T(8,128)(2,1)}, bf16[4,384,1152]{2,1,0:T(8,128)(2,1)S(1)}, u32[]{:S(2)}, u32[]{:S(2)}) %collective-permute-start.15) | collective-permute-done | bytes 3538976 | tf_op jit(solution)/shard_map/ppermute | solution.py:662
  441.4 23.5 %expert.4 = (bf16[768,2304]{1,0:T(8,128)(2,1)}, bf16[768,1152]{1,0:T(8,128)(2,1)}, bf16[768,1152]{1,0:T(8,128)(2,1)}, bf16[768,1536]{1,0:T(8,128)(2,1)}, bf16[768,1536]{1,0:T(8,128)(2,1)}) custom-call(bf16[4,384,1152]{2,1,0:T(8,128)(2,1)} %pad_maximum_fusion.2.refs_0_, bf16[4,384,1152]{2,1,0:T(8,128)(2,1)} %collective-permute-done.2.refs_1_, ...), custom_call_target="tpu_custom_call" | custom-call | flops 1000 | bytes 1000 | tf_op jit(solution)/shard_map/expert/pallas_call | solution.py:585
  464.9 23.3 %expert.5 = (bf16[768,2304]{1,0:T(8,128)(2,1)}, bf16[768,1152]{1,0:T(8,128)(2,1)}, bf16[768,1152]{1,0:T(8,128)(2,1)}, bf16[768,1536]{1,0:T(8,128)(2,1)}, bf16[768,1536]{1,0:T(8,128)(2,1)}) custom-call(bf16[4,384,1152]{2,1,0:T(8,128)(2,1)} %pad_maximum_fusion.2.refs_0_, bf16[4,384,1152]{2,1,0:T(8,128)(2,1)} %collective-permute-done.2.refs_1_, ...), custom_call_target="tpu_custom_call" | custom-call | flops 1000 | bytes 1000 | tf_op jit(solution)/shard_map/expert/pallas_call | solution.py:585
  493.8 22.9 %expert.7 = (bf16[768,2304]{1,0:T(8,128)(2,1)}, bf16[768,1536]{1,0:T(8,128)(2,1)}, bf16[768,1536]{1,0:T(8,128)(2,1)}) custom-call(bf16[4,384,1152]{2,1,0:T(8,128)(2,1)} %collective-permute-done.3.refs_0_, bf16[4,384,1152]{2,1,0:T(8,128)(2,1)} %collective-permute-done.11.refs_1_, bf16[4,384,1152]{2,1,0:T(8,128)(2,1)} %copy-done.6, ...), custom_call_target="tpu_custom_call" | custom-call | flops 1000 | bytes 1000 | tf_op jit(solution)/shard_map/expert/pallas_call | solution.py:585
  522.1 23.1 %expert.6 = (bf16[768,2304]{1,0:T(8,128)(2,1)}, bf16[768,1536]{1,0:T(8,128)(2,1)}, bf16[768,1536]{1,0:T(8,128)(2,1)}) custom-call(bf16[4,384,1152]{2,1,0:T(8,128)(2,1)} %collective-permute-done.3.refs_0_, bf16[4,384,1152]{2,1,0:T(8,128)(2,1)} %collective-permute-done.11.refs_1_, bf16[4,384,1152]{2,1,0:T(8,128)(2,1)} %copy-done.6, ...), custom_call_target="tpu_custom_call" | custom-call | flops 1000 | bytes 1000 | tf_op jit(solution)/shard_map/expert/pallas_call | solution.py:585
  552.5 10.7 weight.4
  563.2 10.7 weight.5
  574.0 10.8 weight.7
  584.7 10.8 weight.6
  606.6 7.8 fusion.8
  633.8 8.1 fusion.53
  643.0 11.9 fusion.55.gb_ref
  654.9 11.5 collective-permute-done.25
  673.9 38.1 %first.1 = (f32[16,8,2304]{2,1,0:T(8,128)}, bf16[1024,2304]{1,0:T(8,128)(2,1)}, f32[1024,2304]{1,0:T(8,128)}) custom-call(f32[1024,2304]{1,0:T(8,128)} %get-tuple-element.196.delta_ref, bf16[16,2304]{1,0:T(8,128)(2,1)} %slice.615.alog_ref, f32[1024,32]{1,0:T(8,128)} %copy.266.bc_ref, f32[1024,128]{1,0:T(8,128)} %broadcast_in_dim.18.cut_ref, ...), custom_call_target="tpu_custom_call" | custom-call | flops 1000 | bytes 1000 | tf_op jit(solution)/shard_map/first/pallas_call | solution.py:391
  712.0 8.6 collective-permute-done.26
  729.4 10.3 fusion.20
  742.9 11.1 fusion.132
  756.2 9.4 collective-permute-done.30
  783.6 69.2 %back.3 = (f32[1024,768]{1,0:T(8,128)}, bf16[1024,768]{1,0:T(8,128)(2,1)}, f32[16,768]{1,0:T(8,128)}, f32[8,768]{1,0:T(8,128)}, f32[1024,128]{1,0:T(8,128)}) custom-call(bf16[1024,2304]{1,0:T(8,128)(2,1)} %copy-done.3, f32[1024,2304]{1,0:T(8,128)} %get-tuple-element.196.delta_ref, bf16[16,2304]{1,0:T(8,128)(2,1)} %slice.615.alog_ref, ...), custom_call_target="tpu_custom_call" | custom-call | flops 100663296 | bytes 213909504 | tf_op jit(solution)/shard_map/back/pallas_call | solution.py:418
  875.1 7.0 positions.2
  883.0 69.0 %back.4 = (f32[1024,768]{1,0:T(8,128)}, bf16[1024,768]{1,0:T(8,128)(2,1)}, f32[16,768]{1,0:T(8,128)}, f32[8,768]{1,0:T(8,128)}, f32[1024,128]{1,0:T(8,128)}) custom-call(bf16[1024,2304]{1,0:T(8,128)(2,1)} %copy-done.3, f32[1024,2304]{1,0:T(8,128)} %get-tuple-element.196.delta_ref, bf16[16,2304]{1,0:T(8,128)(2,1)} %slice.615.alog_ref, ...), custom_call_target="tpu_custom_call" | custom-call | flops 100663296 | bytes 213909504 | tf_op jit(solution)/shard_map/back/pallas_call | solution.py:418
  967.8 68.9 %back.5 = (f32[1024,768]{1,0:T(8,128)}, bf16[1024,768]{1,0:T(8,128)(2,1)}, f32[16,768]{1,0:T(8,128)}, f32[8,768]{1,0:T(8,128)}, f32[1024,128]{1,0:T(8,128)}) custom-call(bf16[1024,2304]{1,0:T(8,128)(2,1)} %copy-done.3, f32[1024,2304]{1,0:T(8,128)} %get-tuple-element.196.delta_ref, bf16[16,2304]{1,0:T(8,128)(2,1)} %slice.615.alog_ref, ...), custom_call_target="tpu_custom_call" | custom-call | flops 100663296 | bytes 213909504 | tf_op jit(solution)/shard_map/back/pallas_call | solution.py:418
  1057.4 8.9 conv.3
  1066.3 8.8 conv.4
  1075.1 8.9 conv.5
  1130.7 6.6 multiply_reduce_fusion.2
  1143.0 7.7 positions.3
  1161.1 6.4 collective-permute-done.46
  1193.1 5.2 copy.257
  (535 shorter events, 339.0 us)
Async XLA Ops:
  7.2 119.4 %all-gather.6.cloned.1.call-start = ((), (), s32[]{:S(2)}) async-start(), calls=%async_computation.6 | async-start | bytes 12165120 | tf_op jit(solution)/shard_map/all_gather | solution.py:825
  14.6 320.7 %all-gather.4.cloned.1.call-start = ((), (), s32[]{:S(2)}) async-start(), calls=%async_computation.3 | async-start | bytes 5474304 | tf_op jit(solution)/shard_map/all_gather | solution.py:832
  15.6 40.3 %collective-permute-start = (bf16[4,3,1152]{2,1,0:T(4,128)(2,1)S(1)}, bf16[4,3,1152]{2,1,0:T(4,128)(2,1)S(1)}, u32[]{:S(2)}, u32[]{:S(2)}) collective-permute-start(bf16[4,3,1152]{2,1,0:T(4,128)(2,1)S(1)} %slice.456), channel_id=1, source_target_pairs={{0,4},{4,8},{8,12},{1,5},{5,9},{9,13},{2,6},{6,10},{10,14},{3,7},{... | collective-permute-start | bytes 82952 | tf_op jit(solution)/shard_map/ppermute | solution.py:34
  21.3 32.6 %collective-permute-start.1 = (f32[4,3]{1,0:T(4,128)S(1)}, f32[4,3]{1,0:T(4,128)S(1)}, u32[]{:S(2)}, u32[]{:S(2)}) collective-permute-start(f32[4,3]{1,0:T(4,128)S(1)} %slice_convert_fusion.4), channel_id=1, source_target_pairs={{0,4},{4,8},{8,12},{1,5},{5,9},{9,13},{2,6},{6,10},{10,14},{3,7},{... | collective-permute-start | bytes 152 | tf_op jit(solution)/shard_map/ppermute | solution.py:34
  43.6 177.8 %collective-permute-start.4 = (bf16[2,192,1152]{2,1,0:T(8,128)(2,1)}, bf16[2,192,1152]{2,1,0:T(8,128)(2,1)}, u32[]{:S(2)}, u32[]{:S(2)}) collective-permute-start(bf16[2,192,1152]{2,1,0:T(8,128)(2,1)} %bitcast.27), channel_id=1, source_target_pairs={{0,1},{1,0},{2,3},{3,2},{4,5},{5,4},{6,7},{7,6},{8,9},{9,8},{10,11... | collective-permute-start | bytes 2654216 | tf_op jit(solution)/shard_map/ppermute | solution.py:667
  43.6 177.8 %collective-permute-start.5 = (bf16[2,192,1152]{2,1,0:T(8,128)(2,1)}, bf16[2,192,1152]{2,1,0:T(8,128)(2,1)}, u32[]{:S(2)}, u32[]{:S(2)}) collective-permute-start(bf16[2,192,1152]{2,1,0:T(8,128)(2,1)} %bitcast.28), channel_id=1, source_target_pairs={{0,2},{1,3},{2,0},{3,1},{4,6},{5,7},{6,4},{7,5},{8,10},{9,11},{10,... | collective-permute-start | bytes 2654216 | tf_op jit(solution)/shard_map/ppermute | solution.py:667
  45.1 176.4 %collective-permute-start.6 = (bf16[2,192,1152]{2,1,0:T(8,128)(2,1)}, bf16[2,192,1152]{2,1,0:T(8,128)(2,1)}, u32[]{:S(2)}, u32[]{:S(2)}) collective-permute-start(bf16[2,192,1152]{2,1,0:T(8,128)(2,1)} %bitcast.29), channel_id=1, source_target_pairs={{0,3},{1,2},{2,1},{3,0},{4,7},{5,6},{6,5},{7,4},{8,11},{9,10},{10,... | collective-permute-start | bytes 2654216 | tf_op jit(solution)/shard_map/ppermute | solution.py:667
  45.5 910.4 %reduce-scatter.10.cloned.1.call-start = ((), (), s32[]{:S(2)}) async-start(), calls=%async_computation.7 | async-start | bytes 5474304
  137.9 83.6 %collective-permute-start.2 = (bf16[4,384,1152]{2,1,0:T(8,128)(2,1)}, bf16[4,384,1152]{2,1,0:T(8,128)(2,1)}, u32[]{:S(2)}, u32[]{:S(2)}) collective-permute-start(bf16[4,384,1152]{2,1,0:T(8,128)(2,1)} %pad_maximum_fusion.2.refs_0_), channel_id=1, source_target_pairs={{0,4},{4,8},{8,12},{12,0},{1,5},{5,9},{9,13},{13,1},{2,6},{6,10},{... | collective-permute-start | bytes 10616840 | tf_op jit(solution)/shard_map/ppermute | solution.py:662
  138.7 82.7 %collective-permute-start.3 = (bf16[4,384,1152]{2,1,0:T(8,128)(2,1)}, bf16[4,384,1152]{2,1,0:T(8,128)(2,1)}, u32[]{:S(2)}, u32[]{:S(2)}) collective-permute-start(bf16[4,384,1152]{2,1,0:T(8,128)(2,1)} %pad_maximum_fusion.2.refs_0_), channel_id=1, source_target_pairs={{0,16},{16,0},{1,17},{17,1},{2,18},{18,2},{3,19},{19,3},{4,20},{20... | collective-permute-start | bytes 10616840 | tf_op jit(solution)/shard_map/ppermute | solution.py:662
  227.7 12.8 %collective-permute-start.7 = (bf16[16,4,2304]{2,1,0:T(4,128)(2,1)S(1)}, bf16[16,4,2304]{2,1,0:T(4,128)(2,1)S(1)}, u32[]{:S(2)}, u32[]{:S(2)}) collective-permute-start(bf16[16,4,2304]{2,1,0:T(4,128)(2,1)S(1)} %fusion.107), channel_id=1, source_target_pairs={{0,4},{4,8},{8,12},{1,5},{5,9},{9,13},{2,6},{6,10},{10,14},{3,7},{... | collective-permute-start | bytes 884744 | tf_op jit(solution)/shard_map/ppermute | solution.py:34
  241.0 15.7 %collective-permute-start.8 = (bf16[16,4,2304]{2,1,0:T(4,128)(2,1)S(1)}, bf16[16,4,2304]{2,1,0:T(4,128)(2,1)S(1)}, u32[]{:S(2)}, u32[]{:S(2)}) collective-permute-start(bf16[16,4,2304]{2,1,0:T(4,128)(2,1)S(1)} %add_convert_fusion.5), channel_id=1, source_target_pairs={{0,4},{4,8},{8,12},{1,5},{5,9},{9,13},{2,6},{6,10},{10,14},{3,7},{... | collective-permute-start | bytes 884744 | tf_op jit(solution)/shard_map/ppermute | solution.py:34
  258.0 13.0 %collective-permute-start.9 = (bf16[16,4,2304]{2,1,0:T(4,128)(2,1)}, bf16[16,4,2304]{2,1,0:T(4,128)(2,1)}, u32[]{:S(2)}, u32[]{:S(2)}) collective-permute-start(bf16[16,4,2304]{2,1,0:T(4,128)(2,1)} %add_convert_fusion.4), channel_id=1, source_target_pairs={{0,4},{4,8},{8,12},{1,5},{5,9},{9,13},{2,6},{6,10},{10,14},{3,7},{... | collective-permute-start | bytes 884744 | tf_op jit(solution)/shard_map/ppermute | solution.py:34
  276.3 82.1 %collective-permute-start.10 = (bf16[4,384,1152]{2,1,0:T(8,128)(2,1)}, bf16[4,384,1152]{2,1,0:T(8,128)(2,1)}, u32[]{:S(2)}, u32[]{:S(2)}) collective-permute-start(bf16[4,384,1152]{2,1,0:T(8,128)(2,1)} %collective-permute-done.2.refs_1_), channel_id=1, source_target_pairs={{0,4},{4,8},{8,12},{12,0},{1,5},{5,9},{9,13},{13,1},{2,6},{6,10},{... | collective-permute-start | bytes 10616840 | tf_op jit(solution)/shard_map/ppermute | solution.py:662
  279.7 78.8 %collective-permute-start.11 = (bf16[4,384,1152]{2,1,0:T(8,128)(2,1)}, bf16[4,384,1152]{2,1,0:T(8,128)(2,1)}, u32[]{:S(2)}, u32[]{:S(2)}) collective-permute-start(bf16[4,384,1152]{2,1,0:T(8,128)(2,1)} %collective-permute-done.2.refs_1_), channel_id=1, source_target_pairs={{0,16},{16,0},{1,17},{17,1},{2,18},{18,2},{3,19},{19,3},{4,20},{20... | collective-permute-start | bytes 10616840 | tf_op jit(solution)/shard_map/ppermute | solution.py:662
  358.4 77.6 %collective-permute-start.15 = (bf16[4,384,1152]{2,1,0:T(8,128)(2,1)}, bf16[4,384,1152]{2,1,0:T(8,128)(2,1)S(1)}, u32[]{:S(2)}, u32[]{:S(2)}) collective-permute-start(bf16[4,384,1152]{2,1,0:T(8,128)(2,1)} %collective-permute-done.10.refs_2_), channel_id=1, source_target_pairs={{0,4},{4,8},{8,12},{12,0},{1,5},{5,9},{9,13},{13,1},{2,6},{6,10},{... | collective-permute-start | bytes 10616840 | tf_op jit(solution)/shard_map/ppermute | solution.py:662
  358.8 77.3 %collective-permute-start.16 = (bf16[4,384,1152]{2,1,0:T(8,128)(2,1)}, bf16[4,384,1152]{2,1,0:T(8,128)(2,1)S(1)}, u32[]{:S(2)}, u32[]{:S(2)}) collective-permute-start(bf16[4,384,1152]{2,1,0:T(8,128)(2,1)} %collective-permute-done.10.refs_2_), channel_id=1, source_target_pairs={{0,16},{16,0},{1,17},{17,1},{2,18},{18,2},{3,19},{19,3},{4,20},{20... | collective-permute-start | bytes 10616840 | tf_op jit(solution)/shard_map/ppermute | solution.py:662
  366.5 24.6 %collective-permute-start.13 = (bf16[2,192,1280]{2,1,0:T(8,128)(2,1)S(1)}, bf16[2,192,1280]{2,1,0:T(8,128)(2,1)S(1)}, u32[]{:S(2)}, u32[]{:S(2)}) collective-permute-start(bf16[2,192,1280]{2,1,0:T(8,128)(2,1)S(1)} %bitcast.371), channel_id=1, source_target_pairs={{0,2},{1,3},{2,0},{3,1},{4,6},{5,7},{6,4},{7,5},{8,10},{9,11},{10,... | collective-permute-start | bytes 2949128 | tf_op jit(solution)/shard_map/ppermute | solution.py:667
  367.8 43.5 %collective-permute-start.14 = (bf16[2,192,1280]{2,1,0:T(8,128)(2,1)S(1)}, bf16[2,192,1280]{2,1,0:T(8,128)(2,1)S(1)}, u32[]{:S(2)}, u32[]{:S(2)}) collective-permute-start(bf16[2,192,1280]{2,1,0:T(8,128)(2,1)S(1)} %bitcast.370), channel_id=1, source_target_pairs={{0,3},{1,2},{2,1},{3,0},{4,7},{5,6},{6,5},{7,4},{8,11},{9,10},{10,... | collective-permute-start | bytes 2949128 | tf_op jit(solution)/shard_map/ppermute | solution.py:667
  437.6 50.6 %collective-permute-start.17 = (bf16[2,384,1152]{2,1,0:T(8,128)(2,1)}, bf16[2,384,1152]{2,1,0:T(8,128)(2,1)}, u32[]{:S(2)}, u32[]{:S(2)}) collective-permute-start(bf16[2,384,1152]{2,1,0:T(8,128)(2,1)} %slice.505), channel_id=1, source_target_pairs={{0,16},{16,0},{1,17},{17,1},{2,18},{18,2},{3,19},{19,3},{4,20},{20... | collective-permute-start | bytes 5308424 | tf_op jit(solution)/shard_map/ppermute | solution.py:662
  441.4 46.8 %collective-permute-start.18 = (bf16[2,384,1152]{2,1,0:T(8,128)(2,1)}, bf16[2,384,1152]{2,1,0:T(8,128)(2,1)}, u32[]{:S(2)}, u32[]{:S(2)}) collective-permute-start(bf16[2,384,1152]{2,1,0:T(8,128)(2,1)} %slice.506), channel_id=1, source_target_pairs={{0,4},{4,8},{8,12},{12,0},{1,5},{5,9},{9,13},{13,1},{2,6},{6,10},{... | collective-permute-start | bytes 5308424 | tf_op jit(solution)/shard_map/ppermute | solution.py:662
  520.2 30.6 %collective-permute-start.19 = (bf16[192,2304]{1,0:T(8,128)(2,1)}, bf16[192,2304]{1,0:T(8,128)(2,1)}, u32[]{:S(2)}, u32[]{:S(2)}) collective-permute-start(bf16[192,2304]{1,0:T(8,128)(2,1)} %get-tuple-element.489), channel_id=1, source_target_pairs={{0,1},{1,0},{2,3},{3,2},{4,5},{5,4},{6,7},{7,6},{8,9},{9,8},{10,11... | collective-permute-start | bytes 2654216 | tf_op jit(solution)/shard_map/ppermute | solution.py:667
  520.2 53.7 %collective-permute-start.20 = (bf16[192,2304]{1,0:T(8,128)(2,1)}, bf16[192,2304]{1,0:T(8,128)(2,1)}, u32[]{:S(2)}, u32[]{:S(2)}) collective-permute-start(bf16[192,2304]{1,0:T(8,128)(2,1)} %get-tuple-element.488), channel_id=1, source_target_pairs={{0,2},{1,3},{2,0},{3,1},{4,6},{5,7},{6,4},{7,5},{8,10},{9,11},{10,... | collective-permute-start | bytes 2654216 | tf_op jit(solution)/shard_map/ppermute | solution.py:667
  521.6 52.4 %collective-permute-start.21 = (bf16[192,2304]{1,0:T(8,128)(2,1)}, bf16[192,2304]{1,0:T(8,128)(2,1)}, u32[]{:S(2)}, u32[]{:S(2)}) collective-permute-start(bf16[192,2304]{1,0:T(8,128)(2,1)} %get-tuple-element.487), channel_id=1, source_target_pairs={{0,3},{1,2},{2,1},{3,0},{4,7},{5,6},{6,5},{7,4},{8,11},{9,10},{10,... | collective-permute-start | bytes 2654216 | tf_op jit(solution)/shard_map/ppermute | solution.py:667
  549.1 46.4 %collective-permute-start.22 = (bf16[192,2304]{1,0:T(8,128)(2,1)}, bf16[192,2304]{1,0:T(8,128)(2,1)}, u32[]{:S(2)}, u32[]{:S(2)}) collective-permute-start(bf16[192,2304]{1,0:T(8,128)(2,1)} %get-tuple-element.493), channel_id=1, source_target_pairs={{0,1},{1,0},{2,3},{3,2},{4,5},{5,4},{6,7},{7,6},{8,9},{9,8},{10,11... | collective-permute-start | bytes 2654216 | tf_op jit(solution)/shard_map/ppermute | solution.py:667
  549.4 46.1 %collective-permute-start.23 = (bf16[192,2304]{1,0:T(8,128)(2,1)}, bf16[192,2304]{1,0:T(8,128)(2,1)}, u32[]{:S(2)}, u32[]{:S(2)}) collective-permute-start(bf16[192,2304]{1,0:T(8,128)(2,1)} %get-tuple-element.492), channel_id=1, source_target_pairs={{0,2},{1,3},{2,0},{3,1},{4,6},{5,7},{6,4},{7,5},{8,10},{9,11},{10,... | collective-permute-start | bytes 2654216 | tf_op jit(solution)/shard_map/ppermute | solution.py:667
  550.8 48.3 %collective-permute-start.24 = (bf16[192,2304]{1,0:T(8,128)(2,1)}, bf16[192,2304]{1,0:T(8,128)(2,1)}, u32[]{:S(2)}, u32[]{:S(2)}) collective-permute-start(bf16[192,2304]{1,0:T(8,128)(2,1)} %get-tuple-element.491), channel_id=1, source_target_pairs={{0,3},{1,2},{2,1},{3,0},{4,7},{5,6},{6,5},{7,4},{8,11},{9,10},{10,... | collective-permute-start | bytes 2654216 | tf_op jit(solution)/shard_map/ppermute | solution.py:667
  624.0 42.4 %collective-permute-start.25 = (bf16[2,384,1152]{2,1,0:T(8,128)(2,1)}, bf16[2,384,1152]{2,1,0:T(8,128)(2,1)}, u32[]{:S(2)}, u32[]{:S(2)}) collective-permute-start(bf16[2,384,1152]{2,1,0:T(8,128)(2,1)} %pad_maximum_fusion.5), channel_id=1, source_target_pairs={{0,12},{4,0},{8,4},{12,8},{1,13},{5,1},{9,5},{13,9},{2,14},{6,2},{... | collective-permute-start | bytes 5308424 | tf_op jit(solution)/shard_map/ppermute | solution.py:662
  641.9 78.7 %collective-permute-start.26 = (bf16[4,384,1152]{2,1,0:T(8,128)(2,1)}, bf16[4,384,1152]{2,1,0:T(8,128)(2,1)}, u32[]{:S(2)}, u32[]{:S(2)}) collective-permute-start(bf16[4,384,1152]{2,1,0:T(8,128)(2,1)} %bitcast.397), channel_id=1, source_target_pairs={{0,16},{16,0},{1,17},{17,1},{2,18},{18,2},{3,19},{19,3},{4,20},{20... | collective-permute-start | bytes 10616840 | tf_op jit(solution)/shard_map/ppermute | solution.py:662
  669.6 42.4 %collective-permute-start.27 = (bf16[2,384,1152]{2,1,0:T(8,128)(2,1)}, bf16[2,384,1152]{2,1,0:T(8,128)(2,1)}, u32[]{:S(2)}, u32[]{:S(2)}) collective-permute-start(bf16[2,384,1152]{2,1,0:T(8,128)(2,1)} %add_convert_fusion.1), channel_id=1, source_target_pairs={{0,12},{4,0},{8,4},{12,8},{1,13},{5,1},{9,5},{13,9},{2,14},{6,2},{... | collective-permute-start | bytes 5308424 | tf_op jit(solution)/shard_map/ppermute | solution.py:662
  769.8 327.3 %reduce-scatter.6.cloned.1.call-start = ((), (), s32[]{:S(2)}) async-start(), calls=%async_computation.4 | async-start | bytes 5640192 | tf_op jit(solution)/shard_map/reduce_scatter | solution.py:970
  769.9 91.7 %collective-permute-start.32 = (bf16[4,384,1152]{2,1,0:T(8,128)(2,1)}, bf16[4,384,1152]{2,1,0:T(8,128)(2,1)}, u32[]{:S(2)}, u32[]{:S(2)}) collective-permute-start(bf16[4,384,1152]{2,1,0:T(8,128)(2,1)} %bitcast.396), channel_id=1, source_target_pairs={{0,16},{16,0},{1,17},{17,1},{2,18},{18,2},{3,19},{19,3},{4,20},{20... | collective-permute-start | bytes 10616840 | tf_op jit(solution)/shard_map/ppermute | solution.py:662
  774.3 87.2 %collective-permute-start.33 = (bf16[2,384,1152]{2,1,0:T(8,128)(2,1)}, bf16[2,384,1152]{2,1,0:T(8,128)(2,1)S(1)}, u32[]{:S(2)}, u32[]{:S(2)}) collective-permute-start(bf16[2,384,1152]{2,1,0:T(8,128)(2,1)} %add_convert_fusion), channel_id=1, source_target_pairs={{0,12},{4,0},{8,4},{12,8},{1,13},{5,1},{9,5},{13,9},{2,14},{6,2},{... | collective-permute-start | bytes 5308424 | tf_op jit(solution)/shard_map/ppermute | solution.py:662
  778.8 82.7 %collective-permute-start.31 = (bf16[384,1152]{1,0:T(8,128)(2,1)}, bf16[384,1152]{1,0:T(8,128)(2,1)}, u32[]{:S(2)}, u32[]{:S(2)}) collective-permute-start(bf16[384,1152]{1,0:T(8,128)(2,1)} %fusion.51), channel_id=1, source_target_pairs={{0,12},{4,0},{8,4},{12,8},{1,13},{5,1},{9,5},{13,9},{2,14},{6,2},{... | collective-permute-start | bytes 2654216 | tf_op jit(solution)/shard_map/ppermute | solution.py:662
  782.6 173.3 %collective-permute-start.36 = (bf16[4,384,1152]{2,1,0:T(8,128)(2,1)}, bf16[4,384,1152]{2,1,0:T(8,128)(2,1)}, u32[]{:S(2)}, u32[]{:S(2)}) collective-permute-start(bf16[4,384,1152]{2,1,0:T(8,128)(2,1)} %bitcast.395), channel_id=1, source_target_pairs={{0,16},{16,0},{1,17},{17,1},{2,18},{18,2},{3,19},{19,3},{4,20},{20... | collective-permute-start | bytes 10616840 | tf_op jit(solution)/shard_map/ppermute | solution.py:662
  863.0 92.9 %collective-permute-start.37 = (bf16[384,1152]{1,0:T(8,128)(2,1)}, bf16[384,1152]{1,0:T(8,128)(2,1)}, u32[]{:S(2)}, u32[]{:S(2)}) collective-permute-start(bf16[384,1152]{1,0:T(8,128)(2,1)} %fusion.59), channel_id=1, source_target_pairs={{0,16},{16,0},{1,17},{17,1},{2,18},{18,2},{3,19},{19,3},{4,20},{20... | collective-permute-start | bytes 2654216 | tf_op jit(solution)/shard_map/ppermute | solution.py:662
  866.8 89.1 %collective-permute-start.35 = (bf16[384,1152]{1,0:T(8,128)(2,1)}, bf16[384,1152]{1,0:T(8,128)(2,1)}, u32[]{:S(2)}, u32[]{:S(2)}) collective-permute-start(bf16[384,1152]{1,0:T(8,128)(2,1)} %fusion.48), channel_id=1, source_target_pairs={{0,12},{4,0},{8,4},{12,8},{1,13},{5,1},{9,5},{13,9},{2,14},{6,2},{... | collective-permute-start | bytes 2654216 | tf_op jit(solution)/shard_map/ppermute | solution.py:662
  871.6 84.3 %collective-permute-start.34 = (bf16[384,1152]{1,0:T(8,128)(2,1)}, bf16[384,1152]{1,0:T(8,128)(2,1)}, u32[]{:S(2)}, u32[]{:S(2)}) collective-permute-start(bf16[384,1152]{1,0:T(8,128)(2,1)} %fusion.50), channel_id=1, source_target_pairs={{0,12},{4,0},{8,4},{12,8},{1,13},{5,1},{9,5},{13,9},{2,14},{6,2},{... | collective-permute-start | bytes 2654216 | tf_op jit(solution)/shard_map/ppermute | solution.py:662
  882.9 303.7 %reduce-scatter.8.cloned.1.call-start = ((), (), s32[]{:S(2)}) async-start(), calls=%async_computation.5 | async-start | bytes 5640192 | tf_op jit(solution)/shard_map/reduce_scatter | solution.py:1011
  958.5 87.3 %collective-permute-start.40 = (bf16[384,1152]{1,0:T(8,128)(2,1)}, bf16[384,1152]{1,0:T(8,128)(2,1)}, u32[]{:S(2)}, u32[]{:S(2)}) collective-permute-start(bf16[384,1152]{1,0:T(8,128)(2,1)} %fusion.43), channel_id=1, source_target_pairs={{0,12},{4,0},{8,4},{12,8},{1,13},{5,1},{9,5},{13,9},{2,14},{6,2},{... | collective-permute-start | bytes 2654216 | tf_op jit(solution)/shard_map/ppermute | solution.py:662
  961.6 84.2 %collective-permute-start.39 = (bf16[384,1152]{1,0:T(8,128)(2,1)}, bf16[384,1152]{1,0:T(8,128)(2,1)}, u32[]{:S(2)}, u32[]{:S(2)}) collective-permute-start(bf16[384,1152]{1,0:T(8,128)(2,1)} %fusion.45), channel_id=1, source_target_pairs={{0,12},{4,0},{8,4},{12,8},{1,13},{5,1},{9,5},{13,9},{2,14},{6,2},{... | collective-permute-start | bytes 2654216 | tf_op jit(solution)/shard_map/ppermute | solution.py:662
  967.3 78.6 %collective-permute-start.38 = (bf16[384,1152]{1,0:T(8,128)(2,1)}, bf16[384,1152]{1,0:T(8,128)(2,1)}, u32[]{:S(2)}, u32[]{:S(2)}) collective-permute-start(bf16[384,1152]{1,0:T(8,128)(2,1)} %fusion.47), channel_id=1, source_target_pairs={{0,12},{4,0},{8,4},{12,8},{1,13},{5,1},{9,5},{13,9},{2,14},{6,2},{... | collective-permute-start | bytes 2654216 | tf_op jit(solution)/shard_map/ppermute | solution.py:662
  1048.8 55.2 %collective-permute-start.42 = (bf16[384,1152]{1,0:T(8,128)(2,1)}, bf16[384,1152]{1,0:T(8,128)(2,1)}, u32[]{:S(2)}, u32[]{:S(2)}) collective-permute-start(bf16[384,1152]{1,0:T(8,128)(2,1)} %fusion.40), channel_id=1, source_target_pairs={{0,12},{4,0},{8,4},{12,8},{1,13},{5,1},{9,5},{13,9},{2,14},{6,2},{... | collective-permute-start | bytes 2654216 | tf_op jit(solution)/shard_map/ppermute | solution.py:662
  1053.4 50.6 %collective-permute-start.41 = (bf16[384,1152]{1,0:T(8,128)(2,1)}, bf16[384,1152]{1,0:T(8,128)(2,1)}, u32[]{:S(2)}, u32[]{:S(2)}) collective-permute-start(bf16[384,1152]{1,0:T(8,128)(2,1)} %fusion.42), channel_id=1, source_target_pairs={{0,12},{4,0},{8,4},{12,8},{1,13},{5,1},{9,5},{13,9},{2,14},{6,2},{... | collective-permute-start | bytes 2654216 | tf_op jit(solution)/shard_map/ppermute | solution.py:662
  1107.2 72.9 %collective-permute-start.57 = (bf16[384,1152]{1,0:T(8,128)(2,1)}, bf16[384,1152]{1,0:T(8,128)(2,1)}, u32[]{:S(2)}, u32[]{:S(2)}) collective-permute-start(bf16[384,1152]{1,0:T(8,128)(2,1)} %fusion.34), channel_id=1, source_target_pairs={{0,12},{4,0},{8,4},{12,8},{1,13},{5,1},{9,5},{13,9},{2,14},{6,2},{... | collective-permute-start | bytes 2654216 | tf_op jit(solution)/shard_map/ppermute | solution.py:662
  1112.2 38.5 %collective-permute-start.54 = (bf16[2,2,72,256]{3,2,1,0:T(8,128)(2,1)S(1)}, bf16[2,2,72,256]{3,2,1,0:T(8,128)(2,1)S(1)}, u32[]{:S(2)}, u32[]{:S(2)}) collective-permute-start(bf16[2,2,72,256]{3,2,1,0:T(8,128)(2,1)S(1)} %fusion.77), channel_id=1, source_target_pairs={{0,16},{16,0},{1,17},{17,1},{2,18},{18,2},{3,19},{19,3},{4,20},{20... | collective-permute-start | bytes 442376 | tf_op jit(solution)/shard_map/ppermute | solution.py:667
  1137.3 16.7 %collective-permute-start.44 = (f32[180,128]{1,0:T(8,128)S(1)}, f32[180,128]{1,0:T(8,128)S(1)}, u32[]{:S(2)}, u32[]{:S(2)}) collective-permute-start(f32[180,128]{1,0:T(8,128)S(1)} %maximum_bitcast_fusion.5), channel_id=1, source_target_pairs={{0,16},{16,0},{1,17},{17,1},{2,18},{18,2},{3,19},{19,3},{4,20},{20... | collective-permute-start | bytes 276488 | tf_op jit(solution)/shard_map/ppermute | solution.py:667
  1154.6 12.9 %collective-permute-start.46 = (f32[180,128]{1,0:T(8,128)S(1)}, f32[180,128]{1,0:T(8,128)S(1)}, u32[]{:S(2)}, u32[]{:S(2)}) collective-permute-start(f32[180,128]{1,0:T(8,128)S(1)} %fusion.171), channel_id=1, source_target_pairs={{0,8},{4,12},{8,0},{12,4},{1,9},{5,13},{9,1},{13,5},{2,10},{6,14},... | collective-permute-start | bytes 276488 | tf_op jit(solution)/shard_map/ppermute | solution.py:667
  (110 other events, 1920.6 us)
Sparse Core Ops, SparseCore 0:
  14.8 111.7 all-gather.5
  129.4 135.7 all-gather.3
  769.9 152.5 reduce-scatter.9
  926.4 132.5 reduce-scatter.5
  1099.0 87.6 reduce-scatter.7
